TPU v7x, 256 devices: a whole 4x4x8 slice. The times are simulated.
256 devices in a mesh: cfg: 2 (over core), seq: 16 (over x_hi, z), fsdp: 8 (over y, x_lo).
Axes of the slice: x: 4 (x_hi: 2, x_lo: 2; x = x_hi * 2 + x_lo), y: 4, z: 8, core: 2. Of those that a mesh axis runs over, the one named last changes fastest.
Arguments:
- queries: bfloat16 [2, 1024, 4096], P('cfg', None, 'seq'), may hold values from -6 to 6
- key_vectors: bfloat16 [2, 16384, 4096], P('cfg', ('seq', 'fsdp')), may hold values from -6 to 6
- value_vectors: bfloat16 [2, 16384, 4096], P('cfg', ('seq', 'fsdp')), may hold values from -6 to 6
- cotangent: bfloat16 [1024, 5120], P(None, 'fsdp'), may hold values from -600 to 600
- out_weight: bfloat16 [4096, 5120], P('seq', 'fsdp'), may hold values from -0.09375 to 0.09375
- frame_valid: int32 [5], replicated, may hold values from 0 to 1, as said below
- group_offset: int32 [1], replicated, may hold values from 0 to 15360
- guide_index: int32 [1], replicated, may hold values from 0 to 4096
Outputs:
- query_grad: bfloat16 [2, 1024, 4096], P('cfg', 'fsdp', 'seq')
- key_grad: bfloat16 [2, 16384, 4096], P('cfg', ('seq', 'fsdp'))
- value_grad: bfloat16 [2, 16384, 4096], P('cfg', ('seq', 'fsdp'))
- weight_grad: float32 [4096, 5120], P('seq', 'fsdp')
Inputs may be any that keep to these rules, and one draw needn't show every extreme that they name: `frame_valid`: at least one frame is valid and at least one frame is not.
All inputs are finite; a program needn't handle non-finite values.
Results may differ from a plain program's by a relative error of at most 0.03.
Values may be sent and summed in bfloat16 or wider, within the bound.
No kernel may reach another device: no remote copies, remote signals or barrier semaphores. Data moves between devices by JAX's collectives and lax.ppermute only.
A program may use at most 128 MiB of HBM per device.

v0:
```python
import math

import jax
import jax.numpy as jnp
from jax import lax
from jax.sharding import PartitionSpec as P

HEAD_DIM = 128
FRAME_TOK = 3600


NEG_LARGE = -1e30
LOSS_SCALE = 128.0


def joined(x, axis, combine):
    everything = jax.tree.map(lambda part: lax.all_gather(part, axis), x)
    initial = jax.tree.map(lambda part: part[0], everything)

    def step(k, so_far):
        return combine(so_far, jax.tree.map(lambda part: part[k], everything))

    return lax.fori_loop(1, lax.axis_size(axis), step, initial)


def rotate_back(gradient, positions, head_dim):
    row_count = gradient.shape[0]
    full_width = gradient.shape[1]
    half_dim = head_dim // 2
    shaped = gradient.reshape(row_count, full_width // head_dim, head_dim)
    frequency = 10000.0 ** (-jnp.arange(half_dim, dtype=jnp.float32) / half_dim)
    angles = positions.astype(jnp.float32)[:, None] * frequency[None, :]
    cosine = jnp.cos(angles)[:, None, :]
    sine_part = jnp.sin(angles)[:, None, :]
    first_half = shaped[:, :, :half_dim]
    second = shaped[:, :, half_dim:]
    turned = jnp.concatenate(
        [first_half * cosine + second * sine_part, second * cosine - first_half * sine_part], axis=2
    )
    return turned.reshape(row_count, full_width)


def merge_parts(first_part, second_part):
    top_max = jnp.maximum(first_part[0], second_part[0])
    first_factor = jnp.exp(first_part[0] - top_max)
    second_factor = jnp.exp(second_part[0] - top_max)
    total_sum = first_part[1] * first_factor + second_part[1] * second_factor
    output = (
        first_part[2] * first_factor.T[:, :, None] + second_part[2] * second_factor.T[:, :, None]
    )
    merged = (top_max, total_sum, output)
    if len(first_part) > 3:
        merged = merged + (first_part[3] + second_part[3],)
    return merged


def heads_last(stacked, branch_count, head_count):
    row_total = stacked.shape[1]
    return (
        stacked.reshape(branch_count, row_total, head_count, HEAD_DIM)
        .transpose(1, 0, 2, 3)
        .reshape(row_total, branch_count * head_count, HEAD_DIM)
    )


def branches_first(stacked, branch_count, head_count):
    row_total = stacked.shape[0]
    return (
        stacked.reshape(row_total, branch_count, head_count, HEAD_DIM)
        .transpose(1, 0, 2, 3)
        .reshape(branch_count, row_total, head_count * HEAD_DIM)
    )


def per_device(
    queries,
    key_vectors,
    value_vectors,
    cotangent,
    out_weight,
    frame_valid,
    group_offset,
    guide_index,
):
    fsdp_index = lax.axis_index("fsdp")
    branch_index = lax.axis_index("cfg")
    fsdp_count = lax.axis_size("fsdp")
    branch_count = queries.shape[0]
    group_rows = queries.shape[1]
    local_width = queries.shape[2]
    head_count = local_width // HEAD_DIM
    all_heads = branch_count * head_count
    scale_factor = 1.0 / math.sqrt(HEAD_DIM)
    guide_scale = 1.5 + guide_index[0].astype(jnp.float32) / 1024.0
    branch_ids = branch_index * branch_count + jnp.arange(branch_count, dtype=jnp.int32)
    own_weights = jnp.where(branch_ids == 0, guide_scale, 1.0 - guide_scale)
    partial_upstream = lax.dot_general(
        cotangent, out_weight, (((1,), (1,)), ((), ())), preferred_element_type=jnp.float32
    )
    upstream_total = lax.psum(partial_upstream.astype(jnp.bfloat16), "fsdp").astype(jnp.float32)
    shard_rows = key_vectors.shape[1]
    gathered_keys, gathered_values = (
        lax.all_to_all(key_vectors, "seq", split_axis=2, concat_axis=1, tiled=True),
        lax.all_to_all(value_vectors, "seq", split_axis=2, concat_axis=1, tiled=True),
    )
    local_keys = gathered_keys.shape[1]
    block_rows = min(1024, local_keys)
    block_count = local_keys // block_rows
    local_index = jnp.arange(local_keys, dtype=jnp.int32)
    global_rows = (
        local_index // shard_rows * fsdp_count + fsdp_index
    ) * shard_rows + local_index % shard_rows
    frame_ids = global_rows // FRAME_TOK
    frame_match = frame_ids[:, None] == jnp.arange(frame_valid.shape[0], dtype=jnp.int32)[None, :]
    key_valid = jnp.sum(jnp.where(frame_match, frame_valid[None, :], 0), axis=1) == 1
    key_blocks = heads_last(gathered_keys, branch_count, head_count).reshape(
        block_count, block_rows, all_heads, HEAD_DIM
    )
    value_blocks = heads_last(gathered_values, branch_count, head_count).reshape(
        block_count, block_rows, all_heads, HEAD_DIM
    )
    valid_blocks = key_valid.reshape(block_count, block_rows)
    query_heads = heads_last(queries, branch_count, head_count)

    def forward_block(state_now, block_data):
        run_max, run_sum, run_out = state_now
        block_keys, block_values, block_valid = block_data
        scores = (
            jnp.einsum("qhd,khd->hqk", query_heads, block_keys, preferred_element_type=jnp.float32)
            * scale_factor
        )
        masked = jnp.where(block_valid[None, None, :], scores, NEG_LARGE)
        new_max = jnp.maximum(run_max, jnp.max(masked, axis=2))
        weights = jnp.where(block_valid[None, None, :], jnp.exp(masked - new_max[:, :, None]), 0.0)
        factor = jnp.exp(run_max - new_max)
        new_sum = run_sum * factor + jnp.sum(weights, axis=2)
        contrib = jnp.einsum(
            "hqk,khd->qhd",
            weights.astype(jnp.bfloat16),
            block_values,
            preferred_element_type=jnp.float32,
        )
        new_out = run_out * factor.T[:, :, None] + contrib
        return ((new_max, new_sum, new_out), None)

    start_state = (
        jnp.full((all_heads, group_rows), NEG_LARGE, jnp.float32),
        jnp.zeros((all_heads, group_rows), jnp.float32),
        jnp.zeros((group_rows, all_heads, HEAD_DIM), jnp.float32),
    )
    local_stats, _ = lax.scan(forward_block, start_state, (key_blocks, value_blocks, valid_blocks))
    glob_max, glob_sum, glob_out = joined(
        (local_stats[0], local_stats[1], local_stats[2]), "fsdp", merge_parts
    )
    attn_out = (glob_out / glob_sum.T[:, :, None]).astype(jnp.bfloat16)
    attn_branches = branches_first(
        attn_out.reshape(group_rows, all_heads * HEAD_DIM), branch_count, head_count
    )
    upstream_branches = (own_weights[:, None, None] * upstream_total[None]).astype(jnp.bfloat16)
    upstream = heads_last(upstream_branches, branch_count, head_count)
    row_delta = jnp.sum(upstream.astype(jnp.float32) * attn_out.astype(jnp.float32), axis=2).T

    def backward_block(query_acc, block_data):
        block_keys, block_values, block_valid = block_data
        scores = (
            jnp.einsum("qhd,khd->hqk", query_heads, block_keys, preferred_element_type=jnp.float32)
            * scale_factor
        )
        probability = (
            jnp.where(block_valid[None, None, :], jnp.exp(scores - glob_max[:, :, None]), 0.0)
            / glob_sum[:, :, None]
        )
        value_part = jnp.einsum(
            "hqk,qhd->khd",
            probability.astype(jnp.bfloat16),
            upstream,
            preferred_element_type=jnp.float32,
        )
        prob_grad = jnp.einsum(
            "qhd,khd->hqk", upstream, block_values, preferred_element_type=jnp.float32
        )
        score_grad = (probability * (prob_grad - row_delta[:, :, None]) * scale_factor).astype(
            jnp.bfloat16
        )
        query_acc = query_acc + jnp.einsum(
            "hqk,khd->qhd", score_grad, block_keys, preferred_element_type=jnp.float32
        )
        key_part = jnp.einsum(
            "hqk,qhd->khd", score_grad, query_heads, preferred_element_type=jnp.float32
        )
        return (query_acc, (key_part, value_part))

    query_partial, block_grads = lax.scan(
        backward_block,
        jnp.zeros((group_rows, all_heads, HEAD_DIM), jnp.float32),
        (key_blocks, value_blocks, valid_blocks),
    )
    key_branches = branches_first(
        block_grads[0].reshape(local_keys, all_heads * HEAD_DIM), branch_count, head_count
    )
    key_rotated = jax.vmap(lambda grads: rotate_back(grads, global_rows, HEAD_DIM))(
        key_branches
    ).astype(jnp.bfloat16)
    value_branches = branches_first(
        block_grads[1].reshape(local_keys, all_heads * HEAD_DIM), branch_count, head_count
    ).astype(jnp.bfloat16)
    key_back, value_back = (
        lax.all_to_all(key_rotated, "seq", split_axis=1, concat_axis=2, tiled=True),
        lax.all_to_all(value_branches, "seq", split_axis=1, concat_axis=2, tiled=True),
    )
    query_branches = branches_first(
        query_partial.reshape(group_rows, all_heads * HEAD_DIM), branch_count, head_count
    )
    query_share = lax.psum_scatter(
        query_branches.astype(jnp.bfloat16), "fsdp", scatter_dimension=1, tiled=True
    ).astype(jnp.float32)
    share_rows = query_share.shape[1]
    query_positions = (
        group_offset[0] + fsdp_index * share_rows + jnp.arange(share_rows, dtype=jnp.int32)
    )
    query_grad = jax.vmap(lambda grads: rotate_back(grads, query_positions, HEAD_DIM))(
        query_share
    ).astype(jnp.bfloat16)
    own_term = sum(
        (
            own_weights[branch]
            * jnp.dot(attn_branches[branch].T, cotangent, preferred_element_type=jnp.float32)
            for branch in range(branch_count)
        )
    )
    weight_total = lax.psum(own_term.astype(jnp.bfloat16), "cfg").astype(jnp.float32)
    weight_grad = weight_total / LOSS_SCALE
    return (query_grad, key_back, value_back, weight_grad)


def solution(mesh):
    placed = (
        P("cfg", None, "seq"),
        P("cfg", ("seq", "fsdp"), None),
        P("cfg", ("seq", "fsdp"), None),
        P(None, "fsdp"),
        P("seq", "fsdp"),
        P(),
        P(),
        P(),
    )
    return jax.shard_map(
        per_device,
        mesh=mesh,
        in_specs=placed,
        out_specs=(
            P("cfg", "fsdp", "seq"),
            P("cfg", ("seq", "fsdp"), None),
            P("cfg", ("seq", "fsdp"), None),
            P("seq", "fsdp"),
        ),
        check_vma=False,
    )
```

profile of v0, /device:TPU:32, one launch (start us, length us, event | category | flops | bytes accessed | tf_op | source)
XLA Modules:
  0.0 664.4 jit_solution(14503719105245218973)
XLA Ops:
  7.2 5.1 copy.132
  12.9 23.3 %reduce.4 = bf16[4096,128]{1,0:T(8,128)(2,1)} reduce(bf16[4096,1,128]{2,1,0:T(2,128)(2,1)S(1)} %bitcast.202, bf16[]{:T(256)} %broadcast.335), dimensions={1}, to_apply=%bitcast.124.reduce_sub_computation | reduce | bytes 2097154
  38.3 11.0 %all-to-all-start = ((bf16[16,2,16384]{2,1,0:T(2,128)(2,1)}), bf16[16,2,16384]{2,1,0:T(2,128)(2,1)}, u32[]{:S(2)}, u32[]{:S(2)}) async-start(bf16[16,2,16384]{2,1,0:T(2,128)(2,1)} %reshape.288), calls=%async_computation | async-start | bytes 2097152 | tf_op jit(solution)/shard_map/all_to_all | solution.py:103
  49.4 5.0 copy.135
  54.4 23.4 %reduce.5 = bf16[4096,128]{1,0:T(8,128)(2,1)} reduce(bf16[4096,1,128]{2,1,0:T(2,128)(2,1)S(1)} %bitcast.205, bf16[]{:T(256)} %broadcast.335), dimensions={1}, to_apply=%bitcast.126.reduce_sub_computation | reduce | bytes 2097154
  80.0 9.6 %all-to-all-start.1 = ((bf16[16,2,16384]{2,1,0:T(2,128)(2,1)}), bf16[16,2,16384]{2,1,0:T(2,128)(2,1)}, u32[]{:S(2)}, u32[]{:S(2)}) async-start(bf16[16,2,16384]{2,1,0:T(2,128)(2,1)} %reshape.290), calls=%async_computation.1 | async-start | bytes 2097152 | tf_op jit(solution)/shard_map/all_to_all | solution.py:104
  92.3 5.8 reshape.289
  104.6 12.5 %all-to-all-done.1 = bf16[16,2,16384]{2,1,0:T(2,128)(2,1)} async-done(((bf16[16,2,16384]{2,1,0:T(2,128)(2,1)}), bf16[16,2,16384]{2,1,0:T(2,128)(2,1)}, u32[]{:S(2)}, u32[]{:S(2)}) %all-to-all-start.1) | async-done | bytes 1048608 | tf_op jit(solution)/shard_map/all_to_all | solution.py:104
  117.1 5.8 reshape.291
  130.0 36.6 %while.50 = (s32[]{:T(128)}, f32[2,1024]{1,0:T(2,128)S(1)}, f32[2,1024]{1,0:T(2,128)S(1)}, f32[1024,2,128]{0,2,1:T(8,128)}, pred[2,1024]{1,0:T(4,128)(4,1)S(1)},...) while((s32[]{:T(128)}, f32[2,1024]{1,0:T(2,128)S(1)}, ...), condition=%wide.region_4.5_spmd.clone, body=%wide.region_1.4_spmd.clone.sunk | while | flops 1101803520 | bytes 31069308 | solution.py:151
  130.0 4.1 bitcast_reduce_fusion.2
  136.6 6.8 %fusion.106 = f32[1024,2,128]{0,2,1:T(8,128)} fusion(f32[2,1024,1024]{2,1,0:T(8,128)} %get-tuple-element.784, f32[2,1024]{1,0:T(2,128)S(1)} %get-tuple-element.819, pred[1024]{0:T(1024)(128)(4,1)S(1)} %dynamic-slice_reduce_fusion.4, f32[1024,2,128]{0,2,1:T(8,128)} %get-tuple-element.811, bf16[1,1024,2,128]{1,3,2,0:T(8,128)(2,1)} %copy.191, ...), kind=kOutput, calls=%fused_computation.21.clone.1 | convolution fusion | flops 548143104 | bytes 11027457 | tf_op jit(solution)/shard_map/while/body/eval_jaxpr/hqk,khd->qhd/dot_general | solution.py:137
  143.4 4.6 fusion.104
  148.1 4.1 bitcast_reduce_fusion.2
  154.8 7.1 %fusion.106 = f32[1024,2,128]{0,2,1:T(8,128)} fusion(f32[2,1024,1024]{2,1,0:T(8,128)} %get-tuple-element.784, f32[2,1024]{1,0:T(2,128)S(1)} %get-tuple-element.819, pred[1024]{0:T(1024)(128)(4,1)S(1)} %dynamic-slice_reduce_fusion.4, f32[1024,2,128]{0,2,1:T(8,128)} %get-tuple-element.811, bf16[1,1024,2,128]{1,3,2,0:T(8,128)(2,1)} %copy.191, ...), kind=kOutput, calls=%fused_computation.21.clone.1 | convolution fusion | flops 548143104 | bytes 11027457 | tf_op jit(solution)/shard_map/while/body/eval_jaxpr/hqk,khd->qhd/dot_general | solution.py:137
  161.8 4.6 fusion.104
  168.2 5.5 multiply_cosine_fusion
  173.7 4.3 all-reduce.3.cloned.1.call-done
  181.2 28.3 %all-gather.4 = f32[8,2,1024]{2,1,0:T(2,128)S(1)} all-gather(f32[1,2,1024]{2,1,0:T(2,128)S(1)} %bitcast.221), channel_id=3, replica_groups=mesh['cfg'=2,'seq'=16,'fsdp'=8] {'fsdp'}, dimensions={0}, use_global_device_ids=true | all-gather | bytes 73728 | tf_op jit(solution)/shard_map/all_gather | solution.py:17
  209.4 28.4 %all-gather.3 = f32[8,2,1024]{2,1,0:T(2,128)S(1)} all-gather(f32[1,2,1024]{2,1,0:T(2,128)S(1)} %bitcast.218), channel_id=2, replica_groups=mesh['cfg'=2,'seq'=16,'fsdp'=8] {'fsdp'}, dimensions={0}, use_global_device_ids=true | all-gather | bytes 73728 | tf_op jit(solution)/shard_map/all_gather | solution.py:17
  237.9 114.4 %all-gather.7.cloned.1.call-done = f32[8192,2,128]{0,2,1:T(8,128)} async-done(((f32[1024,2,128]{0,2,1:T(8,128)}), f32[8192,2,128]{0,2,1:T(8,128)}) %all-gather.7.cloned.1.call-update) | async-done | bytes 8388624 | tf_op jit(solution)/shard_map/all_gather | solution.py:17
  356.9 13.1 %copy.160 = f32[8192,2,128]{2,1,0:T(2,128)} copy(f32[8192,2,128]{0,2,1:T(8,128)} %all-gather.7.cloned.1.call-done) | data formatting | bytes 16777216 | tf_op jit(solution)/shard_map/while | solution.py:23
  370.0 61.9 %while.49 = (s32[]{:T(128)}, f32[2,1024]{1,0:T(2,128)S(1)}, f32[2,1024]{1,0:T(2,128)S(1)}, f32[1024,2,128]{2,1,0:T(2,128)}, f32[8,2,1024]{2,1,0:T(2,128)S(1)}, /...) while((s32[]{:T(128)}, f32[2,1024]{1,0:T(2,128)S(1)}, ...), condition=%wide.region_6.7_spmd, body=%wide.region_5.6_spmd.sunk | while | flops 800773 | bytes 3301531 | solution.py:23
  372.9 6.0 fusion.99
  381.7 6.0 fusion.99
  390.6 6.0 fusion.99
  399.4 6.0 fusion.99
  408.2 6.0 fusion.99
  417.1 6.0 fusion.99
  425.9 6.0 fusion.99
  433.0 17.0 %multiply_reduce_fusion = (f32[1024,2]{1,0:T(8,128)}, bf16[1024,2,128]{2,1,0:T(2,128)(2,1)}) fusion(bf16[1024,2,128]{2,1,0:T(2,128)(2,1)} %reshape_transpose_reshape.7, f32[1024,2,128]{2,1,0:T(2,128)} %get-tuple-element.295, f32[1024,2]{1,0:T(8,128)} %copy.142), kind=kLoop, calls=%fused_computation.66 | loop fusion | flops 1570816 | bytes 2113536 | tf_op jit(solution)/shard_map/reduce_sum | solution.py:161
  451.2 35.3 %while.51 = (s32[]{:T(128)}, f32[1024,2,128]{0,2,1:T(8,128)S(1)}, f32[2,1024,2,128]{3,1,0,2:T(8,128)}, bf16[2,1024,2,128]{3,1,2,0:T(8,128)(2,1)}, bf16[2,1024,2,...) while((s32[]{:T(128)}, f32[1024,2,128]{0,2,1:T(8,128)S(1)}, ...), condition=%wide.region_10.11_spmd.clone, body=%wide.region_9.10_spmd.clone.sunk | while | flops 2703753216 | bytes 134771968 | solution.py:193
  451.2 3.4 select_divide_fusion.2
  462.0 3.4 fusion.116
  468.9 3.4 select_divide_fusion.2
  479.7 3.4 fusion.116
  486.5 3.5 add_convert_fusion
  493.9 5.9 copy.151
  499.8 12.8 %reduce.6 = bf16[2048,256]{1,0:T(8,128)(2,1)} reduce(bf16[2048,1,256]{2,1,0:T(2,128)(2,1)} %bitcast.204, bf16[]{:T(256)} %broadcast.335), dimensions={1}, to_apply=%bitcast.128.reduce_sub_computation | reduce | bytes 2097154
  514.7 9.6 %all-to-all-start.2 = ((bf16[16,2,16384]{2,1,0:T(2,128)(2,1)}), bf16[16,2,16384]{2,1,0:T(2,128)(2,1)}, u32[]{:S(2)}, u32[]{:S(2)}) async-start(bf16[16,2,16384]{2,1,0:T(2,128)(2,1)} %reshape.292), calls=%async_computation.2 | async-start | bytes 2097152 | tf_op jit(solution)/shard_map/all_to_all | solution.py:208
  524.4 3.3 copy.153
  527.6 7.4 %convert_element_type.127 = bf16[1,2048,256]{2,0,1:T(2,128)(2,1)} reshape(bf16[2,1024,2,128]{3,2,1,0:T(2,128)(2,1)} %copy.153) | data formatting | bytes 2097152 | tf_op jit(solution)/shard_map/convert_element_type | solution.py:206
  535.0 12.6 %reduce.7 = bf16[2048,256]{1,0:T(8,128)(2,1)} reduce(bf16[2048,1,256]{2,1,0:T(2,128)(2,1)} %bitcast.203, bf16[]{:T(256)} %broadcast.335), dimensions={1}, to_apply=%bitcast.130.reduce_sub_computation | reduce | bytes 2097154
  552.2 7.2 %all-to-all-start.3 = ((bf16[16,2,16384]{2,1,0:T(2,128)(2,1)}), bf16[16,2,16384]{2,1,0:T(2,128)(2,1)}, u32[]{:S(2)}, u32[]{:S(2)}) async-start(bf16[16,2,16384]{2,1,0:T(2,128)(2,1)} %reshape.294), calls=%async_computation.3 | async-start | bytes 2097152 | tf_op jit(solution)/shard_map/all_to_all | solution.py:209
  563.6 30.3 %all-reduce.5.cloned.1.call-done = bf16[256,640]{1,0:T(8,128)(2,1)} async-done(((bf16[256,640]{1,0:T(8,128)(2,1)}), bf16[256,640]{1,0:T(8,128)(2,1)}) %all-reduce.5.cloned.1.call-update) | async-done | bytes 327696 | tf_op jit(solution)/shard_map/psum | solution.py:231
  595.7 43.3 %reduce-scatter.4.cloned.1.call-done = bf16[128,256]{1,0:T(8,128)(2,1)} async-done(((bf16[1024,256]{1,0:T(8,128)(2,1)}), bf16[128,256]{1,0:T(8,128)(2,1)}) %reduce-scatter.4.cloned.1.call-update) | async-done | bytes 65552
  640.9 4.3 reshape.293
  649.3 4.3 reshape.295
  (154 shorter events, 104.6 us)
Async XLA Ops:
  7.2 82.5 %copy-start = (bf16[1024,640]{1,0:T(8,128)(2,1)S(1)}, bf16[1024,640]{1,0:T(8,128)(2,1)}, u32[]{:S(2)}) copy-start(bf16[1024,640]{1,0:T(8,128)(2,1)} %param.17) | copy-start | bytes 3932164
  38.3 41.7 %all-to-all-start = ((bf16[16,2,16384]{2,1,0:T(2,128)(2,1)}), bf16[16,2,16384]{2,1,0:T(2,128)(2,1)}, u32[]{:S(2)}, u32[]{:S(2)}) async-start(bf16[16,2,16384]{2,1,0:T(2,128)(2,1)} %reshape.288), calls=%async_computation | async-start | bytes 2097152 | tf_op jit(solution)/shard_map/all_to_all | solution.py:103
  77.8 11.9 %copy-start.10 = (bf16[256,640]{1,0:T(8,128)(2,1)S(1)}, bf16[256,640]{1,0:T(8,128)(2,1)}, u32[]{:S(2)}) copy-start(bf16[256,640]{1,0:T(8,128)(2,1)} %param.18) | copy-start | bytes 983044
  77.8 13.9 %copy-start.9 = (s32[5]{0:T(128)S(1)}, s32[5]{0:T(128)}, u32[]{:S(2)}) copy-start(s32[5]{0:T(128)} %param.19) | copy-start | bytes 64
  77.8 14.0 %copy-start.6 = (bf16[1,1024,256]{2,1,0:T(8,128)(2,1)S(1)}, bf16[1,1024,256]{2,1,0:T(8,128)(2,1)}, u32[]{:S(2)}) copy-start(bf16[1,1024,256]{2,1,0:T(8,128)(2,1)} %param.14) | copy-start | bytes 1572868
  80.0 37.1 %all-to-all-start.1 = ((bf16[16,2,16384]{2,1,0:T(2,128)(2,1)}), bf16[16,2,16384]{2,1,0:T(2,128)(2,1)}, u32[]{:S(2)}, u32[]{:S(2)}) async-start(bf16[16,2,16384]{2,1,0:T(2,128)(2,1)} %reshape.290), calls=%async_computation.1 | async-start | bytes 2097152 | tf_op jit(solution)/shard_map/all_to_all | solution.py:104
  89.6 88.3 %all-reduce.3.cloned.1.call-start = ((), (), s32[]{:S(2)}) async-start(), calls=%async_computation.5 | async-start | bytes 1048576 | tf_op jit(solution)/shard_map/psum | solution.py:100
  91.1 261.2 %all-gather.7.cloned.1.call-start = ((), (), s32[]{:S(2)}) async-start(), calls=%async_computation.7 | async-start | bytes 9437184 | tf_op jit(solution)/shard_map/all_gather | solution.py:17
  166.5 1.0 copy-start.4
  209.4 28.4 %copy-start.8 = (f32[8,2,1024]{2,1,0:T(2,128)}, f32[8,2,1024]{2,1,0:T(2,128)S(1)}, u32[]{:S(2)}) copy-start(f32[8,2,1024]{2,1,0:T(2,128)S(1)} %all-gather.4) | copy-start | bytes 196612
  451.2 3.4 copy-start.5
  454.6 3.2 copy-start.2
  457.8 2.0 copy-start.1
  462.0 4.8 copy-start.3
  468.9 3.4 copy-start.5
  472.3 3.2 copy-start.2
  475.5 2.0 copy-start.1
  479.7 4.8 copy-start.3
  514.7 37.5 %all-to-all-start.2 = ((bf16[16,2,16384]{2,1,0:T(2,128)(2,1)}), bf16[16,2,16384]{2,1,0:T(2,128)(2,1)}, u32[]{:S(2)}, u32[]{:S(2)}) async-start(bf16[16,2,16384]{2,1,0:T(2,128)(2,1)} %reshape.292), calls=%async_computation.2 | async-start | bytes 2097152 | tf_op jit(solution)/shard_map/all_to_all | solution.py:208
  535.0 24.5 %copy-start.7 = (bf16[1024,2,128]{2,1,0:T(2,128)(2,1)S(1)}, bf16[1024,2,128]{2,1,0:T(2,128)(2,1)}, u32[]{:S(2)}) copy-start(bf16[1024,2,128]{2,1,0:T(2,128)(2,1)} %get-tuple-element.602) | copy-start | bytes 1572868
  552.2 97.0 %all-to-all-start.3 = ((bf16[16,2,16384]{2,1,0:T(2,128)(2,1)}), bf16[16,2,16384]{2,1,0:T(2,128)(2,1)}, u32[]{:S(2)}, u32[]{:S(2)}) async-start(bf16[16,2,16384]{2,1,0:T(2,128)(2,1)} %reshape.294), calls=%async_computation.3 | async-start | bytes 2097152 | tf_op jit(solution)/shard_map/all_to_all | solution.py:209
  559.5 34.4 %all-reduce.5.cloned.1.call-start = ((), (), s32[]{:S(2)}) async-start(), calls=%async_computation.6 | async-start | bytes 655360 | tf_op jit(solution)/shard_map/psum | solution.py:231
  560.9 78.1 %reduce-scatter.4.cloned.1.call-start = ((), (), s32[]{:S(2)}) async-start(), calls=%async_computation.8 | async-start | bytes 589824
Sparse Core Ops, SparseCore 0:
  93.7 84.2 all-reduce.2
  180.5 171.7 all-gather.6
  563.6 30.2 all-reduce.4
  596.8 42.1 reduce-scatter.3
where the time goes:
time: 676 us; the launch traced here: 664 us
  waiting for transfers between devices  207 us (31%)
  other arithmetic  161 us (24%)
  local copies, waits for them, and re-layouts  136 us (20%)
  blocking collectives  56.7 us (8%)
  matrix products  49.5 us (7%)
  starting transfers between devices  38.2 us (6%)
  between operations  15.6 us (2%)
    all_gather x1, waiting for transfers between devices, joined(): everything = jax.tree.map(lambda part: lax.all_gather(part, axis), x)  114 us
    unnamed x9, other arithmetic  73.3 us
    all_gather x2, blocking collectives, joined(): everything = jax.tree.map(lambda part: lax.all_gather(part, axis), x)  56.7 us
    unnamed x39, local copies, waits for them, and re-layouts  55.6 us
    unnamed x5, waiting for transfers between devices  43.3 us
    add x7, other arithmetic, merge_parts(): first_part[2] * first_factor.T[:, :, None]  42 us
    psum x1, waiting for transfers between devices, per_device(): lax.psum(own_term.astype(jnp.bfloat16), 'cfg').astype(jnp.float32)  30.3 us
    reduce_sum x1, other arithmetic, per_device(): jnp.sum(upstream.astype(jnp.float32) * attn_out.astype(jnp.float32), axis=2)  17 us
  transfers between devices with their start and end apart: 8, of which 6 were waited for; matrix products, arithmetic and copies ran while one was open for 22% of the time, Pallas kernels for 0%

commit v1 on v0

v1 whole, which is shorter than its diff:
```python
import math

import jax
import jax.numpy as jnp
from jax import lax
from jax.experimental import pallas as pl
from jax.experimental.pallas import tpu as pltpu
from jax.sharding import PartitionSpec as P

HEAD_DIM = 128
FRAME_TOK = 3600
NEG_LARGE = -1e30
NEG_FLOOR = -1e29
LOSS_SCALE = 128.0
SCALE = 1.0 / math.sqrt(HEAD_DIM)
EXP2_SCALE = SCALE * math.log2(math.e)
BF16 = jnp.bfloat16
F32 = jnp.float32
MIB = 1024 * 1024

NT = (((1,), (1,)), ((), ()))
TN = (((0,), (0,)), ((), ()))


def matmul(a, b, dims=(((1,), (0,)), ((), ()))):
    return lax.dot_general(a, b, dims, preferred_element_type=F32)


def params(mib):
    return pltpu.CompilerParams(vmem_limit_bytes=mib * MIB)


def pack_blocks(keys, values, parts):
    rows, width = keys.shape[1], keys.shape[2] // parts

    def kernel(k_ref, v_ref, out_ref, sems):
        copies = []
        for which, ref in enumerate((k_ref, v_ref)):
            for part in range(parts):
                copies.append(
                    pltpu.make_async_copy(
                        ref.at[0, :, pl.ds(part * width, width)],
                        out_ref.at[part, which],
                        sems.at[which, part],
                    )
                )
        for copy in copies:
            copy.start()
        for copy in copies:
            copy.wait()

    return pl.pallas_call(
        kernel,
        out_shape=jax.ShapeDtypeStruct((parts, 2, rows, width), keys.dtype),
        in_specs=[pl.BlockSpec(memory_space=pl.ANY)] * 2,
        out_specs=pl.BlockSpec(memory_space=pl.ANY),
        scratch_shapes=[pltpu.SemaphoreType.DMA((2, parts))],
        cost_estimate=pl.CostEstimate(flops=0, bytes_accessed=8 * MIB, transcendentals=0),
    )(keys, values)


def unpack_blocks(packed):
    parts, _, rows, width = packed.shape

    def kernel(in_ref, k_ref, v_ref, sems):
        copies = []
        for which, ref in enumerate((k_ref, v_ref)):
            for part in range(parts):
                copies.append(
                    pltpu.make_async_copy(
                        in_ref.at[part, which],
                        ref.at[0, :, pl.ds(part * width, width)],
                        sems.at[which, part],
                    )
                )
        for copy in copies:
            copy.start()
        for copy in copies:
            copy.wait()

    shape = jax.ShapeDtypeStruct((1, rows, parts * width), packed.dtype)
    return pl.pallas_call(
        kernel,
        out_shape=(shape, shape),
        in_specs=[pl.BlockSpec(memory_space=pl.ANY)],
        out_specs=(pl.BlockSpec(memory_space=pl.ANY),) * 2,
        scratch_shapes=[pltpu.SemaphoreType.DMA((2, parts))],
    )(packed)


def forward_kernel(kv_ref, qu_ref, bias_ref, exp_ref, out_ref, stat_ref):
    key_rows = kv_ref.shape[0] * kv_ref.shape[2]
    query_rows = qu_ref.shape[0] * qu_ref.shape[2]
    heads = kv_ref.shape[3] // HEAD_DIM
    bias = jnp.concatenate([bias_ref[...]] * (query_rows // 128), axis=1)
    rows = []
    for head in range(heads):
        lanes = slice(head * HEAD_DIM, (head + 1) * HEAD_DIM)
        keys = kv_ref[:, 0, :, lanes].reshape(key_rows, HEAD_DIM)
        values = kv_ref[:, 1, :, lanes].reshape(key_rows, HEAD_DIM)
        query = qu_ref[:, 0, :, lanes].reshape(query_rows, HEAD_DIM)
        upstream = qu_ref[:, 1, :, lanes].reshape(query_rows, HEAD_DIM)
        scores = matmul(keys, query, NT) * EXP2_SCALE + bias
        top = jnp.maximum(jnp.max(scores, axis=0, keepdims=True), NEG_FLOOR)
        exponent = jnp.exp2(scores - top)
        total = jnp.sum(exponent, axis=0, keepdims=True)
        exponent_bf = exponent.astype(BF16)
        exp_ref[head] = exponent_bf
        output = matmul(values, exponent_bf, TN)
        delta = jnp.sum(upstream.astype(F32).T * output, axis=0, keepdims=True)
        rows += [top, total, delta]
        for part in range(query_rows // 128):
            out_ref[part, lanes, :] = output[:, part * 128 : (part + 1) * 128].astype(BF16)
    rows.append(jnp.zeros((8 - len(rows), query_rows), F32))
    stat_ref[...] = jnp.concatenate(rows, axis=0)


def forward(kv, qu, bias):
    blocks, _, block_rows, width = kv.shape
    key_rows = blocks * block_rows
    slices, _, slice_rows, _ = qu.shape
    queries = slices * slice_rows
    heads = width // HEAD_DIM
    step = 256
    per = step // slice_rows
    return pl.pallas_call(
        forward_kernel,
        grid=(queries // step,),
        in_specs=[
            pl.BlockSpec((blocks, 2, block_rows, width), lambda i: (0, 0, 0, 0)),
            pl.BlockSpec((per, 2, slice_rows, width), lambda i: (i, 0, 0, 0)),
            pl.BlockSpec((key_rows, 128), lambda i: (0, 0)),
        ],
        out_specs=(
            pl.BlockSpec((heads, key_rows, step), lambda i: (0, 0, i)),
            pl.BlockSpec((per, width, slice_rows), lambda i: (i, 0, 0)),
            pl.BlockSpec((8, step), lambda i: (0, i)),
        ),
        out_shape=(
            jax.ShapeDtypeStruct((heads, key_rows, queries), BF16),
            jax.ShapeDtypeStruct((slices, width, slice_rows), BF16),
            jax.ShapeDtypeStruct((8, queries), F32),
        ),
        compiler_params=params(48),
        cost_estimate=pl.CostEstimate(
            flops=4 * heads * queries * key_rows * HEAD_DIM,
            bytes_accessed=12 * MIB,
            transcendentals=heads * queries * key_rows,
        ),
    )(kv, qu, bias)


def merged_stats(stats, head):
    tops = stats[:, 3 * head, :]
    totals = stats[:, 3 * head + 1, :]
    deltas = stats[:, 3 * head + 2, :]
    top = jnp.max(tops, axis=0, keepdims=True)
    factors = jnp.exp2(tops - top)
    inverse = 1.0 / jnp.sum(totals * factors, axis=0, keepdims=True)
    delta = jnp.sum(deltas * factors, axis=0, keepdims=True) * inverse
    return top, factors, inverse, delta


def backward_kernel(
    kv_ref, qu_ref, exp_ref, stats_ref, own_ref, cos_block, sin_block, cos_row, sin_row, grad_ref, query_ref, acc_ref
):
    step = pl.program_id(0)
    blocks, block_rows = kv_ref.shape[0], kv_ref.shape[2]
    key_rows = blocks * block_rows
    query_rows = qu_ref.shape[0] * qu_ref.shape[2]
    heads = kv_ref.shape[3] // HEAD_DIM
    stats = stats_ref[...]
    for head in range(heads):
        lanes = slice(head * HEAD_DIM, (head + 1) * HEAD_DIM)
        top, _, inverse, delta = merged_stats(stats, head)
        factor = jnp.exp2(own_ref[3 * head : 3 * head + 1, :] - top) * inverse
        keys = kv_ref[:, 0, :, lanes].reshape(key_rows, HEAD_DIM)
        values = kv_ref[:, 1, :, lanes].reshape(key_rows, HEAD_DIM)
        query = qu_ref[:, 0, :, lanes].reshape(query_rows, HEAD_DIM)
        upstream = qu_ref[:, 1, :, lanes].reshape(query_rows, HEAD_DIM)
        probability = exp_ref[head].astype(F32) * factor
        value_grad = matmul(probability.astype(BF16), upstream)
        prob_grad = matmul(values, upstream, NT)
        score_grad = (probability * (prob_grad - delta)).astype(BF16)
        key_grad = matmul(score_grad, query) * SCALE
        query_part = matmul(keys, score_grad, TN)
        for block in range(blocks):
            part = key_grad[block * block_rows : (block + 1) * block_rows, :]
            cos_a = cos_block[block]
            sin_a = sin_block[block]
            cosine = cos_a * cos_row[...] - sin_a * sin_row[...]
            sine = sin_a * cos_row[...] + cos_a * sin_row[...]
            signed = jnp.where(
                lax.broadcasted_iota(jnp.int32, sine.shape, 1) < HEAD_DIM // 2, sine, -sine
            )
            turned = part * cosine + pltpu.roll(part, HEAD_DIM // 2, 1) * signed
            grad_ref[block, 0, :, lanes] = turned.astype(BF16)
            grad_ref[block, 1, :, lanes] = value_grad[
                block * block_rows : (block + 1) * block_rows, :
            ].astype(BF16)

        @pl.when(step == 0)
        def _():
            acc_ref[lanes, :] = query_part

        @pl.when(step > 0)
        def _():
            acc_ref[lanes, :] += query_part

    @pl.when(step == pl.num_programs(0) - 1)
    def _():
        for part in range(query_ref.shape[0]):
            query_ref[part] = (acc_ref[:, part * 128 : (part + 1) * 128] * SCALE).astype(BF16)


def backward(kv, qu, exponent, stats, own, tables):
    blocks, _, block_rows, width = kv.shape
    slices, _, slice_rows, _ = qu.shape
    queries = slices * slice_rows
    heads = width // HEAD_DIM
    per = 4
    key_rows = blocks * block_rows
    whole = lambda shape: pl.BlockSpec(shape, lambda i: (0,) * len(shape))
    return pl.pallas_call(
        backward_kernel,
        grid=(blocks // per,),
        in_specs=[
            pl.BlockSpec((per, 2, block_rows, width), lambda i: (i, 0, 0, 0)),
            whole(qu.shape),
            pl.BlockSpec((heads, per * block_rows, queries), lambda i: (0, i, 0)),
            whole(stats.shape),
            whole(own.shape),
            pl.BlockSpec((per, 1, HEAD_DIM), lambda i: (i, 0, 0)),
            pl.BlockSpec((per, 1, HEAD_DIM), lambda i: (i, 0, 0)),
            whole((block_rows, HEAD_DIM)),
            whole((block_rows, HEAD_DIM)),
        ],
        out_specs=(
            pl.BlockSpec((per, 2, block_rows, width), lambda i: (i, 0, 0, 0)),
            whole((slices, width, slice_rows)),
        ),
        out_shape=(
            jax.ShapeDtypeStruct((blocks, 2, block_rows, width), BF16),
            jax.ShapeDtypeStruct((slices, width, slice_rows), BF16),
        ),
        scratch_shapes=[pltpu.VMEM((width, queries), F32)],
        compiler_params=params(48),
        cost_estimate=pl.CostEstimate(
            flops=8 * heads * queries * key_rows * HEAD_DIM,
            bytes_accessed=14 * MIB,
            transcendentals=0,
        ),
    )(kv, qu, exponent, stats, own, *tables)


def merge_output(parts, stats):
    def kernel(parts_ref, stats_ref, out_ref):
        for head in range(parts_ref.shape[1] // HEAD_DIM):
            lanes = slice(head * HEAD_DIM, (head + 1) * HEAD_DIM)
            _, factors, inverse, _ = merged_stats(stats_ref[...], head)
            weights = factors * inverse
            total = parts_ref[0, lanes, :].astype(F32) * weights[0:1, :]
            for block in range(1, parts_ref.shape[0]):
                total += parts_ref[block, lanes, :].astype(F32) * weights[block : block + 1, :]
            out_ref[lanes, :] = total.astype(BF16)

    return pl.pallas_call(
        kernel, out_shape=jax.ShapeDtypeStruct(parts.shape[1:], BF16), compiler_params=params(16)
    )(parts, stats)


def merge_query_grad(parts, cosine, sine):
    def kernel(parts_ref, cos_ref, sin_ref, out_ref):
        total = jnp.sum(parts_ref[...].astype(F32), axis=0)
        half = HEAD_DIM // 2
        turned = []
        for head in range(parts_ref.shape[1] // HEAD_DIM):
            first = total[head * HEAD_DIM : head * HEAD_DIM + half, :]
            second = total[head * HEAD_DIM + half : (head + 1) * HEAD_DIM, :]
            turned.append(first * cos_ref[...] + second * sin_ref[...])
            turned.append(second * cos_ref[...] - first * sin_ref[...])
        out_ref[...] = jnp.concatenate(turned, axis=0).T.astype(BF16)

    return pl.pallas_call(
        kernel,
        out_shape=jax.ShapeDtypeStruct((parts.shape[2], parts.shape[1]), BF16),
        compiler_params=params(16),
    )(parts, cosine, sine)


def projection_grad(parts, cotangent):
    def kernel(parts_ref, cot_ref, out_ref):
        joined = jnp.concatenate([parts_ref[part] for part in range(parts_ref.shape[0])], axis=1)
        out_ref[...] = matmul(joined, cot_ref[...]) * (1.0 / LOSS_SCALE)

    return pl.pallas_call(
        kernel,
        out_shape=jax.ShapeDtypeStruct((parts.shape[1], cotangent.shape[1]), F32),
        compiler_params=params(32),
    )(parts, cotangent)


def upstream_part(cotangent, out_weight):
    def kernel(cot_ref, weight_ref, out_ref):
        out_ref[...] = matmul(cot_ref[...], weight_ref[...], NT).astype(BF16)

    return pl.pallas_call(
        kernel,
        out_shape=jax.ShapeDtypeStruct((cotangent.shape[0], out_weight.shape[0]), BF16),
        compiler_params=params(32),
    )(cotangent, out_weight)


def per_device(
    queries, key_vectors, value_vectors, cotangent, out_weight, frame_valid, group_offset, guide_index
):
    seq_count, fsdp_count = lax.axis_size("seq"), lax.axis_size("fsdp")
    z_count = fsdp_count
    x_count = seq_count // z_count
    seq_index, fsdp_index = lax.axis_index("seq"), lax.axis_index("fsdp")
    z_index = seq_index % z_count
    cfg_index = lax.axis_index("cfg")
    block_rows = key_vectors.shape[1]
    group_rows, width = queries.shape[1], queries.shape[2]
    slice_rows = group_rows // z_count

    def place(x, z, f):
        return (x * z_count + z) * fsdp_count + f

    spots = [
        (x, z, f) for x in range(x_count) for z in range(z_count) for f in range(fsdp_count)
    ]
    plane_groups = [
        [place(x, z, f) for x in range(x_count) for f in range(fsdp_count)] for z in range(z_count)
    ]
    column_groups = [[x * z_count + z for z in range(z_count)] for x in range(x_count)]
    turn = [(place(x, z, f), place(x, f, z)) for x, z, f in spots]
    cfg_stride = seq_count * fsdp_count
    turn_across = [
        (c * cfg_stride + s, (1 - c) * cfg_stride + d) for c in range(2) for s, d in turn
    ]

    def over_plane(x):
        return lax.all_to_all(x, ("seq", "fsdp"), 0, 0, axis_index_groups=plane_groups, tiled=True)

    def over_column(x):
        return lax.all_to_all(x, "seq", 0, 0, axis_index_groups=column_groups, tiled=True)

    def over_fsdp(x):
        return lax.all_to_all(x, "fsdp", 0, 0, tiled=True)

    def copies(x, count):
        return jnp.broadcast_to(x[None], (count,) + x.shape)

    guide = 1.5 + guide_index[0].astype(F32) / 1024.0
    own_weight = jnp.where(cfg_index == 0, guide, 1.0 - guide)

    kv = over_plane(pack_blocks(key_vectors, value_vectors, x_count * fsdp_count))

    partial = upstream_part(cotangent, out_weight).reshape(fsdp_count, slice_rows, width)
    summed = jnp.sum(over_fsdp(partial).astype(F32), axis=0)
    upstream_rows = (own_weight * summed).astype(BF16)
    query_rows = lax.dynamic_slice(
        queries[0], (fsdp_index * slice_rows, 0), (slice_rows, width)
    )
    both = lax.ppermute(jnp.stack([query_rows, upstream_rows]), ("seq", "fsdp"), turn)
    qu = over_column(copies(both, z_count))

    block_ids = jnp.arange(x_count * fsdp_count, dtype=jnp.int32)
    block_start = place(block_ids // fsdp_count, z_index, block_ids % fsdp_count) * block_rows
    row_ids = jnp.arange(block_rows, dtype=jnp.int32)
    positions = (block_start[:, None] + row_ids[None, :]).reshape(-1)
    frame_match = (positions // FRAME_TOK)[:, None] == jnp.arange(
        frame_valid.shape[0], dtype=jnp.int32
    )[None, :]
    valid = jnp.sum(jnp.where(frame_match, frame_valid[None, :], 0), axis=1) == 1
    bias = jnp.broadcast_to(
        jnp.where(valid, 0.0, NEG_LARGE).astype(F32)[:, None], (positions.shape[0], 128)
    )
    frequency = 10000.0 ** (-jnp.arange(HEAD_DIM // 2, dtype=F32) / (HEAD_DIM // 2))
    twice = jnp.concatenate([frequency, frequency])
    block_angle = (block_start.astype(F32)[:, None] * twice[None, :])[:, None, :]
    row_angle = row_ids.astype(F32)[:, None] * twice[None, :]
    tables = (jnp.cos(block_angle), jnp.sin(block_angle), jnp.cos(row_angle), jnp.sin(row_angle))

    exponent, out_parts, own_stats = forward(kv, qu, bias)
    stats = over_column(copies(own_stats, z_count))
    grads, query_parts = backward(kv, qu, exponent, stats, own_stats, tables)
    key_grad, value_grad = unpack_blocks(over_plane(grads))

    out_slices = over_column(out_parts)
    slice_stats = lax.dynamic_slice_in_dim(stats, z_index * slice_rows, slice_rows, axis=2)
    attn_rows = merge_output(out_slices, slice_stats)
    own_rows = lax.ppermute(attn_rows, ("seq", "fsdp"), turn)
    other_rows = lax.ppermute(attn_rows, ("cfg", "seq", "fsdp"), turn_across)
    mixed = own_weight * own_rows.astype(F32) + (1.0 - own_weight) * other_rows.astype(F32)
    weight_grad = projection_grad(over_fsdp(copies(mixed.astype(BF16), fsdp_count)), cotangent)

    query_positions = (
        group_offset[0] + z_index * slice_rows + jnp.arange(slice_rows, dtype=jnp.int32)
    )
    query_angle = query_positions.astype(F32)[None, :] * frequency[:, None]
    query_slice = merge_query_grad(
        over_column(query_parts), jnp.cos(query_angle), jnp.sin(query_angle)
    )
    query_grad = lax.ppermute(query_slice, ("seq", "fsdp"), turn)[None]
    return (query_grad, key_grad, value_grad, weight_grad)


def solution(mesh):
    placed = (
        P("cfg", None, "seq"),
        P("cfg", ("seq", "fsdp"), None),
        P("cfg", ("seq", "fsdp"), None),
        P(None, "fsdp"),
        P("seq", "fsdp"),
        P(),
        P(),
        P(),
    )
    return jax.shard_map(
        per_device,
        mesh=mesh,
        in_specs=placed,
        out_specs=(
            P("cfg", "fsdp", "seq"),
            P("cfg", ("seq", "fsdp"), None),
            P("cfg", ("seq", "fsdp"), None),
            P("seq", "fsdp"),
        ),
        check_vma=False,
    )
```

time: 676 us -> 350 us (0.52); the launches traced: 664 us -> 345 us
  other arithmetic: 161 us -> 1.15 us
  Pallas kernels: 0 us -> 159 us
  local copies, waits for them, and re-layouts: 136 us -> 8.9 us
  waiting for transfers between devices: 207 us -> 101 us
  matrix products: 49.5 us -> 0 us
  blocking collectives: 56.7 us -> 15.9 us
  starting transfers between devices: 38.2 us -> 57.2 us
  between operations: 15.6 us -> 2.22 us
    pallas_call x0 -> x8, Pallas kernels: none -> 159 us  [the longest x1 64.9 us: unpack_blocks(): pl.pallas_call(kernel, out_shape=(shape, shape), in_specs=[pl.BlockSpec(m...]
    all_gather x1 -> x0, waiting for transfers between devices: 114 us -> none  [joined(): everything = jax.tree.map(lambda part: lax.all_gather(part, axis), x)]
    unnamed x9 -> x0, other arithmetic: 73.3 us -> none
    all_to_all x4 -> x7, waiting for transfers between devices: 14.8 us -> 75.6 us  [the longest x2 41.4 us: over_plane(): lax.all_to_all(x, ('seq', 'fsdp'), 0, 0, axis_index_groups=plane_groups,...]
    all_gather x2 -> x0, blocking collectives: 56.7 us -> none  [joined(): everything = jax.tree.map(lambda part: lax.all_gather(part, axis), x)]
    unnamed x39 -> x19, local copies, waits for them, and re-layouts: 55.6 us -> 5.88 us
    dot_general x16 -> x0, matrix products: 49.5 us -> none  [the longest x2 13.9 us: forward_block(): jnp.einsum('hqk,khd->qhd', weights.astype(jnp.bfloat16), block_values, pr...]
    unnamed x5 -> x0, waiting for transfers between devices: 43.3 us -> none
  transfers between devices with their start and end apart: 8 -> 11, of which waited for: 6 -> 8; matrix products, arithmetic and copies ran while one was open for 22% -> 1% of each run, Pallas kernels for 0% -> 23%
where the time goes in v1:
time: 350 us; the launch traced here: 345 us
  Pallas kernels  159 us (45%)
  waiting for transfers between devices  101 us (29%)
  starting transfers between devices  57.2 us (16%)
  blocking collectives  15.9 us (5%)
  local copies, waits for them, and re-layouts  8.9 us (3%)
    pallas_call x1, Pallas kernels, unpack_blocks(): pl.pallas_call(kernel, out_shape=(shape, shape), in_specs=[pl.BlockSpec(m...  64.9 us
    pallas_call x1, Pallas kernels, pack_blocks(): pl.pallas_call(kernel, out_shape=jax.ShapeDtypeStruct((parts, 2, rows, wi...  64.9 us
    all_to_all x2, waiting for transfers between devices, over_plane(): lax.all_to_all(x, ('seq', 'fsdp'), 0, 0, axis_index_groups=plane_groups,...  41.4 us
    all_to_all x4, waiting for transfers between devices, over_column(): lax.all_to_all(x, 'seq', 0, 0, axis_index_groups=column_groups, tiled=True)  34.2 us
    all_to_all x4, starting transfers between devices, over_column(): lax.all_to_all(x, 'seq', 0, 0, axis_index_groups=column_groups, tiled=True)  27.3 us
    all_to_all x1, blocking collectives, over_fsdp(): return lax.all_to_all(x, 'fsdp', 0, 0, tiled=True)  15.9 us
    pallas_call x1, Pallas kernels, forward(): pl.pallas_call(forward_kernel, grid=(queries // step,), in_specs=[pl.Bloc...  13.6 us
    ppermute x1, waiting for transfers between devices, per_device(): other_rows = lax.ppermute(attn_rows, ('cfg', 'seq', 'fsdp'), turn_across)  12.4 us
  transfers between devices with their start and end apart: 11, of which 8 were waited for; matrix products, arithmetic and copies ran while one was open for 1% of the time, Pallas kernels for 23%

profile of v1, /device:TPU:32, one launch (start us, length us, event | category | flops | bytes accessed | tf_op | source)
XLA Modules:
  0.0 345.4 jit_solution(9566542792548924477)
XLA Ops:
  0.6 0.0 copy-start
  0.7 1.4 copy-done.1
  2.0 1.0 copy-done.7
  3.0 1.4 shard_map.112
  4.4 5.4 %all-to-all-start.1 = ((bf16[8,128,256]{2,1,0:T(8,128)(2,1)}), bf16[8,128,256]{2,1,0:T(8,128)(2,1)S(1)}, u32[]{:S(2)}, u32[]{:S(2)}) async-start(bf16[8,128,256]{2,1,0:T(8,128)(2,1)} %bitcast.1), calls=%async_computation.1 | async-start | bytes 1048576 | tf_op jit(solution)/shard_map/all_to_all | solution.py:350
  9.8 64.9 %shard_map.111 = bf16[16,2,128,256]{3,2,1,0:T(8,128)(2,1)} custom-call(bf16[1,128,4096]{2,1,0:T(8,128)(2,1)} %k_ref.1, bf16[1,128,4096]{2,1,0:T(8,128)(2,1)} %v_ref.1), custom_call_target="tpu_custom_call" | custom-call | bytes 8388608 | tf_op jit(solution)/shard_map/pallas_call | solution.py:52
  74.7 7.1 %all-to-all-start = ((bf16[16,2,128,256]{3,2,1,0:T(8,128)(2,1)}), bf16[16,2,128,256]{3,2,1,0:T(8,128)(2,1)S(1)}, u32[]{:S(2)}, u32[]{:S(2)}) async-start(bf16[16,2,128,256]{3,2,1,0:T(8,128)(2,1)} %shard_map.111), calls=%async_computation | async-start | bytes 4194304 | tf_op jit(solution)/shard_map/all_to_all | solution.py:344
  82.5 0.1 convert_reduce_fusion
  82.6 3.4 collective-permute-start
  86.0 8.5 %collective-permute-done = bf16[2,128,256]{2,1,0:T(8,128)(2,1)S(1)} collective-permute-done((bf16[2,128,256]{2,1,0:T(8,128)(2,1)S(1)}, bf16[2,128,256]{2,1,0:T(8,128)(2,1)S(1)}, u32[]{:S(2)}, u32[]{:S(2)}) %collective-permute-start) | collective-permute-done | bytes 131104 | tf_op jit(solution)/shard_map/ppermute | solution.py:366
  94.5 23.6 %all-to-all-done.kv_ref = bf16[16,2,128,256]{3,2,1,0:T(8,128)(2,1)S(1)} async-done(((bf16[16,2,128,256]{3,2,1,0:T(8,128)(2,1)}), bf16[16,2,128,256]{3,2,1,0:T(8,128)(2,1)S(1)}, u32[]{:S(2)}, u32[]{:S(2)}) %all-to-all-start) | async-done | bytes 2097184 | tf_op jit(solution)/shard_map/all_to_all | solution.py:344
  118.1 1.1 broadcast_in_dim.30
  119.2 10.4 %all-to-all-start.2 = ((bf16[8,2,128,256]{3,2,1,0:T(8,128)(2,1)}), bf16[8,2,128,256]{3,2,1,0:T(8,128)(2,1)}, u32[]{:S(2)}, u32[]{:S(2)}) async-start(bf16[8,2,128,256]{3,2,1,0:T(8,128)(2,1)} %broadcast_in_dim.30), calls=%async_computation.2 | async-start | bytes 2097152 | tf_op jit(solution)/shard_map/all_to_all | solution.py:347
  129.7 0.1 add_select_fusion
  129.7 0.1 select_reduce_fusion
  129.9 25.2 %all-to-all-done.2.qu_ref = bf16[8,2,128,256]{3,2,1,0:T(8,128)(2,1)} async-done(((bf16[8,2,128,256]{3,2,1,0:T(8,128)(2,1)}), bf16[8,2,128,256]{3,2,1,0:T(8,128)(2,1)}, u32[]{:S(2)}, u32[]{:S(2)}) %all-to-all-start.2) | async-done | bytes 1048608 | tf_op jit(solution)/shard_map/all_to_all | solution.py:347
  155.0 0.3 broadcast_in_dim.35.bias_ref
  155.3 13.6 %shard_map.113 = (bf16[2,2048,1024]{2,1,0:T(8,128)(2,1)}, bf16[8,256,128]{2,1,0:T(8,128)(2,1)S(1)}, f32[8,1024]{1,0:T(8,128)S(1)}) custom-call(bf16[16,2,128,256]{3,2,1,0:T(8,128)(2,1)S(1)} %all-to-all-done.kv_ref, bf16[8,2,128,256]{3,2,1,0:T(8,128)(2,1)} %all-to-all-done.2.qu_ref, f32[2048,128]{1,0:T(8,128)S(1)} %broadcast_in_dim.35.bias_ref), custom_call_target="tpu_custom_call" | custom-call | flops 2147483648 | bytes 12582912 | tf_op jit(solution)/shard_map/pallas_call | solution.py:126
  168.9 0.8 copy-done.5
  169.7 0.7 broadcast_in_dim.36
  170.4 4.8 %all-to-all-start.3 = ((f32[8,8,1024]{2,1,0:T(8,128)}), f32[8,8,1024]{2,1,0:T(8,128)S(1)}, u32[]{:S(2)}, u32[]{:S(2)}) async-start(f32[8,8,1024]{2,1,0:T(8,128)} %broadcast_in_dim.36), calls=%async_computation.3 | async-start | bytes 524288 | tf_op jit(solution)/shard_map/all_to_all | solution.py:347
  175.3 9.0 %all-to-all-done.3.stats_ref = f32[8,8,1024]{2,1,0:T(8,128)S(1)} async-done(((f32[8,8,1024]{2,1,0:T(8,128)}), f32[8,8,1024]{2,1,0:T(8,128)S(1)}, u32[]{:S(2)}, u32[]{:S(2)}) %all-to-all-start.3) | async-done | bytes 262176 | tf_op jit(solution)/shard_map/all_to_all | solution.py:347
  184.3 4.9 %all-to-all-start.6 = ((bf16[8,256,128]{2,1,0:T(8,128)(2,1)}), bf16[8,256,128]{2,1,0:T(8,128)(2,1)S(1)}, u32[]{:S(2)}, u32[]{:S(2)}) async-start(bf16[8,256,128]{2,1,0:T(8,128)(2,1)} %copy-done.5), calls=%async_computation.6 | async-start | bytes 1048576 | tf_op jit(solution)/shard_map/all_to_all | solution.py:347
  189.2 0.1 pad_maximum_fusion.1
  189.2 0.1 mul.119
  189.3 0.2 multiply_sine_fusion.2
  189.6 0.3 multiply_sine_fusion
  189.9 12.2 %shard_map.114 = (bf16[16,2,128,256]{3,2,1,0:T(8,128)(2,1)S(1)}, bf16[8,256,128]{2,1,0:T(8,128)(2,1)S(1)}) custom-call(bf16[16,2,128,256]{3,2,1,0:T(8,128)(2,1)S(1)} %all-to-all-done.kv_ref, bf16[8,2,128,256]{3,2,1,0:T(8,128)(2,1)} %all-to-all-done.2.qu_ref, bf16[2,2048,1024]{2,1,0:T(8,128)(2,1)} %get-tuple-element.11.exp_ref, ...), custom_call_target="tpu_custom_call" | custom-call | flops 4294967296 | bytes 14680064 | tf_op jit(solution)/shard_map/pallas_call | solution.py:224
  202.1 1.3 copy-done.3
  203.4 0.8 copy-done.4
  204.2 7.2 %all-to-all-start.4 = ((bf16[8,256,128]{2,1,0:T(8,128)(2,1)}), bf16[8,256,128]{2,1,0:T(8,128)(2,1)S(1)}, u32[]{:S(2)}, u32[]{:S(2)}) async-start(bf16[8,256,128]{2,1,0:T(8,128)(2,1)} %copy-done.4), calls=%async_computation.4 | async-start | bytes 1048576 | tf_op jit(solution)/shard_map/all_to_all | solution.py:347
  211.4 0.8 constant_dynamic-slice_fusion.stats_ref
  212.2 0.2 shard_map.117
  212.3 0.1 collective-permute-start.3
  212.4 1.9 collective-permute-start.2
  214.4 12.4 %collective-permute-done.3 = bf16[256,128]{1,0:T(8,128)(2,1)S(1)} collective-permute-done((bf16[256,128]{1,0:T(8,128)(2,1)S(1)}, bf16[256,128]{1,0:T(8,128)(2,1)S(1)}, u32[]{:S(2)}, u32[]{:S(2)}) %collective-permute-start.3) | collective-permute-done | bytes 65568 | tf_op jit(solution)/shard_map/ppermute | solution.py:395
  226.8 1.6 collective-permute-done.2
  228.5 0.1 broadcast_in_dim.38
  228.5 15.9 %all_to_all.40.parts_ref = bf16[8,256,128]{2,1,0:T(8,128)(2,1)S(1)} all-to-all(bf16[8,256,128]{2,1,0:T(8,128)(2,1)S(1)} %broadcast_in_dim.38), channel_id=1, replica_groups=mesh['cfg'=2,'seq'=16,'fsdp'=8] {'fsdp'}, dimensions={0} | all-to-all | bytes 1048576 | tf_op jit(solution)/shard_map/all_to_all | solution.py:350
  244.5 4.6 %all-to-all-start.5 = ((bf16[16,2,128,256]{3,2,1,0:T(8,128)(2,1)}), bf16[16,2,128,256]{3,2,1,0:T(8,128)(2,1)}, u32[]{:S(2)}, u32[]{:S(2)}) async-start(bf16[16,2,128,256]{3,2,1,0:T(8,128)(2,1)} %copy-done.3), calls=%async_computation.5 | async-start | bytes 4194304 | tf_op jit(solution)/shard_map/all_to_all | solution.py:344
  249.7 0.2 multiply_sine_fusion.1
  249.9 0.2 shard_map.115
  250.1 7.4 %collective-permute-start.1 = (bf16[128,256]{1,0:T(8,128)(2,1)S(1)}, bf16[128,256]{1,0:T(8,128)(2,1)S(1)}, u32[]{:S(2)}, u32[]{:S(2)}) collective-permute-start(bf16[128,256]{1,0:T(8,128)(2,1)S(1)} %shard_map.115), channel_id=1, source_target_pairs={{0,0},{1,8},{2,16},{3,24},{4,32},{5,40},{6,48},{7,56},{8,1},{9,9},... | collective-permute-start | bytes 196616 | tf_op jit(solution)/shard_map/ppermute | solution.py:406
  257.5 3.2 collective-permute-done.1
  260.7 1.4 shard_map.118
  262.1 17.8 %all-to-all-done.5.in_ref = bf16[16,2,128,256]{3,2,1,0:T(8,128)(2,1)} async-done(((bf16[16,2,128,256]{3,2,1,0:T(8,128)(2,1)}), bf16[16,2,128,256]{3,2,1,0:T(8,128)(2,1)}, u32[]{:S(2)}, u32[]{:S(2)}) %all-to-all-start.5) | async-done | bytes 2097184 | tf_op jit(solution)/shard_map/all_to_all | solution.py:344
  279.9 64.9 %shard_map.116 = (bf16[1,128,4096]{2,1,0:T(8,128)(2,1)}, bf16[1,128,4096]{2,1,0:T(8,128)(2,1)}) custom-call(bf16[16,2,128,256]{3,2,1,0:T(8,128)(2,1)} %all-to-all-done.5.in_ref), custom_call_target="tpu_custom_call" | custom-call | tf_op jit(solution)/shard_map/pallas_call | solution.py:82
  344.8 0.6 copy.16
  (24 shorter events, 0.1 us)
Async XLA Ops:
  0.6 81.9 %copy-start = (bf16[1,1024,256]{2,1,0:T(8,128)(2,1)S(1)}, bf16[1,1024,256]{2,1,0:T(8,128)(2,1)}, u32[]{:S(2)}) copy-start(bf16[1,1024,256]{2,1,0:T(8,128)(2,1)} %param.8) | copy-start | bytes 1572868
  0.6 1.4 copy-start.1
  2.0 1.0 copy-start.7
  4.4 70.3 %all-to-all-start.1 = ((bf16[8,128,256]{2,1,0:T(8,128)(2,1)}), bf16[8,128,256]{2,1,0:T(8,128)(2,1)S(1)}, u32[]{:S(2)}, u32[]{:S(2)}) async-start(bf16[8,128,256]{2,1,0:T(8,128)(2,1)} %bitcast.1), calls=%async_computation.1 | async-start | bytes 1048576 | tf_op jit(solution)/shard_map/all_to_all | solution.py:350
  74.7 43.4 %all-to-all-start = ((bf16[16,2,128,256]{3,2,1,0:T(8,128)(2,1)}), bf16[16,2,128,256]{3,2,1,0:T(8,128)(2,1)S(1)}, u32[]{:S(2)}, u32[]{:S(2)}) async-start(bf16[16,2,128,256]{3,2,1,0:T(8,128)(2,1)} %shard_map.111), calls=%async_computation | async-start | bytes 4194304 | tf_op jit(solution)/shard_map/all_to_all | solution.py:344
  82.5 47.2 %copy-start.8 = (s32[5]{0:T(128)S(1)}, s32[5]{0:T(128)}, u32[]{:S(2)}) copy-start(s32[5]{0:T(128)} %param.13) | copy-start | bytes 64
  82.6 11.9 %collective-permute-start = (bf16[2,128,256]{2,1,0:T(8,128)(2,1)S(1)}, bf16[2,128,256]{2,1,0:T(8,128)(2,1)S(1)}, u32[]{:S(2)}, u32[]{:S(2)}) collective-permute-start(bf16[2,128,256]{2,1,0:T(8,128)(2,1)S(1)} %pad_maximum_fusion), channel_id=1, source_target_pairs={{0,0},{1,8},{2,16},{3,24},{4,32},{5,40},{6,48},{7,56},{8,1},{9,9},... | collective-permute-start | bytes 393224 | tf_op jit(solution)/shard_map/ppermute | solution.py:366
  119.2 35.8 %all-to-all-start.2 = ((bf16[8,2,128,256]{3,2,1,0:T(8,128)(2,1)}), bf16[8,2,128,256]{3,2,1,0:T(8,128)(2,1)}, u32[]{:S(2)}, u32[]{:S(2)}) async-start(bf16[8,2,128,256]{3,2,1,0:T(8,128)(2,1)} %broadcast_in_dim.30), calls=%async_computation.2 | async-start | bytes 2097152 | tf_op jit(solution)/shard_map/all_to_all | solution.py:347
  168.9 0.8 copy-start.5
  170.4 13.9 %all-to-all-start.3 = ((f32[8,8,1024]{2,1,0:T(8,128)}), f32[8,8,1024]{2,1,0:T(8,128)S(1)}, u32[]{:S(2)}, u32[]{:S(2)}) async-start(f32[8,8,1024]{2,1,0:T(8,128)} %broadcast_in_dim.36), calls=%async_computation.3 | async-start | bytes 524288 | tf_op jit(solution)/shard_map/all_to_all | solution.py:347
  184.3 17.8 %copy-start.6 = (f32[8,8,1024]{2,1,0:T(8,128)}, f32[8,8,1024]{2,1,0:T(8,128)S(1)}, u32[]{:S(2)}) copy-start(f32[8,8,1024]{2,1,0:T(8,128)S(1)} %all-to-all-done.3.stats_ref) | copy-start | bytes 786436
  184.3 19.9 %all-to-all-start.6 = ((bf16[8,256,128]{2,1,0:T(8,128)(2,1)}), bf16[8,256,128]{2,1,0:T(8,128)(2,1)S(1)}, u32[]{:S(2)}, u32[]{:S(2)}) async-start(bf16[8,256,128]{2,1,0:T(8,128)(2,1)} %copy-done.5), calls=%async_computation.6 | async-start | bytes 1048576 | tf_op jit(solution)/shard_map/all_to_all | solution.py:347
  202.1 1.3 copy-start.3
  203.4 0.8 copy-start.4
  204.2 24.3 %all-to-all-start.4 = ((bf16[8,256,128]{2,1,0:T(8,128)(2,1)}), bf16[8,256,128]{2,1,0:T(8,128)(2,1)S(1)}, u32[]{:S(2)}, u32[]{:S(2)}) async-start(bf16[8,256,128]{2,1,0:T(8,128)(2,1)} %copy-done.4), calls=%async_computation.4 | async-start | bytes 1048576 | tf_op jit(solution)/shard_map/all_to_all | solution.py:347
  212.3 14.5 %collective-permute-start.3 = (bf16[256,128]{1,0:T(8,128)(2,1)S(1)}, bf16[256,128]{1,0:T(8,128)(2,1)S(1)}, u32[]{:S(2)}, u32[]{:S(2)}) collective-permute-start(bf16[256,128]{1,0:T(8,128)(2,1)S(1)} %shard_map.117), channel_id=1, source_target_pairs={{0,128},{1,136},{2,144},{3,152},{4,160},{5,168},{6,176},{7,184},{8... | collective-permute-start | bytes 196616 | tf_op jit(solution)/shard_map/ppermute | solution.py:395
  212.4 16.0 %collective-permute-start.2 = (bf16[256,128]{1,0:T(8,128)(2,1)S(1)}, bf16[256,128]{1,0:T(8,128)(2,1)S(1)}, u32[]{:S(2)}, u32[]{:S(2)}) collective-permute-start(bf16[256,128]{1,0:T(8,128)(2,1)S(1)} %shard_map.117), channel_id=1, source_target_pairs={{0,0},{1,8},{2,16},{3,24},{4,32},{5,40},{6,48},{7,56},{8,1},{9,9},... | collective-permute-start | bytes 196616 | tf_op jit(solution)/shard_map/ppermute | solution.py:394
  244.5 16.2 %copy-start.2 = (bf16[1024,640]{1,0:T(8,128)(2,1)S(1)}, bf16[1024,640]{1,0:T(8,128)(2,1)}, u32[]{:S(2)}) copy-start(bf16[1024,640]{1,0:T(8,128)(2,1)} %cot_ref.3) | copy-start | bytes 3932164
  244.5 35.4 %all-to-all-start.5 = ((bf16[16,2,128,256]{3,2,1,0:T(8,128)(2,1)}), bf16[16,2,128,256]{3,2,1,0:T(8,128)(2,1)}, u32[]{:S(2)}, u32[]{:S(2)}) async-start(bf16[16,2,128,256]{3,2,1,0:T(8,128)(2,1)} %copy-done.3), calls=%async_computation.5 | async-start | bytes 4194304 | tf_op jit(solution)/shard_map/all_to_all | solution.py:344
  250.1 10.6 %collective-permute-start.1 = (bf16[128,256]{1,0:T(8,128)(2,1)S(1)}, bf16[128,256]{1,0:T(8,128)(2,1)S(1)}, u32[]{:S(2)}, u32[]{:S(2)}) collective-permute-start(bf16[128,256]{1,0:T(8,128)(2,1)S(1)} %shard_map.115), channel_id=1, source_target_pairs={{0,0},{1,8},{2,16},{3,24},{4,32},{5,40},{6,48},{7,56},{8,1},{9,9},... | collective-permute-start | bytes 196616 | tf_op jit(solution)/shard_map/ppermute | solution.py:406

commit v2 on v1

v2 whole, which is shorter than its diff:
```python
import math

import jax
import jax.numpy as jnp
from jax import lax
from jax.experimental import pallas as pl
from jax.experimental.pallas import tpu as pltpu
from jax.sharding import PartitionSpec as P

HEAD_DIM = 128
FRAME_TOK = 3600
NEG_LARGE = -1e30
NEG_FLOOR = -1e29
LOSS_SCALE = 128.0
SCALE = 1.0 / math.sqrt(HEAD_DIM)
EXP2_SCALE = SCALE * math.log2(math.e)
BF16 = jnp.bfloat16
F32 = jnp.float32
MIB = 1024 * 1024

PATH = (0, 4, 2, 6, 1, 5, 3, 7)
NT = (((1,), (1,)), ((), ()))
TN = (((0,), (0,)), ((), ()))


def matmul(a, b, dims=(((1,), (0,)), ((), ()))):
    return lax.dot_general(a, b, dims, preferred_element_type=F32)


def params(mib):
    return pltpu.CompilerParams(vmem_limit_bytes=mib * MIB)


def pack_blocks(keys, values, parts):
    rows, width = keys.shape[1], keys.shape[2] // parts
    per = 4

    def kernel(k_ref, v_ref, out_ref):
        for which, ref in enumerate((k_ref, v_ref)):
            for part in range(per):
                out_ref[part, which] = ref[0, :, part * width : (part + 1) * width]

    return pl.pallas_call(
        kernel,
        grid=(parts // per,),
        out_shape=jax.ShapeDtypeStruct((parts, 2, rows, width), keys.dtype),
        in_specs=[pl.BlockSpec((1, rows, per * width), lambda i: (0, 0, i))] * 2,
        out_specs=pl.BlockSpec((per, 2, rows, width), lambda i: (i, 0, 0, 0)),
        compiler_params=params(16),
    )(keys, values)


def unpack_blocks(packed):
    parts, _, rows, width = packed.shape
    per = 4

    def kernel(in_ref, k_ref, v_ref):
        for which, ref in enumerate((k_ref, v_ref)):
            for part in range(per):
                ref[0, :, part * width : (part + 1) * width] = in_ref[part, which]

    shape = jax.ShapeDtypeStruct((1, rows, parts * width), packed.dtype)
    return pl.pallas_call(
        kernel,
        grid=(parts // per,),
        out_shape=(shape, shape),
        in_specs=[pl.BlockSpec((per, 2, rows, width), lambda i: (i, 0, 0, 0))],
        out_specs=(pl.BlockSpec((1, rows, per * width), lambda i: (0, 0, i)),) * 2,
        compiler_params=params(16),
    )(packed)


def forward_kernel(kv_ref, qu_ref, bias_ref, exp_ref, out_ref, stat_ref, top_ref):
    key_rows = kv_ref.shape[0] * kv_ref.shape[2]
    query_rows = qu_ref.shape[0] * qu_ref.shape[2]
    heads = kv_ref.shape[3] // HEAD_DIM
    bias = jnp.concatenate([bias_ref[...]] * (query_rows // 128), axis=1)
    rows, tops = [], []
    for head in range(heads):
        lanes = slice(head * HEAD_DIM, (head + 1) * HEAD_DIM)
        keys = kv_ref[:, 0, :, lanes].reshape(key_rows, HEAD_DIM)
        values = kv_ref[:, 1, :, lanes].reshape(key_rows, HEAD_DIM)
        query = qu_ref[:, 0, :, lanes].reshape(query_rows, HEAD_DIM)
        upstream = qu_ref[:, 1, :, lanes].reshape(query_rows, HEAD_DIM)
        scores = matmul(keys, query, NT) * EXP2_SCALE + bias
        top = jnp.maximum(jnp.max(scores, axis=0, keepdims=True), NEG_FLOOR)
        exponent = jnp.exp2(scores - top)
        total = jnp.sum(exponent, axis=0, keepdims=True)
        exponent_bf = exponent.astype(BF16)
        exp_ref[head] = exponent_bf
        safe = jnp.maximum(total, 1e-30)
        output = matmul(values, exponent_bf, TN) * (1.0 / safe)
        delta = jnp.sum(upstream.astype(F32).T * output, axis=0, keepdims=True)
        rows += [jnp.where(total > 0.0, top + jnp.log2(safe), NEG_FLOOR), delta]
        tops.append(top)
        for part in range(query_rows // 128):
            out_ref[part, lanes, :] = output[:, part * 128 : (part + 1) * 128].astype(BF16)
    stat_ref[...] = jnp.concatenate(rows, axis=0)
    top_ref[...] = jnp.concatenate(tops, axis=0)


def forward(kv, qu, bias):
    blocks, _, block_rows, width = kv.shape
    key_rows = blocks * block_rows
    slices, _, slice_rows, _ = qu.shape
    queries = slices * slice_rows
    heads = width // HEAD_DIM
    step = 256
    per = step // slice_rows
    return pl.pallas_call(
        forward_kernel,
        grid=(queries // step,),
        in_specs=[
            pl.BlockSpec((blocks, 2, block_rows, width), lambda i: (0, 0, 0, 0)),
            pl.BlockSpec((per, 2, slice_rows, width), lambda i: (i, 0, 0, 0)),
            pl.BlockSpec((key_rows, 128), lambda i: (0, 0)),
        ],
        out_specs=(
            pl.BlockSpec((heads, key_rows, step), lambda i: (0, 0, i)),
            pl.BlockSpec((per, width, slice_rows), lambda i: (i, 0, 0)),
            pl.BlockSpec((2 * heads, step), lambda i: (0, i)),
            pl.BlockSpec((heads, step), lambda i: (0, i)),
        ),
        out_shape=(
            jax.ShapeDtypeStruct((heads, key_rows, queries), BF16),
            jax.ShapeDtypeStruct((slices, width, slice_rows), BF16),
            jax.ShapeDtypeStruct((2 * heads, queries), F32),
            jax.ShapeDtypeStruct((heads, queries), F32),
        ),
        compiler_params=params(48),
        cost_estimate=pl.CostEstimate(
            flops=4 * heads * queries * key_rows * HEAD_DIM,
            bytes_accessed=12 * MIB,
            transcendentals=heads * queries * key_rows,
        ),
    )(kv, qu, bias)


def merged_stats(stats, head):
    logs = stats[:, 2 * head, :]
    deltas = stats[:, 2 * head + 1, :]
    top = jnp.max(logs, axis=0, keepdims=True)
    shares = jnp.exp2(logs - top)
    total = jnp.sum(shares, axis=0, keepdims=True)
    shares = shares / total
    return top + jnp.log2(total), shares, jnp.sum(deltas * shares, axis=0, keepdims=True)


def backward_kernel(
    spot_ref,
    kv_ref,
    qu_ref,
    exp_ref,
    stats_ref,
    own_ref,
    cos_block,
    sin_block,
    cos_row,
    sin_row,
    grad_ref,
    keep_ref,
    send_ref,
    acc_ref,
):
    step = pl.program_id(0)
    blocks, block_rows = kv_ref.shape[0], kv_ref.shape[2]
    key_rows = blocks * block_rows
    query_rows = qu_ref.shape[0] * qu_ref.shape[2]
    heads = kv_ref.shape[3] // HEAD_DIM
    stats = stats_ref[...]
    for head in range(heads):
        lanes = slice(head * HEAD_DIM, (head + 1) * HEAD_DIM)
        log_total, _, delta = merged_stats(stats, head)
        factor = jnp.exp2(own_ref[head : head + 1, :] - log_total)
        keys = kv_ref[:, 0, :, lanes].reshape(key_rows, HEAD_DIM)
        values = kv_ref[:, 1, :, lanes].reshape(key_rows, HEAD_DIM)
        query = qu_ref[:, 0, :, lanes].reshape(query_rows, HEAD_DIM)
        upstream = qu_ref[:, 1, :, lanes].reshape(query_rows, HEAD_DIM)
        probability = exp_ref[head].astype(F32) * factor
        value_grad = matmul(probability.astype(BF16), upstream)
        prob_grad = matmul(values, upstream, NT)
        score_grad = (probability * (prob_grad - delta)).astype(BF16)
        key_grad = matmul(score_grad, query) * SCALE
        query_part = matmul(keys, score_grad, TN)
        for block in range(blocks):
            part = key_grad[block * block_rows : (block + 1) * block_rows, :]
            cos_a = cos_block[block]
            sin_a = sin_block[block]
            cosine = cos_a * cos_row[...] - sin_a * sin_row[...]
            sine = sin_a * cos_row[...] + cos_a * sin_row[...]
            signed = jnp.where(
                lax.broadcasted_iota(jnp.int32, sine.shape, 1) < HEAD_DIM // 2, sine, -sine
            )
            turned = part * cosine + pltpu.roll(part, HEAD_DIM // 2, 1) * signed
            grad_ref[block, 0, :, lanes] = turned.astype(BF16)
            grad_ref[block, 1, :, lanes] = value_grad[
                block * block_rows : (block + 1) * block_rows, :
            ].astype(BF16)

        @pl.when(step == 0)
        def _():
            acc_ref[lanes, :] = query_part

        @pl.when(step > 0)
        def _():
            acc_ref[lanes, :] += query_part

    @pl.when(step == pl.num_programs(0) - 1)
    def _():
        half = keep_ref.shape[0]
        for slot in range(2 * half):
            first = pl.multiple_of(lax.bitwise_xor(spot_ref[0], PATH[slot]) * 128, 128)
            part = (acc_ref[:, pl.ds(first, 128)] * SCALE).astype(BF16)
            if slot < half:
                keep_ref[slot] = part
            else:
                send_ref[slot - half] = part


def backward(spot, kv, qu, exponent, stats, own, tables):
    blocks, _, block_rows, width = kv.shape
    slices, _, slice_rows, _ = qu.shape
    queries = slices * slice_rows
    heads = width // HEAD_DIM
    per = 4
    key_rows = blocks * block_rows
    whole = lambda shape: pl.BlockSpec(shape, lambda i, s: (0,) * len(shape))
    half = jax.ShapeDtypeStruct((slices // 2, width, slice_rows), BF16)
    return pl.pallas_call(
        backward_kernel,
        grid_spec=pltpu.PrefetchScalarGridSpec(
            num_scalar_prefetch=1,
            grid=(blocks // per,),
            in_specs=[
                pl.BlockSpec((per, 2, block_rows, width), lambda i, s: (i, 0, 0, 0)),
                whole(qu.shape),
                pl.BlockSpec((heads, per * block_rows, queries), lambda i, s: (0, i, 0)),
                whole(stats.shape),
                whole(own.shape),
                pl.BlockSpec((per, 1, HEAD_DIM), lambda i, s: (i, 0, 0)),
                pl.BlockSpec((per, 1, HEAD_DIM), lambda i, s: (i, 0, 0)),
                whole((block_rows, HEAD_DIM)),
                whole((block_rows, HEAD_DIM)),
            ],
            out_specs=(
                pl.BlockSpec((per, 2, block_rows, width), lambda i, s: (i, 0, 0, 0)),
                whole(half.shape),
                whole(half.shape),
            ),
            scratch_shapes=[pltpu.VMEM((width, queries), F32)],
        ),
        out_shape=(jax.ShapeDtypeStruct((blocks, 2, block_rows, width), BF16), half, half),
        compiler_params=params(48),
        cost_estimate=pl.CostEstimate(
            flops=8 * heads * queries * key_rows * HEAD_DIM,
            bytes_accessed=14 * MIB,
            transcendentals=0,
        ),
    )(spot, kv, qu, exponent, stats, own, *tables)


def merge_output(parts, stats):
    def kernel(parts_ref, stats_ref, out_ref):
        for head in range(parts_ref.shape[1] // HEAD_DIM):
            lanes = slice(head * HEAD_DIM, (head + 1) * HEAD_DIM)
            _, shares, _ = merged_stats(stats_ref[...], head)
            total = jnp.zeros((HEAD_DIM, parts_ref.shape[2]), F32)
            for block in range(parts_ref.shape[0]):
                total += parts_ref[block, lanes, :].astype(F32) * shares[block : block + 1, :]
            out_ref[lanes, :] = total.astype(BF16)

    return pl.pallas_call(
        kernel, out_shape=jax.ShapeDtypeStruct(parts.shape[1:], BF16), compiler_params=params(8)
    )(parts, stats)


def merge_query_grad(kept, arrived, cosine, sine):
    def kernel(kept_ref, arrived_ref, cos_ref, sin_ref, out_ref):
        total = kept_ref[0].astype(F32) + arrived_ref[0].astype(F32)
        half = HEAD_DIM // 2
        turned = []
        for head in range(total.shape[0] // HEAD_DIM):
            first = total[head * HEAD_DIM : head * HEAD_DIM + half, :]
            second = total[head * HEAD_DIM + half : (head + 1) * HEAD_DIM, :]
            turned.append(first * cos_ref[...] + second * sin_ref[...])
            turned.append(second * cos_ref[...] - first * sin_ref[...])
        out_ref[...] = jnp.concatenate(turned, axis=0).T.astype(BF16)

    return pl.pallas_call(
        kernel,
        out_shape=jax.ShapeDtypeStruct((kept.shape[2], kept.shape[1]), BF16),
        compiler_params=params(8),
    )(kept, arrived, cosine, sine)


def projection_grad(spot, near, far, cotangent):
    count = 2 * near.shape[0]

    def kernel(spot_ref, near_ref, far_ref, cot_ref, out_ref, joined_ref):
        for slot in range(count):
            first = pl.multiple_of(lax.bitwise_xor(spot_ref[0], PATH[slot]) * 128, 128)
            ref = near_ref if slot < count // 2 else far_ref
            joined_ref[:, pl.ds(first, 128)] = ref[slot % (count // 2)]
        out_ref[...] = matmul(joined_ref[...], cot_ref[...]) * (1.0 / LOSS_SCALE)

    vmem = pl.BlockSpec(memory_space=pltpu.VMEM)
    return pl.pallas_call(
        kernel,
        out_shape=jax.ShapeDtypeStruct((near.shape[1], cotangent.shape[1]), F32),
        in_specs=[pl.BlockSpec(memory_space=pltpu.SMEM), vmem, vmem, vmem],
        out_specs=vmem,
        scratch_shapes=[pltpu.VMEM((near.shape[1], count * 128), BF16)],
        compiler_params=params(16),
    )(spot, near, far, cotangent)


def assemble(spot, query_near, query_far, upstream_near, upstream_far):
    count = 2 * query_near.shape[0]

    def kernel(spot_ref, q_near, q_far, u_near, u_far, out_ref):
        for slot in range(count):
            place = lax.bitwise_xor(spot_ref[0], PATH[slot])
            out_ref[place, 0] = (q_near if slot < count // 2 else q_far)[slot % (count // 2)]
            out_ref[place, 1] = (u_near if slot < count // 2 else u_far)[slot % (count // 2)]

    vmem = pl.BlockSpec(memory_space=pltpu.VMEM)
    return pl.pallas_call(
        kernel,
        out_shape=jax.ShapeDtypeStruct((count, 2) + query_near.shape[1:], BF16),
        in_specs=[pl.BlockSpec(memory_space=pltpu.SMEM)] + [vmem] * 4,
        out_specs=vmem,
        compiler_params=params(16),
    )(spot, query_near, query_far, upstream_near, upstream_far)


def upstream_part(cotangent, out_weight):
    def kernel(cot_ref, weight_ref, out_ref):
        out_ref[...] = matmul(cot_ref[...], weight_ref[...], NT).astype(BF16)

    return pl.pallas_call(
        kernel,
        out_shape=jax.ShapeDtypeStruct((cotangent.shape[0], out_weight.shape[0]), BF16),
        compiler_params=params(32),
    )(cotangent, out_weight)


def per_device(
    queries, key_vectors, value_vectors, cotangent, out_weight, frame_valid, group_offset, guide_index
):
    seq_count, fsdp_count = lax.axis_size("seq"), lax.axis_size("fsdp")
    z_count = fsdp_count
    x_count = seq_count // z_count
    seq_index, fsdp_index = lax.axis_index("seq"), lax.axis_index("fsdp")
    z_index = seq_index % z_count
    cfg_index = lax.axis_index("cfg")
    block_rows = key_vectors.shape[1]
    group_rows, width = queries.shape[1], queries.shape[2]
    slice_rows = group_rows // z_count

    def place(x, z, f):
        return (x * z_count + z) * fsdp_count + f

    spots = [
        (x, z, f) for x in range(x_count) for z in range(z_count) for f in range(fsdp_count)
    ]
    plane_groups = [
        [place(x, z, f) for x in range(x_count) for f in range(fsdp_count)] for z in range(z_count)
    ]
    column_groups = [[x * z_count + z for z in range(z_count)] for x in range(x_count)]
    turn = [(place(x, z, f), place(x, (f + z) % z_count, z)) for x, z, f in spots]
    back = [(d, s) for s, d in turn]
    cfg_stride = seq_count * fsdp_count
    back_across = [
        (c * cfg_stride + s, (1 - c) * cfg_stride + d) for c in range(2) for s, d in back
    ]

    def over_plane(x):
        return lax.all_to_all(x, ("seq", "fsdp"), 0, 0, axis_index_groups=plane_groups, tiled=True)

    def over_column(x):
        return lax.all_to_all(x, "seq", 0, 0, axis_index_groups=column_groups, tiled=True)

    def over_fsdp(x):
        return lax.all_to_all(x, "fsdp", 0, 0, tiled=True)

    def z_partner(x, bit):
        return lax.ppermute(x, "seq", [(s, s ^ bit) for s in range(seq_count)])

    def fsdp_partner(x, bit):
        return lax.ppermute(x, "fsdp", [(s, s ^ bit) for s in range(fsdp_count)])

    def doubled(x, partner):
        near = x[None]
        for bit in (4, 2):
            near = jnp.concatenate([near, partner(near, bit)])
        return near, partner(near, 1)

    def tied(first, second):
        return lax.optimization_barrier((first, second))

    z_spot = z_index.astype(jnp.int32)[None]
    fsdp_spot = fsdp_index.astype(jnp.int32)[None]
    guide = 1.5 + guide_index[0].astype(F32) / 1024.0
    own_weight = jnp.where(cfg_index == 0, guide, 1.0 - guide)

    query_rows = lax.dynamic_slice(
        queries[0], (fsdp_index * slice_rows, 0), (slice_rows, width)
    )
    query_near, query_far = doubled(
        lax.ppermute(query_rows, ("seq", "fsdp"), turn), z_partner
    )
    partial = upstream_part(cotangent, out_weight).reshape(fsdp_count, slice_rows, width)
    partial = over_fsdp(partial)
    packed = pack_blocks(key_vectors, value_vectors, x_count * fsdp_count)
    partial, packed = tied(partial, packed)
    kv = over_plane(packed)

    summed = jnp.sum(partial.astype(F32), axis=0)
    upstream_rows = (own_weight * summed).astype(BF16)
    upstream_near, upstream_far = doubled(
        lax.ppermute(upstream_rows, ("seq", "fsdp"), turn), z_partner
    )
    qu = assemble(z_spot, query_near, query_far, upstream_near, upstream_far)

    block_ids = jnp.arange(x_count * fsdp_count, dtype=jnp.int32)
    block_start = place(block_ids // fsdp_count, z_index, block_ids % fsdp_count) * block_rows
    row_ids = jnp.arange(block_rows, dtype=jnp.int32)
    positions = (block_start[:, None] + row_ids[None, :]).reshape(-1)
    frame_match = (positions // FRAME_TOK)[:, None] == jnp.arange(
        frame_valid.shape[0], dtype=jnp.int32
    )[None, :]
    valid = jnp.sum(jnp.where(frame_match, frame_valid[None, :], 0), axis=1) == 1
    bias = jnp.broadcast_to(
        jnp.where(valid, 0.0, NEG_LARGE).astype(F32)[:, None], (positions.shape[0], 128)
    )
    frequency = 10000.0 ** (-jnp.arange(HEAD_DIM // 2, dtype=F32) / (HEAD_DIM // 2))
    twice = jnp.concatenate([frequency, frequency])
    block_angle = (block_start.astype(F32)[:, None] * twice[None, :])[:, None, :]
    row_angle = row_ids.astype(F32)[:, None] * twice[None, :]
    tables = (jnp.cos(block_angle), jnp.sin(block_angle), jnp.cos(row_angle), jnp.sin(row_angle))
    slice_id = (z_index - fsdp_index) % z_count
    query_positions = (
        group_offset[0] + slice_id * slice_rows + jnp.arange(slice_rows, dtype=jnp.int32)
    )
    query_angle = query_positions.astype(F32)[None, :] * frequency[:, None]

    exponent, out_parts, own_stats, own_top = forward(kv, qu, bias)
    stats = over_column(jnp.broadcast_to(own_stats[None], (z_count,) + own_stats.shape))
    stats, out_parts = tied(stats, out_parts)
    out_slices = over_column(out_parts)
    grads, query_keep, query_send = backward(z_spot, kv, qu, exponent, stats, own_top, tables)
    grads, out_slices, query_send = lax.optimization_barrier((grads, out_slices, query_send))
    key_grad, value_grad = unpack_blocks(over_plane(grads))

    for bit in (1, 2):
        arrived = z_partner(query_send, bit)
        total = (query_keep.astype(F32) + arrived.astype(F32)).astype(BF16)
        half = total.shape[0] // 2
        query_keep, query_send = total[:half], total[half:]
    arrived = z_partner(query_send, 4)
    query_slice = merge_query_grad(query_keep, arrived, jnp.cos(query_angle), jnp.sin(query_angle))
    query_grad = lax.ppermute(query_slice, ("seq", "fsdp"), back)[None]

    slice_stats = lax.dynamic_slice_in_dim(stats, z_index * slice_rows, slice_rows, axis=2)
    attn_rows = merge_output(out_slices, slice_stats)
    own_rows = lax.ppermute(attn_rows, ("seq", "fsdp"), back)
    other_rows = lax.ppermute(attn_rows, ("cfg", "seq", "fsdp"), back_across)
    mixed = own_weight * own_rows.astype(F32) + (1.0 - own_weight) * other_rows.astype(F32)
    mixed_near, mixed_far = doubled(mixed.astype(BF16), fsdp_partner)
    weight_grad = projection_grad(fsdp_spot, mixed_near, mixed_far, cotangent)
    return (query_grad, key_grad, value_grad, weight_grad)


def solution(mesh):
    placed = (
        P("cfg", None, "seq"),
        P("cfg", ("seq", "fsdp"), None),
        P("cfg", ("seq", "fsdp"), None),
        P(None, "fsdp"),
        P("seq", "fsdp"),
        P(),
        P(),
        P(),
    )
    return jax.shard_map(
        per_device,
        mesh=mesh,
        in_specs=placed,
        out_specs=(
            P("cfg", "fsdp", "seq"),
            P("cfg", ("seq", "fsdp"), None),
            P("cfg", ("seq", "fsdp"), None),
            P("seq", "fsdp"),
        ),
        check_vma=False,
    )
```

time: 350 us -> 221 us (0.63)
  the two profiles are of different devices: /device:TPU:32 before, /device:TPU:232 now
where the time goes in v2:
time: 221 us; the launch traced here: 220 us
  waiting for transfers between devices  88.9 us (40%)
  starting transfers between devices  85.3 us (39%)
  Pallas kernels  32 us (14%)
  local copies, waits for them, and re-layouts  10.4 us (5%)
  between operations  2.3 us (1%)
    ppermute x9, waiting for transfers between devices, z_partner(): return lax.ppermute(x, 'seq', [(s, s ^ bit) for s in range(seq_count)])  32.2 us
    all_to_all x2, starting transfers between devices, over_plane(): lax.all_to_all(x, ('seq', 'fsdp'), 0, 0, axis_index_groups=plane_groups,...  28.7 us
    all_to_all x2, starting transfers between devices, over_column(): lax.all_to_all(x, 'seq', 0, 0, axis_index_groups=column_groups, tiled=True)  13.1 us
    pallas_call x1, Pallas kernels, forward(): pl.pallas_call(forward_kernel, grid=(queries // step,), in_specs=[pl.Bloc...  12.9 us
    pallas_call x1, Pallas kernels, backward(): pl.pallas_call(backward_kernel, grid_spec=pltpu.PrefetchScalarGridSpec(nu...  11.9 us
    ppermute x3, starting transfers between devices, fsdp_partner(): return lax.ppermute(x, 'fsdp', [(s, s ^ bit) for s in range(fsdp_count)])  10.4 us
    ppermute x9, starting transfers between devices, z_partner(): return lax.ppermute(x, 'seq', [(s, s ^ bit) for s in range(seq_count)])  9.88 us
    ppermute x1, waiting for transfers between devices, per_device(): query_grad = lax.ppermute(query_slice, ('seq', 'fsdp'), back)[None]  9.64 us
  transfers between devices with their start and end apart: 22, of which 16 were waited for; matrix products, arithmetic and copies ran while one was open for 1% of the time, Pallas kernels for 7%

profile of v2, /device:TPU:232, one launch (start us, length us, event | category | flops | bytes accessed | tf_op | source)
XLA Modules:
  0.0 220.2 jit_solution(10450587024661778642)
XLA Ops:
  0.7 1.4 copy-done.1
  2.0 1.0 copy-done.10
  3.0 1.4 shard_map.111
  4.4 5.8 %all-to-all-start = ((bf16[8,128,256]{2,1,0:T(8,128)(2,1)}), bf16[8,128,256]{2,1,0:T(8,128)(2,1)S(1)}, u32[]{:S(2)}, u32[]{:S(2)}) async-start(bf16[8,128,256]{2,1,0:T(8,128)(2,1)} %bitcast.1), calls=%async_computation | async-start | bytes 1048576 | tf_op jit(solution)/shard_map/all_to_all | solution.py:384
  10.2 2.0 shard_map.112
  12.2 6.0 %all-to-all-done = bf16[8,128,256]{2,1,0:T(8,128)(2,1)S(1)} async-done(((bf16[8,128,256]{2,1,0:T(8,128)(2,1)}), bf16[8,128,256]{2,1,0:T(8,128)(2,1)S(1)}, u32[]{:S(2)}, u32[]{:S(2)}) %all-to-all-start) | async-done | bytes 524320 | tf_op jit(solution)/shard_map/all_to_all | solution.py:384
  18.3 6.4 %all-to-all-start.1 = ((bf16[16,2,128,256]{3,2,1,0:T(8,128)(2,1)}), bf16[16,2,128,256]{3,2,1,0:T(8,128)(2,1)S(1)}, u32[]{:S(2)}, u32[]{:S(2)}) async-start(bf16[16,2,128,256]{3,2,1,0:T(8,128)(2,1)} %shard_map.112), calls=%async_computation.1 | async-start | bytes 4194304 | tf_op jit(solution)/shard_map/all_to_all | solution.py:378
  24.7 3.0 %collective-permute-start = (bf16[128,256]{1,0:T(8,128)(2,1)S(1)}, bf16[128,256]{1,0:T(8,128)(2,1)S(1)}, u32[]{:S(2)}, u32[]{:S(2)}) collective-permute-start(bf16[128,256]{1,0:T(8,128)(2,1)S(1)} %dynamic-slice_bitcast_fusion), channel_id=1, source_target_pairs={{0,0},{1,8},{2,16},{3,24},{4,32},{5,40},{6,48},{7,56},{8,9},{9,17}... | collective-permute-start | bytes 196616 | tf_op jit(solution)/shard_map/ppermute | solution.py:410
  28.4 8.3 %collective-permute-done = bf16[128,256]{1,0:T(8,128)(2,1)S(1)} collective-permute-done((bf16[128,256]{1,0:T(8,128)(2,1)S(1)}, bf16[128,256]{1,0:T(8,128)(2,1)S(1)}, u32[]{:S(2)}, u32[]{:S(2)}) %collective-permute-start) | collective-permute-done | bytes 65568 | tf_op jit(solution)/shard_map/ppermute | solution.py:410
  36.9 6.0 %collective-permute-start.4 = (bf16[128,256]{1,0:T(8,128)(2,1)S(1)}, bf16[128,256]{1,0:T(8,128)(2,1)S(1)}, u32[]{:S(2)}, u32[]{:S(2)}) collective-permute-start(bf16[128,256]{1,0:T(8,128)(2,1)S(1)} %multiply_convert_fusion), channel_id=1, source_target_pairs={{0,0},{1,8},{2,16},{3,24},{4,32},{5,40},{6,48},{7,56},{8,9},{9,17}... | collective-permute-start | bytes 196616 | tf_op jit(solution)/shard_map/ppermute | solution.py:421
  42.9 5.7 %collective-permute-done.4 = bf16[128,256]{1,0:T(8,128)(2,1)S(1)} collective-permute-done((bf16[128,256]{1,0:T(8,128)(2,1)S(1)}, bf16[128,256]{1,0:T(8,128)(2,1)S(1)}, u32[]{:S(2)}, u32[]{:S(2)}) %collective-permute-start.4) | collective-permute-done | bytes 65568 | tf_op jit(solution)/shard_map/ppermute | solution.py:421
  48.6 3.8 %collective-permute-start.5 = (bf16[1,128,256]{2,1,0:T(8,128)(2,1)S(1)}, bf16[1,128,256]{2,1,0:T(8,128)(2,1)S(1)}, u32[]{:S(2)}, u32[]{:S(2)}) collective-permute-start(bf16[1,128,256]{2,1,0:T(8,128)(2,1)S(1)} %bitcast.23), channel_id=1, source_target_pairs={{0,32},{8,40},{16,48},{24,56},{32,0},{40,8},{48,16},{56,24},{64,96... | collective-permute-start | bytes 196616 | tf_op jit(solution)/shard_map/ppermute | solution.py:387
  52.4 0.4 collective-permute-start.2
  52.9 4.3 %collective-permute-done.5 = bf16[1,128,256]{2,1,0:T(8,128)(2,1)S(1)} collective-permute-done((bf16[1,128,256]{2,1,0:T(8,128)(2,1)S(1)}, bf16[1,128,256]{2,1,0:T(8,128)(2,1)S(1)}, u32[]{:S(2)}, u32[]{:S(2)}) %collective-permute-start.5) | collective-permute-done | bytes 65568 | tf_op jit(solution)/shard_map/ppermute | solution.py:387
  57.2 0.3 collective-permute-start.6
  57.7 4.6 %collective-permute-done.2 = bf16[2,128,256]{2,1,0:T(8,128)(2,1)S(1)} collective-permute-done((bf16[2,128,256]{2,1,0:T(8,128)(2,1)S(1)}, bf16[2,128,256]{2,1,0:T(8,128)(2,1)S(1)}, u32[]{:S(2)}, u32[]{:S(2)}) %collective-permute-start.2) | collective-permute-done | bytes 131104 | tf_op jit(solution)/shard_map/ppermute | solution.py:387
  62.4 1.6 collective-permute-done.6
  64.0 2.4 %collective-permute-start.7 = (bf16[4,128,256]{2,1,0:T(8,128)(2,1)S(1)}, bf16[4,128,256]{2,1,0:T(8,128)(2,1)S(1)}, u32[]{:S(2)}, u32[]{:S(2)}) collective-permute-start(bf16[4,128,256]{2,1,0:T(8,128)(2,1)S(1)} %pad_maximum_fusion.1.u_near), channel_id=1, source_target_pairs={{0,8},{8,0},{16,24},{24,16},{32,40},{40,32},{48,56},{56,48},{64,72... | collective-permute-start | bytes 786440 | tf_op jit(solution)/shard_map/ppermute | solution.py:387
  66.5 5.1 %collective-permute-done.3.q_far = bf16[4,128,256]{2,1,0:T(8,128)(2,1)S(1)} collective-permute-done((bf16[4,128,256]{2,1,0:T(8,128)(2,1)S(1)}, bf16[4,128,256]{2,1,0:T(8,128)(2,1)S(1)}, u32[]{:S(2)}, u32[]{:S(2)}) %collective-permute-start.3) | collective-permute-done | bytes 262176 | tf_op jit(solution)/shard_map/ppermute | solution.py:387
  71.6 3.5 %collective-permute-done.7.u_far = bf16[4,128,256]{2,1,0:T(8,128)(2,1)S(1)} collective-permute-done((bf16[4,128,256]{2,1,0:T(8,128)(2,1)S(1)}, bf16[4,128,256]{2,1,0:T(8,128)(2,1)S(1)}, u32[]{:S(2)}, u32[]{:S(2)}) %collective-permute-start.7) | collective-permute-done | bytes 262176 | tf_op jit(solution)/shard_map/ppermute | solution.py:387
  75.2 1.0 copy-done.4
  76.5 1.2 copy-done.5
  77.7 12.9 %shard_map.114 = (bf16[2,2048,1024]{2,1,0:T(8,128)(2,1)}, bf16[8,256,128]{2,1,0:T(8,128)(2,1)S(1)}, f32[4,1024]{1,0:T(4,128)S(1)}, f32[2,1024]{1,0:T(2,128)S(1)}) custom-call(bf16[16,2,128,256]{3,2,1,0:T(8,128)(2,1)S(1)} %all-to-all-done.1.kv_ref, bf16[8,2,128,256]{3,2,1,0:T(8,128)(2,1)S(1)} %copy-done.5, f32[2048,128]{1,0:T(8,128)S(1)} %broadcast_in_dim.69.bias_ref), custom_call_target="tpu_custom_call" | custom-call | flops 2147483648 | bytes 12582912 | tf_op jit(solution)/shard_map/pallas_call | solution.py:110
  90.7 0.8 copy-done.9
  91.5 0.7 broadcast_in_dim.70
  92.1 7.0 %all-to-all-start.2 = ((f32[8,4,1024]{2,1,0:T(4,128)}), f32[8,4,1024]{2,1,0:T(4,128)S(1)}, u32[]{:S(2)}, u32[]{:S(2)}) async-start(f32[8,4,1024]{2,1,0:T(4,128)} %broadcast_in_dim.70), calls=%async_computation.2 | async-start | bytes 262144 | tf_op jit(solution)/shard_map/all_to_all | solution.py:381
  99.2 6.4 %all-to-all-done.2.stats_ref = f32[8,4,1024]{2,1,0:T(4,128)S(1)} async-done(((f32[8,4,1024]{2,1,0:T(4,128)}), f32[8,4,1024]{2,1,0:T(4,128)S(1)}, u32[]{:S(2)}, u32[]{:S(2)}) %all-to-all-start.2) | async-done | bytes 131104 | tf_op jit(solution)/shard_map/all_to_all | solution.py:381
  105.5 6.1 %all-to-all-start.3 = ((bf16[8,256,128]{2,1,0:T(8,128)(2,1)}), bf16[8,256,128]{2,1,0:T(8,128)(2,1)S(1)}, u32[]{:S(2)}, u32[]{:S(2)}) async-start(bf16[8,256,128]{2,1,0:T(8,128)(2,1)} %copy-done.9), calls=%async_computation.3 | async-start | bytes 1048576 | tf_op jit(solution)/shard_map/all_to_all | solution.py:381
  112.4 1.2 copy-done.6
  113.6 11.9 %shard_map.115 = (bf16[16,2,128,256]{3,2,1,0:T(8,128)(2,1)S(1)}, bf16[4,256,128]{2,1,0:T(8,128)(2,1)S(1)}, bf16[4,256,128]{2,1,0:T(8,128)(2,1)S(1)}) custom-call(s32[1]{0:T(128)} %bitcast.spot_ref, bf16[16,2,128,256]{3,2,1,0:T(8,128)(2,1)S(1)} %all-to-all-done.1.kv_ref, bf16[8,2,128,256]{3,2,1,0:T(8,128)(2,1)S(1)} %copy-done.6, ...), custom_call_target="tpu_custom_call" | custom-call | flops 4294967296 | bytes 14680064 | tf_op jit(solution)/shard_map/pallas_call | solution.py:229
  125.5 1.4 copy-done.3
  126.9 0.7 copy-done.11
  127.6 22.3 %all-to-all-start.4 = ((bf16[16,2,128,256]{3,2,1,0:T(8,128)(2,1)}), bf16[16,2,128,256]{3,2,1,0:T(8,128)(2,1)S(1)}, u32[]{:S(2)}, u32[]{:S(2)}) async-start(bf16[16,2,128,256]{3,2,1,0:T(8,128)(2,1)} %copy-done.3), calls=%async_computation.4 | async-start | bytes 4194304 | tf_op jit(solution)/shard_map/all_to_all | solution.py:378
  150.1 6.0 %collective-permute-start.12 = (bf16[256,128]{1,0:T(8,128)(2,1)S(1)}, bf16[256,128]{1,0:T(8,128)(2,1)S(1)}, u32[]{:S(2)}, u32[]{:S(2)}) collective-permute-start(bf16[256,128]{1,0:T(8,128)(2,1)S(1)} %shard_map.118), channel_id=1, source_target_pairs={{0,0},{8,1},{16,2},{24,3},{32,4},{40,5},{48,6},{56,7},{9,8},{17,9}... | collective-permute-start | bytes 196616 | tf_op jit(solution)/shard_map/ppermute | solution.py:466
  156.4 0.7 collective-permute-start.8
  157.0 5.2 %collective-permute-done.12 = bf16[256,128]{1,0:T(8,128)(2,1)S(1)} collective-permute-done((bf16[256,128]{1,0:T(8,128)(2,1)S(1)}, bf16[256,128]{1,0:T(8,128)(2,1)S(1)}, u32[]{:S(2)}, u32[]{:S(2)}) %collective-permute-start.12) | collective-permute-done | bytes 65568 | tf_op jit(solution)/shard_map/ppermute | solution.py:466
  162.2 6.5 %collective-permute-done.13 = bf16[256,128]{1,0:T(8,128)(2,1)S(1)} collective-permute-done((bf16[256,128]{1,0:T(8,128)(2,1)S(1)}, bf16[256,128]{1,0:T(8,128)(2,1)S(1)}, u32[]{:S(2)}, u32[]{:S(2)}) %collective-permute-start.13) | collective-permute-done | bytes 65568 | tf_op jit(solution)/shard_map/ppermute | solution.py:467
  169.5 7.6 %collective-permute-done.14 = bf16[1,256,128]{2,1,0:T(8,128)(2,1)S(1)} collective-permute-done((bf16[1,256,128]{2,1,0:T(8,128)(2,1)S(1)}, bf16[1,256,128]{2,1,0:T(8,128)(2,1)S(1)}, u32[]{:S(2)}, u32[]{:S(2)}) %collective-permute-start.14) | collective-permute-done | bytes 65568 | tf_op jit(solution)/shard_map/ppermute | solution.py:390
  177.1 10.3 %collective-permute-start.15 = (bf16[2,256,128]{2,1,0:T(8,128)(2,1)S(1)}, bf16[2,256,128]{2,1,0:T(8,128)(2,1)S(1)}, u32[]{:S(2)}, u32[]{:S(2)}) collective-permute-start(bf16[2,256,128]{2,1,0:T(8,128)(2,1)S(1)} %pad_maximum_fusion.5), channel_id=1, source_target_pairs={{0,2},{1,3},{2,0},{3,1},{4,6},{5,7},{6,4},{7,5},{8,10},{9,11},{10,... | collective-permute-start | bytes 393224 | tf_op jit(solution)/shard_map/ppermute | solution.py:390
  187.4 2.0 collective-permute-start.9
  189.5 1.3 collective-permute-done.15
  190.9 5.2 %collective-permute-done.9 = bf16[2,256,128]{2,1,0:T(8,128)(2,1)S(1)} collective-permute-done((bf16[2,256,128]{2,1,0:T(8,128)(2,1)S(1)}, bf16[2,256,128]{2,1,0:T(8,128)(2,1)S(1)}, u32[]{:S(2)}, u32[]{:S(2)}) %collective-permute-start.9) | collective-permute-done | bytes 131104 | tf_op jit(solution)/shard_map/ppermute | solution.py:387
  196.5 8.0 %collective-permute-done.10.arrived_ref = bf16[1,256,128]{2,1,0:T(8,128)(2,1)S(1)} collective-permute-done((bf16[1,256,128]{2,1,0:T(8,128)(2,1)S(1)}, bf16[1,256,128]{2,1,0:T(8,128)(2,1)S(1)}, u32[]{:S(2)}, u32[]{:S(2)}) %collective-permute-start.10) | collective-permute-done | bytes 65568 | tf_op jit(solution)/shard_map/ppermute | solution.py:387
  204.5 1.9 collective-permute-start.11
  206.5 9.6 %collective-permute-done.11 = bf16[128,256]{1,0:T(8,128)(2,1)S(1)} collective-permute-done((bf16[128,256]{1,0:T(8,128)(2,1)S(1)}, bf16[128,256]{1,0:T(8,128)(2,1)S(1)}, u32[]{:S(2)}, u32[]{:S(2)}) %collective-permute-start.11) | collective-permute-done | bytes 65568 | tf_op jit(solution)/shard_map/ppermute | solution.py:462
  216.1 1.5 shard_map.119
  217.7 1.9 shard_map.117
  219.5 0.6 copy.16
  (61 shorter events, 2.8 us)
Async XLA Ops:
  0.6 24.0 %copy-start = (bf16[1,1024,256]{2,1,0:T(8,128)(2,1)S(1)}, bf16[1,1024,256]{2,1,0:T(8,128)(2,1)}, u32[]{:S(2)}) copy-start(bf16[1,1024,256]{2,1,0:T(8,128)(2,1)} %param.8) | copy-start | bytes 1572868
  0.6 1.4 copy-start.1
  2.0 1.0 copy-start.10
  3.0 7.2 %copy-start.7 = (bf16[1,128,4096]{2,1,0:T(8,128)(2,1)S(1)}, bf16[1,128,4096]{2,1,0:T(8,128)(2,1)}, u32[]{:S(2)}) copy-start(bf16[1,128,4096]{2,1,0:T(8,128)(2,1)} %k_ref.1) | copy-start | bytes 3145732
  3.0 7.2 %copy-start.8 = (bf16[1,128,4096]{2,1,0:T(8,128)(2,1)S(1)}, bf16[1,128,4096]{2,1,0:T(8,128)(2,1)}, u32[]{:S(2)}) copy-start(bf16[1,128,4096]{2,1,0:T(8,128)(2,1)} %v_ref.1) | copy-start | bytes 3145732
  4.4 13.9 %all-to-all-start = ((bf16[8,128,256]{2,1,0:T(8,128)(2,1)}), bf16[8,128,256]{2,1,0:T(8,128)(2,1)S(1)}, u32[]{:S(2)}, u32[]{:S(2)}) async-start(bf16[8,128,256]{2,1,0:T(8,128)(2,1)} %bitcast.1), calls=%async_computation | async-start | bytes 1048576 | tf_op jit(solution)/shard_map/all_to_all | solution.py:384
  18.3 57.9 %all-to-all-start.1 = ((bf16[16,2,128,256]{3,2,1,0:T(8,128)(2,1)}), bf16[16,2,128,256]{3,2,1,0:T(8,128)(2,1)S(1)}, u32[]{:S(2)}, u32[]{:S(2)}) async-start(bf16[16,2,128,256]{3,2,1,0:T(8,128)(2,1)} %shard_map.112), calls=%async_computation.1 | async-start | bytes 4194304 | tf_op jit(solution)/shard_map/all_to_all | solution.py:378
  24.6 41.8 %copy-start.12 = (s32[5]{0:T(128)S(1)}, s32[5]{0:T(128)}, u32[]{:S(2)}) copy-start(s32[5]{0:T(128)} %param.13) | copy-start | bytes 64
  24.7 12.1 %collective-permute-start = (bf16[128,256]{1,0:T(8,128)(2,1)S(1)}, bf16[128,256]{1,0:T(8,128)(2,1)S(1)}, u32[]{:S(2)}, u32[]{:S(2)}) collective-permute-start(bf16[128,256]{1,0:T(8,128)(2,1)S(1)} %dynamic-slice_bitcast_fusion), channel_id=1, source_target_pairs={{0,0},{1,8},{2,16},{3,24},{4,32},{5,40},{6,48},{7,56},{8,9},{9,17}... | collective-permute-start | bytes 196616 | tf_op jit(solution)/shard_map/ppermute | solution.py:410
  36.8 15.7 %collective-permute-start.1 = (bf16[1,128,256]{2,1,0:T(8,128)(2,1)S(1)}, bf16[1,128,256]{2,1,0:T(8,128)(2,1)S(1)}, u32[]{:S(2)}, u32[]{:S(2)}) collective-permute-start(bf16[1,128,256]{2,1,0:T(8,128)(2,1)S(1)} %bitcast.20), channel_id=1, source_target_pairs={{0,32},{8,40},{16,48},{24,56},{32,0},{40,8},{48,16},{56,24},{64,96... | collective-permute-start | bytes 196616 | tf_op jit(solution)/shard_map/ppermute | solution.py:387
  36.9 11.8 %collective-permute-start.4 = (bf16[128,256]{1,0:T(8,128)(2,1)S(1)}, bf16[128,256]{1,0:T(8,128)(2,1)S(1)}, u32[]{:S(2)}, u32[]{:S(2)}) collective-permute-start(bf16[128,256]{1,0:T(8,128)(2,1)S(1)} %multiply_convert_fusion), channel_id=1, source_target_pairs={{0,0},{1,8},{2,16},{3,24},{4,32},{5,40},{6,48},{7,56},{8,9},{9,17}... | collective-permute-start | bytes 196616 | tf_op jit(solution)/shard_map/ppermute | solution.py:421
  48.6 8.6 %collective-permute-start.5 = (bf16[1,128,256]{2,1,0:T(8,128)(2,1)S(1)}, bf16[1,128,256]{2,1,0:T(8,128)(2,1)S(1)}, u32[]{:S(2)}, u32[]{:S(2)}) collective-permute-start(bf16[1,128,256]{2,1,0:T(8,128)(2,1)S(1)} %bitcast.23), channel_id=1, source_target_pairs={{0,32},{8,40},{16,48},{24,56},{32,0},{40,8},{48,16},{56,24},{64,96... | collective-permute-start | bytes 196616 | tf_op jit(solution)/shard_map/ppermute | solution.py:387
  52.4 9.8 %collective-permute-start.2 = (bf16[2,128,256]{2,1,0:T(8,128)(2,1)S(1)}, bf16[2,128,256]{2,1,0:T(8,128)(2,1)S(1)}, u32[]{:S(2)}, u32[]{:S(2)}) collective-permute-start(bf16[2,128,256]{2,1,0:T(8,128)(2,1)S(1)} %pad_maximum_fusion.3), channel_id=1, source_target_pairs={{0,16},{8,24},{16,0},{24,8},{32,48},{40,56},{48,32},{56,40},{64,80... | collective-permute-start | bytes 393224 | tf_op jit(solution)/shard_map/ppermute | solution.py:387
  57.2 6.7 %collective-permute-start.6 = (bf16[2,128,256]{2,1,0:T(8,128)(2,1)S(1)}, bf16[2,128,256]{2,1,0:T(8,128)(2,1)S(1)}, u32[]{:S(2)}, u32[]{:S(2)}) collective-permute-start(bf16[2,128,256]{2,1,0:T(8,128)(2,1)S(1)} %pad_maximum_fusion.4), channel_id=1, source_target_pairs={{0,16},{8,24},{16,0},{24,8},{32,48},{40,56},{48,32},{56,40},{64,80... | collective-permute-start | bytes 393224 | tf_op jit(solution)/shard_map/ppermute | solution.py:387
  62.3 9.3 %collective-permute-start.3 = (bf16[4,128,256]{2,1,0:T(8,128)(2,1)S(1)}, bf16[4,128,256]{2,1,0:T(8,128)(2,1)S(1)}, u32[]{:S(2)}, u32[]{:S(2)}) collective-permute-start(bf16[4,128,256]{2,1,0:T(8,128)(2,1)S(1)} %pad_maximum_fusion.q_near), channel_id=1, source_target_pairs={{0,8},{8,0},{16,24},{24,16},{32,40},{40,32},{48,56},{56,48},{64,72... | collective-permute-start | bytes 786440 | tf_op jit(solution)/shard_map/ppermute | solution.py:387
  64.0 11.1 %collective-permute-start.7 = (bf16[4,128,256]{2,1,0:T(8,128)(2,1)S(1)}, bf16[4,128,256]{2,1,0:T(8,128)(2,1)S(1)}, u32[]{:S(2)}, u32[]{:S(2)}) collective-permute-start(bf16[4,128,256]{2,1,0:T(8,128)(2,1)S(1)} %pad_maximum_fusion.1.u_near), channel_id=1, source_target_pairs={{0,8},{8,0},{16,24},{24,16},{32,40},{40,32},{48,56},{56,48},{64,72... | collective-permute-start | bytes 786440 | tf_op jit(solution)/shard_map/ppermute | solution.py:387
  75.2 1.0 copy-start.4
  76.5 1.2 copy-start.5
  90.7 0.8 copy-start.9
  92.1 13.4 %all-to-all-start.2 = ((f32[8,4,1024]{2,1,0:T(4,128)}), f32[8,4,1024]{2,1,0:T(4,128)S(1)}, u32[]{:S(2)}, u32[]{:S(2)}) async-start(f32[8,4,1024]{2,1,0:T(4,128)} %broadcast_in_dim.70), calls=%async_computation.2 | async-start | bytes 262144 | tf_op jit(solution)/shard_map/all_to_all | solution.py:381
  105.5 22.0 %all-to-all-start.3 = ((bf16[8,256,128]{2,1,0:T(8,128)(2,1)}), bf16[8,256,128]{2,1,0:T(8,128)(2,1)S(1)}, u32[]{:S(2)}, u32[]{:S(2)}) async-start(bf16[8,256,128]{2,1,0:T(8,128)(2,1)} %copy-done.9), calls=%async_computation.3 | async-start | bytes 1048576 | tf_op jit(solution)/shard_map/all_to_all | solution.py:381
  112.4 1.2 copy-start.6
  125.5 1.4 copy-start.3
  126.9 0.7 copy-start.11
  127.6 90.1 %all-to-all-start.4 = ((bf16[16,2,128,256]{3,2,1,0:T(8,128)(2,1)}), bf16[16,2,128,256]{3,2,1,0:T(8,128)(2,1)S(1)}, u32[]{:S(2)}, u32[]{:S(2)}) async-start(bf16[16,2,128,256]{3,2,1,0:T(8,128)(2,1)} %copy-done.3), calls=%async_computation.4 | async-start | bytes 4194304 | tf_op jit(solution)/shard_map/all_to_all | solution.py:378
  150.1 12.1 %collective-permute-start.12 = (bf16[256,128]{1,0:T(8,128)(2,1)S(1)}, bf16[256,128]{1,0:T(8,128)(2,1)S(1)}, u32[]{:S(2)}, u32[]{:S(2)}) collective-permute-start(bf16[256,128]{1,0:T(8,128)(2,1)S(1)} %shard_map.118), channel_id=1, source_target_pairs={{0,0},{8,1},{16,2},{24,3},{32,4},{40,5},{48,6},{56,7},{9,8},{17,9}... | collective-permute-start | bytes 196616 | tf_op jit(solution)/shard_map/ppermute | solution.py:466
  156.1 12.6 %collective-permute-start.13 = (bf16[256,128]{1,0:T(8,128)(2,1)S(1)}, bf16[256,128]{1,0:T(8,128)(2,1)S(1)}, u32[]{:S(2)}, u32[]{:S(2)}) collective-permute-start(bf16[256,128]{1,0:T(8,128)(2,1)S(1)} %shard_map.118), channel_id=1, source_target_pairs={{0,128},{8,129},{16,130},{24,131},{32,132},{40,133},{48,134},{56,1... | collective-permute-start | bytes 196616 | tf_op jit(solution)/shard_map/ppermute | solution.py:467
  156.4 31.0 %collective-permute-start.8 = (bf16[4,256,128]{2,1,0:T(8,128)(2,1)}, bf16[4,256,128]{2,1,0:T(8,128)(2,1)S(1)}, u32[]{:S(2)}, u32[]{:S(2)}) collective-permute-start(bf16[4,256,128]{2,1,0:T(8,128)(2,1)} %copy-done.11), channel_id=1, source_target_pairs={{0,8},{8,0},{16,24},{24,16},{32,40},{40,32},{48,56},{56,48},{64,72... | collective-permute-start | bytes 786440 | tf_op jit(solution)/shard_map/ppermute | solution.py:387
  168.7 8.3 %collective-permute-start.14 = (bf16[1,256,128]{2,1,0:T(8,128)(2,1)S(1)}, bf16[1,256,128]{2,1,0:T(8,128)(2,1)S(1)}, u32[]{:S(2)}, u32[]{:S(2)}) collective-permute-start(bf16[1,256,128]{2,1,0:T(8,128)(2,1)S(1)} %fusion), channel_id=1, source_target_pairs={{0,4},{1,5},{2,6},{3,7},{4,0},{5,1},{6,2},{7,3},{8,12},{9,13},{10,... | collective-permute-start | bytes 196616 | tf_op jit(solution)/shard_map/ppermute | solution.py:390
  169.5 46.6 %copy-start.2 = (bf16[1024,640]{1,0:T(8,128)(2,1)S(1)}, bf16[1024,640]{1,0:T(8,128)(2,1)}, u32[]{:S(2)}) copy-start(bf16[1024,640]{1,0:T(8,128)(2,1)} %cot_ref.3) | copy-start | bytes 3932164
  177.1 13.7 %collective-permute-start.15 = (bf16[2,256,128]{2,1,0:T(8,128)(2,1)S(1)}, bf16[2,256,128]{2,1,0:T(8,128)(2,1)S(1)}, u32[]{:S(2)}, u32[]{:S(2)}) collective-permute-start(bf16[2,256,128]{2,1,0:T(8,128)(2,1)S(1)} %pad_maximum_fusion.5), channel_id=1, source_target_pairs={{0,2},{1,3},{2,0},{3,1},{4,6},{5,7},{6,4},{7,5},{8,10},{9,11},{10,... | collective-permute-start | bytes 393224 | tf_op jit(solution)/shard_map/ppermute | solution.py:390
  187.4 8.7 %collective-permute-start.9 = (bf16[2,256,128]{2,1,0:T(8,128)(2,1)S(1)}, bf16[2,256,128]{2,1,0:T(8,128)(2,1)S(1)}, u32[]{:S(2)}, u32[]{:S(2)}) collective-permute-start(bf16[2,256,128]{2,1,0:T(8,128)(2,1)S(1)} %slice.17), channel_id=1, source_target_pairs={{0,16},{8,24},{16,0},{24,8},{32,48},{40,56},{48,32},{56,40},{64,80... | collective-permute-start | bytes 393224 | tf_op jit(solution)/shard_map/ppermute | solution.py:387
  190.8 25.3 %collective-permute-start.16 = (bf16[4,256,128]{2,1,0:T(8,128)(2,1)S(1)}, bf16[4,256,128]{2,1,0:T(8,128)(2,1)S(1)}, u32[]{:S(2)}, u32[]{:S(2)}) collective-permute-start(bf16[4,256,128]{2,1,0:T(8,128)(2,1)S(1)} %pad_maximum_fusion.2.near_ref), channel_id=1, source_target_pairs={{0,1},{1,0},{2,3},{3,2},{4,5},{5,4},{6,7},{7,6},{8,9},{9,8},{10,11... | collective-permute-start | bytes 786440 | tf_op jit(solution)/shard_map/ppermute | solution.py:390
  196.2 8.3 %collective-permute-start.10 = (bf16[1,256,128]{2,1,0:T(8,128)(2,1)S(1)}, bf16[1,256,128]{2,1,0:T(8,128)(2,1)S(1)}, u32[]{:S(2)}, u32[]{:S(2)}) collective-permute-start(bf16[1,256,128]{2,1,0:T(8,128)(2,1)S(1)} %get-tuple-element.36), channel_id=1, source_target_pairs={{0,32},{8,40},{16,48},{24,56},{32,0},{40,8},{48,16},{56,24},{64,96... | collective-permute-start | bytes 196616 | tf_op jit(solution)/shard_map/ppermute | solution.py:387
  204.5 11.6 %collective-permute-start.11 = (bf16[128,256]{1,0:T(8,128)(2,1)S(1)}, bf16[128,256]{1,0:T(8,128)(2,1)S(1)}, u32[]{:S(2)}, u32[]{:S(2)}) collective-permute-start(bf16[128,256]{1,0:T(8,128)(2,1)S(1)} %shard_map.116), channel_id=1, source_target_pairs={{0,0},{8,1},{16,2},{24,3},{32,4},{40,5},{48,6},{56,7},{9,8},{17,9}... | collective-permute-start | bytes 196616 | tf_op jit(solution)/shard_map/ppermute | solution.py:462

commit v3 on v2

--- a/solution.py
+++ b/solution.py
@@ -70,18 +70,19 @@
     )(packed)
 
 
-def forward_kernel(kv_ref, qu_ref, bias_ref, exp_ref, out_ref, stat_ref, top_ref):
+def forward_kernel(spot_ref, kv_ref, query_ref, bias_ref, exp_ref, out_ref, log_ref, top_ref):
     key_rows = kv_ref.shape[0] * kv_ref.shape[2]
-    query_rows = qu_ref.shape[0] * qu_ref.shape[2]
+    per, slice_rows = query_ref.shape[0], query_ref.shape[1]
+    query_rows = per * slice_rows
+    slices = out_ref.shape[0]
     heads = kv_ref.shape[3] // HEAD_DIM
     bias = jnp.concatenate([bias_ref[...]] * (query_rows // 128), axis=1)
-    rows, tops = [], []
+    logs, tops = [], []
     for head in range(heads):
         lanes = slice(head * HEAD_DIM, (head + 1) * HEAD_DIM)
         keys = kv_ref[:, 0, :, lanes].reshape(key_rows, HEAD_DIM)
         values = kv_ref[:, 1, :, lanes].reshape(key_rows, HEAD_DIM)
-        query = qu_ref[:, 0, :, lanes].reshape(query_rows, HEAD_DIM)
-        upstream = qu_ref[:, 1, :, lanes].reshape(query_rows, HEAD_DIM)
+        query = query_ref[:, :, lanes].reshape(query_rows, HEAD_DIM)
         scores = matmul(keys, query, NT) * EXP2_SCALE + bias
         top = jnp.maximum(jnp.max(scores, axis=0, keepdims=True), NEG_FLOOR)
         exponent = jnp.exp2(scores - top)
@@ -89,42 +90,45 @@
         exponent_bf = exponent.astype(BF16)
         exp_ref[head] = exponent_bf
         safe = jnp.maximum(total, 1e-30)
-        output = matmul(values, exponent_bf, TN) * (1.0 / safe)
-        delta = jnp.sum(upstream.astype(F32).T * output, axis=0, keepdims=True)
-        rows += [jnp.where(total > 0.0, top + jnp.log2(safe), NEG_FLOOR), delta]
+        output = (matmul(values, exponent_bf, TN) * (1.0 / safe)).astype(BF16)
+        logs.append(jnp.where(total > 0.0, top + jnp.log2(safe), NEG_FLOOR))
         tops.append(top)
-        for part in range(query_rows // 128):
-            out_ref[part, lanes, :] = output[:, part * 128 : (part + 1) * 128].astype(BF16)
-    stat_ref[...] = jnp.concatenate(rows, axis=0)
+        for part in range(per):
+            place = lax.rem(pl.program_id(0) * per + part + spot_ref[1], slices)
+            out_ref[place, lanes, :] = output[:, part * slice_rows : (part + 1) * slice_rows]
+    log_ref[...] = jnp.concatenate(logs, axis=0)
     top_ref[...] = jnp.concatenate(tops, axis=0)
 
 
-def forward(kv, qu, bias):
+def forward(spot, kv, query, bias):
     blocks, _, block_rows, width = kv.shape
     key_rows = blocks * block_rows
-    slices, _, slice_rows, _ = qu.shape
+    slices, slice_rows, _ = query.shape
     queries = slices * slice_rows
     heads = width // HEAD_DIM
     step = 256
     per = step // slice_rows
     return pl.pallas_call(
         forward_kernel,
-        grid=(queries // step,),
-        in_specs=[
-            pl.BlockSpec((blocks, 2, block_rows, width), lambda i: (0, 0, 0, 0)),
-            pl.BlockSpec((per, 2, slice_rows, width), lambda i: (i, 0, 0, 0)),
-            pl.BlockSpec((key_rows, 128), lambda i: (0, 0)),
-        ],
-        out_specs=(
-            pl.BlockSpec((heads, key_rows, step), lambda i: (0, 0, i)),
-            pl.BlockSpec((per, width, slice_rows), lambda i: (i, 0, 0)),
-            pl.BlockSpec((2 * heads, step), lambda i: (0, i)),
-            pl.BlockSpec((heads, step), lambda i: (0, i)),
+        grid_spec=pltpu.PrefetchScalarGridSpec(
+            num_scalar_prefetch=1,
+            grid=(queries // step,),
+            in_specs=[
+                pl.BlockSpec((blocks, 2, block_rows, width), lambda i, s: (0, 0, 0, 0)),
+                pl.BlockSpec((per, slice_rows, width), lambda i, s: (i, 0, 0)),
+                pl.BlockSpec((key_rows, 128), lambda i, s: (0, 0)),
+            ],
+            out_specs=(
+                pl.BlockSpec((heads, key_rows, step), lambda i, s: (0, 0, i)),
+                pl.BlockSpec((slices, width, slice_rows), lambda i, s: (0, 0, 0)),
+                pl.BlockSpec((heads, step), lambda i, s: (0, i)),
+                pl.BlockSpec((heads, step), lambda i, s: (0, i)),
+            ),
         ),
         out_shape=(
             jax.ShapeDtypeStruct((heads, key_rows, queries), BF16),
             jax.ShapeDtypeStruct((slices, width, slice_rows), BF16),
-            jax.ShapeDtypeStruct((2 * heads, queries), F32),
+            jax.ShapeDtypeStruct((heads, queries), F32),
             jax.ShapeDtypeStruct((heads, queries), F32),
         ),
         compiler_params=params(48),
@@ -133,7 +137,40 @@
             bytes_accessed=12 * MIB,
             transcendentals=heads * queries * key_rows,
         ),
-    )(kv, qu, bias)
+    )(spot, kv, query, bias)
+
+
+def local_stats(spot, upstream, parts, logs):
+    slices, slice_rows, width = upstream.shape
+    heads = width // HEAD_DIM
+
+    def kernel(spot_ref, up_ref, parts_ref, log_ref, out_ref):
+        deltas = []
+        for part in range(slices):
+            place = lax.rem(part + spot_ref[1], slices)
+            product = up_ref[part].astype(F32).T * parts_ref[place].astype(F32)
+            deltas.append(
+                [
+                    jnp.sum(product[head * HEAD_DIM : (head + 1) * HEAD_DIM], axis=0, keepdims=True)
+                    for head in range(heads)
+                ]
+            )
+        rows = []
+        for head in range(heads):
+            rows.append(log_ref[head : head + 1, :])
+            rows.append(jnp.concatenate([delta[head] for delta in deltas], axis=1))
+        stats = jnp.concatenate(rows, axis=0)
+        for copy in range(slices):
+            out_ref[copy] = stats
+
+    vmem = pl.BlockSpec(memory_space=pltpu.VMEM)
+    return pl.pallas_call(
+        kernel,
+        out_shape=jax.ShapeDtypeStruct((slices, 2 * heads, slices * slice_rows), F32),
+        in_specs=[pl.BlockSpec(memory_space=pltpu.SMEM), vmem, vmem, vmem],
+        out_specs=vmem,
+        compiler_params=params(16),
+    )(spot, upstream, parts, logs)
 
 
 def merged_stats(stats, head):
@@ -149,7 +186,8 @@
 def backward_kernel(
     spot_ref,
     kv_ref,
-    qu_ref,
+    query_ref,
+    up_ref,
     exp_ref,
     stats_ref,
     own_ref,
@@ -165,7 +203,7 @@
     step = pl.program_id(0)
     blocks, block_rows = kv_ref.shape[0], kv_ref.shape[2]
     key_rows = blocks * block_rows
-    query_rows = qu_ref.shape[0] * qu_ref.shape[2]
+    query_rows = query_ref.shape[0] * query_ref.shape[1]
     heads = kv_ref.shape[3] // HEAD_DIM
     stats = stats_ref[...]
     for head in range(heads):
@@ -174,8 +212,8 @@
         factor = jnp.exp2(own_ref[head : head + 1, :] - log_total)
         keys = kv_ref[:, 0, :, lanes].reshape(key_rows, HEAD_DIM)
         values = kv_ref[:, 1, :, lanes].reshape(key_rows, HEAD_DIM)
-        query = qu_ref[:, 0, :, lanes].reshape(query_rows, HEAD_DIM)
-        upstream = qu_ref[:, 1, :, lanes].reshape(query_rows, HEAD_DIM)
+        query = query_ref[:, :, lanes].reshape(query_rows, HEAD_DIM)
+        upstream = up_ref[:, :, lanes].reshape(query_rows, HEAD_DIM)
         probability = exp_ref[head].astype(F32) * factor
         value_grad = matmul(probability.astype(BF16), upstream)
         prob_grad = matmul(values, upstream, NT)
@@ -209,7 +247,8 @@
     def _():
         half = keep_ref.shape[0]
         for slot in range(2 * half):
-            first = pl.multiple_of(lax.bitwise_xor(spot_ref[0], PATH[slot]) * 128, 128)
+            place = lax.bitwise_xor(spot_ref[0], PATH[slot]) + 2 * half - spot_ref[1]
+            first = pl.multiple_of(lax.rem(place, 2 * half) * 128, 128)
             part = (acc_ref[:, pl.ds(first, 128)] * SCALE).astype(BF16)
             if slot < half:
                 keep_ref[slot] = part
@@ -217,9 +256,9 @@
                 send_ref[slot - half] = part
 
 
-def backward(spot, kv, qu, exponent, stats, own, tables):
+def backward(spot, kv, query, upstream, exponent, stats, own, tables):
     blocks, _, block_rows, width = kv.shape
-    slices, _, slice_rows, _ = qu.shape
+    slices, slice_rows, _ = query.shape
     queries = slices * slice_rows
     heads = width // HEAD_DIM
     per = 4
@@ -233,7 +272,8 @@
             grid=(blocks // per,),
             in_specs=[
                 pl.BlockSpec((per, 2, block_rows, width), lambda i, s: (i, 0, 0, 0)),
-                whole(qu.shape),
+                whole(query.shape),
+                whole(query.shape),
                 pl.BlockSpec((heads, per * block_rows, queries), lambda i, s: (0, i, 0)),
                 whole(stats.shape),
                 whole(own.shape),
@@ -256,7 +296,7 @@
             bytes_accessed=14 * MIB,
             transcendentals=0,
         ),
-    )(spot, kv, qu, exponent, stats, own, *tables)
+    )(spot, kv, query, upstream, exponent, stats, own, *tables)
 
 
 def merge_output(parts, stats):
@@ -293,44 +333,46 @@
     )(kept, arrived, cosine, sine)
 
 
-def projection_grad(spot, near, far, cotangent):
+def projection_grad(spot, parts, cotangent):
+    count = len(parts)
+
+    def kernel(spot_ref, *refs):
+        cot_ref, out_ref, joined_ref = refs[count:]
+        for k in range(count):
+            place = lax.rem(spot_ref[1] - spot_ref[0] + 2 * count - k, count)
+            joined_ref[:, pl.ds(pl.multiple_of(place * 128, 128), 128)] = refs[k][...]
+        out_ref[...] = matmul(joined_ref[...], cot_ref[...]) * (1.0 / LOSS_SCALE)
+
+    vmem = pl.BlockSpec(memory_space=pltpu.VMEM)
+    width = parts[0].shape[0]
+    return pl.pallas_call(
+        kernel,
+        out_shape=jax.ShapeDtypeStruct((width, cotangent.shape[1]), F32),
+        in_specs=[pl.BlockSpec(memory_space=pltpu.SMEM)] + [vmem] * (count + 1),
+        out_specs=vmem,
+        scratch_shapes=[pltpu.VMEM((width, count * 128), BF16)],
+        compiler_params=params(16),
+    )(spot, *parts, cotangent)
+
+
+def assemble(spot, near, far, shifted):
     count = 2 * near.shape[0]
 
-    def kernel(spot_ref, near_ref, far_ref, cot_ref, out_ref, joined_ref):
-        for slot in range(count):
-            first = pl.multiple_of(lax.bitwise_xor(spot_ref[0], PATH[slot]) * 128, 128)
-            ref = near_ref if slot < count // 2 else far_ref
-            joined_ref[:, pl.ds(first, 128)] = ref[slot % (count // 2)]
-        out_ref[...] = matmul(joined_ref[...], cot_ref[...]) * (1.0 / LOSS_SCALE)
-
-    vmem = pl.BlockSpec(memory_space=pltpu.VMEM)
-    return pl.pallas_call(
-        kernel,
-        out_shape=jax.ShapeDtypeStruct((near.shape[1], cotangent.shape[1]), F32),
-        in_specs=[pl.BlockSpec(memory_space=pltpu.SMEM), vmem, vmem, vmem],
-        out_specs=vmem,
-        scratch_shapes=[pltpu.VMEM((near.shape[1], count * 128), BF16)],
-        compiler_params=params(16),
-    )(spot, near, far, cotangent)
-
-
-def assemble(spot, query_near, query_far, upstream_near, upstream_far):
-    count = 2 * query_near.shape[0]
-
-    def kernel(spot_ref, q_near, q_far, u_near, u_far, out_ref):
+    def kernel(spot_ref, near_ref, far_ref, out_ref):
         for slot in range(count):
             place = lax.bitwise_xor(spot_ref[0], PATH[slot])
-            out_ref[place, 0] = (q_near if slot < count // 2 else q_far)[slot % (count // 2)]
-            out_ref[place, 1] = (u_near if slot < count // 2 else u_far)[slot % (count // 2)]
+            if shifted:
+                place = lax.rem(place + count - spot_ref[1], count)
+            out_ref[place] = (near_ref if slot < count // 2 else far_ref)[slot % (count // 2)]
 
     vmem = pl.BlockSpec(memory_space=pltpu.VMEM)
     return pl.pallas_call(
         kernel,
-        out_shape=jax.ShapeDtypeStruct((count, 2) + query_near.shape[1:], BF16),
-        in_specs=[pl.BlockSpec(memory_space=pltpu.SMEM)] + [vmem] * 4,
+        out_shape=jax.ShapeDtypeStruct((count,) + near.shape[1:], BF16),
+        in_specs=[pl.BlockSpec(memory_space=pltpu.SMEM), vmem, vmem],
         out_specs=vmem,
         compiler_params=params(16),
-    )(spot, query_near, query_far, upstream_near, upstream_far)
+    )(spot, near, far)
 
 
 def upstream_part(cotangent, out_weight):
@@ -369,9 +411,9 @@
     column_groups = [[x * z_count + z for z in range(z_count)] for x in range(x_count)]
     turn = [(place(x, z, f), place(x, (f + z) % z_count, z)) for x, z, f in spots]
     back = [(d, s) for s, d in turn]
-    cfg_stride = seq_count * fsdp_count
-    back_across = [
-        (c * cfg_stride + s, (1 - c) * cfg_stride + d) for c in range(2) for s, d in back
+    spread = [
+        [(place(x, z, f), place(x, f, (z + k) % fsdp_count)) for x, z, f in spots]
+        for k in range(fsdp_count)
     ]
 
     def over_plane(x):
@@ -385,9 +427,6 @@
 
     def z_partner(x, bit):
         return lax.ppermute(x, "seq", [(s, s ^ bit) for s in range(seq_count)])
-
-    def fsdp_partner(x, bit):
-        return lax.ppermute(x, "fsdp", [(s, s ^ bit) for s in range(fsdp_count)])
 
     def doubled(x, partner):
         near = x[None]
@@ -395,32 +434,25 @@
             near = jnp.concatenate([near, partner(near, bit)])
         return near, partner(near, 1)
 
-    def tied(first, second):
-        return lax.optimization_barrier((first, second))
-
-    z_spot = z_index.astype(jnp.int32)[None]
-    fsdp_spot = fsdp_index.astype(jnp.int32)[None]
+    tied = lax.optimization_barrier
+    spot = jnp.stack([z_index, fsdp_index]).astype(jnp.int32)
     guide = 1.5 + guide_index[0].astype(F32) / 1024.0
     own_weight = jnp.where(cfg_index == 0, guide, 1.0 - guide)
 
     query_rows = lax.dynamic_slice(
         queries[0], (fsdp_index * slice_rows, 0), (slice_rows, width)
     )
-    query_near, query_far = doubled(
-        lax.ppermute(query_rows, ("seq", "fsdp"), turn), z_partner
-    )
+    query_rows = lax.ppermute(query_rows, ("seq", "fsdp"), turn)
     partial = upstream_part(cotangent, out_weight).reshape(fsdp_count, slice_rows, width)
     partial = over_fsdp(partial)
     packed = pack_blocks(key_vectors, value_vectors, x_count * fsdp_count)
-    partial, packed = tied(partial, packed)
+    query_rows, partial, packed = tied((query_rows, partial, packed))
+
     kv = over_plane(packed)
-
     summed = jnp.sum(partial.astype(F32), axis=0)
     upstream_rows = (own_weight * summed).astype(BF16)
-    upstream_near, upstream_far = doubled(
-        lax.ppermute(upstream_rows, ("seq", "fsdp"), turn), z_partner
-    )
-    qu = assemble(z_spot, query_near, query_far, upstream_near, upstream_far)
+    query = assemble(spot, *doubled(query_rows, z_partner), True)
+    upstream_heads = assemble(spot, *doubled(upstream_rows, z_partner), False)
 
     block_ids = jnp.arange(x_count * fsdp_count, dtype=jnp.int32)
     block_start = place(block_ids // fsdp_count, z_index, block_ids % fsdp_count) * block_rows
@@ -444,13 +476,26 @@
     )
     query_angle = query_positions.astype(F32)[None, :] * frequency[:, None]
 
-    exponent, out_parts, own_stats, own_top = forward(kv, qu, bias)
-    stats = over_column(jnp.broadcast_to(own_stats[None], (z_count,) + own_stats.shape))
-    stats, out_parts = tied(stats, out_parts)
+    kv, query, upstream_heads = tied((kv, query, upstream_heads))
+    upstream = over_fsdp(upstream_heads)
+    exponent, out_parts, own_logs, own_top = forward(spot, kv, query, bias)
+    stats = over_column(local_stats(spot, upstream, out_parts, own_logs))
+    stats, out_parts = tied((stats, out_parts))
     out_slices = over_column(out_parts)
-    grads, query_keep, query_send = backward(z_spot, kv, qu, exponent, stats, own_top, tables)
-    grads, out_slices, query_send = lax.optimization_barrier((grads, out_slices, query_send))
+    grads, query_keep, query_send = backward(
+        spot, kv, query, upstream, exponent, stats, own_top, tables
+    )
+    grads, out_slices, query_send = tied((grads, out_slices, query_send))
     key_grad, value_grad = unpack_blocks(over_plane(grads))
+
+    slice_stats = lax.dynamic_slice_in_dim(stats, slice_id * slice_rows, slice_rows, axis=2)
+    attn_rows = merge_output(out_slices, slice_stats)
+    other_rows = lax.ppermute(attn_rows, "cfg", [(0, 1), (1, 0)])
+    mixed = own_weight * attn_rows.astype(F32) + (1.0 - own_weight) * other_rows.astype(F32)
+    mixed = mixed.astype(BF16)
+    weight_grad = projection_grad(
+        spot, [lax.ppermute(mixed, ("seq", "fsdp"), perm) for perm in spread], cotangent
+    )
 
     for bit in (1, 2):
         arrived = z_partner(query_send, bit)
@@ -460,14 +505,6 @@
     arrived = z_partner(query_send, 4)
     query_slice = merge_query_grad(query_keep, arrived, jnp.cos(query_angle), jnp.sin(query_angle))
     query_grad = lax.ppermute(query_slice, ("seq", "fsdp"), back)[None]
-
-    slice_stats = lax.dynamic_slice_in_dim(stats, z_index * slice_rows, slice_rows, axis=2)
-    attn_rows = merge_output(out_slices, slice_stats)
-    own_rows = lax.ppermute(attn_rows, ("seq", "fsdp"), back)
-    other_rows = lax.ppermute(attn_rows, ("cfg", "seq", "fsdp"), back_across)
-    mixed = own_weight * own_rows.astype(F32) + (1.0 - own_weight) * other_rows.astype(F32)
-    mixed_near, mixed_far = doubled(mixed.astype(BF16), fsdp_partner)
-    weight_grad = projection_grad(fsdp_spot, mixed_near, mixed_far, cotangent)
     return (query_grad, key_grad, value_grad, weight_grad)
 
 

time: 221 us -> 217 us (0.982)
  the two profiles are of different devices: /device:TPU:232 before, /device:TPU:14 now
where the time goes in v3:
time: 217 us; the launch traced here: 216 us
  starting transfers between devices  120 us (55%)
  waiting for transfers between devices  42.7 us (20%)
  Pallas kernels  36.7 us (17%)
  local copies, waits for them, and re-layouts  12.2 us (6%)
  other arithmetic  2.37 us (1%)
  between operations  2.32 us (1%)
    ppermute x8, starting transfers between devices, per_device(): lax.ppermute(mixed, ('seq', 'fsdp'), perm)  47.3 us
    ppermute x9, starting transfers between devices, z_partner(): return lax.ppermute(x, 'seq', [(s, s ^ bit) for s in range(seq_count)])  26.9 us
    ppermute x9, waiting for transfers between devices, z_partner(): return lax.ppermute(x, 'seq', [(s, s ^ bit) for s in range(seq_count)])  26.6 us
    all_to_all x2, starting transfers between devices, over_plane(): lax.all_to_all(x, ('seq', 'fsdp'), 0, 0, axis_index_groups=plane_groups,...  16.2 us
    pallas_call x1, Pallas kernels, forward(): pl.pallas_call(forward_kernel, grid_spec=pltpu.PrefetchScalarGridSpec(num...  13.9 us
    pallas_call x1, Pallas kernels, backward(): pl.pallas_call(backward_kernel, grid_spec=pltpu.PrefetchScalarGridSpec(nu...  12.6 us
    unnamed x35, local copies, waits for them, and re-layouts  11.8 us
    all_to_all x2, starting transfers between devices, over_fsdp(): return lax.all_to_all(x, 'fsdp', 0, 0, tiled=True)  11.2 us
  transfers between devices with their start and end apart: 26, of which 11 were waited for; matrix products, arithmetic and copies ran while one was open for 1% of the time, Pallas kernels for 15%

profile of v3, /device:TPU:14, one launch (start us, length us, event | category | flops | bytes accessed | tf_op | source)
XLA Modules:
  0.0 216.0 jit_solution(18434885770789833151)
XLA Ops:
  0.7 1.4 copy-done.1
  2.0 1.0 copy-done.14
  3.0 1.4 shard_map.111
  4.4 5.8 %all-to-all-start = ((bf16[8,128,256]{2,1,0:T(8,128)(2,1)}), bf16[8,128,256]{2,1,0:T(8,128)(2,1)S(1)}, u32[]{:S(2)}, u32[]{:S(2)}) async-start(bf16[8,128,256]{2,1,0:T(8,128)(2,1)} %bitcast.3), calls=%async_computation | async-start | bytes 1048576 | tf_op jit(solution)/shard_map/all_to_all | solution.py:426
  10.2 6.0 %collective-permute-start = (bf16[128,256]{1,0:T(8,128)(2,1)S(1)}, bf16[128,256]{1,0:T(8,128)(2,1)S(1)}, u32[]{:S(2)}, u32[]{:S(2)}) collective-permute-start(bf16[128,256]{1,0:T(8,128)(2,1)S(1)} %dynamic-slice_bitcast_fusion), channel_id=1, source_target_pairs={{0,0},{1,8},{2,16},{3,24},{4,32},{5,40},{6,48},{7,56},{8,9},{9,17}... | collective-permute-start | bytes 196616 | tf_op jit(solution)/shard_map/ppermute | solution.py:445
  16.2 2.0 shard_map.112
  18.2 1.7 collective-permute-done
  19.9 9.3 %all-to-all-start.1 = ((bf16[16,2,128,256]{3,2,1,0:T(8,128)(2,1)}), bf16[16,2,128,256]{3,2,1,0:T(8,128)(2,1)S(1)}, u32[]{:S(2)}, u32[]{:S(2)}) async-start(bf16[16,2,128,256]{3,2,1,0:T(8,128)(2,1)} %shard_map.112), calls=%async_computation.1 | async-start | bytes 4194304 | tf_op jit(solution)/shard_map/all_to_all | solution.py:420
  29.9 4.9 %collective-permute-start.4 = (bf16[1,128,256]{2,1,0:T(8,128)(2,1)S(1)}, bf16[1,128,256]{2,1,0:T(8,128)(2,1)S(1)}, u32[]{:S(2)}, u32[]{:S(2)}) collective-permute-start(bf16[1,128,256]{2,1,0:T(8,128)(2,1)S(1)} %fusion), channel_id=1, source_target_pairs={{0,32},{8,40},{16,48},{24,56},{32,0},{40,8},{48,16},{56,24},{64,96... | collective-permute-start | bytes 196616 | tf_op jit(solution)/shard_map/ppermute | solution.py:429
  34.8 1.1 collective-permute-start.1
  36.0 3.0 %collective-permute-done.4 = bf16[1,128,256]{2,1,0:T(8,128)(2,1)S(1)} collective-permute-done((bf16[1,128,256]{2,1,0:T(8,128)(2,1)S(1)}, bf16[1,128,256]{2,1,0:T(8,128)(2,1)S(1)}, u32[]{:S(2)}, u32[]{:S(2)}) %collective-permute-start.4) | collective-permute-done | bytes 65568 | tf_op jit(solution)/shard_map/ppermute | solution.py:429
  39.0 4.5 %collective-permute-start.5 = (bf16[2,128,256]{2,1,0:T(8,128)(2,1)S(1)}, bf16[2,128,256]{2,1,0:T(8,128)(2,1)S(1)}, u32[]{:S(2)}, u32[]{:S(2)}) collective-permute-start(bf16[2,128,256]{2,1,0:T(8,128)(2,1)S(1)} %pad_maximum_fusion.3), channel_id=1, source_target_pairs={{0,16},{8,24},{16,0},{24,8},{32,48},{40,56},{48,32},{56,40},{64,80... | collective-permute-start | bytes 393224 | tf_op jit(solution)/shard_map/ppermute | solution.py:429
  43.5 1.2 collective-permute-done.1
  45.3 6.3 %collective-permute-done.5 = bf16[2,128,256]{2,1,0:T(8,128)(2,1)S(1)} collective-permute-done((bf16[2,128,256]{2,1,0:T(8,128)(2,1)S(1)}, bf16[2,128,256]{2,1,0:T(8,128)(2,1)S(1)}, u32[]{:S(2)}, u32[]{:S(2)}) %collective-permute-start.5) | collective-permute-done | bytes 131104 | tf_op jit(solution)/shard_map/ppermute | solution.py:429
  51.8 2.4 %collective-permute-done.2 = bf16[2,128,256]{2,1,0:T(8,128)(2,1)S(1)} collective-permute-done((bf16[2,128,256]{2,1,0:T(8,128)(2,1)S(1)}, bf16[2,128,256]{2,1,0:T(8,128)(2,1)S(1)}, u32[]{:S(2)}, u32[]{:S(2)}) %collective-permute-start.2) | collective-permute-done | bytes 131104 | tf_op jit(solution)/shard_map/ppermute | solution.py:429
  54.4 5.9 %collective-permute-done.6.far_ref = bf16[4,128,256]{2,1,0:T(8,128)(2,1)S(1)} collective-permute-done((bf16[4,128,256]{2,1,0:T(8,128)(2,1)S(1)}, bf16[4,128,256]{2,1,0:T(8,128)(2,1)S(1)}, u32[]{:S(2)}, u32[]{:S(2)}) %collective-permute-start.6) | collective-permute-done | bytes 262176 | tf_op jit(solution)/shard_map/ppermute | solution.py:429
  61.7 1.4 collective-permute-done.3.far_ref
  64.5 5.4 %all-to-all-start.2 = ((bf16[8,128,256]{2,1,0:T(8,128)(2,1)}), bf16[8,128,256]{2,1,0:T(8,128)(2,1)S(1)}, u32[]{:S(2)}, u32[]{:S(2)}) async-start(bf16[8,128,256]{2,1,0:T(8,128)(2,1)} %copy-done.8), calls=%async_computation.2 | async-start | bytes 1048576 | tf_op jit(solution)/shard_map/all_to_all | solution.py:426
  70.3 1.0 copy-done.12
  71.4 13.9 %shard_map.115 = (bf16[2,2048,1024]{2,1,0:T(8,128)(2,1)}, bf16[8,256,128]{2,1,0:T(8,128)(2,1)S(1)}, f32[2,1024]{1,0:T(2,128)S(1)}, f32[2,1024]{1,0:T(2,128)S(1)}) custom-call(s32[2]{0:T(128)S(1)} %pad_add_fusion.spot_ref, bf16[16,2,128,256]{3,2,1,0:T(8,128)(2,1)S(1)} %all-to-all-done.1.kv_ref, bf16[8,128,256]{2,1,0:T(8,128)(2,1)S(1)} %copy-done.12, ...), custom_call_target="tpu_custom_call" | custom-call | flops 2147483648 | bytes 12582912 | tf_op jit(solution)/shard_map/pallas_call | solution.py:111
  86.1 1.2 copy-done.7
  87.3 1.4 shard_map.116
  88.7 6.3 %all-to-all-start.3 = ((f32[8,4,1024]{2,1,0:T(4,128)}), f32[8,4,1024]{2,1,0:T(4,128)S(1)}, u32[]{:S(2)}, u32[]{:S(2)}) async-start(f32[8,4,1024]{2,1,0:T(4,128)} %shard_map.116), calls=%async_computation.3 | async-start | bytes 262144 | tf_op jit(solution)/shard_map/all_to_all | solution.py:423
  95.1 9.1 %all-to-all-done.3.stats_ref = f32[8,4,1024]{2,1,0:T(4,128)S(1)} async-done(((f32[8,4,1024]{2,1,0:T(4,128)}), f32[8,4,1024]{2,1,0:T(4,128)S(1)}, u32[]{:S(2)}, u32[]{:S(2)}) %all-to-all-start.3) | async-done | bytes 131104 | tf_op jit(solution)/shard_map/all_to_all | solution.py:423
  104.1 3.5 %all-to-all-start.4 = ((bf16[8,256,128]{2,1,0:T(8,128)(2,1)}), bf16[8,256,128]{2,1,0:T(8,128)(2,1)S(1)}, u32[]{:S(2)}, u32[]{:S(2)}) async-start(bf16[8,256,128]{2,1,0:T(8,128)(2,1)} %copy-done.6), calls=%async_computation.4 | async-start | bytes 1048576 | tf_op jit(solution)/shard_map/all_to_all | solution.py:423
  108.3 1.0 copy-done.5
  109.4 1.0 copy-done.13
  110.4 12.6 %shard_map.117 = (bf16[16,2,128,256]{3,2,1,0:T(8,128)(2,1)S(1)}, bf16[4,256,128]{2,1,0:T(8,128)(2,1)S(1)}, bf16[4,256,128]{2,1,0:T(8,128)(2,1)S(1)}) custom-call(s32[2]{0:T(128)S(1)} %pad_add_fusion.spot_ref, bf16[16,2,128,256]{3,2,1,0:T(8,128)(2,1)S(1)} %all-to-all-done.1.kv_ref, bf16[8,128,256]{2,1,0:T(8,128)(2,1)S(1)} %copy-done.13, ...), custom_call_target="tpu_custom_call" | custom-call | flops 4294967296 | bytes 14680064 | tf_op jit(solution)/shard_map/pallas_call | solution.py:268
  123.0 1.3 copy-done.3
  125.1 6.9 %all-to-all-start.5 = ((bf16[16,2,128,256]{3,2,1,0:T(8,128)(2,1)}), bf16[16,2,128,256]{3,2,1,0:T(8,128)(2,1)S(1)}, u32[]{:S(2)}, u32[]{:S(2)}) async-start(bf16[16,2,128,256]{3,2,1,0:T(8,128)(2,1)} %copy-done.3), calls=%async_computation.5 | async-start | bytes 4194304 | tf_op jit(solution)/shard_map/all_to_all | solution.py:420
  132.0 1.9 collective-permute-start.7
  134.9 3.8 %collective-permute-done.7 = bf16[4,256,128]{2,1,0:T(8,128)(2,1)} collective-permute-done((bf16[4,256,128]{2,1,0:T(8,128)(2,1)}, bf16[4,256,128]{2,1,0:T(8,128)(2,1)}, u32[]{:S(2)}, u32[]{:S(2)}) %collective-permute-start.7) | collective-permute-done | bytes 262176 | tf_op jit(solution)/shard_map/ppermute | solution.py:429
  138.7 1.0 add_convert_fusion
  139.7 3.9 %collective-permute-start.8 = (bf16[2,256,128]{2,1,0:T(8,128)(2,1)S(1)}, bf16[2,256,128]{2,1,0:T(8,128)(2,1)S(1)}, u32[]{:S(2)}, u32[]{:S(2)}) collective-permute-start(bf16[2,256,128]{2,1,0:T(8,128)(2,1)S(1)} %slice.17), channel_id=1, source_target_pairs={{0,16},{8,24},{16,0},{24,8},{32,48},{40,56},{48,32},{56,40},{64,80... | collective-permute-start | bytes 393224 | tf_op jit(solution)/shard_map/ppermute | solution.py:429
  143.7 2.7 %collective-permute-start.12 = (bf16[256,128]{1,0:T(8,128)(2,1)S(1)}, bf16[256,128]{1,0:T(8,128)(2,1)S(1)}, u32[]{:S(2)}, u32[]{:S(2)}) collective-permute-start(bf16[256,128]{1,0:T(8,128)(2,1)S(1)} %add_convert_fusion.2), channel_id=1, source_target_pairs={{0,0},{1,8},{2,16},{3,24},{4,32},{5,40},{6,48},{7,56},{8,1},{9,9},... | collective-permute-start | bytes 196616 | tf_op jit(solution)/shard_map/ppermute | solution.py:497
  146.4 3.0 %collective-permute-start.13 = (bf16[256,128]{1,0:T(8,128)(2,1)S(1)}, bf16[256,128]{1,0:T(8,128)(2,1)S(1)}, u32[]{:S(2)}, u32[]{:S(2)}) collective-permute-start(bf16[256,128]{1,0:T(8,128)(2,1)S(1)} %add_convert_fusion.2), channel_id=1, source_target_pairs={{0,1},{1,9},{2,17},{3,25},{4,33},{5,41},{6,49},{7,57},{8,2},{9,10}... | collective-permute-start | bytes 196616 | tf_op jit(solution)/shard_map/ppermute | solution.py:497
  149.4 2.1 collective-permute-start.14
  151.5 1.2 collective-permute-start.15
  152.8 9.7 %collective-permute-start.9 = (bf16[1,256,128]{2,1,0:T(8,128)(2,1)S(1)}, bf16[1,256,128]{2,1,0:T(8,128)(2,1)S(1)}, u32[]{:S(2)}, u32[]{:S(2)}) collective-permute-start(bf16[1,256,128]{2,1,0:T(8,128)(2,1)S(1)} %get-tuple-element.44), channel_id=1, source_target_pairs={{0,32},{8,40},{16,48},{24,56},{32,0},{40,8},{48,16},{56,24},{64,96... | collective-permute-start | bytes 196616 | tf_op jit(solution)/shard_map/ppermute | solution.py:429
  162.7 2.6 %collective-permute-done.9.arrived_ref = bf16[1,256,128]{2,1,0:T(8,128)(2,1)S(1)} collective-permute-done((bf16[1,256,128]{2,1,0:T(8,128)(2,1)S(1)}, bf16[1,256,128]{2,1,0:T(8,128)(2,1)S(1)}, u32[]{:S(2)}, u32[]{:S(2)}) %collective-permute-start.9) | collective-permute-done | bytes 65568 | tf_op jit(solution)/shard_map/ppermute | solution.py:429
  165.3 2.3 %collective-permute-start.16 = (bf16[256,128]{1,0:T(8,128)(2,1)S(1)}, bf16[256,128]{1,0:T(8,128)(2,1)S(1)}, u32[]{:S(2)}, u32[]{:S(2)}) collective-permute-start(bf16[256,128]{1,0:T(8,128)(2,1)S(1)} %add_convert_fusion.2), channel_id=1, source_target_pairs={{0,4},{1,12},{2,20},{3,28},{4,36},{5,44},{6,52},{7,60},{8,5},{9,13... | collective-permute-start | bytes 196616 | tf_op jit(solution)/shard_map/ppermute | solution.py:497
  167.8 9.9 %collective-permute-start.17 = (bf16[256,128]{1,0:T(8,128)(2,1)S(1)}, bf16[256,128]{1,0:T(8,128)(2,1)S(1)}, u32[]{:S(2)}, u32[]{:S(2)}) collective-permute-start(bf16[256,128]{1,0:T(8,128)(2,1)S(1)} %add_convert_fusion.2), channel_id=1, source_target_pairs={{0,5},{1,13},{2,21},{3,29},{4,37},{5,45},{6,53},{7,61},{8,6},{9,14... | collective-permute-start | bytes 196616 | tf_op jit(solution)/shard_map/ppermute | solution.py:497
  177.7 5.9 %collective-permute-start.18 = (bf16[256,128]{1,0:T(8,128)(2,1)S(1)}, bf16[256,128]{1,0:T(8,128)(2,1)S(1)}, u32[]{:S(2)}, u32[]{:S(2)}) collective-permute-start(bf16[256,128]{1,0:T(8,128)(2,1)S(1)} %add_convert_fusion.2), channel_id=1, source_target_pairs={{0,6},{1,14},{2,22},{3,30},{4,38},{5,46},{6,54},{7,62},{8,7},{9,15... | collective-permute-start | bytes 196616 | tf_op jit(solution)/shard_map/ppermute | solution.py:497
  183.5 20.2 %collective-permute-start.19 = (bf16[256,128]{1,0:T(8,128)(2,1)S(1)}, bf16[256,128]{1,0:T(8,128)(2,1)S(1)}, u32[]{:S(2)}, u32[]{:S(2)}) collective-permute-start(bf16[256,128]{1,0:T(8,128)(2,1)S(1)} %add_convert_fusion.2), channel_id=1, source_target_pairs={{0,7},{1,15},{2,23},{3,31},{4,39},{5,47},{6,55},{7,63},{8,0},{9,8}... | collective-permute-start | bytes 196616 | tf_op jit(solution)/shard_map/ppermute | solution.py:497
  203.8 2.2 %collective-permute-start.10 = (bf16[128,256]{1,0:T(8,128)(2,1)S(1)}, bf16[128,256]{1,0:T(8,128)(2,1)S(1)}, u32[]{:S(2)}, u32[]{:S(2)}) collective-permute-start(bf16[128,256]{1,0:T(8,128)(2,1)S(1)} %shard_map.118), channel_id=1, source_target_pairs={{0,0},{8,1},{16,2},{24,3},{32,4},{40,5},{48,6},{56,7},{9,8},{17,9}... | collective-permute-start | bytes 196616 | tf_op jit(solution)/shard_map/ppermute | solution.py:507
  206.0 2.1 shard_map.121
  208.1 5.4 %collective-permute-done.10 = bf16[128,256]{1,0:T(8,128)(2,1)S(1)} collective-permute-done((bf16[128,256]{1,0:T(8,128)(2,1)S(1)}, bf16[128,256]{1,0:T(8,128)(2,1)S(1)}, u32[]{:S(2)}, u32[]{:S(2)}) %collective-permute-start.10) | collective-permute-done | bytes 65568 | tf_op jit(solution)/shard_map/ppermute | solution.py:507
  213.5 1.9 shard_map.119
  (77 shorter events, 7.9 us)
Async XLA Ops:
  0.6 9.6 %copy-start = (bf16[1,1024,256]{2,1,0:T(8,128)(2,1)S(1)}, bf16[1,1024,256]{2,1,0:T(8,128)(2,1)}, u32[]{:S(2)}) copy-start(bf16[1,1024,256]{2,1,0:T(8,128)(2,1)} %param.8) | copy-start | bytes 1572868
  0.6 1.4 copy-start.1
  2.0 1.0 copy-start.14
  3.0 13.2 %copy-start.9 = (bf16[1,128,4096]{2,1,0:T(8,128)(2,1)S(1)}, bf16[1,128,4096]{2,1,0:T(8,128)(2,1)}, u32[]{:S(2)}) copy-start(bf16[1,128,4096]{2,1,0:T(8,128)(2,1)} %k_ref.1) | copy-start | bytes 3145732
  3.0 13.2 %copy-start.10 = (bf16[1,128,4096]{2,1,0:T(8,128)(2,1)S(1)}, bf16[1,128,4096]{2,1,0:T(8,128)(2,1)}, u32[]{:S(2)}) copy-start(bf16[1,128,4096]{2,1,0:T(8,128)(2,1)} %v_ref.1) | copy-start | bytes 3145732
  4.4 15.5 %all-to-all-start = ((bf16[8,128,256]{2,1,0:T(8,128)(2,1)}), bf16[8,128,256]{2,1,0:T(8,128)(2,1)S(1)}, u32[]{:S(2)}, u32[]{:S(2)}) async-start(bf16[8,128,256]{2,1,0:T(8,128)(2,1)} %bitcast.3), calls=%async_computation | async-start | bytes 1048576 | tf_op jit(solution)/shard_map/all_to_all | solution.py:426
  10.2 9.7 %collective-permute-start = (bf16[128,256]{1,0:T(8,128)(2,1)S(1)}, bf16[128,256]{1,0:T(8,128)(2,1)S(1)}, u32[]{:S(2)}, u32[]{:S(2)}) collective-permute-start(bf16[128,256]{1,0:T(8,128)(2,1)S(1)} %dynamic-slice_bitcast_fusion), channel_id=1, source_target_pairs={{0,0},{1,8},{2,16},{3,24},{4,32},{5,40},{6,48},{7,56},{8,9},{9,17}... | collective-permute-start | bytes 196616 | tf_op jit(solution)/shard_map/ppermute | solution.py:445
  19.9 44.6 %all-to-all-start.1 = ((bf16[16,2,128,256]{3,2,1,0:T(8,128)(2,1)}), bf16[16,2,128,256]{3,2,1,0:T(8,128)(2,1)S(1)}, u32[]{:S(2)}, u32[]{:S(2)}) async-start(bf16[16,2,128,256]{3,2,1,0:T(8,128)(2,1)} %shard_map.112), calls=%async_computation.1 | async-start | bytes 4194304 | tf_op jit(solution)/shard_map/all_to_all | solution.py:420
  29.9 9.1 %collective-permute-start.4 = (bf16[1,128,256]{2,1,0:T(8,128)(2,1)S(1)}, bf16[1,128,256]{2,1,0:T(8,128)(2,1)S(1)}, u32[]{:S(2)}, u32[]{:S(2)}) collective-permute-start(bf16[1,128,256]{2,1,0:T(8,128)(2,1)S(1)} %fusion), channel_id=1, source_target_pairs={{0,32},{8,40},{16,48},{24,56},{32,0},{40,8},{48,16},{56,24},{64,96... | collective-permute-start | bytes 196616 | tf_op jit(solution)/shard_map/ppermute | solution.py:429
  34.8 9.8 %collective-permute-start.1 = (bf16[1,128,256]{2,1,0:T(8,128)(2,1)S(1)}, bf16[1,128,256]{2,1,0:T(8,128)(2,1)S(1)}, u32[]{:S(2)}, u32[]{:S(2)}) collective-permute-start(bf16[1,128,256]{2,1,0:T(8,128)(2,1)S(1)} %bitcast.19), channel_id=1, source_target_pairs={{0,32},{8,40},{16,48},{24,56},{32,0},{40,8},{48,16},{56,24},{64,96... | collective-permute-start | bytes 196616 | tf_op jit(solution)/shard_map/ppermute | solution.py:429
  39.0 12.6 %collective-permute-start.5 = (bf16[2,128,256]{2,1,0:T(8,128)(2,1)S(1)}, bf16[2,128,256]{2,1,0:T(8,128)(2,1)S(1)}, u32[]{:S(2)}, u32[]{:S(2)}) collective-permute-start(bf16[2,128,256]{2,1,0:T(8,128)(2,1)S(1)} %pad_maximum_fusion.3), channel_id=1, source_target_pairs={{0,16},{8,24},{16,0},{24,8},{32,48},{40,56},{48,32},{56,40},{64,80... | collective-permute-start | bytes 393224 | tf_op jit(solution)/shard_map/ppermute | solution.py:429
  44.7 9.5 %collective-permute-start.2 = (bf16[2,128,256]{2,1,0:T(8,128)(2,1)S(1)}, bf16[2,128,256]{2,1,0:T(8,128)(2,1)S(1)}, u32[]{:S(2)}, u32[]{:S(2)}) collective-permute-start(bf16[2,128,256]{2,1,0:T(8,128)(2,1)S(1)} %pad_maximum_fusion.2), channel_id=1, source_target_pairs={{0,16},{8,24},{16,0},{24,8},{32,48},{40,56},{48,32},{56,40},{64,80... | collective-permute-start | bytes 393224 | tf_op jit(solution)/shard_map/ppermute | solution.py:429
  45.3 24.6 %copy-start.16 = (s32[5]{0:T(128)S(1)}, s32[5]{0:T(128)}, u32[]{:S(2)}) copy-start(s32[5]{0:T(128)} %param.13) | copy-start | bytes 64
  51.7 8.6 %collective-permute-start.6 = (bf16[4,128,256]{2,1,0:T(8,128)(2,1)S(1)}, bf16[4,128,256]{2,1,0:T(8,128)(2,1)S(1)}, u32[]{:S(2)}, u32[]{:S(2)}) collective-permute-start(bf16[4,128,256]{2,1,0:T(8,128)(2,1)S(1)} %pad_maximum_fusion.1.near_ref), channel_id=1, source_target_pairs={{0,8},{8,0},{16,24},{24,16},{32,40},{40,32},{48,56},{56,48},{64,72... | collective-permute-start | bytes 786440 | tf_op jit(solution)/shard_map/ppermute | solution.py:429
  54.2 8.9 %collective-permute-start.3 = (bf16[4,128,256]{2,1,0:T(8,128)(2,1)S(1)}, bf16[4,128,256]{2,1,0:T(8,128)(2,1)S(1)}, u32[]{:S(2)}, u32[]{:S(2)}) collective-permute-start(bf16[4,128,256]{2,1,0:T(8,128)(2,1)S(1)} %pad_maximum_fusion.near_ref), channel_id=1, source_target_pairs={{0,8},{8,0},{16,24},{24,16},{32,40},{40,32},{48,56},{56,48},{64,72... | collective-permute-start | bytes 786440 | tf_op jit(solution)/shard_map/ppermute | solution.py:429
  60.9 0.8 copy-start.8
  63.7 0.8 copy-start.11
  64.5 21.6 %all-to-all-start.2 = ((bf16[8,128,256]{2,1,0:T(8,128)(2,1)}), bf16[8,128,256]{2,1,0:T(8,128)(2,1)S(1)}, u32[]{:S(2)}, u32[]{:S(2)}) async-start(bf16[8,128,256]{2,1,0:T(8,128)(2,1)} %copy-done.8), calls=%async_computation.2 | async-start | bytes 1048576 | tf_op jit(solution)/shard_map/all_to_all | solution.py:426
  70.3 1.0 copy-start.12
  85.3 0.8 copy-start.6
  86.1 18.1 %copy-start.4 = (bf16[8,128,256]{2,1,0:T(8,128)(2,1)}, bf16[8,128,256]{2,1,0:T(8,128)(2,1)S(1)}, u32[]{:S(2)}) copy-start(bf16[8,128,256]{2,1,0:T(8,128)(2,1)S(1)} %all-to-all-done.2.up_ref) | copy-start | bytes 1572868
  86.1 1.2 copy-start.7
  88.7 15.4 %all-to-all-start.3 = ((f32[8,4,1024]{2,1,0:T(4,128)}), f32[8,4,1024]{2,1,0:T(4,128)S(1)}, u32[]{:S(2)}, u32[]{:S(2)}) async-start(f32[8,4,1024]{2,1,0:T(4,128)} %shard_map.116), calls=%async_computation.3 | async-start | bytes 262144 | tf_op jit(solution)/shard_map/all_to_all | solution.py:423
  104.1 21.0 %all-to-all-start.4 = ((bf16[8,256,128]{2,1,0:T(8,128)(2,1)}), bf16[8,256,128]{2,1,0:T(8,128)(2,1)S(1)}, u32[]{:S(2)}, u32[]{:S(2)}) async-start(bf16[8,256,128]{2,1,0:T(8,128)(2,1)} %copy-done.6), calls=%async_computation.4 | async-start | bytes 1048576 | tf_op jit(solution)/shard_map/all_to_all | solution.py:423
  108.3 1.0 copy-start.5
  109.4 1.0 copy-start.13
  123.0 1.3 copy-start.3
  124.4 0.7 copy-start.15
  125.1 88.5 %all-to-all-start.5 = ((bf16[16,2,128,256]{3,2,1,0:T(8,128)(2,1)}), bf16[16,2,128,256]{3,2,1,0:T(8,128)(2,1)S(1)}, u32[]{:S(2)}, u32[]{:S(2)}) async-start(bf16[16,2,128,256]{3,2,1,0:T(8,128)(2,1)} %copy-done.3), calls=%async_computation.5 | async-start | bytes 4194304 | tf_op jit(solution)/shard_map/all_to_all | solution.py:420
  132.0 6.7 %collective-permute-start.7 = (bf16[4,256,128]{2,1,0:T(8,128)(2,1)}, bf16[4,256,128]{2,1,0:T(8,128)(2,1)}, u32[]{:S(2)}, u32[]{:S(2)}) collective-permute-start(bf16[4,256,128]{2,1,0:T(8,128)(2,1)} %copy-done.15), channel_id=1, source_target_pairs={{0,8},{8,0},{16,24},{24,16},{32,40},{40,32},{48,56},{56,48},{64,72... | collective-permute-start | bytes 786440 | tf_op jit(solution)/shard_map/ppermute | solution.py:429
  134.6 71.4 %copy-start.2 = (bf16[1024,640]{1,0:T(8,128)(2,1)S(1)}, bf16[1024,640]{1,0:T(8,128)(2,1)}, u32[]{:S(2)}) copy-start(bf16[1024,640]{1,0:T(8,128)(2,1)} %refs_8_.1) | copy-start | bytes 3932164
  134.8 8.9 %collective-permute-start.11 = (bf16[256,128]{1,0:T(8,128)(2,1)S(1)}, bf16[256,128]{1,0:T(8,128)(2,1)S(1)}, u32[]{:S(2)}, u32[]{:S(2)}) collective-permute-start(bf16[256,128]{1,0:T(8,128)(2,1)S(1)} %shard_map.120), channel_id=1, source_target_pairs={{0,128},{128,0},{1,129},{129,1},{2,130},{130,2},{3,131},{131,3},{4... | collective-permute-start | bytes 196616 | tf_op jit(solution)/shard_map/ppermute | solution.py:493
  139.7 13.0 %collective-permute-start.8 = (bf16[2,256,128]{2,1,0:T(8,128)(2,1)S(1)}, bf16[2,256,128]{2,1,0:T(8,128)(2,1)S(1)}, u32[]{:S(2)}, u32[]{:S(2)}) collective-permute-start(bf16[2,256,128]{2,1,0:T(8,128)(2,1)S(1)} %slice.17), channel_id=1, source_target_pairs={{0,16},{8,24},{16,0},{24,8},{32,48},{40,56},{48,32},{56,40},{64,80... | collective-permute-start | bytes 393224 | tf_op jit(solution)/shard_map/ppermute | solution.py:429
  143.7 24.0 %collective-permute-start.12 = (bf16[256,128]{1,0:T(8,128)(2,1)S(1)}, bf16[256,128]{1,0:T(8,128)(2,1)S(1)}, u32[]{:S(2)}, u32[]{:S(2)}) collective-permute-start(bf16[256,128]{1,0:T(8,128)(2,1)S(1)} %add_convert_fusion.2), channel_id=1, source_target_pairs={{0,0},{1,8},{2,16},{3,24},{4,32},{5,40},{6,48},{7,56},{8,1},{9,9},... | collective-permute-start | bytes 196616 | tf_op jit(solution)/shard_map/ppermute | solution.py:497
  146.4 31.3 %collective-permute-start.13 = (bf16[256,128]{1,0:T(8,128)(2,1)S(1)}, bf16[256,128]{1,0:T(8,128)(2,1)S(1)}, u32[]{:S(2)}, u32[]{:S(2)}) collective-permute-start(bf16[256,128]{1,0:T(8,128)(2,1)S(1)} %add_convert_fusion.2), channel_id=1, source_target_pairs={{0,1},{1,9},{2,17},{3,25},{4,33},{5,41},{6,49},{7,57},{8,2},{9,10}... | collective-permute-start | bytes 196616 | tf_op jit(solution)/shard_map/ppermute | solution.py:497
  149.4 34.1 %collective-permute-start.14 = (bf16[256,128]{1,0:T(8,128)(2,1)S(1)}, bf16[256,128]{1,0:T(8,128)(2,1)S(1)}, u32[]{:S(2)}, u32[]{:S(2)}) collective-permute-start(bf16[256,128]{1,0:T(8,128)(2,1)S(1)} %add_convert_fusion.2), channel_id=1, source_target_pairs={{0,2},{1,10},{2,18},{3,26},{4,34},{5,42},{6,50},{7,58},{8,3},{9,11... | collective-permute-start | bytes 196616 | tf_op jit(solution)/shard_map/ppermute | solution.py:497
  151.5 52.3 %collective-permute-start.15 = (bf16[256,128]{1,0:T(8,128)(2,1)S(1)}, bf16[256,128]{1,0:T(8,128)(2,1)S(1)}, u32[]{:S(2)}, u32[]{:S(2)}) collective-permute-start(bf16[256,128]{1,0:T(8,128)(2,1)S(1)} %add_convert_fusion.2), channel_id=1, source_target_pairs={{0,3},{1,11},{2,19},{3,27},{4,35},{5,43},{6,51},{7,59},{8,4},{9,12... | collective-permute-start | bytes 196616 | tf_op jit(solution)/shard_map/ppermute | solution.py:497
  152.8 12.5 %collective-permute-start.9 = (bf16[1,256,128]{2,1,0:T(8,128)(2,1)S(1)}, bf16[1,256,128]{2,1,0:T(8,128)(2,1)S(1)}, u32[]{:S(2)}, u32[]{:S(2)}) collective-permute-start(bf16[1,256,128]{2,1,0:T(8,128)(2,1)S(1)} %get-tuple-element.44), channel_id=1, source_target_pairs={{0,32},{8,40},{16,48},{24,56},{32,0},{40,8},{48,16},{56,24},{64,96... | collective-permute-start | bytes 196616 | tf_op jit(solution)/shard_map/ppermute | solution.py:429
  165.3 40.7 %collective-permute-start.16 = (bf16[256,128]{1,0:T(8,128)(2,1)S(1)}, bf16[256,128]{1,0:T(8,128)(2,1)S(1)}, u32[]{:S(2)}, u32[]{:S(2)}) collective-permute-start(bf16[256,128]{1,0:T(8,128)(2,1)S(1)} %add_convert_fusion.2), channel_id=1, source_target_pairs={{0,4},{1,12},{2,20},{3,28},{4,36},{5,44},{6,52},{7,60},{8,5},{9,13... | collective-permute-start | bytes 196616 | tf_op jit(solution)/shard_map/ppermute | solution.py:497
  167.8 38.2 %collective-permute-start.17 = (bf16[256,128]{1,0:T(8,128)(2,1)S(1)}, bf16[256,128]{1,0:T(8,128)(2,1)S(1)}, u32[]{:S(2)}, u32[]{:S(2)}) collective-permute-start(bf16[256,128]{1,0:T(8,128)(2,1)S(1)} %add_convert_fusion.2), channel_id=1, source_target_pairs={{0,5},{1,13},{2,21},{3,29},{4,37},{5,45},{6,53},{7,61},{8,6},{9,14... | collective-permute-start | bytes 196616 | tf_op jit(solution)/shard_map/ppermute | solution.py:497
  177.7 28.3 %collective-permute-start.18 = (bf16[256,128]{1,0:T(8,128)(2,1)S(1)}, bf16[256,128]{1,0:T(8,128)(2,1)S(1)}, u32[]{:S(2)}, u32[]{:S(2)}) collective-permute-start(bf16[256,128]{1,0:T(8,128)(2,1)S(1)} %add_convert_fusion.2), channel_id=1, source_target_pairs={{0,6},{1,14},{2,22},{3,30},{4,38},{5,46},{6,54},{7,62},{8,7},{9,15... | collective-permute-start | bytes 196616 | tf_op jit(solution)/shard_map/ppermute | solution.py:497
  183.5 22.5 %collective-permute-start.19 = (bf16[256,128]{1,0:T(8,128)(2,1)S(1)}, bf16[256,128]{1,0:T(8,128)(2,1)S(1)}, u32[]{:S(2)}, u32[]{:S(2)}) collective-permute-start(bf16[256,128]{1,0:T(8,128)(2,1)S(1)} %add_convert_fusion.2), channel_id=1, source_target_pairs={{0,7},{1,15},{2,23},{3,31},{4,39},{5,47},{6,55},{7,63},{8,0},{9,8}... | collective-permute-start | bytes 196616 | tf_op jit(solution)/shard_map/ppermute | solution.py:497
  203.8 9.7 %collective-permute-start.10 = (bf16[128,256]{1,0:T(8,128)(2,1)S(1)}, bf16[128,256]{1,0:T(8,128)(2,1)S(1)}, u32[]{:S(2)}, u32[]{:S(2)}) collective-permute-start(bf16[128,256]{1,0:T(8,128)(2,1)S(1)} %shard_map.118), channel_id=1, source_target_pairs={{0,0},{8,1},{16,2},{24,3},{32,4},{40,5},{48,6},{56,7},{9,8},{17,9}... | collective-permute-start | bytes 196616 | tf_op jit(solution)/shard_map/ppermute | solution.py:507

commit v4 on v3

--- a/solution.py
+++ b/solution.py
@@ -131,7 +131,7 @@
             jax.ShapeDtypeStruct((heads, queries), F32),
             jax.ShapeDtypeStruct((heads, queries), F32),
         ),
-        compiler_params=params(48),
+        compiler_params=params(60),
         cost_estimate=pl.CostEstimate(
             flops=4 * heads * queries * key_rows * HEAD_DIM,
             bytes_accessed=12 * MIB,
@@ -290,7 +290,7 @@
             scratch_shapes=[pltpu.VMEM((width, queries), F32)],
         ),
         out_shape=(jax.ShapeDtypeStruct((blocks, 2, block_rows, width), BF16), half, half),
-        compiler_params=params(48),
+        compiler_params=params(60),
         cost_estimate=pl.CostEstimate(
             flops=8 * heads * queries * key_rows * HEAD_DIM,
             bytes_accessed=14 * MIB,
@@ -333,26 +333,37 @@
     )(kept, arrived, cosine, sine)
 
 
-def projection_grad(spot, parts, cotangent):
-    count = len(parts)
-
-    def kernel(spot_ref, *refs):
-        cot_ref, out_ref, joined_ref = refs[count:]
-        for k in range(count):
-            place = lax.rem(spot_ref[1] - spot_ref[0] + 2 * count - k, count)
-            joined_ref[:, pl.ds(pl.multiple_of(place * 128, 128), 128)] = refs[k][...]
-        out_ref[...] = matmul(joined_ref[...], cot_ref[...]) * (1.0 / LOSS_SCALE)
-
-    vmem = pl.BlockSpec(memory_space=pltpu.VMEM)
-    width = parts[0].shape[0]
+def projection_grad(parts, cotangent):
+    count, width, _ = parts.shape
+
+    def kernel(parts_ref, cot_ref, out_ref):
+        joined = jnp.concatenate([parts_ref[part] for part in range(count)], axis=1)
+        out_ref[...] = matmul(joined, cot_ref[...]) * (1.0 / LOSS_SCALE)
+
     return pl.pallas_call(
         kernel,
         out_shape=jax.ShapeDtypeStruct((width, cotangent.shape[1]), F32),
-        in_specs=[pl.BlockSpec(memory_space=pltpu.SMEM)] + [vmem] * (count + 1),
-        out_specs=vmem,
-        scratch_shapes=[pltpu.VMEM((width, count * 128), BF16)],
         compiler_params=params(16),
-    )(spot, *parts, cotangent)
+    )(parts, cotangent)
+
+
+def own_slice(spot, queries, slice_rows):
+    width = queries.shape[2]
+
+    def kernel(spot_ref, in_ref, out_ref):
+        out_ref[...] = in_ref[0]
+
+    return pl.pallas_call(
+        kernel,
+        grid_spec=pltpu.PrefetchScalarGridSpec(
+            num_scalar_prefetch=1,
+            grid=(1,),
+            in_specs=[pl.BlockSpec((1, slice_rows, width), lambda i, s: (0, s[1], 0))],
+            out_specs=pl.BlockSpec((slice_rows, width), lambda i, s: (0, 0)),
+        ),
+        out_shape=jax.ShapeDtypeStruct((slice_rows, width), queries.dtype),
+        compiler_params=params(60),
+    )(spot, queries)
 
 
 def assemble(spot, near, far, shifted):
@@ -371,7 +382,7 @@
         out_shape=jax.ShapeDtypeStruct((count,) + near.shape[1:], BF16),
         in_specs=[pl.BlockSpec(memory_space=pltpu.SMEM), vmem, vmem],
         out_specs=vmem,
-        compiler_params=params(16),
+        compiler_params=params(8),
     )(spot, near, far)
 
 
@@ -382,7 +393,7 @@
     return pl.pallas_call(
         kernel,
         out_shape=jax.ShapeDtypeStruct((cotangent.shape[0], out_weight.shape[0]), BF16),
-        compiler_params=params(32),
+        compiler_params=params(60),
     )(cotangent, out_weight)
 
 
@@ -411,10 +422,6 @@
     column_groups = [[x * z_count + z for z in range(z_count)] for x in range(x_count)]
     turn = [(place(x, z, f), place(x, (f + z) % z_count, z)) for x, z, f in spots]
     back = [(d, s) for s, d in turn]
-    spread = [
-        [(place(x, z, f), place(x, f, (z + k) % fsdp_count)) for x, z, f in spots]
-        for k in range(fsdp_count)
-    ]
 
     def over_plane(x):
         return lax.all_to_all(x, ("seq", "fsdp"), 0, 0, axis_index_groups=plane_groups, tiled=True)
@@ -428,22 +435,21 @@
     def z_partner(x, bit):
         return lax.ppermute(x, "seq", [(s, s ^ bit) for s in range(seq_count)])
 
-    def doubled(x, partner):
-        near = x[None]
-        for bit in (4, 2):
-            near = jnp.concatenate([near, partner(near, bit)])
-        return near, partner(near, 1)
+    def doubled(near, bits):
+        for bit in bits[:-1]:
+            near = jnp.concatenate([near, z_partner(near, bit)])
+        return near, z_partner(near, bits[-1])
 
     tied = lax.optimization_barrier
     spot = jnp.stack([z_index, fsdp_index]).astype(jnp.int32)
     guide = 1.5 + guide_index[0].astype(F32) / 1024.0
     own_weight = jnp.where(cfg_index == 0, guide, 1.0 - guide)
 
-    query_rows = lax.dynamic_slice(
-        queries[0], (fsdp_index * slice_rows, 0), (slice_rows, width)
-    )
-    query_rows = lax.ppermute(query_rows, ("seq", "fsdp"), turn)
-    partial = upstream_part(cotangent, out_weight).reshape(fsdp_count, slice_rows, width)
+    query_rows = own_slice(spot, queries, slice_rows)
+    query_rows, cotangent_first = tied((query_rows, cotangent))
+    query_rows = lax.ppermute(query_rows, ("seq", "fsdp"), turn)[None]
+    query_rows = jnp.concatenate([query_rows, z_partner(query_rows, 4)])
+    partial = upstream_part(cotangent_first, out_weight).reshape(fsdp_count, slice_rows, width)
     partial = over_fsdp(partial)
     packed = pack_blocks(key_vectors, value_vectors, x_count * fsdp_count)
     query_rows, partial, packed = tied((query_rows, partial, packed))
@@ -451,8 +457,8 @@
     kv = over_plane(packed)
     summed = jnp.sum(partial.astype(F32), axis=0)
     upstream_rows = (own_weight * summed).astype(BF16)
-    query = assemble(spot, *doubled(query_rows, z_partner), True)
-    upstream_heads = assemble(spot, *doubled(upstream_rows, z_partner), False)
+    query = assemble(spot, *doubled(query_rows, (2, 1)), True)
+    upstream_heads = assemble(spot, *doubled(upstream_rows[None], (4, 2, 1)), False)
 
     block_ids = jnp.arange(x_count * fsdp_count, dtype=jnp.int32)
     block_start = place(block_ids // fsdp_count, z_index, block_ids % fsdp_count) * block_rows
@@ -486,16 +492,17 @@
         spot, kv, query, upstream, exponent, stats, own_top, tables
     )
     grads, out_slices, query_send = tied((grads, out_slices, query_send))
-    key_grad, value_grad = unpack_blocks(over_plane(grads))
+    grads = over_plane(grads)
 
     slice_stats = lax.dynamic_slice_in_dim(stats, slice_id * slice_rows, slice_rows, axis=2)
     attn_rows = merge_output(out_slices, slice_stats)
     other_rows = lax.ppermute(attn_rows, "cfg", [(0, 1), (1, 0)])
     mixed = own_weight * attn_rows.astype(F32) + (1.0 - own_weight) * other_rows.astype(F32)
-    mixed = mixed.astype(BF16)
-    weight_grad = projection_grad(
-        spot, [lax.ppermute(mixed, ("seq", "fsdp"), perm) for perm in spread], cotangent
-    )
+    mixed = lax.ppermute(mixed.astype(BF16), ("seq", "fsdp"), back)
+    mixed = jnp.broadcast_to(mixed[None], (fsdp_count,) + mixed.shape)
+    mixed, grads = tied((mixed, grads))
+    key_grad, value_grad = unpack_blocks(grads)
+    weight_grad = projection_grad(over_fsdp(mixed), cotangent)
 
     for bit in (1, 2):
         arrived = z_partner(query_send, bit)

time: 217 us -> 201 us (0.926)
  the two profiles are of different devices: /device:TPU:14 before, /device:TPU:48 now
where the time goes in v4:
time: 201 us; the launch traced here: 200 us
  starting transfers between devices  90.8 us (45%)
  waiting for transfers between devices  52.3 us (26%)
  Pallas kernels  44.6 us (22%)
  local copies, waits for them, and re-layouts  7.23 us (4%)
  other arithmetic  3.16 us (2%)
  between operations  2.26 us (1%)
    ppermute x9, starting transfers between devices, z_partner(): return lax.ppermute(x, 'seq', [(s, s ^ bit) for s in range(seq_count)])  26.3 us
    ppermute x9, waiting for transfers between devices, z_partner(): return lax.ppermute(x, 'seq', [(s, s ^ bit) for s in range(seq_count)])  22.6 us
    all_to_all x3, starting transfers between devices, over_fsdp(): return lax.all_to_all(x, 'fsdp', 0, 0, tiled=True)  20.2 us
    pallas_call x1, Pallas kernels, forward(): pl.pallas_call(forward_kernel, grid_spec=pltpu.PrefetchScalarGridSpec(num...  15.7 us
    pallas_call x1, Pallas kernels, backward(): pl.pallas_call(backward_kernel, grid_spec=pltpu.PrefetchScalarGridSpec(nu...  14.1 us
    all_to_all x2, starting transfers between devices, over_plane(): lax.all_to_all(x, ('seq', 'fsdp'), 0, 0, axis_index_groups=plane_groups,...  14.1 us
    all_to_all x2, starting transfers between devices, over_column(): lax.all_to_all(x, 'seq', 0, 0, axis_index_groups=column_groups, tiled=True)  10.6 us
    ppermute x1, waiting for transfers between devices, per_device(): mixed = lax.ppermute(mixed.astype(BF16), ('seq', 'fsdp'), back)  9.16 us
  transfers between devices with their start and end apart: 20, of which 12 were waited for; matrix products, arithmetic and copies ran while one was open for 2% of the time, Pallas kernels for 18%

profile of v4, /device:TPU:48, one launch (start us, length us, event | category | flops | bytes accessed | tf_op | source)
XLA Modules:
  0.0 200.4 jit_solution(1122229631794940700)
XLA Ops:
  0.7 0.6 pad_add_fusion.spot_ref
  1.3 2.1 %shard_map.111 = bf16[128,256]{1,0:T(8,128)(2,1)} custom-call(s32[2]{0:T(128)} %pad_add_fusion.spot_ref, bf16[1,1024,256]{2,1,0:T(8,128)(2,1)} %in_ref.1), custom_call_target="tpu_custom_call" | custom-call | tf_op jit(solution)/shard_map/pallas_call | solution.py:356
  3.4 2.8 %shard_map.112 = bf16[1024,256]{1,0:T(8,128)(2,1)} custom-call(bf16[1024,640]{1,0:T(8,128)(2,1)} %cot_ref.2, bf16[256,640]{1,0:T(8,128)(2,1)} %weight_ref.1), custom_call_target="tpu_custom_call" | custom-call | tf_op jit(solution)/shard_map/pallas_call | solution.py:393
  6.2 5.7 %all-to-all-start = ((bf16[8,128,256]{2,1,0:T(8,128)(2,1)}), bf16[8,128,256]{2,1,0:T(8,128)(2,1)S(1)}, u32[]{:S(2)}, u32[]{:S(2)}) async-start(bf16[8,128,256]{2,1,0:T(8,128)(2,1)} %bitcast.17), calls=%async_computation | async-start | bytes 1048576 | tf_op jit(solution)/shard_map/all_to_all | solution.py:433
  11.9 9.1 %collective-permute-start = (bf16[128,256]{1,0:T(8,128)(2,1)S(1)}, bf16[128,256]{1,0:T(8,128)(2,1)S(1)}, u32[]{:S(2)}, u32[]{:S(2)}) collective-permute-start(bf16[128,256]{1,0:T(8,128)(2,1)S(1)} %copy-done.11), channel_id=1, source_target_pairs={{0,0},{1,8},{2,16},{3,24},{4,32},{5,40},{6,48},{7,56},{8,9},{9,17}... | collective-permute-start | bytes 196616 | tf_op jit(solution)/shard_map/ppermute | solution.py:450
  21.0 3.2 %collective-permute-done = bf16[128,256]{1,0:T(8,128)(2,1)S(1)} collective-permute-done((bf16[128,256]{1,0:T(8,128)(2,1)S(1)}, bf16[128,256]{1,0:T(8,128)(2,1)S(1)}, u32[]{:S(2)}, u32[]{:S(2)}) %collective-permute-start) | collective-permute-done | bytes 65568 | tf_op jit(solution)/shard_map/ppermute | solution.py:450
  24.2 3.5 %collective-permute-start.1 = (bf16[1,128,256]{2,1,0:T(8,128)(2,1)S(1)}, bf16[1,128,256]{2,1,0:T(8,128)(2,1)S(1)}, u32[]{:S(2)}, u32[]{:S(2)}) collective-permute-start(bf16[1,128,256]{2,1,0:T(8,128)(2,1)S(1)} %bitcast.19), channel_id=1, source_target_pairs={{0,32},{8,40},{16,48},{24,56},{32,0},{40,8},{48,16},{56,24},{64,96... | collective-permute-start | bytes 196616 | tf_op jit(solution)/shard_map/ppermute | solution.py:436
  27.7 2.0 shard_map.113
  29.6 3.1 %collective-permute-done.1 = bf16[1,128,256]{2,1,0:T(8,128)(2,1)S(1)} collective-permute-done((bf16[1,128,256]{2,1,0:T(8,128)(2,1)S(1)}, bf16[1,128,256]{2,1,0:T(8,128)(2,1)S(1)}, u32[]{:S(2)}, u32[]{:S(2)}) %collective-permute-start.1) | collective-permute-done | bytes 65568 | tf_op jit(solution)/shard_map/ppermute | solution.py:436
  32.8 7.0 %all-to-all-start.1 = ((bf16[16,2,128,256]{3,2,1,0:T(8,128)(2,1)}), bf16[16,2,128,256]{3,2,1,0:T(8,128)(2,1)}, u32[]{:S(2)}, u32[]{:S(2)}) async-start(bf16[16,2,128,256]{3,2,1,0:T(8,128)(2,1)} %shard_map.113), calls=%async_computation.1 | async-start | bytes 4194304 | tf_op jit(solution)/shard_map/all_to_all | solution.py:427
  40.6 5.9 %collective-permute-start.4 = (bf16[1,128,256]{2,1,0:T(8,128)(2,1)S(1)}, bf16[1,128,256]{2,1,0:T(8,128)(2,1)S(1)}, u32[]{:S(2)}, u32[]{:S(2)}) collective-permute-start(bf16[1,128,256]{2,1,0:T(8,128)(2,1)S(1)} %fusion), channel_id=1, source_target_pairs={{0,32},{8,40},{16,48},{24,56},{32,0},{40,8},{48,16},{56,24},{64,96... | collective-permute-start | bytes 196616 | tf_op jit(solution)/shard_map/ppermute | solution.py:436
  46.5 2.6 %collective-permute-done.4 = bf16[1,128,256]{2,1,0:T(8,128)(2,1)S(1)} collective-permute-done((bf16[1,128,256]{2,1,0:T(8,128)(2,1)S(1)}, bf16[1,128,256]{2,1,0:T(8,128)(2,1)S(1)}, u32[]{:S(2)}, u32[]{:S(2)}) %collective-permute-start.4) | collective-permute-done | bytes 65568 | tf_op jit(solution)/shard_map/ppermute | solution.py:436
  49.2 2.9 %collective-permute-start.5 = (bf16[2,128,256]{2,1,0:T(8,128)(2,1)S(1)}, bf16[2,128,256]{2,1,0:T(8,128)(2,1)S(1)}, u32[]{:S(2)}, u32[]{:S(2)}) collective-permute-start(bf16[2,128,256]{2,1,0:T(8,128)(2,1)S(1)} %pad_maximum_fusion.2), channel_id=1, source_target_pairs={{0,16},{8,24},{16,0},{24,8},{32,48},{40,56},{48,32},{56,40},{64,80... | collective-permute-start | bytes 393224 | tf_op jit(solution)/shard_map/ppermute | solution.py:436
  52.1 3.1 %collective-permute-done.2 = bf16[2,128,256]{2,1,0:T(8,128)(2,1)S(1)} collective-permute-done((bf16[2,128,256]{2,1,0:T(8,128)(2,1)S(1)}, bf16[2,128,256]{2,1,0:T(8,128)(2,1)S(1)}, u32[]{:S(2)}, u32[]{:S(2)}) %collective-permute-start.2) | collective-permute-done | bytes 131104 | tf_op jit(solution)/shard_map/ppermute | solution.py:436
  55.2 2.6 %collective-permute-start.3 = (bf16[4,128,256]{2,1,0:T(8,128)(2,1)S(1)}, bf16[4,128,256]{2,1,0:T(8,128)(2,1)S(1)}, u32[]{:S(2)}, u32[]{:S(2)}) collective-permute-start(bf16[4,128,256]{2,1,0:T(8,128)(2,1)S(1)} %constant_dynamic-update-slice_fusion.near_ref), channel_id=1, source_target_pairs={{0,8},{8,0},{16,24},{24,16},{32,40},{40,32},{48,56},{56,48},{64,72... | collective-permute-start | bytes 786440 | tf_op jit(solution)/shard_map/ppermute | solution.py:436
  57.8 2.1 %collective-permute-start.6 = (bf16[4,128,256]{2,1,0:T(8,128)(2,1)S(1)}, bf16[4,128,256]{2,1,0:T(8,128)(2,1)S(1)}, u32[]{:S(2)}, u32[]{:S(2)}) collective-permute-start(bf16[4,128,256]{2,1,0:T(8,128)(2,1)S(1)} %pad_maximum_fusion.near_ref), channel_id=1, source_target_pairs={{0,8},{8,0},{16,24},{24,16},{32,40},{40,32},{48,56},{56,48},{64,72... | collective-permute-start | bytes 786440 | tf_op jit(solution)/shard_map/ppermute | solution.py:436
  60.1 4.5 %collective-permute-done.3.far_ref = bf16[4,128,256]{2,1,0:T(8,128)(2,1)S(1)} collective-permute-done((bf16[4,128,256]{2,1,0:T(8,128)(2,1)S(1)}, bf16[4,128,256]{2,1,0:T(8,128)(2,1)S(1)}, u32[]{:S(2)}, u32[]{:S(2)}) %collective-permute-start.3) | collective-permute-done | bytes 262176 | tf_op jit(solution)/shard_map/ppermute | solution.py:436
  65.2 0.8 copy-done.5
  66.0 2.6 %collective-permute-done.6.far_ref = bf16[4,128,256]{2,1,0:T(8,128)(2,1)S(1)} collective-permute-done((bf16[4,128,256]{2,1,0:T(8,128)(2,1)S(1)}, bf16[4,128,256]{2,1,0:T(8,128)(2,1)S(1)}, u32[]{:S(2)}, u32[]{:S(2)}) %collective-permute-start.6) | collective-permute-done | bytes 262176 | tf_op jit(solution)/shard_map/ppermute | solution.py:436
  68.5 1.4 shard_map.115
  69.9 5.7 %all-to-all-start.2 = ((bf16[8,128,256]{2,1,0:T(8,128)(2,1)}), bf16[8,128,256]{2,1,0:T(8,128)(2,1)S(1)}, u32[]{:S(2)}, u32[]{:S(2)}) async-start(bf16[8,128,256]{2,1,0:T(8,128)(2,1)} %shard_map.115), calls=%async_computation.2 | async-start | bytes 1048576 | tf_op jit(solution)/shard_map/all_to_all | solution.py:433
  75.7 1.3 broadcast_in_dim.33.bias_ref
  77.0 15.7 %shard_map.116 = (bf16[2,2048,1024]{2,1,0:T(8,128)(2,1)}, bf16[8,256,128]{2,1,0:T(8,128)(2,1)}, f32[2,1024]{1,0:T(2,128)}, f32[2,1024]{1,0:T(2,128)}) custom-call(s32[2]{0:T(128)} %pad_add_fusion.spot_ref, bf16[16,2,128,256]{3,2,1,0:T(8,128)(2,1)} %all-to-all-done.1.kv_ref, bf16[8,128,256]{2,1,0:T(8,128)(2,1)} %copy-done.5, ...), custom_call_target="tpu_custom_call" | custom-call | flops 2147483648 | bytes 12582912 | tf_op jit(solution)/shard_map/pallas_call | solution.py:111
  92.7 1.2 copy-done.2
  93.9 0.7 copy-done.6
  94.6 1.4 shard_map.117
  96.1 5.8 %all-to-all-start.3 = ((f32[8,4,1024]{2,1,0:T(4,128)}), f32[8,4,1024]{2,1,0:T(4,128)S(1)}, u32[]{:S(2)}, u32[]{:S(2)}) async-start(f32[8,4,1024]{2,1,0:T(4,128)} %shard_map.117), calls=%async_computation.3 | async-start | bytes 262144 | tf_op jit(solution)/shard_map/all_to_all | solution.py:430
  101.8 7.6 %all-to-all-done.3.stats_ref = f32[8,4,1024]{2,1,0:T(4,128)S(1)} async-done(((f32[8,4,1024]{2,1,0:T(4,128)}), f32[8,4,1024]{2,1,0:T(4,128)S(1)}, u32[]{:S(2)}, u32[]{:S(2)}) %all-to-all-start.3) | async-done | bytes 131104 | tf_op jit(solution)/shard_map/all_to_all | solution.py:430
  109.5 4.8 %all-to-all-start.4 = ((bf16[8,256,128]{2,1,0:T(8,128)(2,1)}), bf16[8,256,128]{2,1,0:T(8,128)(2,1)S(1)}, u32[]{:S(2)}, u32[]{:S(2)}) async-start(bf16[8,256,128]{2,1,0:T(8,128)(2,1)} %get-tuple-element.43.parts_ref), calls=%async_computation.4 | async-start | bytes 1048576 | tf_op jit(solution)/shard_map/all_to_all | solution.py:430
  114.5 0.8 multiply_sine_fusion.2
  115.3 1.0 multiply_sine_fusion
  116.3 14.1 %shard_map.118 = (bf16[16,2,128,256]{3,2,1,0:T(8,128)(2,1)}, bf16[4,256,128]{2,1,0:T(8,128)(2,1)}, bf16[4,256,128]{2,1,0:T(8,128)(2,1)}) custom-call(s32[2]{0:T(128)} %pad_add_fusion.spot_ref, bf16[16,2,128,256]{3,2,1,0:T(8,128)(2,1)} %all-to-all-done.1.kv_ref, bf16[8,128,256]{2,1,0:T(8,128)(2,1)} %copy-done.5, bf16[8,128,256]{2,1,0:T(8,128)(2,1)} %copy-done.1, ...), custom_call_target="tpu_custom_call" | custom-call | flops 4294967296 | bytes 14680064 | tf_op jit(solution)/shard_map/pallas_call | solution.py:268
  130.4 7.1 %all-to-all-start.5 = ((bf16[16,2,128,256]{3,2,1,0:T(8,128)(2,1)}), bf16[16,2,128,256]{3,2,1,0:T(8,128)(2,1)S(1)}, u32[]{:S(2)}, u32[]{:S(2)}) async-start(bf16[16,2,128,256]{3,2,1,0:T(8,128)(2,1)} %get-tuple-element.47), calls=%async_computation.5 | async-start | bytes 4194304 | tf_op jit(solution)/shard_map/all_to_all | solution.py:427
  138.4 0.7 constant_dynamic-slice_fusion.stats_ref
  139.3 4.6 %collective-permute-done.7 = bf16[4,256,128]{2,1,0:T(8,128)(2,1)S(1)} collective-permute-done((bf16[4,256,128]{2,1,0:T(8,128)(2,1)S(1)}, bf16[4,256,128]{2,1,0:T(8,128)(2,1)S(1)}, u32[]{:S(2)}, u32[]{:S(2)}) %collective-permute-start.7) | collective-permute-done | bytes 262176 | tf_op jit(solution)/shard_map/ppermute | solution.py:436
  144.1 2.5 %collective-permute-start.8 = (bf16[2,256,128]{2,1,0:T(8,128)(2,1)S(1)}, bf16[2,256,128]{2,1,0:T(8,128)(2,1)S(1)}, u32[]{:S(2)}, u32[]{:S(2)}) collective-permute-start(bf16[2,256,128]{2,1,0:T(8,128)(2,1)S(1)} %slice.17), channel_id=1, source_target_pairs={{0,16},{8,24},{16,0},{24,8},{32,48},{40,56},{48,32},{56,40},{64,80... | collective-permute-start | bytes 393224 | tf_op jit(solution)/shard_map/ppermute | solution.py:436
  146.6 5.5 %collective-permute-start.12 = (bf16[256,128]{1,0:T(8,128)(2,1)S(1)}, bf16[256,128]{1,0:T(8,128)(2,1)}, u32[]{:S(2)}, u32[]{:S(2)}) collective-permute-start(bf16[256,128]{1,0:T(8,128)(2,1)S(1)} %add_convert_fusion.2), channel_id=1, source_target_pairs={{0,0},{8,1},{16,2},{24,3},{32,4},{40,5},{48,6},{56,7},{9,8},{17,9}... | collective-permute-start | bytes 196616 | tf_op jit(solution)/shard_map/ppermute | solution.py:501
  152.1 9.2 %collective-permute-done.12 = bf16[256,128]{1,0:T(8,128)(2,1)} collective-permute-done((bf16[256,128]{1,0:T(8,128)(2,1)S(1)}, bf16[256,128]{1,0:T(8,128)(2,1)}, u32[]{:S(2)}, u32[]{:S(2)}) %collective-permute-start.12) | collective-permute-done | bytes 65568 | tf_op jit(solution)/shard_map/ppermute | solution.py:501
  161.3 1.3 all-to-all-done.5.in_ref
  162.6 1.7 broadcast_in_dim.58
  164.3 8.7 %all-to-all-start.6 = ((bf16[8,256,128]{2,1,0:T(8,128)(2,1)}), bf16[8,256,128]{2,1,0:T(8,128)(2,1)}, u32[]{:S(2)}, u32[]{:S(2)}) async-start(bf16[8,256,128]{2,1,0:T(8,128)(2,1)} %broadcast_in_dim.58), calls=%async_computation.6 | async-start | bytes 1048576 | tf_op jit(solution)/shard_map/all_to_all | solution.py:433
  173.1 6.6 %collective-permute-start.9 = (bf16[1,256,128]{2,1,0:T(8,128)(2,1)S(1)}, bf16[1,256,128]{2,1,0:T(8,128)(2,1)S(1)}, u32[]{:S(2)}, u32[]{:S(2)}) collective-permute-start(bf16[1,256,128]{2,1,0:T(8,128)(2,1)S(1)} %get-tuple-element.52), channel_id=1, source_target_pairs={{0,32},{8,40},{16,48},{24,56},{32,0},{40,8},{48,16},{56,24},{64,96... | collective-permute-start | bytes 196616 | tf_op jit(solution)/shard_map/ppermute | solution.py:436
  179.9 2.0 %collective-permute-done.9.arrived_ref = bf16[1,256,128]{2,1,0:T(8,128)(2,1)S(1)} collective-permute-done((bf16[1,256,128]{2,1,0:T(8,128)(2,1)S(1)}, bf16[1,256,128]{2,1,0:T(8,128)(2,1)S(1)}, u32[]{:S(2)}, u32[]{:S(2)}) %collective-permute-start.9) | collective-permute-done | bytes 65568 | tf_op jit(solution)/shard_map/ppermute | solution.py:436
  182.1 5.0 %collective-permute-start.10 = (bf16[128,256]{1,0:T(8,128)(2,1)S(1)}, bf16[128,256]{1,0:T(8,128)(2,1)S(1)}, u32[]{:S(2)}, u32[]{:S(2)}) collective-permute-start(bf16[128,256]{1,0:T(8,128)(2,1)S(1)} %shard_map.119), channel_id=1, source_target_pairs={{0,0},{8,1},{16,2},{24,3},{32,4},{40,5},{48,6},{56,7},{9,8},{17,9}... | collective-permute-start | bytes 196616 | tf_op jit(solution)/shard_map/ppermute | solution.py:514
  187.0 8.4 %collective-permute-done.10 = bf16[128,256]{1,0:T(8,128)(2,1)S(1)} collective-permute-done((bf16[128,256]{1,0:T(8,128)(2,1)S(1)}, bf16[128,256]{1,0:T(8,128)(2,1)S(1)}, u32[]{:S(2)}, u32[]{:S(2)}) %collective-permute-start.10) | collective-permute-done | bytes 65568 | tf_op jit(solution)/shard_map/ppermute | solution.py:514
  195.4 1.9 shard_map.121
  197.3 2.5 %shard_map.122 = f32[256,640]{1,0:T(8,128)} custom-call(bf16[8,256,128]{2,1,0:T(8,128)(2,1)} %all-to-all-done.6.parts_ref, bf16[1024,640]{1,0:T(8,128)(2,1)S(1)} %copy-done), custom_call_target="tpu_custom_call" | custom-call | tf_op jit(solution)/shard_map/pallas_call | solution.py:343
  199.7 0.6 copy.17
  (61 shorter events, 2.1 us)
Async XLA Ops:
  0.6 27.1 %copy-start.4 = (bf16[1,128,4096]{2,1,0:T(8,128)(2,1)S(1)}, bf16[1,128,4096]{2,1,0:T(8,128)(2,1)}, u32[]{:S(2)}) copy-start(bf16[1,128,4096]{2,1,0:T(8,128)(2,1)} %v_ref.1) | copy-start | bytes 3145732
  0.6 27.0 %copy-start.3 = (bf16[1,128,4096]{2,1,0:T(8,128)(2,1)S(1)}, bf16[1,128,4096]{2,1,0:T(8,128)(2,1)}, u32[]{:S(2)}) copy-start(bf16[1,128,4096]{2,1,0:T(8,128)(2,1)} %k_ref.1) | copy-start | bytes 3145732
  3.4 8.5 %copy-start.11 = (bf16[128,256]{1,0:T(8,128)(2,1)S(1)}, bf16[128,256]{1,0:T(8,128)(2,1)}, u32[]{:S(2)}) copy-start(bf16[128,256]{1,0:T(8,128)(2,1)} %shard_map.111) | copy-start | bytes 196612
  6.2 26.6 %all-to-all-start = ((bf16[8,128,256]{2,1,0:T(8,128)(2,1)}), bf16[8,128,256]{2,1,0:T(8,128)(2,1)S(1)}, u32[]{:S(2)}, u32[]{:S(2)}) async-start(bf16[8,128,256]{2,1,0:T(8,128)(2,1)} %bitcast.17), calls=%async_computation | async-start | bytes 1048576 | tf_op jit(solution)/shard_map/all_to_all | solution.py:433
  11.9 12.3 %collective-permute-start = (bf16[128,256]{1,0:T(8,128)(2,1)S(1)}, bf16[128,256]{1,0:T(8,128)(2,1)S(1)}, u32[]{:S(2)}, u32[]{:S(2)}) collective-permute-start(bf16[128,256]{1,0:T(8,128)(2,1)S(1)} %copy-done.11), channel_id=1, source_target_pairs={{0,0},{1,8},{2,16},{3,24},{4,32},{5,40},{6,48},{7,56},{8,9},{9,17}... | collective-permute-start | bytes 196616 | tf_op jit(solution)/shard_map/ppermute | solution.py:450
  24.2 8.6 %collective-permute-start.1 = (bf16[1,128,256]{2,1,0:T(8,128)(2,1)S(1)}, bf16[1,128,256]{2,1,0:T(8,128)(2,1)S(1)}, u32[]{:S(2)}, u32[]{:S(2)}) collective-permute-start(bf16[1,128,256]{2,1,0:T(8,128)(2,1)S(1)} %bitcast.19), channel_id=1, source_target_pairs={{0,32},{8,40},{16,48},{24,56},{32,0},{40,8},{48,16},{56,24},{64,96... | collective-permute-start | bytes 196616 | tf_op jit(solution)/shard_map/ppermute | solution.py:436
  32.8 37.1 %all-to-all-start.1 = ((bf16[16,2,128,256]{3,2,1,0:T(8,128)(2,1)}), bf16[16,2,128,256]{3,2,1,0:T(8,128)(2,1)}, u32[]{:S(2)}, u32[]{:S(2)}) async-start(bf16[16,2,128,256]{3,2,1,0:T(8,128)(2,1)} %shard_map.113), calls=%async_computation.1 | async-start | bytes 4194304 | tf_op jit(solution)/shard_map/all_to_all | solution.py:427
  39.8 24.7 %copy-start.7 = (s32[2]{0:T(128)S(1)}, s32[2]{0:T(128)}, u32[]{:S(2)}) copy-start(s32[2]{0:T(128)} %pad_add_fusion.spot_ref) | copy-start | bytes 28
  40.6 8.5 %collective-permute-start.4 = (bf16[1,128,256]{2,1,0:T(8,128)(2,1)S(1)}, bf16[1,128,256]{2,1,0:T(8,128)(2,1)S(1)}, u32[]{:S(2)}, u32[]{:S(2)}) collective-permute-start(bf16[1,128,256]{2,1,0:T(8,128)(2,1)S(1)} %fusion), channel_id=1, source_target_pairs={{0,32},{8,40},{16,48},{24,56},{32,0},{40,8},{48,16},{56,24},{64,96... | collective-permute-start | bytes 196616 | tf_op jit(solution)/shard_map/ppermute | solution.py:436
  46.5 8.7 %collective-permute-start.2 = (bf16[2,128,256]{2,1,0:T(8,128)(2,1)S(1)}, bf16[2,128,256]{2,1,0:T(8,128)(2,1)S(1)}, u32[]{:S(2)}, u32[]{:S(2)}) collective-permute-start(bf16[2,128,256]{2,1,0:T(8,128)(2,1)S(1)} %pad_maximum_fusion.1), channel_id=1, source_target_pairs={{0,16},{8,24},{16,0},{24,8},{32,48},{40,56},{48,32},{56,40},{64,80... | collective-permute-start | bytes 393224 | tf_op jit(solution)/shard_map/ppermute | solution.py:436
  49.1 26.4 %copy-start.12 = (s32[5]{0:T(128)S(1)}, s32[5]{0:T(128)}, u32[]{:S(2)}) copy-start(s32[5]{0:T(128)} %param.13) | copy-start | bytes 64
  49.2 8.6 %collective-permute-start.5 = (bf16[2,128,256]{2,1,0:T(8,128)(2,1)S(1)}, bf16[2,128,256]{2,1,0:T(8,128)(2,1)S(1)}, u32[]{:S(2)}, u32[]{:S(2)}) collective-permute-start(bf16[2,128,256]{2,1,0:T(8,128)(2,1)S(1)} %pad_maximum_fusion.2), channel_id=1, source_target_pairs={{0,16},{8,24},{16,0},{24,8},{32,48},{40,56},{48,32},{56,40},{64,80... | collective-permute-start | bytes 393224 | tf_op jit(solution)/shard_map/ppermute | solution.py:436
  55.2 9.4 %collective-permute-start.3 = (bf16[4,128,256]{2,1,0:T(8,128)(2,1)S(1)}, bf16[4,128,256]{2,1,0:T(8,128)(2,1)S(1)}, u32[]{:S(2)}, u32[]{:S(2)}) collective-permute-start(bf16[4,128,256]{2,1,0:T(8,128)(2,1)S(1)} %constant_dynamic-update-slice_fusion.near_ref), channel_id=1, source_target_pairs={{0,8},{8,0},{16,24},{24,16},{32,40},{40,32},{48,56},{56,48},{64,72... | collective-permute-start | bytes 786440 | tf_op jit(solution)/shard_map/ppermute | solution.py:436
  57.8 10.7 %collective-permute-start.6 = (bf16[4,128,256]{2,1,0:T(8,128)(2,1)S(1)}, bf16[4,128,256]{2,1,0:T(8,128)(2,1)S(1)}, u32[]{:S(2)}, u32[]{:S(2)}) collective-permute-start(bf16[4,128,256]{2,1,0:T(8,128)(2,1)S(1)} %pad_maximum_fusion.near_ref), channel_id=1, source_target_pairs={{0,8},{8,0},{16,24},{24,16},{32,40},{40,32},{48,56},{56,48},{64,72... | collective-permute-start | bytes 786440 | tf_op jit(solution)/shard_map/ppermute | solution.py:436
  65.2 0.8 copy-start.5
  69.9 22.8 %all-to-all-start.2 = ((bf16[8,128,256]{2,1,0:T(8,128)(2,1)}), bf16[8,128,256]{2,1,0:T(8,128)(2,1)S(1)}, u32[]{:S(2)}, u32[]{:S(2)}) async-start(bf16[8,128,256]{2,1,0:T(8,128)(2,1)} %shard_map.115), calls=%async_computation.2 | async-start | bytes 1048576 | tf_op jit(solution)/shard_map/all_to_all | solution.py:433
  77.0 15.7 %copy-start.8 = (s32[2]{0:T(128)S(1)}, s32[2]{0:T(128)}, u32[]{:S(2)}) copy-start(s32[2]{0:T(128)} %pad_add_fusion.spot_ref) | copy-start | bytes 28
  92.7 23.6 %copy-start.1 = (bf16[8,128,256]{2,1,0:T(8,128)(2,1)}, bf16[8,128,256]{2,1,0:T(8,128)(2,1)S(1)}, u32[]{:S(2)}) copy-start(bf16[8,128,256]{2,1,0:T(8,128)(2,1)S(1)} %all-to-all-done.2.up_ref) | copy-start | bytes 1572868
  92.7 1.2 copy-start.2
  93.9 0.7 copy-start.6
  96.1 13.4 %all-to-all-start.3 = ((f32[8,4,1024]{2,1,0:T(4,128)}), f32[8,4,1024]{2,1,0:T(4,128)S(1)}, u32[]{:S(2)}, u32[]{:S(2)}) async-start(f32[8,4,1024]{2,1,0:T(4,128)} %shard_map.117), calls=%async_computation.3 | async-start | bytes 262144 | tf_op jit(solution)/shard_map/all_to_all | solution.py:430
  109.5 6.8 %copy-start.10 = (f32[8,4,1024]{2,1,0:T(4,128)}, f32[8,4,1024]{2,1,0:T(4,128)S(1)}, u32[]{:S(2)}) copy-start(f32[8,4,1024]{2,1,0:T(4,128)S(1)} %all-to-all-done.3.stats_ref) | copy-start | bytes 393220
  109.5 20.9 %all-to-all-start.4 = ((bf16[8,256,128]{2,1,0:T(8,128)(2,1)}), bf16[8,256,128]{2,1,0:T(8,128)(2,1)S(1)}, u32[]{:S(2)}, u32[]{:S(2)}) async-start(bf16[8,256,128]{2,1,0:T(8,128)(2,1)} %get-tuple-element.43.parts_ref), calls=%async_computation.4 | async-start | bytes 1048576 | tf_op jit(solution)/shard_map/all_to_all | solution.py:430
  130.4 7.1 %copy-start.13 = (bf16[4,256,128]{2,1,0:T(8,128)(2,1)S(1)}, bf16[4,256,128]{2,1,0:T(8,128)(2,1)}, u32[]{:S(2)}) copy-start(bf16[4,256,128]{2,1,0:T(8,128)(2,1)} %get-tuple-element.45) | copy-start | bytes 786436
  130.4 13.6 %copy-start.9 = (bf16[4,256,128]{2,1,0:T(8,128)(2,1)S(1)}, bf16[4,256,128]{2,1,0:T(8,128)(2,1)}, u32[]{:S(2)}) copy-start(bf16[4,256,128]{2,1,0:T(8,128)(2,1)} %get-tuple-element.41) | copy-start | bytes 786436
  130.4 32.2 %all-to-all-start.5 = ((bf16[16,2,128,256]{3,2,1,0:T(8,128)(2,1)}), bf16[16,2,128,256]{3,2,1,0:T(8,128)(2,1)S(1)}, u32[]{:S(2)}, u32[]{:S(2)}) async-start(bf16[16,2,128,256]{3,2,1,0:T(8,128)(2,1)} %get-tuple-element.47), calls=%async_computation.5 | async-start | bytes 4194304 | tf_op jit(solution)/shard_map/all_to_all | solution.py:427
  137.5 6.5 %collective-permute-start.7 = (bf16[4,256,128]{2,1,0:T(8,128)(2,1)S(1)}, bf16[4,256,128]{2,1,0:T(8,128)(2,1)S(1)}, u32[]{:S(2)}, u32[]{:S(2)}) collective-permute-start(bf16[4,256,128]{2,1,0:T(8,128)(2,1)S(1)} %copy-done.13), channel_id=1, source_target_pairs={{0,8},{8,0},{16,24},{24,16},{32,40},{40,32},{48,56},{56,48},{64,72... | collective-permute-start | bytes 786440 | tf_op jit(solution)/shard_map/ppermute | solution.py:436
  139.2 7.3 %collective-permute-start.11 = (bf16[256,128]{1,0:T(8,128)(2,1)S(1)}, bf16[256,128]{1,0:T(8,128)(2,1)S(1)}, u32[]{:S(2)}, u32[]{:S(2)}) collective-permute-start(bf16[256,128]{1,0:T(8,128)(2,1)S(1)} %shard_map.120), channel_id=1, source_target_pairs={{0,128},{128,0},{1,129},{129,1},{2,130},{130,2},{3,131},{131,3},{4... | collective-permute-start | bytes 196616 | tf_op jit(solution)/shard_map/ppermute | solution.py:499
  144.1 8.0 %collective-permute-start.8 = (bf16[2,256,128]{2,1,0:T(8,128)(2,1)S(1)}, bf16[2,256,128]{2,1,0:T(8,128)(2,1)S(1)}, u32[]{:S(2)}, u32[]{:S(2)}) collective-permute-start(bf16[2,256,128]{2,1,0:T(8,128)(2,1)S(1)} %slice.17), channel_id=1, source_target_pairs={{0,16},{8,24},{16,0},{24,8},{32,48},{40,56},{48,32},{56,40},{64,80... | collective-permute-start | bytes 393224 | tf_op jit(solution)/shard_map/ppermute | solution.py:436
  146.6 14.7 %collective-permute-start.12 = (bf16[256,128]{1,0:T(8,128)(2,1)S(1)}, bf16[256,128]{1,0:T(8,128)(2,1)}, u32[]{:S(2)}, u32[]{:S(2)}) collective-permute-start(bf16[256,128]{1,0:T(8,128)(2,1)S(1)} %add_convert_fusion.2), channel_id=1, source_target_pairs={{0,0},{8,1},{16,2},{24,3},{32,4},{40,5},{48,6},{56,7},{9,8},{17,9}... | collective-permute-start | bytes 196616 | tf_op jit(solution)/shard_map/ppermute | solution.py:501
  152.1 45.2 %copy-start = (bf16[1024,640]{1,0:T(8,128)(2,1)S(1)}, bf16[1024,640]{1,0:T(8,128)(2,1)}, u32[]{:S(2)}) copy-start(bf16[1024,640]{1,0:T(8,128)(2,1)} %cot_ref.2) | copy-start | bytes 3932164
  164.3 33.0 %all-to-all-start.6 = ((bf16[8,256,128]{2,1,0:T(8,128)(2,1)}), bf16[8,256,128]{2,1,0:T(8,128)(2,1)}, u32[]{:S(2)}, u32[]{:S(2)}) async-start(bf16[8,256,128]{2,1,0:T(8,128)(2,1)} %broadcast_in_dim.58), calls=%async_computation.6 | async-start | bytes 1048576 | tf_op jit(solution)/shard_map/all_to_all | solution.py:433
  173.1 8.9 %collective-permute-start.9 = (bf16[1,256,128]{2,1,0:T(8,128)(2,1)S(1)}, bf16[1,256,128]{2,1,0:T(8,128)(2,1)S(1)}, u32[]{:S(2)}, u32[]{:S(2)}) collective-permute-start(bf16[1,256,128]{2,1,0:T(8,128)(2,1)S(1)} %get-tuple-element.52), channel_id=1, source_target_pairs={{0,32},{8,40},{16,48},{24,56},{32,0},{40,8},{48,16},{56,24},{64,96... | collective-permute-start | bytes 196616 | tf_op jit(solution)/shard_map/ppermute | solution.py:436
  182.1 13.4 %collective-permute-start.10 = (bf16[128,256]{1,0:T(8,128)(2,1)S(1)}, bf16[128,256]{1,0:T(8,128)(2,1)S(1)}, u32[]{:S(2)}, u32[]{:S(2)}) collective-permute-start(bf16[128,256]{1,0:T(8,128)(2,1)S(1)} %shard_map.119), channel_id=1, source_target_pairs={{0,0},{8,1},{16,2},{24,3},{32,4},{40,5},{48,6},{56,7},{9,8},{17,9}... | collective-permute-start | bytes 196616 | tf_op jit(solution)/shard_map/ppermute | solution.py:514

commit v5 on v4

--- a/solution.py
+++ b/solution.py
@@ -70,14 +70,13 @@
     )(packed)
 
 
-def forward_kernel(spot_ref, kv_ref, query_ref, bias_ref, exp_ref, out_ref, log_ref, top_ref):
+def forward_kernel(kv_ref, query_ref, up_ref, bias_ref, exp_ref, out_ref, stat_ref, top_ref):
     key_rows = kv_ref.shape[0] * kv_ref.shape[2]
     per, slice_rows = query_ref.shape[0], query_ref.shape[1]
     query_rows = per * slice_rows
-    slices = out_ref.shape[0]
     heads = kv_ref.shape[3] // HEAD_DIM
     bias = jnp.concatenate([bias_ref[...]] * (query_rows // 128), axis=1)
-    logs, tops = [], []
+    rows, tops = [], []
     for head in range(heads):
         lanes = slice(head * HEAD_DIM, (head + 1) * HEAD_DIM)
         keys = kv_ref[:, 0, :, lanes].reshape(key_rows, HEAD_DIM)
@@ -90,17 +89,22 @@
         exponent_bf = exponent.astype(BF16)
         exp_ref[head] = exponent_bf
         safe = jnp.maximum(total, 1e-30)
-        output = (matmul(values, exponent_bf, TN) * (1.0 / safe)).astype(BF16)
-        logs.append(jnp.where(total > 0.0, top + jnp.log2(safe), NEG_FLOOR))
+        output = matmul(values, exponent_bf, TN) * (1.0 / safe)
+        upstream = up_ref[:, :, lanes].reshape(query_rows, HEAD_DIM).astype(F32)
+        rows.append(jnp.where(total > 0.0, top + jnp.log2(safe), NEG_FLOOR))
+        rows.append(jnp.sum(upstream.T * output, axis=0, keepdims=True))
         tops.append(top)
         for part in range(per):
-            place = lax.rem(pl.program_id(0) * per + part + spot_ref[1], slices)
-            out_ref[place, lanes, :] = output[:, part * slice_rows : (part + 1) * slice_rows]
-    log_ref[...] = jnp.concatenate(logs, axis=0)
+            out_ref[part, lanes, :] = output[
+                :, part * slice_rows : (part + 1) * slice_rows
+            ].astype(BF16)
+    stats = jnp.concatenate(rows, axis=0)
+    for copy in range(stat_ref.shape[0]):
+        stat_ref[copy] = stats
     top_ref[...] = jnp.concatenate(tops, axis=0)
 
 
-def forward(spot, kv, query, bias):
+def forward(kv, query, upstream, bias):
     blocks, _, block_rows, width = kv.shape
     key_rows = blocks * block_rows
     slices, slice_rows, _ = query.shape
@@ -110,67 +114,32 @@
     per = step // slice_rows
     return pl.pallas_call(
         forward_kernel,
-        grid_spec=pltpu.PrefetchScalarGridSpec(
-            num_scalar_prefetch=1,
-            grid=(queries // step,),
-            in_specs=[
-                pl.BlockSpec((blocks, 2, block_rows, width), lambda i, s: (0, 0, 0, 0)),
-                pl.BlockSpec((per, slice_rows, width), lambda i, s: (i, 0, 0)),
-                pl.BlockSpec((key_rows, 128), lambda i, s: (0, 0)),
-            ],
-            out_specs=(
-                pl.BlockSpec((heads, key_rows, step), lambda i, s: (0, 0, i)),
-                pl.BlockSpec((slices, width, slice_rows), lambda i, s: (0, 0, 0)),
-                pl.BlockSpec((heads, step), lambda i, s: (0, i)),
-                pl.BlockSpec((heads, step), lambda i, s: (0, i)),
-            ),
+        grid=(queries // step,),
+        in_specs=[
+            pl.BlockSpec((blocks, 2, block_rows, width), lambda i: (0, 0, 0, 0)),
+            pl.BlockSpec((per, slice_rows, width), lambda i: (i, 0, 0)),
+            pl.BlockSpec((per, slice_rows, width), lambda i: (i, 0, 0)),
+            pl.BlockSpec((key_rows, 128), lambda i: (0, 0)),
+        ],
+        out_specs=(
+            pl.BlockSpec((heads, key_rows, step), lambda i: (0, 0, i)),
+            pl.BlockSpec((per, width, slice_rows), lambda i: (i, 0, 0)),
+            pl.BlockSpec((slices, 2 * heads, step), lambda i: (0, 0, i)),
+            pl.BlockSpec((heads, step), lambda i: (0, i)),
         ),
         out_shape=(
             jax.ShapeDtypeStruct((heads, key_rows, queries), BF16),
             jax.ShapeDtypeStruct((slices, width, slice_rows), BF16),
+            jax.ShapeDtypeStruct((slices, 2 * heads, queries), F32),
             jax.ShapeDtypeStruct((heads, queries), F32),
-            jax.ShapeDtypeStruct((heads, queries), F32),
-        ),
-        compiler_params=params(60),
+        ),
+        compiler_params=params(48),
         cost_estimate=pl.CostEstimate(
             flops=4 * heads * queries * key_rows * HEAD_DIM,
             bytes_accessed=12 * MIB,
             transcendentals=heads * queries * key_rows,
         ),
-    )(spot, kv, query, bias)
-
-
-def local_stats(spot, upstream, parts, logs):
-    slices, slice_rows, width = upstream.shape
-    heads = width // HEAD_DIM
-
-    def kernel(spot_ref, up_ref, parts_ref, log_ref, out_ref):
-        deltas = []
-        for part in range(slices):
-            place = lax.rem(part + spot_ref[1], slices)
-            product = up_ref[part].astype(F32).T * parts_ref[place].astype(F32)
-            deltas.append(
-                [
-                    jnp.sum(product[head * HEAD_DIM : (head + 1) * HEAD_DIM], axis=0, keepdims=True)
-                    for head in range(heads)
-                ]
-            )
-        rows = []
-        for head in range(heads):
-            rows.append(log_ref[head : head + 1, :])
-            rows.append(jnp.concatenate([delta[head] for delta in deltas], axis=1))
-        stats = jnp.concatenate(rows, axis=0)
-        for copy in range(slices):
-            out_ref[copy] = stats
-
-    vmem = pl.BlockSpec(memory_space=pltpu.VMEM)
-    return pl.pallas_call(
-        kernel,
-        out_shape=jax.ShapeDtypeStruct((slices, 2 * heads, slices * slice_rows), F32),
-        in_specs=[pl.BlockSpec(memory_space=pltpu.SMEM), vmem, vmem, vmem],
-        out_specs=vmem,
-        compiler_params=params(16),
-    )(spot, upstream, parts, logs)
+    )(kv, query, upstream, bias)
 
 
 def merged_stats(stats, head):
@@ -247,8 +216,7 @@
     def _():
         half = keep_ref.shape[0]
         for slot in range(2 * half):
-            place = lax.bitwise_xor(spot_ref[0], PATH[slot]) + 2 * half - spot_ref[1]
-            first = pl.multiple_of(lax.rem(place, 2 * half) * 128, 128)
+            first = pl.multiple_of(lax.bitwise_xor(spot_ref[0], PATH[slot]) * 128, 128)
             part = (acc_ref[:, pl.ds(first, 128)] * SCALE).astype(BF16)
             if slot < half:
                 keep_ref[slot] = part
@@ -347,33 +315,12 @@
     )(parts, cotangent)
 
 
-def own_slice(spot, queries, slice_rows):
-    width = queries.shape[2]
-
-    def kernel(spot_ref, in_ref, out_ref):
-        out_ref[...] = in_ref[0]
-
-    return pl.pallas_call(
-        kernel,
-        grid_spec=pltpu.PrefetchScalarGridSpec(
-            num_scalar_prefetch=1,
-            grid=(1,),
-            in_specs=[pl.BlockSpec((1, slice_rows, width), lambda i, s: (0, s[1], 0))],
-            out_specs=pl.BlockSpec((slice_rows, width), lambda i, s: (0, 0)),
-        ),
-        out_shape=jax.ShapeDtypeStruct((slice_rows, width), queries.dtype),
-        compiler_params=params(60),
-    )(spot, queries)
-
-
-def assemble(spot, near, far, shifted):
+def assemble(spot, near, far):
     count = 2 * near.shape[0]
 
     def kernel(spot_ref, near_ref, far_ref, out_ref):
         for slot in range(count):
             place = lax.bitwise_xor(spot_ref[0], PATH[slot])
-            if shifted:
-                place = lax.rem(place + count - spot_ref[1], count)
             out_ref[place] = (near_ref if slot < count // 2 else far_ref)[slot % (count // 2)]
 
     vmem = pl.BlockSpec(memory_space=pltpu.VMEM)
@@ -386,82 +333,76 @@
     )(spot, near, far)
 
 
-def upstream_part(cotangent, out_weight):
-    def kernel(cot_ref, weight_ref, out_ref):
-        out_ref[...] = matmul(cot_ref[...], weight_ref[...], NT).astype(BF16)
-
-    return pl.pallas_call(
-        kernel,
-        out_shape=jax.ShapeDtypeStruct((cotangent.shape[0], out_weight.shape[0]), BF16),
-        compiler_params=params(60),
-    )(cotangent, out_weight)
+def upstream_part(spot, cotangent, out_weight, slices):
+    slice_rows = cotangent.shape[0] // slices
+
+    def kernel(spot_ref, cot_ref, weight_ref, keep_ref, send_ref):
+        for slot in range(slices):
+            first = pl.multiple_of(lax.bitwise_xor(spot_ref[0], PATH[slot]) * slice_rows, slice_rows)
+            part = matmul(cot_ref[pl.ds(first, slice_rows), :], weight_ref[...], NT).astype(BF16)
+            if slot < slices // 2:
+                keep_ref[slot] = part
+            else:
+                send_ref[slot - slices // 2] = part
+
+    vmem = pl.BlockSpec(memory_space=pltpu.VMEM)
+    half = jax.ShapeDtypeStruct((slices // 2, slice_rows, out_weight.shape[0]), BF16)
+    return pl.pallas_call(
+        kernel,
+        out_shape=(half, half),
+        in_specs=[pl.BlockSpec(memory_space=pltpu.SMEM), vmem, vmem],
+        out_specs=(vmem, vmem),
+        compiler_params=params(16),
+    )(spot, cotangent, out_weight)
 
 
 def per_device(
     queries, key_vectors, value_vectors, cotangent, out_weight, frame_valid, group_offset, guide_index
 ):
     seq_count, fsdp_count = lax.axis_size("seq"), lax.axis_size("fsdp")
-    z_count = fsdp_count
-    x_count = seq_count // z_count
-    seq_index, fsdp_index = lax.axis_index("seq"), lax.axis_index("fsdp")
-    z_index = seq_index % z_count
-    cfg_index = lax.axis_index("cfg")
+    fsdp_index = lax.axis_index("fsdp")
     block_rows = key_vectors.shape[1]
     group_rows, width = queries.shape[1], queries.shape[2]
-    slice_rows = group_rows // z_count
-
-    def place(x, z, f):
-        return (x * z_count + z) * fsdp_count + f
-
-    spots = [
-        (x, z, f) for x in range(x_count) for z in range(z_count) for f in range(fsdp_count)
-    ]
-    plane_groups = [
-        [place(x, z, f) for x in range(x_count) for f in range(fsdp_count)] for z in range(z_count)
-    ]
-    column_groups = [[x * z_count + z for z in range(z_count)] for x in range(x_count)]
-    turn = [(place(x, z, f), place(x, (f + z) % z_count, z)) for x, z, f in spots]
-    back = [(d, s) for s, d in turn]
-
-    def over_plane(x):
-        return lax.all_to_all(x, ("seq", "fsdp"), 0, 0, axis_index_groups=plane_groups, tiled=True)
-
-    def over_column(x):
-        return lax.all_to_all(x, "seq", 0, 0, axis_index_groups=column_groups, tiled=True)
+    slice_rows = group_rows // fsdp_count
+    tied = lax.optimization_barrier
+
+    def over_seq(x):
+        return lax.all_to_all(x, "seq", 0, 0, tiled=True)
 
     def over_fsdp(x):
         return lax.all_to_all(x, "fsdp", 0, 0, tiled=True)
 
-    def z_partner(x, bit):
-        return lax.ppermute(x, "seq", [(s, s ^ bit) for s in range(seq_count)])
-
-    def doubled(near, bits):
-        for bit in bits[:-1]:
-            near = jnp.concatenate([near, z_partner(near, bit)])
-        return near, z_partner(near, bits[-1])
-
-    tied = lax.optimization_barrier
-    spot = jnp.stack([z_index, fsdp_index]).astype(jnp.int32)
+    def partner(x, bit):
+        return lax.ppermute(x, "fsdp", [(s, s ^ bit) for s in range(fsdp_count)])
+
+    def halved(keep, send):
+        for bit in (1, 2):
+            total = (keep.astype(F32) + partner(send, bit).astype(F32)).astype(BF16)
+            half = total.shape[0] // 2
+            keep, send = total[:half], total[half:]
+        return keep, partner(send, 4)
+
+    def doubled(block):
+        near = block[None]
+        for bit in (4, 2):
+            near = jnp.concatenate([near, partner(near, bit)])
+        return assemble(spot, near, partner(near, 1))
+
+    spot = fsdp_index.astype(jnp.int32)[None]
     guide = 1.5 + guide_index[0].astype(F32) / 1024.0
-    own_weight = jnp.where(cfg_index == 0, guide, 1.0 - guide)
-
-    query_rows = own_slice(spot, queries, slice_rows)
-    query_rows, cotangent_first = tied((query_rows, cotangent))
-    query_rows = lax.ppermute(query_rows, ("seq", "fsdp"), turn)[None]
-    query_rows = jnp.concatenate([query_rows, z_partner(query_rows, 4)])
-    partial = upstream_part(cotangent_first, out_weight).reshape(fsdp_count, slice_rows, width)
-    partial = over_fsdp(partial)
-    packed = pack_blocks(key_vectors, value_vectors, x_count * fsdp_count)
-    query_rows, partial, packed = tied((query_rows, partial, packed))
-
-    kv = over_plane(packed)
-    summed = jnp.sum(partial.astype(F32), axis=0)
-    upstream_rows = (own_weight * summed).astype(BF16)
-    query = assemble(spot, *doubled(query_rows, (2, 1)), True)
-    upstream_heads = assemble(spot, *doubled(upstream_rows[None], (4, 2, 1)), False)
-
-    block_ids = jnp.arange(x_count * fsdp_count, dtype=jnp.int32)
-    block_start = place(block_ids // fsdp_count, z_index, block_ids % fsdp_count) * block_rows
+    own_weight = jnp.where(lax.axis_index("cfg") == 0, guide, 1.0 - guide)
+
+    packed = pack_blocks(key_vectors, value_vectors, seq_count)
+    packed, cotangent_after = tied((packed, cotangent))
+    kv = over_seq(packed)
+
+    keep, arrived = halved(*upstream_part(spot, cotangent_after, out_weight, fsdp_count))
+    upstream = own_weight * (keep[0].astype(F32) + arrived[0].astype(F32))
+    upstream = doubled(upstream.astype(BF16))
+    query = queries.reshape(fsdp_count, slice_rows, width)
+
+    block_ids = jnp.arange(seq_count, dtype=jnp.int32)
+    block_start = (block_ids * fsdp_count + fsdp_index) * block_rows
     row_ids = jnp.arange(block_rows, dtype=jnp.int32)
     positions = (block_start[:, None] + row_ids[None, :]).reshape(-1)
     frame_match = (positions // FRAME_TOK)[:, None] == jnp.arange(
@@ -476,42 +417,31 @@
     block_angle = (block_start.astype(F32)[:, None] * twice[None, :])[:, None, :]
     row_angle = row_ids.astype(F32)[:, None] * twice[None, :]
     tables = (jnp.cos(block_angle), jnp.sin(block_angle), jnp.cos(row_angle), jnp.sin(row_angle))
-    slice_id = (z_index - fsdp_index) % z_count
     query_positions = (
-        group_offset[0] + slice_id * slice_rows + jnp.arange(slice_rows, dtype=jnp.int32)
+        group_offset[0] + fsdp_index * slice_rows + jnp.arange(slice_rows, dtype=jnp.int32)
     )
     query_angle = query_positions.astype(F32)[None, :] * frequency[:, None]
-
-    kv, query, upstream_heads = tied((kv, query, upstream_heads))
-    upstream = over_fsdp(upstream_heads)
-    exponent, out_parts, own_logs, own_top = forward(spot, kv, query, bias)
-    stats = over_column(local_stats(spot, upstream, out_parts, own_logs))
+    query_tables = (jnp.cos(query_angle), jnp.sin(query_angle))
+    kv, upstream, bias, tables, query_tables = tied((kv, upstream, bias, tables, query_tables))
+
+    exponent, out_parts, own_stats, own_top = forward(kv, query, upstream, bias)
+    stats = over_fsdp(own_stats)
     stats, out_parts = tied((stats, out_parts))
-    out_slices = over_column(out_parts)
+    out_slices = over_fsdp(out_parts)
     grads, query_keep, query_send = backward(
         spot, kv, query, upstream, exponent, stats, own_top, tables
     )
     grads, out_slices, query_send = tied((grads, out_slices, query_send))
-    grads = over_plane(grads)
-
-    slice_stats = lax.dynamic_slice_in_dim(stats, slice_id * slice_rows, slice_rows, axis=2)
+    key_grad, value_grad = unpack_blocks(over_seq(grads))
+
+    query_slice = merge_query_grad(*halved(query_keep, query_send), *query_tables)
+    query_grad = query_slice[None]
+
+    slice_stats = lax.dynamic_slice_in_dim(stats, fsdp_index * slice_rows, slice_rows, axis=2)
     attn_rows = merge_output(out_slices, slice_stats)
     other_rows = lax.ppermute(attn_rows, "cfg", [(0, 1), (1, 0)])
     mixed = own_weight * attn_rows.astype(F32) + (1.0 - own_weight) * other_rows.astype(F32)
-    mixed = lax.ppermute(mixed.astype(BF16), ("seq", "fsdp"), back)
-    mixed = jnp.broadcast_to(mixed[None], (fsdp_count,) + mixed.shape)
-    mixed, grads = tied((mixed, grads))
-    key_grad, value_grad = unpack_blocks(grads)
-    weight_grad = projection_grad(over_fsdp(mixed), cotangent)
-
-    for bit in (1, 2):
-        arrived = z_partner(query_send, bit)
-        total = (query_keep.astype(F32) + arrived.astype(F32)).astype(BF16)
-        half = total.shape[0] // 2
-        query_keep, query_send = total[:half], total[half:]
-    arrived = z_partner(query_send, 4)
-    query_slice = merge_query_grad(query_keep, arrived, jnp.cos(query_angle), jnp.sin(query_angle))
-    query_grad = lax.ppermute(query_slice, ("seq", "fsdp"), back)[None]
+    weight_grad = projection_grad(doubled(mixed.astype(BF16)), cotangent)
     return (query_grad, key_grad, value_grad, weight_grad)
 
 

time: 201 us -> 171 us (0.85)
  the two profiles are of different devices: /device:TPU:48 before, /device:TPU:32 now
where the time goes in v5:
time: 171 us; the launch traced here: 169 us
  starting transfers between devices  51.5 us (30%)
  waiting for transfers between devices  51.2 us (30%)
  Pallas kernels  34.3 us (20%)
  local copies, waits for them, and re-layouts  12.4 us (7%)
  blocking collectives  11.1 us (6%)
  other arithmetic  6.34 us (4%)
  between operations  2.18 us (1%)
    ppermute x12, waiting for transfers between devices, partner(): return lax.ppermute(x, 'fsdp', [(s, s ^ bit) for s in range(fsdp_count)])  38.4 us
    ppermute x12, starting transfers between devices, partner(): return lax.ppermute(x, 'fsdp', [(s, s ^ bit) for s in range(fsdp_count)])  25.5 us
    all_to_all x2, starting transfers between devices, over_seq(): return lax.all_to_all(x, 'seq', 0, 0, tiled=True)  22.2 us
    pallas_call x1, Pallas kernels, backward(): pl.pallas_call(backward_kernel, grid_spec=pltpu.PrefetchScalarGridSpec(nu...  13.5 us
    pallas_call x1, Pallas kernels, forward(): pl.pallas_call(forward_kernel, grid=(queries // step,), in_specs=[pl.Bloc...  13 us
    all_to_all x2, waiting for transfers between devices, over_seq(): return lax.all_to_all(x, 'seq', 0, 0, tiled=True)  12.8 us
    all_to_all x1, blocking collectives, over_fsdp(): return lax.all_to_all(x, 'fsdp', 0, 0, tiled=True)  11.1 us
    unnamed x30, local copies, waits for them, and re-layouts  10.7 us
  transfers between devices with their start and end apart: 16, of which 12 were waited for; matrix products, arithmetic and copies ran while one was open for 5% of the time, Pallas kernels for 10%

profile of v5, /device:TPU:32, one launch (start us, length us, event | category | flops | bytes accessed | tf_op | source)
XLA Modules:
  0.0 169.0 jit_solution(4212901310319265429)
XLA Ops:
  0.6 1.2 copy-done.4
  1.9 1.2 copy-done.5
  3.1 2.0 %shard_map.111 = bf16[16,2,128,256]{3,2,1,0:T(8,128)(2,1)} custom-call(bf16[1,128,4096]{2,1,0:T(8,128)(2,1)S(1)} %copy-done.4, bf16[1,128,4096]{2,1,0:T(8,128)(2,1)S(1)} %copy-done.5), custom_call_target="tpu_custom_call" | custom-call | tf_op jit(solution)/shard_map/pallas_call | solution.py:43
  5.0 11.2 %all-to-all-start = ((bf16[16,2,128,256]{3,2,1,0:T(8,128)(2,1)}), bf16[16,2,128,256]{3,2,1,0:T(8,128)(2,1)S(1)}, u32[]{:S(2)}, u32[]{:S(2)}) async-start(bf16[16,2,128,256]{3,2,1,0:T(8,128)(2,1)} %shard_map.111), calls=%async_computation | async-start | bytes 4194304 | tf_op jit(solution)/shard_map/all_to_all | solution.py:370
  16.3 1.0 copy-done.9
  17.2 1.6 shard_map.112
  21.1 10.6 %collective-permute-done = bf16[4,128,256]{2,1,0:T(8,128)(2,1)} collective-permute-done((bf16[4,128,256]{2,1,0:T(8,128)(2,1)}, bf16[4,128,256]{2,1,0:T(8,128)(2,1)}, u32[]{:S(2)}, u32[]{:S(2)}) %collective-permute-start) | collective-permute-done | bytes 262176 | tf_op jit(solution)/shard_map/ppermute | solution.py:376
  31.7 1.1 add_convert_fusion.1
  32.9 1.7 collective-permute-start.1
  34.5 0.9 multiply_sine_fusion.2
  35.4 2.5 %collective-permute-done.1 = bf16[2,128,256]{2,1,0:T(8,128)(2,1)S(1)} collective-permute-done((bf16[2,128,256]{2,1,0:T(8,128)(2,1)S(1)}, bf16[2,128,256]{2,1,0:T(8,128)(2,1)S(1)}, u32[]{:S(2)}, u32[]{:S(2)}) %collective-permute-start.1) | collective-permute-done | bytes 131104 | tf_op jit(solution)/shard_map/ppermute | solution.py:376
  39.2 3.2 %collective-permute-start.2 = (bf16[1,128,256]{2,1,0:T(8,128)(2,1)}, bf16[1,128,256]{2,1,0:T(8,128)(2,1)S(1)}, u32[]{:S(2)}, u32[]{:S(2)}) collective-permute-start(bf16[1,128,256]{2,1,0:T(8,128)(2,1)} %slice.35), channel_id=1, source_target_pairs={{0,4},{1,5},{2,6},{3,7},{4,0},{5,1},{6,2},{7,3},{8,12},{9,13},{10,... | collective-permute-start | bytes 196616 | tf_op jit(solution)/shard_map/ppermute | solution.py:376
  43.2 2.0 %collective-permute-done.2 = bf16[1,128,256]{2,1,0:T(8,128)(2,1)S(1)} collective-permute-done((bf16[1,128,256]{2,1,0:T(8,128)(2,1)}, bf16[1,128,256]{2,1,0:T(8,128)(2,1)S(1)}, u32[]{:S(2)}, u32[]{:S(2)}) %collective-permute-start.2) | collective-permute-done | bytes 65568 | tf_op jit(solution)/shard_map/ppermute | solution.py:376
  45.2 0.9 multiply_convert_fusion
  46.1 3.3 %collective-permute-start.3 = (bf16[1,128,256]{2,1,0:T(8,128)(2,1)S(1)}, bf16[1,128,256]{2,1,0:T(8,128)(2,1)S(1)}, u32[]{:S(2)}, u32[]{:S(2)}) collective-permute-start(bf16[1,128,256]{2,1,0:T(8,128)(2,1)S(1)} %multiply_convert_fusion), channel_id=1, source_target_pairs={{0,4},{1,5},{2,6},{3,7},{4,0},{5,1},{6,2},{7,3},{8,12},{9,13},{10,... | collective-permute-start | bytes 196616 | tf_op jit(solution)/shard_map/ppermute | solution.py:376
  49.5 2.5 %collective-permute-done.3 = bf16[1,128,256]{2,1,0:T(8,128)(2,1)S(1)} collective-permute-done((bf16[1,128,256]{2,1,0:T(8,128)(2,1)S(1)}, bf16[1,128,256]{2,1,0:T(8,128)(2,1)S(1)}, u32[]{:S(2)}, u32[]{:S(2)}) %collective-permute-start.3) | collective-permute-done | bytes 65568 | tf_op jit(solution)/shard_map/ppermute | solution.py:376
  52.0 2.1 %collective-permute-start.4 = (bf16[2,128,256]{2,1,0:T(8,128)(2,1)S(1)}, bf16[2,128,256]{2,1,0:T(8,128)(2,1)S(1)}, u32[]{:S(2)}, u32[]{:S(2)}) collective-permute-start(bf16[2,128,256]{2,1,0:T(8,128)(2,1)S(1)} %pad_maximum_fusion.2), channel_id=1, source_target_pairs={{0,2},{1,3},{2,0},{3,1},{4,6},{5,7},{6,4},{7,5},{8,10},{9,11},{10,... | collective-permute-start | bytes 393224 | tf_op jit(solution)/shard_map/ppermute | solution.py:376
  54.0 3.0 %collective-permute-done.4 = bf16[2,128,256]{2,1,0:T(8,128)(2,1)S(1)} collective-permute-done((bf16[2,128,256]{2,1,0:T(8,128)(2,1)S(1)}, bf16[2,128,256]{2,1,0:T(8,128)(2,1)S(1)}, u32[]{:S(2)}, u32[]{:S(2)}) %collective-permute-start.4) | collective-permute-done | bytes 131104 | tf_op jit(solution)/shard_map/ppermute | solution.py:376
  57.0 1.0 collective-permute-start.5
  58.0 1.0 multiply_sine_fusion
  59.0 6.4 %collective-permute-done.5.far_ref = bf16[4,128,256]{2,1,0:T(8,128)(2,1)S(1)} collective-permute-done((bf16[4,128,256]{2,1,0:T(8,128)(2,1)S(1)}, bf16[4,128,256]{2,1,0:T(8,128)(2,1)S(1)}, u32[]{:S(2)}, u32[]{:S(2)}) %collective-permute-start.5) | collective-permute-done | bytes 262176 | tf_op jit(solution)/shard_map/ppermute | solution.py:376
  65.4 0.8 copy-done.7
  67.0 1.4 copy-done.8
  68.4 1.0 copy-done.11
  69.5 13.0 %shard_map.114 = (bf16[2,2048,1024]{2,1,0:T(8,128)(2,1)}, bf16[8,256,128]{2,1,0:T(8,128)(2,1)S(1)}, f32[8,4,1024]{2,1,0:T(4,128)S(1)}, f32[2,1024]{1,0:T(2,128)S(1)}) custom-call(bf16[16,2,128,256]{3,2,1,0:T(8,128)(2,1)S(1)} %all-to-all-done.kv_ref, bf16[8,128,256]{2,1,0:T(8,128)(2,1)S(1)} %bitcast.15, bf16[8,128,256]{2,1,0:T(8,128)(2,1)S(1)} %copy-done.8, ...), custom_call_target="tpu_custom_call" | custom-call | flops 2147483648 | bytes 12582912 | tf_op jit(solution)/shard_map/pallas_call | solution.py:115
  82.5 0.8 copy-done.6
  83.3 11.1 %all_to_all.20.stats_ref = f32[8,4,1024]{2,1,0:T(4,128)} all-to-all(f32[8,4,1024]{2,1,0:T(4,128)S(1)} %get-tuple-element.39), channel_id=1, replica_groups=mesh['cfg'=2,'seq'=16,'fsdp'=8] {'fsdp'}, dimensions={0} | all-to-all | bytes 262144 | tf_op jit(solution)/shard_map/all_to_all | solution.py:373
  94.4 3.5 %all-to-all-start.2 = ((bf16[8,256,128]{2,1,0:T(8,128)(2,1)}), bf16[8,256,128]{2,1,0:T(8,128)(2,1)S(1)}, u32[]{:S(2)}, u32[]{:S(2)}) async-start(bf16[8,256,128]{2,1,0:T(8,128)(2,1)} %copy-done.6), calls=%async_computation.2 | async-start | bytes 1048576 | tf_op jit(solution)/shard_map/all_to_all | solution.py:373
  97.9 13.5 %shard_map.115 = (bf16[16,2,128,256]{3,2,1,0:T(8,128)(2,1)}, bf16[4,256,128]{2,1,0:T(8,128)(2,1)}, bf16[4,256,128]{2,1,0:T(8,128)(2,1)}) custom-call(s32[1]{0:T(128)} %bitcast.spot_ref, bf16[16,2,128,256]{3,2,1,0:T(8,128)(2,1)} %copy-done.1, bf16[8,128,256]{2,1,0:T(8,128)(2,1)} %bitcast.14, bf16[8,128,256]{2,1,0:T(8,128)(2,1)} %copy-done.7, ...), custom_call_target="tpu_custom_call" | custom-call | flops 4294967296 | bytes 14680064 | tf_op jit(solution)/shard_map/pallas_call | solution.py:236
  111.4 0.8 copy-done.2
  112.1 11.0 %all-to-all-start.3 = ((bf16[16,2,128,256]{3,2,1,0:T(8,128)(2,1)}), bf16[16,2,128,256]{3,2,1,0:T(8,128)(2,1)S(1)}, u32[]{:S(2)}, u32[]{:S(2)}) async-start(bf16[16,2,128,256]{3,2,1,0:T(8,128)(2,1)} %get-tuple-element.54), calls=%async_computation.3 | async-start | bytes 4194304 | tf_op jit(solution)/shard_map/all_to_all | solution.py:370
  123.2 0.7 constant_dynamic-slice_fusion.stats_ref
  123.9 1.0 copy-done.3
  125.4 1.4 collective-permute-start.6
  126.7 0.9 fusion
  127.6 3.5 %collective-permute-start.10 = (bf16[1,256,128]{2,1,0:T(8,128)(2,1)S(1)}, bf16[1,256,128]{2,1,0:T(8,128)(2,1)S(1)}, u32[]{:S(2)}, u32[]{:S(2)}) collective-permute-start(bf16[1,256,128]{2,1,0:T(8,128)(2,1)S(1)} %fusion), channel_id=1, source_target_pairs={{0,4},{1,5},{2,6},{3,7},{4,0},{5,1},{6,2},{7,3},{8,12},{9,13},{10,... | collective-permute-start | bytes 196616 | tf_op jit(solution)/shard_map/ppermute | solution.py:376
  131.1 2.4 %collective-permute-done.10 = bf16[1,256,128]{2,1,0:T(8,128)(2,1)S(1)} collective-permute-done((bf16[1,256,128]{2,1,0:T(8,128)(2,1)S(1)}, bf16[1,256,128]{2,1,0:T(8,128)(2,1)S(1)}, u32[]{:S(2)}, u32[]{:S(2)}) %collective-permute-start.10) | collective-permute-done | bytes 65568 | tf_op jit(solution)/shard_map/ppermute | solution.py:376
  133.5 1.9 %collective-permute-start.11 = (bf16[2,256,128]{2,1,0:T(8,128)(2,1)S(1)}, bf16[2,256,128]{2,1,0:T(8,128)(2,1)S(1)}, u32[]{:S(2)}, u32[]{:S(2)}) collective-permute-start(bf16[2,256,128]{2,1,0:T(8,128)(2,1)S(1)} %pad_maximum_fusion.3), channel_id=1, source_target_pairs={{0,2},{1,3},{2,0},{3,1},{4,6},{5,7},{6,4},{7,5},{8,10},{9,11},{10,... | collective-permute-start | bytes 393224 | tf_op jit(solution)/shard_map/ppermute | solution.py:376
  135.5 4.6 %collective-permute-done.6 = bf16[4,256,128]{2,1,0:T(8,128)(2,1)S(1)} collective-permute-done((bf16[4,256,128]{2,1,0:T(8,128)(2,1)}, bf16[4,256,128]{2,1,0:T(8,128)(2,1)S(1)}, u32[]{:S(2)}, u32[]{:S(2)}) %collective-permute-start.6) | collective-permute-done | bytes 262176 | tf_op jit(solution)/shard_map/ppermute | solution.py:376
  140.0 1.0 add_convert_fusion
  141.1 2.6 %collective-permute-start.7 = (bf16[2,256,128]{2,1,0:T(8,128)(2,1)S(1)}, bf16[2,256,128]{2,1,0:T(8,128)(2,1)S(1)}, u32[]{:S(2)}, u32[]{:S(2)}) collective-permute-start(bf16[2,256,128]{2,1,0:T(8,128)(2,1)S(1)} %slice.37), channel_id=1, source_target_pairs={{0,2},{1,3},{2,0},{3,1},{4,6},{5,7},{6,4},{7,5},{8,10},{9,11},{10,... | collective-permute-start | bytes 393224 | tf_op jit(solution)/shard_map/ppermute | solution.py:376
  144.5 2.2 %collective-permute-done.7 = bf16[2,256,128]{2,1,0:T(8,128)(2,1)S(1)} collective-permute-done((bf16[2,256,128]{2,1,0:T(8,128)(2,1)S(1)}, bf16[2,256,128]{2,1,0:T(8,128)(2,1)S(1)}, u32[]{:S(2)}, u32[]{:S(2)}) %collective-permute-start.7) | collective-permute-done | bytes 131104 | tf_op jit(solution)/shard_map/ppermute | solution.py:376
  146.7 3.6 %collective-permute-start.8 = (bf16[1,256,128]{2,1,0:T(8,128)(2,1)S(1)}, bf16[1,256,128]{2,1,0:T(8,128)(2,1)S(1)}, u32[]{:S(2)}, u32[]{:S(2)}) collective-permute-start(bf16[1,256,128]{2,1,0:T(8,128)(2,1)S(1)} %get-tuple-element.58), channel_id=1, source_target_pairs={{0,4},{1,5},{2,6},{3,7},{4,0},{5,1},{6,2},{7,3},{8,12},{9,13},{10,... | collective-permute-start | bytes 196616 | tf_op jit(solution)/shard_map/ppermute | solution.py:376
  150.3 2.2 %collective-permute-done.8.arrived_ref = bf16[1,256,128]{2,1,0:T(8,128)(2,1)S(1)} collective-permute-done((bf16[1,256,128]{2,1,0:T(8,128)(2,1)S(1)}, bf16[1,256,128]{2,1,0:T(8,128)(2,1)S(1)}, u32[]{:S(2)}, u32[]{:S(2)}) %collective-permute-start.8) | collective-permute-done | bytes 65568 | tf_op jit(solution)/shard_map/ppermute | solution.py:376
  152.6 0.7 shard_map.116
  153.4 1.4 shard_map.120
  154.8 12.3 %all-to-all-done.3.in_ref = bf16[16,2,128,256]{3,2,1,0:T(8,128)(2,1)S(1)} async-done(((bf16[16,2,128,256]{3,2,1,0:T(8,128)(2,1)}), bf16[16,2,128,256]{3,2,1,0:T(8,128)(2,1)S(1)}, u32[]{:S(2)}, u32[]{:S(2)}) %all-to-all-start.3) | async-done | bytes 2097184 | tf_op jit(solution)/shard_map/all_to_all | solution.py:370
  167.1 1.9 %shard_map.117 = (bf16[1,128,4096]{2,1,0:T(8,128)(2,1)}, bf16[1,128,4096]{2,1,0:T(8,128)(2,1)}) custom-call(bf16[16,2,128,256]{3,2,1,0:T(8,128)(2,1)S(1)} %all-to-all-done.3.in_ref), custom_call_target="tpu_custom_call" | custom-call | tf_op jit(solution)/shard_map/pallas_call | solution.py:63
  (52 shorter events, 5.3 us)
Async XLA Ops:
  0.6 1.2 copy-start.4
  1.9 1.2 copy-start.5
  5.0 11.2 %copy-start = (bf16[1024,640]{1,0:T(8,128)(2,1)S(1)}, bf16[1024,640]{1,0:T(8,128)(2,1)}, u32[]{:S(2)}) copy-start(bf16[1024,640]{1,0:T(8,128)(2,1)} %cot_ref.2) | copy-start | bytes 3932164
  5.0 61.6 %all-to-all-start = ((bf16[16,2,128,256]{3,2,1,0:T(8,128)(2,1)}), bf16[16,2,128,256]{3,2,1,0:T(8,128)(2,1)S(1)}, u32[]{:S(2)}, u32[]{:S(2)}) async-start(bf16[16,2,128,256]{3,2,1,0:T(8,128)(2,1)} %shard_map.111), calls=%async_computation | async-start | bytes 4194304 | tf_op jit(solution)/shard_map/all_to_all | solution.py:370
  16.2 33.1 %copy-start.14 = (s32[5]{0:T(128)S(1)}, s32[5]{0:T(128)}, u32[]{:S(2)}) copy-start(s32[5]{0:T(128)} %param.13) | copy-start | bytes 64
  16.2 1.0 copy-start.9
  18.9 0.7 copy-start.10
  19.6 12.2 %collective-permute-start = (bf16[4,128,256]{2,1,0:T(8,128)(2,1)}, bf16[4,128,256]{2,1,0:T(8,128)(2,1)}, u32[]{:S(2)}, u32[]{:S(2)}) collective-permute-start(bf16[4,128,256]{2,1,0:T(8,128)(2,1)} %get-tuple-element.34), channel_id=1, source_target_pairs={{0,1},{1,0},{2,3},{3,2},{4,5},{5,4},{6,7},{7,6},{8,9},{9,8},{10,11... | collective-permute-start | bytes 786440 | tf_op jit(solution)/shard_map/ppermute | solution.py:376
  32.9 5.1 %collective-permute-start.1 = (bf16[2,128,256]{2,1,0:T(8,128)(2,1)S(1)}, bf16[2,128,256]{2,1,0:T(8,128)(2,1)S(1)}, u32[]{:S(2)}, u32[]{:S(2)}) collective-permute-start(bf16[2,128,256]{2,1,0:T(8,128)(2,1)S(1)} %slice.33), channel_id=1, source_target_pairs={{0,2},{1,3},{2,0},{3,1},{4,6},{5,7},{6,4},{7,5},{8,10},{9,11},{10,... | collective-permute-start | bytes 393224 | tf_op jit(solution)/shard_map/ppermute | solution.py:376
  37.9 0.7 copy-start.13
  39.2 6.0 %collective-permute-start.2 = (bf16[1,128,256]{2,1,0:T(8,128)(2,1)}, bf16[1,128,256]{2,1,0:T(8,128)(2,1)S(1)}, u32[]{:S(2)}, u32[]{:S(2)}) collective-permute-start(bf16[1,128,256]{2,1,0:T(8,128)(2,1)} %slice.35), channel_id=1, source_target_pairs={{0,4},{1,5},{2,6},{3,7},{4,0},{5,1},{6,2},{7,3},{8,12},{9,13},{10,... | collective-permute-start | bytes 196616 | tf_op jit(solution)/shard_map/ppermute | solution.py:376
  46.1 5.9 %collective-permute-start.3 = (bf16[1,128,256]{2,1,0:T(8,128)(2,1)S(1)}, bf16[1,128,256]{2,1,0:T(8,128)(2,1)S(1)}, u32[]{:S(2)}, u32[]{:S(2)}) collective-permute-start(bf16[1,128,256]{2,1,0:T(8,128)(2,1)S(1)} %multiply_convert_fusion), channel_id=1, source_target_pairs={{0,4},{1,5},{2,6},{3,7},{4,0},{5,1},{6,2},{7,3},{8,12},{9,13},{10,... | collective-permute-start | bytes 196616 | tf_op jit(solution)/shard_map/ppermute | solution.py:376
  52.0 5.1 %collective-permute-start.4 = (bf16[2,128,256]{2,1,0:T(8,128)(2,1)S(1)}, bf16[2,128,256]{2,1,0:T(8,128)(2,1)S(1)}, u32[]{:S(2)}, u32[]{:S(2)}) collective-permute-start(bf16[2,128,256]{2,1,0:T(8,128)(2,1)S(1)} %pad_maximum_fusion.2), channel_id=1, source_target_pairs={{0,2},{1,3},{2,0},{3,1},{4,6},{5,7},{6,4},{7,5},{8,10},{9,11},{10,... | collective-permute-start | bytes 393224 | tf_op jit(solution)/shard_map/ppermute | solution.py:376
  57.0 8.3 %collective-permute-start.5 = (bf16[4,128,256]{2,1,0:T(8,128)(2,1)S(1)}, bf16[4,128,256]{2,1,0:T(8,128)(2,1)S(1)}, u32[]{:S(2)}, u32[]{:S(2)}) collective-permute-start(bf16[4,128,256]{2,1,0:T(8,128)(2,1)S(1)} %pad_maximum_fusion.near_ref), channel_id=1, source_target_pairs={{0,1},{1,0},{2,3},{3,2},{4,5},{5,4},{6,7},{7,6},{8,9},{9,8},{10,11... | collective-permute-start | bytes 786440 | tf_op jit(solution)/shard_map/ppermute | solution.py:376
  65.4 0.8 copy-start.7
  66.7 15.8 %copy-start.1 = (bf16[16,2,128,256]{3,2,1,0:T(8,128)(2,1)}, bf16[16,2,128,256]{3,2,1,0:T(8,128)(2,1)S(1)}, u32[]{:S(2)}) copy-start(bf16[16,2,128,256]{3,2,1,0:T(8,128)(2,1)S(1)} %all-to-all-done.kv_ref) | copy-start | bytes 6291460
  67.0 1.4 copy-start.8
  68.4 1.0 copy-start.11
  82.5 0.8 copy-start.6
  83.3 11.1 %copy-start.12 = (f32[2,1024]{1,0:T(2,128)}, f32[2,1024]{1,0:T(2,128)S(1)}, u32[]{:S(2)}) copy-start(f32[2,1024]{1,0:T(2,128)S(1)} %get-tuple-element.42.own_ref) | copy-start | bytes 24580
  94.4 17.0 %all-to-all-start.2 = ((bf16[8,256,128]{2,1,0:T(8,128)(2,1)}), bf16[8,256,128]{2,1,0:T(8,128)(2,1)S(1)}, u32[]{:S(2)}, u32[]{:S(2)}) async-start(bf16[8,256,128]{2,1,0:T(8,128)(2,1)} %copy-done.6), calls=%async_computation.2 | async-start | bytes 1048576 | tf_op jit(solution)/shard_map/all_to_all | solution.py:373
  111.3 0.8 copy-start.2
  112.1 55.0 %all-to-all-start.3 = ((bf16[16,2,128,256]{3,2,1,0:T(8,128)(2,1)}), bf16[16,2,128,256]{3,2,1,0:T(8,128)(2,1)S(1)}, u32[]{:S(2)}, u32[]{:S(2)}) async-start(bf16[16,2,128,256]{3,2,1,0:T(8,128)(2,1)} %get-tuple-element.54), calls=%async_computation.3 | async-start | bytes 4194304 | tf_op jit(solution)/shard_map/all_to_all | solution.py:370
  123.9 1.0 copy-start.3
  125.1 1.7 collective-permute-start.9
  125.4 14.7 %collective-permute-start.6 = (bf16[4,256,128]{2,1,0:T(8,128)(2,1)}, bf16[4,256,128]{2,1,0:T(8,128)(2,1)S(1)}, u32[]{:S(2)}, u32[]{:S(2)}) collective-permute-start(bf16[4,256,128]{2,1,0:T(8,128)(2,1)} %get-tuple-element.51), channel_id=1, source_target_pairs={{0,1},{1,0},{2,3},{3,2},{4,5},{5,4},{6,7},{7,6},{8,9},{9,8},{10,11... | collective-permute-start | bytes 786440 | tf_op jit(solution)/shard_map/ppermute | solution.py:376
  127.6 5.9 %collective-permute-start.10 = (bf16[1,256,128]{2,1,0:T(8,128)(2,1)S(1)}, bf16[1,256,128]{2,1,0:T(8,128)(2,1)S(1)}, u32[]{:S(2)}, u32[]{:S(2)}) collective-permute-start(bf16[1,256,128]{2,1,0:T(8,128)(2,1)S(1)} %fusion), channel_id=1, source_target_pairs={{0,4},{1,5},{2,6},{3,7},{4,0},{5,1},{6,2},{7,3},{8,12},{9,13},{10,... | collective-permute-start | bytes 196616 | tf_op jit(solution)/shard_map/ppermute | solution.py:376
  133.5 10.2 %collective-permute-start.11 = (bf16[2,256,128]{2,1,0:T(8,128)(2,1)S(1)}, bf16[2,256,128]{2,1,0:T(8,128)(2,1)S(1)}, u32[]{:S(2)}, u32[]{:S(2)}) collective-permute-start(bf16[2,256,128]{2,1,0:T(8,128)(2,1)S(1)} %pad_maximum_fusion.3), channel_id=1, source_target_pairs={{0,2},{1,3},{2,0},{3,1},{4,6},{5,7},{6,4},{7,5},{8,10},{9,11},{10,... | collective-permute-start | bytes 393224 | tf_op jit(solution)/shard_map/ppermute | solution.py:376
  141.1 5.6 %collective-permute-start.7 = (bf16[2,256,128]{2,1,0:T(8,128)(2,1)S(1)}, bf16[2,256,128]{2,1,0:T(8,128)(2,1)S(1)}, u32[]{:S(2)}, u32[]{:S(2)}) collective-permute-start(bf16[2,256,128]{2,1,0:T(8,128)(2,1)S(1)} %slice.37), channel_id=1, source_target_pairs={{0,2},{1,3},{2,0},{3,1},{4,6},{5,7},{6,4},{7,5},{8,10},{9,11},{10,... | collective-permute-start | bytes 393224 | tf_op jit(solution)/shard_map/ppermute | solution.py:376
  143.7 9.6 %collective-permute-start.12 = (bf16[4,256,128]{2,1,0:T(8,128)(2,1)S(1)}, bf16[4,256,128]{2,1,0:T(8,128)(2,1)S(1)}, u32[]{:S(2)}, u32[]{:S(2)}) collective-permute-start(bf16[4,256,128]{2,1,0:T(8,128)(2,1)S(1)} %pad_maximum_fusion.1.near_ref), channel_id=1, source_target_pairs={{0,1},{1,0},{2,3},{3,2},{4,5},{5,4},{6,7},{7,6},{8,9},{9,8},{10,11... | collective-permute-start | bytes 786440 | tf_op jit(solution)/shard_map/ppermute | solution.py:376
  146.7 5.9 %collective-permute-start.8 = (bf16[1,256,128]{2,1,0:T(8,128)(2,1)S(1)}, bf16[1,256,128]{2,1,0:T(8,128)(2,1)S(1)}, u32[]{:S(2)}, u32[]{:S(2)}) collective-permute-start(bf16[1,256,128]{2,1,0:T(8,128)(2,1)S(1)} %get-tuple-element.58), channel_id=1, source_target_pairs={{0,4},{1,5},{2,6},{3,7},{4,0},{5,1},{6,2},{7,3},{8,12},{9,13},{10,... | collective-permute-start | bytes 196616 | tf_op jit(solution)/shard_map/ppermute | solution.py:376

commit v6 on v5

--- a/solution.py
+++ b/solution.py
@@ -17,8 +17,9 @@
 BF16 = jnp.bfloat16
 F32 = jnp.float32
 MIB = 1024 * 1024
-
-PATH = (0, 4, 2, 6, 1, 5, 3, 7)
+GRANT = 44
+
+PATH = (0, 1, 4, 5, 2, 3, 6, 7)
 NT = (((1,), (1,)), ((), ()))
 TN = (((0,), (0,)), ((), ()))
 
@@ -43,10 +44,10 @@
     return pl.pallas_call(
         kernel,
         grid=(parts // per,),
-        out_shape=jax.ShapeDtypeStruct((parts, 2, rows, width), keys.dtype),
+        out_shape=pltpu.HBM((parts, 2, rows, width), keys.dtype),
         in_specs=[pl.BlockSpec((1, rows, per * width), lambda i: (0, 0, i))] * 2,
         out_specs=pl.BlockSpec((per, 2, rows, width), lambda i: (i, 0, 0, 0)),
-        compiler_params=params(16),
+        compiler_params=params(60),
     )(keys, values)
 
 
@@ -129,11 +130,11 @@
         ),
         out_shape=(
             jax.ShapeDtypeStruct((heads, key_rows, queries), BF16),
-            jax.ShapeDtypeStruct((slices, width, slice_rows), BF16),
-            jax.ShapeDtypeStruct((slices, 2 * heads, queries), F32),
+            pltpu.HBM((slices, width, slice_rows), BF16),
+            pltpu.HBM((slices, 2 * heads, queries), F32),
             jax.ShapeDtypeStruct((heads, queries), F32),
         ),
-        compiler_params=params(48),
+        compiler_params=params(GRANT),
         cost_estimate=pl.CostEstimate(
             flops=4 * heads * queries * key_rows * HEAD_DIM,
             bytes_accessed=12 * MIB,
@@ -232,7 +233,7 @@
     per = 4
     key_rows = blocks * block_rows
     whole = lambda shape: pl.BlockSpec(shape, lambda i, s: (0,) * len(shape))
-    half = jax.ShapeDtypeStruct((slices // 2, width, slice_rows), BF16)
+    half = pltpu.HBM((slices // 2, width, slice_rows), BF16)
     return pl.pallas_call(
         backward_kernel,
         grid_spec=pltpu.PrefetchScalarGridSpec(
@@ -252,13 +253,13 @@
             ],
             out_specs=(
                 pl.BlockSpec((per, 2, block_rows, width), lambda i, s: (i, 0, 0, 0)),
-                whole(half.shape),
-                whole(half.shape),
+                whole((slices // 2, width, slice_rows)),
+                whole((slices // 2, width, slice_rows)),
             ),
             scratch_shapes=[pltpu.VMEM((width, queries), F32)],
         ),
-        out_shape=(jax.ShapeDtypeStruct((blocks, 2, block_rows, width), BF16), half, half),
-        compiler_params=params(60),
+        out_shape=(pltpu.HBM((blocks, 2, block_rows, width), BF16), half, half),
+        compiler_params=params(GRANT),
         cost_estimate=pl.CostEstimate(
             flops=8 * heads * queries * key_rows * HEAD_DIM,
             bytes_accessed=14 * MIB,
@@ -326,7 +327,7 @@
     vmem = pl.BlockSpec(memory_space=pltpu.VMEM)
     return pl.pallas_call(
         kernel,
-        out_shape=jax.ShapeDtypeStruct((count,) + near.shape[1:], BF16),
+        out_shape=pltpu.HBM((count,) + near.shape[1:], BF16),
         in_specs=[pl.BlockSpec(memory_space=pltpu.SMEM), vmem, vmem],
         out_specs=vmem,
         compiler_params=params(8),
@@ -376,17 +377,17 @@
         return lax.ppermute(x, "fsdp", [(s, s ^ bit) for s in range(fsdp_count)])
 
     def halved(keep, send):
-        for bit in (1, 2):
+        for bit in (2, 4):
             total = (keep.astype(F32) + partner(send, bit).astype(F32)).astype(BF16)
             half = total.shape[0] // 2
             keep, send = total[:half], total[half:]
-        return keep, partner(send, 4)
+        return keep, partner(send, 1)
 
     def doubled(block):
         near = block[None]
-        for bit in (4, 2):
+        for bit in (1, 4):
             near = jnp.concatenate([near, partner(near, bit)])
-        return assemble(spot, near, partner(near, 1))
+        return assemble(spot, near, partner(near, 2))
 
     spot = fsdp_index.astype(jnp.int32)[None]
     guide = 1.5 + guide_index[0].astype(F32) / 1024.0
@@ -398,7 +399,6 @@
 
     keep, arrived = halved(*upstream_part(spot, cotangent_after, out_weight, fsdp_count))
     upstream = own_weight * (keep[0].astype(F32) + arrived[0].astype(F32))
-    upstream = doubled(upstream.astype(BF16))
     query = queries.reshape(fsdp_count, slice_rows, width)
 
     block_ids = jnp.arange(seq_count, dtype=jnp.int32)
@@ -422,7 +422,10 @@
     )
     query_angle = query_positions.astype(F32)[None, :] * frequency[:, None]
     query_tables = (jnp.cos(query_angle), jnp.sin(query_angle))
-    kv, upstream, bias, tables, query_tables = tied((kv, upstream, bias, tables, query_tables))
+    upstream, bias, tables, query_tables = tied(
+        (upstream.astype(BF16), bias, tables, query_tables)
+    )
+    upstream = doubled(upstream)
 
     exponent, out_parts, own_stats, own_top = forward(kv, query, upstream, bias)
     stats = over_fsdp(own_stats)

time: 171 us -> 175 us (1.023)
  Pallas kernels: 34.3 us -> 38.2 us
  starting transfers between devices: 51.5 us -> 47.9 us
    ppermute x12, waiting for transfers between devices: 38.4 us -> 45.9 us  [partner(): return lax.ppermute(x, 'fsdp', [(s, s ^ bit) for s in range(fsdp_count)])]
    ppermute x12, starting transfers between devices: 25.5 us -> 18.8 us  [partner(): return lax.ppermute(x, 'fsdp', [(s, s ^ bit) for s in range(fsdp_count)])]
    all_to_all x2, waiting for transfers between devices: 12.8 us -> 6.31 us  [over_seq(): return lax.all_to_all(x, 'seq', 0, 0, tiled=True)]
    pallas_call x3, Pallas kernels: 2.04 us -> 5.42 us  [the longest x1 3.76 us: pack_blocks(): pl.pallas_call(kernel, grid=(parts // per,), out_shape=pltpu.HBM((parts,...]
    all_to_all x2, starting transfers between devices: 22.2 us -> 24.7 us  [over_seq(): return lax.all_to_all(x, 'seq', 0, 0, tiled=True)]
    unnamed x30 -> x32, local copies, waits for them, and re-layouts: 10.7 us -> 11.1 us
  transfers between devices with their start and end apart: 16 -> 16, of which waited for: 12 -> 12; matrix products, arithmetic and copies ran while one was open for 5% -> 6% of each run, Pallas kernels for 10% -> 11%
where the time goes in v6:
time: 175 us; the launch traced here: 173 us
  waiting for transfers between devices  52.2 us (30%)
  starting transfers between devices  47.9 us (27%)
  Pallas kernels  38.2 us (22%)
  local copies, waits for them, and re-layouts  13.8 us (8%)
  blocking collectives  11.4 us (7%)
  other arithmetic  6.97 us (4%)
  between operations  2.15 us (1%)
    ppermute x12, waiting for transfers between devices, partner(): return lax.ppermute(x, 'fsdp', [(s, s ^ bit) for s in range(fsdp_count)])  45.9 us
    all_to_all x2, starting transfers between devices, over_seq(): return lax.all_to_all(x, 'seq', 0, 0, tiled=True)  24.7 us
    ppermute x12, starting transfers between devices, partner(): return lax.ppermute(x, 'fsdp', [(s, s ^ bit) for s in range(fsdp_count)])  18.8 us
    pallas_call x1, Pallas kernels, forward(): pl.pallas_call(forward_kernel, grid=(queries // step,), in_specs=[pl.Bloc...  13 us
    pallas_call x1, Pallas kernels, backward(): pl.pallas_call(backward_kernel, grid_spec=pltpu.PrefetchScalarGridSpec(nu...  12.9 us
    all_to_all x1, blocking collectives, over_fsdp(): return lax.all_to_all(x, 'fsdp', 0, 0, tiled=True)  11.4 us
    unnamed x32, local copies, waits for them, and re-layouts  11.1 us
    all_to_all x2, waiting for transfers between devices, over_seq(): return lax.all_to_all(x, 'seq', 0, 0, tiled=True)  6.31 us
  transfers between devices with their start and end apart: 16, of which 12 were waited for; matrix products, arithmetic and copies ran while one was open for 6% of the time, Pallas kernels for 11%

profile of v6, /device:TPU:32, one launch (start us, length us, event | category | flops | bytes accessed | tf_op | source)
XLA Modules:
  0.0 172.5 jit_solution(7354934709685832568)
XLA Ops:
  0.6 3.8 %shard_map.111 = bf16[16,2,128,256]{3,2,1,0:T(8,128)(2,1)} custom-call(bf16[1,128,4096]{2,1,0:T(8,128)(2,1)} %k_ref.1, bf16[1,128,4096]{2,1,0:T(8,128)(2,1)} %v_ref.1), custom_call_target="tpu_custom_call" | custom-call | tf_op jit(solution)/shard_map/pallas_call | solution.py:44
  4.4 11.2 %all-to-all-start = ((bf16[16,2,128,256]{3,2,1,0:T(8,128)(2,1)}), bf16[16,2,128,256]{3,2,1,0:T(8,128)(2,1)S(1)}, u32[]{:S(2)}, u32[]{:S(2)}) async-start(bf16[16,2,128,256]{3,2,1,0:T(8,128)(2,1)} %shard_map.111), calls=%async_computation | async-start | bytes 4194304 | tf_op jit(solution)/shard_map/all_to_all | solution.py:371
  15.6 1.0 copy-done.5
  16.6 1.7 shard_map.112
  18.9 1.6 collective-permute-start
  22.4 1.0 multiply_sine_fusion
  23.4 3.4 %collective-permute-done = bf16[4,128,256]{2,1,0:T(8,128)(2,1)} collective-permute-done((bf16[4,128,256]{2,1,0:T(8,128)(2,1)}, bf16[4,128,256]{2,1,0:T(8,128)(2,1)}, u32[]{:S(2)}, u32[]{:S(2)}) %collective-permute-start) | collective-permute-done | bytes 262176 | tf_op jit(solution)/shard_map/ppermute | solution.py:377
  26.7 1.1 add_convert_fusion.1
  27.8 3.3 %collective-permute-start.1 = (bf16[2,128,256]{2,1,0:T(8,128)(2,1)S(1)}, bf16[2,128,256]{2,1,0:T(8,128)(2,1)S(1)}, u32[]{:S(2)}, u32[]{:S(2)}) collective-permute-start(bf16[2,128,256]{2,1,0:T(8,128)(2,1)S(1)} %slice.33), channel_id=1, source_target_pairs={{0,4},{1,5},{2,6},{3,7},{4,0},{5,1},{6,2},{7,3},{8,12},{9,13},{10,... | collective-permute-start | bytes 393224 | tf_op jit(solution)/shard_map/ppermute | solution.py:377
  31.3 3.1 %collective-permute-done.1 = bf16[2,128,256]{2,1,0:T(8,128)(2,1)S(1)} collective-permute-done((bf16[2,128,256]{2,1,0:T(8,128)(2,1)S(1)}, bf16[2,128,256]{2,1,0:T(8,128)(2,1)S(1)}, u32[]{:S(2)}, u32[]{:S(2)}) %collective-permute-start.1) | collective-permute-done | bytes 131104 | tf_op jit(solution)/shard_map/ppermute | solution.py:377
  36.9 3.4 %collective-permute-done.2 = bf16[1,128,256]{2,1,0:T(8,128)(2,1)} collective-permute-done((bf16[1,128,256]{2,1,0:T(8,128)(2,1)}, bf16[1,128,256]{2,1,0:T(8,128)(2,1)}, u32[]{:S(2)}, u32[]{:S(2)}) %collective-permute-start.2) | collective-permute-done | bytes 65568 | tf_op jit(solution)/shard_map/ppermute | solution.py:377
  40.3 0.9 fusion
  41.2 2.0 %broadcast_in_dim.55.bias_ref = f32[2048,128]{1,0:T(8,128)} broadcast(f32[2048]{0:T(1024)} %compare_select_fusion), dimensions={0} | broadcast | bytes 1056768 | tf_op jit(solution)/shard_map/broadcast_in_dim | solution.py:412
  43.4 7.9 %collective-permute-done.3 = bf16[1,128,256]{2,1,0:T(8,128)(2,1)S(1)} collective-permute-done((bf16[1,128,256]{2,1,0:T(8,128)(2,1)S(1)}, bf16[1,128,256]{2,1,0:T(8,128)(2,1)S(1)}, u32[]{:S(2)}, u32[]{:S(2)}) %collective-permute-start.3) | collective-permute-done | bytes 65568 | tf_op jit(solution)/shard_map/ppermute | solution.py:377
  51.4 3.3 %collective-permute-start.4 = (bf16[2,128,256]{2,1,0:T(8,128)(2,1)S(1)}, bf16[2,128,256]{2,1,0:T(8,128)(2,1)S(1)}, u32[]{:S(2)}, u32[]{:S(2)}) collective-permute-start(bf16[2,128,256]{2,1,0:T(8,128)(2,1)S(1)} %pad_maximum_fusion.2), channel_id=1, source_target_pairs={{0,4},{1,5},{2,6},{3,7},{4,0},{5,1},{6,2},{7,3},{8,12},{9,13},{10,... | collective-permute-start | bytes 393224 | tf_op jit(solution)/shard_map/ppermute | solution.py:377
  54.7 3.8 %collective-permute-done.4 = bf16[2,128,256]{2,1,0:T(8,128)(2,1)S(1)} collective-permute-done((bf16[2,128,256]{2,1,0:T(8,128)(2,1)S(1)}, bf16[2,128,256]{2,1,0:T(8,128)(2,1)S(1)}, u32[]{:S(2)}, u32[]{:S(2)}) %collective-permute-start.4) | collective-permute-done | bytes 131104 | tf_op jit(solution)/shard_map/ppermute | solution.py:377
  58.5 1.1 collective-permute-start.5
  59.7 5.3 %collective-permute-done.5.far_ref = bf16[4,128,256]{2,1,0:T(8,128)(2,1)S(1)} collective-permute-done((bf16[4,128,256]{2,1,0:T(8,128)(2,1)S(1)}, bf16[4,128,256]{2,1,0:T(8,128)(2,1)S(1)}, u32[]{:S(2)}, u32[]{:S(2)}) %collective-permute-start.5) | collective-permute-done | bytes 262176 | tf_op jit(solution)/shard_map/ppermute | solution.py:377
  65.0 0.8 shard_map.113.up_ref
  66.0 1.2 copy-done.2
  67.2 1.0 copy-done.3
  68.2 1.0 copy-done.11
  69.3 13.0 %shard_map.114 = (bf16[2,2048,1024]{2,1,0:T(8,128)(2,1)}, bf16[8,256,128]{2,1,0:T(8,128)(2,1)}, f32[8,4,1024]{2,1,0:T(4,128)}, f32[2,1024]{1,0:T(2,128)S(1)}) custom-call(bf16[16,2,128,256]{3,2,1,0:T(8,128)(2,1)S(1)} %all-to-all-done.kv_ref, bf16[8,128,256]{2,1,0:T(8,128)(2,1)S(1)} %bitcast.17, bf16[8,128,256]{2,1,0:T(8,128)(2,1)S(1)} %copy-done.3, ...), custom_call_target="tpu_custom_call" | custom-call | flops 2147483648 | bytes 12582912 | tf_op jit(solution)/shard_map/pallas_call | solution.py:116
  82.9 11.4 %all_to_all.20.stats_ref = f32[8,4,1024]{2,1,0:T(4,128)S(1)} all-to-all(f32[8,4,1024]{2,1,0:T(4,128)} %get-tuple-element.37), channel_id=1, replica_groups=mesh['cfg'=2,'seq'=16,'fsdp'=8] {'fsdp'}, dimensions={0} | all-to-all | bytes 262144 | tf_op jit(solution)/shard_map/all_to_all | solution.py:374
  94.2 4.2 %all-to-all-start.2 = ((bf16[8,256,128]{2,1,0:T(8,128)(2,1)}), bf16[8,256,128]{2,1,0:T(8,128)(2,1)}, u32[]{:S(2)}, u32[]{:S(2)}) async-start(bf16[8,256,128]{2,1,0:T(8,128)(2,1)} %get-tuple-element.47), calls=%async_computation.2 | async-start | bytes 1048576 | tf_op jit(solution)/shard_map/all_to_all | solution.py:374
  98.4 1.0 copy-done.4
  99.4 0.8 copy-done.9
  100.3 0.8 copy-done.10
  101.1 1.0 copy-done.12
  102.8 12.9 %shard_map.115 = (bf16[16,2,128,256]{3,2,1,0:T(8,128)(2,1)}, bf16[4,256,128]{2,1,0:T(8,128)(2,1)}, bf16[4,256,128]{2,1,0:T(8,128)(2,1)}) custom-call(s32[1]{0:T(128)} %bitcast.spot_ref, bf16[16,2,128,256]{3,2,1,0:T(8,128)(2,1)S(1)} %all-to-all-done.kv_ref, bf16[8,128,256]{2,1,0:T(8,128)(2,1)S(1)} %bitcast.18, bf16[8,128,256]{2,1,0:T(8,128)(2,1)S(1)} %copy-done.4, ...), custom_call_target="tpu_custom_call" | custom-call | flops 4294967296 | bytes 14680064 | tf_op jit(solution)/shard_map/pallas_call | solution.py:237
  115.7 13.6 %all-to-all-start.3 = ((bf16[16,2,128,256]{3,2,1,0:T(8,128)(2,1)}), bf16[16,2,128,256]{3,2,1,0:T(8,128)(2,1)S(1)}, u32[]{:S(2)}, u32[]{:S(2)}) async-start(bf16[16,2,128,256]{3,2,1,0:T(8,128)(2,1)} %get-tuple-element.52), calls=%async_computation.3 | async-start | bytes 4194304 | tf_op jit(solution)/shard_map/all_to_all | solution.py:371
  129.3 1.2 shard_map.118
  130.8 2.0 %collective-permute-start.6 = (bf16[4,256,128]{2,1,0:T(8,128)(2,1)}, bf16[4,256,128]{2,1,0:T(8,128)(2,1)S(1)}, u32[]{:S(2)}, u32[]{:S(2)}) collective-permute-start(bf16[4,256,128]{2,1,0:T(8,128)(2,1)} %get-tuple-element.49), channel_id=1, source_target_pairs={{0,2},{1,3},{2,0},{3,1},{4,6},{5,7},{6,4},{7,5},{8,10},{9,11},{10,... | collective-permute-start | bytes 786440 | tf_op jit(solution)/shard_map/ppermute | solution.py:377
  132.8 0.9 fusion.1
  133.7 1.0 collective-permute-start.10
  134.6 8.5 %collective-permute-done.10 = bf16[1,256,128]{2,1,0:T(8,128)(2,1)S(1)} collective-permute-done((bf16[1,256,128]{2,1,0:T(8,128)(2,1)S(1)}, bf16[1,256,128]{2,1,0:T(8,128)(2,1)S(1)}, u32[]{:S(2)}, u32[]{:S(2)}) %collective-permute-start.10) | collective-permute-done | bytes 65568 | tf_op jit(solution)/shard_map/ppermute | solution.py:377
  143.1 2.5 %collective-permute-start.11 = (bf16[2,256,128]{2,1,0:T(8,128)(2,1)S(1)}, bf16[2,256,128]{2,1,0:T(8,128)(2,1)S(1)}, u32[]{:S(2)}, u32[]{:S(2)}) collective-permute-start(bf16[2,256,128]{2,1,0:T(8,128)(2,1)S(1)} %pad_maximum_fusion.3), channel_id=1, source_target_pairs={{0,4},{1,5},{2,6},{3,7},{4,0},{5,1},{6,2},{7,3},{8,12},{9,13},{10,... | collective-permute-start | bytes 393224 | tf_op jit(solution)/shard_map/ppermute | solution.py:377
  145.6 1.0 add_convert_fusion
  146.6 1.2 collective-permute-start.7
  147.8 2.6 %collective-permute-done.11 = bf16[2,256,128]{2,1,0:T(8,128)(2,1)S(1)} collective-permute-done((bf16[2,256,128]{2,1,0:T(8,128)(2,1)S(1)}, bf16[2,256,128]{2,1,0:T(8,128)(2,1)S(1)}, u32[]{:S(2)}, u32[]{:S(2)}) %collective-permute-start.11) | collective-permute-done | bytes 131104 | tf_op jit(solution)/shard_map/ppermute | solution.py:377
  150.4 1.3 collective-permute-start.12
  151.7 2.8 %collective-permute-done.7 = bf16[2,256,128]{2,1,0:T(8,128)(2,1)S(1)} collective-permute-done((bf16[2,256,128]{2,1,0:T(8,128)(2,1)S(1)}, bf16[2,256,128]{2,1,0:T(8,128)(2,1)S(1)}, u32[]{:S(2)}, u32[]{:S(2)}) %collective-permute-start.7) | collective-permute-done | bytes 131104 | tf_op jit(solution)/shard_map/ppermute | solution.py:377
  155.3 5.2 %collective-permute-done.8.arrived_ref = bf16[1,256,128]{2,1,0:T(8,128)(2,1)S(1)} collective-permute-done((bf16[1,256,128]{2,1,0:T(8,128)(2,1)S(1)}, bf16[1,256,128]{2,1,0:T(8,128)(2,1)S(1)}, u32[]{:S(2)}, u32[]{:S(2)}) %collective-permute-start.8) | collective-permute-done | bytes 65568 | tf_op jit(solution)/shard_map/ppermute | solution.py:377
  161.2 0.8 shard_map.119.parts_ref
  162.0 1.0 copy-done.1
  163.1 1.4 shard_map.120
  164.5 6.2 %all-to-all-done.3.in_ref = bf16[16,2,128,256]{3,2,1,0:T(8,128)(2,1)S(1)} async-done(((bf16[16,2,128,256]{3,2,1,0:T(8,128)(2,1)}), bf16[16,2,128,256]{3,2,1,0:T(8,128)(2,1)S(1)}, u32[]{:S(2)}, u32[]{:S(2)}) %all-to-all-start.3) | async-done | bytes 2097184 | tf_op jit(solution)/shard_map/all_to_all | solution.py:371
  170.7 1.9 %shard_map.117 = (bf16[1,128,4096]{2,1,0:T(8,128)(2,1)}, bf16[1,128,4096]{2,1,0:T(8,128)(2,1)}) custom-call(bf16[16,2,128,256]{3,2,1,0:T(8,128)(2,1)S(1)} %all-to-all-done.3.in_ref), custom_call_target="tpu_custom_call" | custom-call | tf_op jit(solution)/shard_map/pallas_call | solution.py:64
  (54 shorter events, 7.6 us)
Async XLA Ops:
  4.4 11.2 %copy-start = (bf16[1024,640]{1,0:T(8,128)(2,1)S(1)}, bf16[1024,640]{1,0:T(8,128)(2,1)}, u32[]{:S(2)}) copy-start(bf16[1024,640]{1,0:T(8,128)(2,1)} %cot_ref.2) | copy-start | bytes 3932164
  4.4 61.6 %all-to-all-start = ((bf16[16,2,128,256]{3,2,1,0:T(8,128)(2,1)}), bf16[16,2,128,256]{3,2,1,0:T(8,128)(2,1)S(1)}, u32[]{:S(2)}, u32[]{:S(2)}) async-start(bf16[16,2,128,256]{3,2,1,0:T(8,128)(2,1)} %shard_map.111), calls=%async_computation | async-start | bytes 4194304 | tf_op jit(solution)/shard_map/all_to_all | solution.py:371
  15.6 15.6 %copy-start.15 = (s32[5]{0:T(128)S(1)}, s32[5]{0:T(128)}, u32[]{:S(2)}) copy-start(s32[5]{0:T(128)} %param.13) | copy-start | bytes 64
  15.6 1.0 copy-start.5
  18.2 0.7 copy-start.6
  18.9 7.8 %collective-permute-start = (bf16[4,128,256]{2,1,0:T(8,128)(2,1)}, bf16[4,128,256]{2,1,0:T(8,128)(2,1)}, u32[]{:S(2)}, u32[]{:S(2)}) collective-permute-start(bf16[4,128,256]{2,1,0:T(8,128)(2,1)} %get-tuple-element.33), channel_id=1, source_target_pairs={{0,2},{1,3},{2,0},{3,1},{4,6},{5,7},{6,4},{7,5},{8,10},{9,11},{10,... | collective-permute-start | bytes 786440 | tf_op jit(solution)/shard_map/ppermute | solution.py:377
  27.8 6.6 %collective-permute-start.1 = (bf16[2,128,256]{2,1,0:T(8,128)(2,1)S(1)}, bf16[2,128,256]{2,1,0:T(8,128)(2,1)S(1)}, u32[]{:S(2)}, u32[]{:S(2)}) collective-permute-start(bf16[2,128,256]{2,1,0:T(8,128)(2,1)S(1)} %slice.33), channel_id=1, source_target_pairs={{0,4},{1,5},{2,6},{3,7},{4,0},{5,1},{6,2},{7,3},{8,12},{9,13},{10,... | collective-permute-start | bytes 393224 | tf_op jit(solution)/shard_map/ppermute | solution.py:377
  35.1 5.2 %collective-permute-start.2 = (bf16[1,128,256]{2,1,0:T(8,128)(2,1)}, bf16[1,128,256]{2,1,0:T(8,128)(2,1)}, u32[]{:S(2)}, u32[]{:S(2)}) collective-permute-start(bf16[1,128,256]{2,1,0:T(8,128)(2,1)} %slice.35), channel_id=1, source_target_pairs={{0,1},{1,0},{2,3},{3,2},{4,5},{5,4},{6,7},{7,6},{8,9},{9,8},{10,11... | collective-permute-start | bytes 196616 | tf_op jit(solution)/shard_map/ppermute | solution.py:377
  43.2 8.2 %collective-permute-start.3 = (bf16[1,128,256]{2,1,0:T(8,128)(2,1)S(1)}, bf16[1,128,256]{2,1,0:T(8,128)(2,1)S(1)}, u32[]{:S(2)}, u32[]{:S(2)}) collective-permute-start(bf16[1,128,256]{2,1,0:T(8,128)(2,1)S(1)} %bitcast.19), channel_id=1, source_target_pairs={{0,1},{1,0},{2,3},{3,2},{4,5},{5,4},{6,7},{7,6},{8,9},{9,8},{10,11... | collective-permute-start | bytes 196616 | tf_op jit(solution)/shard_map/ppermute | solution.py:377
  51.4 7.1 %collective-permute-start.4 = (bf16[2,128,256]{2,1,0:T(8,128)(2,1)S(1)}, bf16[2,128,256]{2,1,0:T(8,128)(2,1)S(1)}, u32[]{:S(2)}, u32[]{:S(2)}) collective-permute-start(bf16[2,128,256]{2,1,0:T(8,128)(2,1)S(1)} %pad_maximum_fusion.2), channel_id=1, source_target_pairs={{0,4},{1,5},{2,6},{3,7},{4,0},{5,1},{6,2},{7,3},{8,12},{9,13},{10,... | collective-permute-start | bytes 393224 | tf_op jit(solution)/shard_map/ppermute | solution.py:377
  58.5 6.5 %collective-permute-start.5 = (bf16[4,128,256]{2,1,0:T(8,128)(2,1)S(1)}, bf16[4,128,256]{2,1,0:T(8,128)(2,1)S(1)}, u32[]{:S(2)}, u32[]{:S(2)}) collective-permute-start(bf16[4,128,256]{2,1,0:T(8,128)(2,1)S(1)} %pad_maximum_fusion.near_ref), channel_id=1, source_target_pairs={{0,2},{1,3},{2,0},{3,1},{4,6},{5,7},{6,4},{7,5},{8,10},{9,11},{10,... | collective-permute-start | bytes 786440 | tf_op jit(solution)/shard_map/ppermute | solution.py:377
  66.0 1.2 copy-start.2
  67.2 1.0 copy-start.3
  68.2 1.0 copy-start.11
  82.3 0.6 copy-start.13
  94.2 21.5 %all-to-all-start.2 = ((bf16[8,256,128]{2,1,0:T(8,128)(2,1)}), bf16[8,256,128]{2,1,0:T(8,128)(2,1)}, u32[]{:S(2)}, u32[]{:S(2)}) async-start(bf16[8,256,128]{2,1,0:T(8,128)(2,1)} %get-tuple-element.47), calls=%async_computation.2 | async-start | bytes 1048576 | tf_op jit(solution)/shard_map/all_to_all | solution.py:374
  98.4 1.0 copy-start.4
  99.4 0.8 copy-start.9
  100.3 0.8 copy-start.10
  101.1 1.0 copy-start.12
  102.1 0.7 copy-start.14
  115.7 54.9 %all-to-all-start.3 = ((bf16[16,2,128,256]{3,2,1,0:T(8,128)(2,1)}), bf16[16,2,128,256]{3,2,1,0:T(8,128)(2,1)S(1)}, u32[]{:S(2)}, u32[]{:S(2)}) async-start(bf16[16,2,128,256]{3,2,1,0:T(8,128)(2,1)} %get-tuple-element.52), calls=%async_computation.3 | async-start | bytes 4194304 | tf_op jit(solution)/shard_map/all_to_all | solution.py:371
  129.3 31.2 %copy-start.7 = (f32[64,128]{1,0:T(8,128)S(1)}, f32[64,128]{1,0:T(8,128)}, u32[]{:S(2)}) copy-start(f32[64,128]{1,0:T(8,128)} %get-tuple-element.51.sin_ref) | copy-start | bytes 98308
  129.3 31.2 %copy-start.8 = (f32[64,128]{1,0:T(8,128)S(1)}, f32[64,128]{1,0:T(8,128)}, u32[]{:S(2)}) copy-start(f32[64,128]{1,0:T(8,128)} %get-tuple-element.50.cos_ref) | copy-start | bytes 98308
  130.5 2.3 %collective-permute-start.9 = (bf16[256,128]{1,0:T(8,128)(2,1)S(1)}, bf16[256,128]{1,0:T(8,128)(2,1)}, u32[]{:S(2)}, u32[]{:S(2)}) collective-permute-start(bf16[256,128]{1,0:T(8,128)(2,1)S(1)} %shard_map.118), channel_id=1, source_target_pairs={{0,128},{128,0},{1,129},{129,1},{2,130},{130,2},{3,131},{131,3},{4... | collective-permute-start | bytes 196616 | tf_op jit(solution)/shard_map/ppermute | solution.py:445
  130.8 14.8 %collective-permute-start.6 = (bf16[4,256,128]{2,1,0:T(8,128)(2,1)}, bf16[4,256,128]{2,1,0:T(8,128)(2,1)S(1)}, u32[]{:S(2)}, u32[]{:S(2)}) collective-permute-start(bf16[4,256,128]{2,1,0:T(8,128)(2,1)} %get-tuple-element.49), channel_id=1, source_target_pairs={{0,2},{1,3},{2,0},{3,1},{4,6},{5,7},{6,4},{7,5},{8,10},{9,11},{10,... | collective-permute-start | bytes 786440 | tf_op jit(solution)/shard_map/ppermute | solution.py:377
  133.7 9.4 %collective-permute-start.10 = (bf16[1,256,128]{2,1,0:T(8,128)(2,1)S(1)}, bf16[1,256,128]{2,1,0:T(8,128)(2,1)S(1)}, u32[]{:S(2)}, u32[]{:S(2)}) collective-permute-start(bf16[1,256,128]{2,1,0:T(8,128)(2,1)S(1)} %fusion.1), channel_id=1, source_target_pairs={{0,1},{1,0},{2,3},{3,2},{4,5},{5,4},{6,7},{7,6},{8,9},{9,8},{10,11... | collective-permute-start | bytes 196616 | tf_op jit(solution)/shard_map/ppermute | solution.py:377
  143.1 7.3 %collective-permute-start.11 = (bf16[2,256,128]{2,1,0:T(8,128)(2,1)S(1)}, bf16[2,256,128]{2,1,0:T(8,128)(2,1)S(1)}, u32[]{:S(2)}, u32[]{:S(2)}) collective-permute-start(bf16[2,256,128]{2,1,0:T(8,128)(2,1)S(1)} %pad_maximum_fusion.3), channel_id=1, source_target_pairs={{0,4},{1,5},{2,6},{3,7},{4,0},{5,1},{6,2},{7,3},{8,12},{9,13},{10,... | collective-permute-start | bytes 393224 | tf_op jit(solution)/shard_map/ppermute | solution.py:377
  146.6 7.9 %collective-permute-start.7 = (bf16[2,256,128]{2,1,0:T(8,128)(2,1)S(1)}, bf16[2,256,128]{2,1,0:T(8,128)(2,1)S(1)}, u32[]{:S(2)}, u32[]{:S(2)}) collective-permute-start(bf16[2,256,128]{2,1,0:T(8,128)(2,1)S(1)} %slice.37), channel_id=1, source_target_pairs={{0,4},{1,5},{2,6},{3,7},{4,0},{5,1},{6,2},{7,3},{8,12},{9,13},{10,... | collective-permute-start | bytes 393224 | tf_op jit(solution)/shard_map/ppermute | solution.py:377
  150.4 10.8 %collective-permute-start.12 = (bf16[4,256,128]{2,1,0:T(8,128)(2,1)S(1)}, bf16[4,256,128]{2,1,0:T(8,128)(2,1)S(1)}, u32[]{:S(2)}, u32[]{:S(2)}) collective-permute-start(bf16[4,256,128]{2,1,0:T(8,128)(2,1)S(1)} %pad_maximum_fusion.1.near_ref), channel_id=1, source_target_pairs={{0,2},{1,3},{2,0},{3,1},{4,6},{5,7},{6,4},{7,5},{8,10},{9,11},{10,... | collective-permute-start | bytes 786440 | tf_op jit(solution)/shard_map/ppermute | solution.py:377
  154.6 5.9 %collective-permute-start.8 = (bf16[1,256,128]{2,1,0:T(8,128)(2,1)S(1)}, bf16[1,256,128]{2,1,0:T(8,128)(2,1)S(1)}, u32[]{:S(2)}, u32[]{:S(2)}) collective-permute-start(bf16[1,256,128]{2,1,0:T(8,128)(2,1)S(1)} %get-tuple-element.56), channel_id=1, source_target_pairs={{0,1},{1,0},{2,3},{3,2},{4,5},{5,4},{6,7},{7,6},{8,9},{9,8},{10,11... | collective-permute-start | bytes 196616 | tf_op jit(solution)/shard_map/ppermute | solution.py:377
  162.0 1.0 copy-start.1

commit v7 on v6

--- a/solution.py
+++ b/solution.py
@@ -17,9 +17,9 @@
 BF16 = jnp.bfloat16
 F32 = jnp.float32
 MIB = 1024 * 1024
-GRANT = 44
-
-PATH = (0, 1, 4, 5, 2, 3, 6, 7)
+
+HALVING = (0, 1, 4, 5, 2, 3, 6, 7)
+DOUBLING = (0, 4, 2, 6, 1, 5, 3, 7)
 NT = (((1,), (1,)), ((), ()))
 TN = (((0,), (0,)), ((), ()))
 
@@ -134,7 +134,7 @@
             pltpu.HBM((slices, 2 * heads, queries), F32),
             jax.ShapeDtypeStruct((heads, queries), F32),
         ),
-        compiler_params=params(GRANT),
+        compiler_params=pltpu.CompilerParams(vmem_limit_bytes=61_300_000),
         cost_estimate=pl.CostEstimate(
             flops=4 * heads * queries * key_rows * HEAD_DIM,
             bytes_accessed=12 * MIB,
@@ -149,8 +149,7 @@
     top = jnp.max(logs, axis=0, keepdims=True)
     shares = jnp.exp2(logs - top)
     total = jnp.sum(shares, axis=0, keepdims=True)
-    shares = shares / total
-    return top + jnp.log2(total), shares, jnp.sum(deltas * shares, axis=0, keepdims=True)
+    return top + jnp.log2(total), jnp.sum(deltas * shares, axis=0, keepdims=True) / total
 
 
 def backward_kernel(
@@ -160,7 +159,9 @@
     up_ref,
     exp_ref,
     stats_ref,
+    log_ref,
     own_ref,
+    parts_ref,
     cos_block,
     sin_block,
     cos_row,
@@ -178,7 +179,7 @@
     stats = stats_ref[...]
     for head in range(heads):
         lanes = slice(head * HEAD_DIM, (head + 1) * HEAD_DIM)
-        log_total, _, delta = merged_stats(stats, head)
+        log_total, delta = merged_stats(stats, head)
         factor = jnp.exp2(own_ref[head : head + 1, :] - log_total)
         keys = kv_ref[:, 0, :, lanes].reshape(key_rows, HEAD_DIM)
         values = kv_ref[:, 1, :, lanes].reshape(key_rows, HEAD_DIM)
@@ -217,15 +218,22 @@
     def _():
         half = keep_ref.shape[0]
         for slot in range(2 * half):
-            first = pl.multiple_of(lax.bitwise_xor(spot_ref[0], PATH[slot]) * 128, 128)
-            part = (acc_ref[:, pl.ds(first, 128)] * SCALE).astype(BF16)
-            if slot < half:
-                keep_ref[slot] = part
-            else:
-                send_ref[slot - half] = part
-
-
-def backward(spot, kv, query, upstream, exponent, stats, own, tables):
+            place = lax.bitwise_xor(spot_ref[0], HALVING[slot])
+            spread = pl.ds(pl.multiple_of(place * 128, 128), 128)
+            query_part = (acc_ref[:, spread] * SCALE).astype(BF16)
+            part = parts_ref[place].astype(F32)
+            weighted = []
+            for head in range(heads):
+                log_total, _ = merged_stats(stats_ref[:, :, spread], head)
+                share = jnp.exp2(log_ref[0, 2 * head : 2 * head + 1, spread] - log_total)
+                weighted.append(part[head * HEAD_DIM : (head + 1) * HEAD_DIM, :] * share)
+            ref = keep_ref if slot < half else send_ref
+            width = query_part.shape[0]
+            ref[slot % half, :width] = jnp.concatenate(weighted, axis=0).astype(BF16)
+            ref[slot % half, width:] = query_part
+
+
+def backward(spot, kv, query, upstream, exponent, stats, own_stats, own_top, out_parts, tables):
     blocks, _, block_rows, width = kv.shape
     slices, slice_rows, _ = query.shape
     queries = slices * slice_rows
@@ -233,7 +241,7 @@
     per = 4
     key_rows = blocks * block_rows
     whole = lambda shape: pl.BlockSpec(shape, lambda i, s: (0,) * len(shape))
-    half = pltpu.HBM((slices // 2, width, slice_rows), BF16)
+    half = pltpu.HBM((slices // 2, 2 * width, slice_rows), BF16)
     return pl.pallas_call(
         backward_kernel,
         grid_spec=pltpu.PrefetchScalarGridSpec(
@@ -245,7 +253,9 @@
                 whole(query.shape),
                 pl.BlockSpec((heads, per * block_rows, queries), lambda i, s: (0, i, 0)),
                 whole(stats.shape),
-                whole(own.shape),
+                whole((1,) + own_stats.shape[1:]),
+                whole(own_top.shape),
+                whole(out_parts.shape),
                 pl.BlockSpec((per, 1, HEAD_DIM), lambda i, s: (i, 0, 0)),
                 pl.BlockSpec((per, 1, HEAD_DIM), lambda i, s: (i, 0, 0)),
                 whole((block_rows, HEAD_DIM)),
@@ -253,39 +263,25 @@
             ],
             out_specs=(
                 pl.BlockSpec((per, 2, block_rows, width), lambda i, s: (i, 0, 0, 0)),
-                whole((slices // 2, width, slice_rows)),
-                whole((slices // 2, width, slice_rows)),
-            ),
+            )
+            + (whole((slices // 2, 2 * width, slice_rows)),) * 2,
             scratch_shapes=[pltpu.VMEM((width, queries), F32)],
         ),
         out_shape=(pltpu.HBM((blocks, 2, block_rows, width), BF16), half, half),
-        compiler_params=params(GRANT),
+        compiler_params=params(60),
         cost_estimate=pl.CostEstimate(
             flops=8 * heads * queries * key_rows * HEAD_DIM,
             bytes_accessed=14 * MIB,
             transcendentals=0,
         ),
-    )(spot, kv, query, upstream, exponent, stats, own, *tables)
-
-
-def merge_output(parts, stats):
-    def kernel(parts_ref, stats_ref, out_ref):
-        for head in range(parts_ref.shape[1] // HEAD_DIM):
-            lanes = slice(head * HEAD_DIM, (head + 1) * HEAD_DIM)
-            _, shares, _ = merged_stats(stats_ref[...], head)
-            total = jnp.zeros((HEAD_DIM, parts_ref.shape[2]), F32)
-            for block in range(parts_ref.shape[0]):
-                total += parts_ref[block, lanes, :].astype(F32) * shares[block : block + 1, :]
-            out_ref[lanes, :] = total.astype(BF16)
-
-    return pl.pallas_call(
-        kernel, out_shape=jax.ShapeDtypeStruct(parts.shape[1:], BF16), compiler_params=params(8)
-    )(parts, stats)
+    )(spot, kv, query, upstream, exponent, stats, own_stats, own_top, out_parts, *tables)
 
 
 def merge_query_grad(kept, arrived, cosine, sine):
+    width = kept.shape[1] // 2
+
     def kernel(kept_ref, arrived_ref, cos_ref, sin_ref, out_ref):
-        total = kept_ref[0].astype(F32) + arrived_ref[0].astype(F32)
+        total = kept_ref[0, width:].astype(F32) + arrived_ref[0, width:].astype(F32)
         half = HEAD_DIM // 2
         turned = []
         for head in range(total.shape[0] // HEAD_DIM):
@@ -297,7 +293,7 @@
 
     return pl.pallas_call(
         kernel,
-        out_shape=jax.ShapeDtypeStruct((kept.shape[2], kept.shape[1]), BF16),
+        out_shape=jax.ShapeDtypeStruct((kept.shape[2], width), BF16),
         compiler_params=params(8),
     )(kept, arrived, cosine, sine)
 
@@ -321,7 +317,7 @@
 
     def kernel(spot_ref, near_ref, far_ref, out_ref):
         for slot in range(count):
-            place = lax.bitwise_xor(spot_ref[0], PATH[slot])
+            place = lax.bitwise_xor(spot_ref[0], DOUBLING[slot])
             out_ref[place] = (near_ref if slot < count // 2 else far_ref)[slot % (count // 2)]
 
     vmem = pl.BlockSpec(memory_space=pltpu.VMEM)
@@ -339,7 +335,7 @@
 
     def kernel(spot_ref, cot_ref, weight_ref, keep_ref, send_ref):
         for slot in range(slices):
-            first = pl.multiple_of(lax.bitwise_xor(spot_ref[0], PATH[slot]) * slice_rows, slice_rows)
+            first = pl.multiple_of(lax.bitwise_xor(spot_ref[0], HALVING[slot]) * slice_rows, slice_rows)
             part = matmul(cot_ref[pl.ds(first, slice_rows), :], weight_ref[...], NT).astype(BF16)
             if slot < slices // 2:
                 keep_ref[slot] = part
@@ -385,9 +381,9 @@
 
     def doubled(block):
         near = block[None]
-        for bit in (1, 4):
+        for bit in (4, 2):
             near = jnp.concatenate([near, partner(near, bit)])
-        return assemble(spot, near, partner(near, 2))
+        return assemble(spot, near, partner(near, 1))
 
     spot = fsdp_index.astype(jnp.int32)[None]
     guide = 1.5 + guide_index[0].astype(F32) / 1024.0
@@ -429,19 +425,15 @@
 
     exponent, out_parts, own_stats, own_top = forward(kv, query, upstream, bias)
     stats = over_fsdp(own_stats)
-    stats, out_parts = tied((stats, out_parts))
-    out_slices = over_fsdp(out_parts)
-    grads, query_keep, query_send = backward(
-        spot, kv, query, upstream, exponent, stats, own_top, tables
-    )
-    grads, out_slices, query_send = tied((grads, out_slices, query_send))
+    grads, keep, send = backward(
+        spot, kv, query, upstream, exponent, stats, own_stats, own_top, out_parts, tables
+    )
     key_grad, value_grad = unpack_blocks(over_seq(grads))
 
-    query_slice = merge_query_grad(*halved(query_keep, query_send), *query_tables)
-    query_grad = query_slice[None]
-
-    slice_stats = lax.dynamic_slice_in_dim(stats, fsdp_index * slice_rows, slice_rows, axis=2)
-    attn_rows = merge_output(out_slices, slice_stats)
+    keep, arrived = halved(keep, send)
+    query_grad = merge_query_grad(keep, arrived, *query_tables)[None]
+    attn_rows = keep[0, :width].astype(F32) + arrived[0, :width].astype(F32)
+    attn_rows = attn_rows.astype(BF16)
     other_rows = lax.ppermute(attn_rows, "cfg", [(0, 1), (1, 0)])
     mixed = own_weight * attn_rows.astype(F32) + (1.0 - own_weight) * other_rows.astype(F32)
     weight_grad = projection_grad(doubled(mixed.astype(BF16)), cotangent)

time: 175 us -> 173 us (0.989)
  waiting for transfers between devices: 52.2 us -> 66.7 us
  local copies, waits for them, and re-layouts: 13.8 us -> 5.48 us
  starting transfers between devices: 47.9 us -> 40.3 us
    ppermute x12, waiting for transfers between devices: 45.9 us -> 57.3 us  [partner(): return lax.ppermute(x, 'fsdp', [(s, s ^ bit) for s in range(fsdp_count)])]
    all_to_all x2, starting transfers between devices: 24.7 us -> 17.6 us  [over_seq(): return lax.all_to_all(x, 'seq', 0, 0, tiled=True)]
    unnamed x32 -> x16, local copies, waits for them, and re-layouts: 11.1 us -> 4.12 us
    all_to_all x1 -> x0, starting transfers between devices: 4.15 us -> none  [over_fsdp(): return lax.all_to_all(x, 'fsdp', 0, 0, tiled=True)]
    ppermute x12, starting transfers between devices: 18.8 us -> 22.6 us  [partner(): return lax.ppermute(x, 'fsdp', [(s, s ^ bit) for s in range(fsdp_count)])]
    pallas_call x1, Pallas kernels: 13 us -> 14.8 us  [forward(): pl.pallas_call(forward_kernel, grid=(queries // step,), in_specs=[pl.Bloc...]
  transfers between devices with their start and end apart: 16 -> 15, of which waited for: 12 -> 14; matrix products, arithmetic and copies ran while one was open for 6% -> 4% of each run, Pallas kernels for 11% -> 3%
where the time goes in v7:
time: 173 us; the launch traced here: 171 us
  waiting for transfers between devices  66.7 us (39%)
  starting transfers between devices  40.3 us (23%)
  Pallas kernels  39.2 us (23%)
  blocking collectives  11.3 us (7%)
  other arithmetic  5.95 us (3%)
  local copies, waits for them, and re-layouts  5.48 us (3%)
  between operations  2.12 us (1%)
    ppermute x12, waiting for transfers between devices, partner(): return lax.ppermute(x, 'fsdp', [(s, s ^ bit) for s in range(fsdp_count)])  57.3 us
    ppermute x12, starting transfers between devices, partner(): return lax.ppermute(x, 'fsdp', [(s, s ^ bit) for s in range(fsdp_count)])  22.6 us
    all_to_all x2, starting transfers between devices, over_seq(): return lax.all_to_all(x, 'seq', 0, 0, tiled=True)  17.6 us
    pallas_call x1, Pallas kernels, forward(): pl.pallas_call(forward_kernel, grid=(queries // step,), in_specs=[pl.Bloc...  14.8 us
    pallas_call x1, Pallas kernels, backward(): pl.pallas_call(backward_kernel, grid_spec=pltpu.PrefetchScalarGridSpec(nu...  14 us
    all_to_all x1, blocking collectives, over_fsdp(): return lax.all_to_all(x, 'fsdp', 0, 0, tiled=True)  11.3 us
    all_to_all x2, waiting for transfers between devices, over_seq(): return lax.all_to_all(x, 'seq', 0, 0, tiled=True)  7.86 us
    unnamed x16, local copies, waits for them, and re-layouts  4.12 us
  transfers between devices with their start and end apart: 15, of which 14 were waited for; matrix products, arithmetic and copies ran while one was open for 4% of the time, Pallas kernels for 3%

profile of v7, /device:TPU:32, one launch (start us, length us, event | category | flops | bytes accessed | tf_op | source)
XLA Modules:
  0.0 171.0 jit_solution(8811378702246436838)
XLA Ops:
  0.6 3.8 %shard_map.111 = bf16[16,2,128,256]{3,2,1,0:T(8,128)(2,1)} custom-call(bf16[1,128,4096]{2,1,0:T(8,128)(2,1)} %k_ref.1, bf16[1,128,4096]{2,1,0:T(8,128)(2,1)} %v_ref.1), custom_call_target="tpu_custom_call" | custom-call | tf_op jit(solution)/shard_map/pallas_call | solution.py:44
  4.4 11.2 %all-to-all-start = ((bf16[16,2,128,256]{3,2,1,0:T(8,128)(2,1)}), bf16[16,2,128,256]{3,2,1,0:T(8,128)(2,1)}, u32[]{:S(2)}, u32[]{:S(2)}) async-start(bf16[16,2,128,256]{3,2,1,0:T(8,128)(2,1)} %shard_map.111), calls=%async_computation | async-start | bytes 4194304 | tf_op jit(solution)/shard_map/all_to_all | solution.py:367
  15.6 1.0 shard_map.112
  16.6 1.7 collective-permute-start
  19.0 0.9 multiply_sine_fusion.2
  19.9 0.8 multiply_sine_fusion.1
  20.7 1.0 multiply_sine_fusion
  21.7 2.5 %collective-permute-done = bf16[4,128,256]{2,1,0:T(8,128)(2,1)S(1)} collective-permute-done((bf16[4,128,256]{2,1,0:T(8,128)(2,1)S(1)}, bf16[4,128,256]{2,1,0:T(8,128)(2,1)S(1)}, u32[]{:S(2)}, u32[]{:S(2)}) %collective-permute-start) | collective-permute-done | bytes 262176 | tf_op jit(solution)/shard_map/ppermute | solution.py:373
  24.3 3.3 %collective-permute-start.1 = (bf16[2,128,256]{2,1,0:T(8,128)(2,1)S(1)}, bf16[2,128,256]{2,1,0:T(8,128)(2,1)S(1)}, u32[]{:S(2)}, u32[]{:S(2)}) collective-permute-start(bf16[2,128,256]{2,1,0:T(8,128)(2,1)S(1)} %slice.42), channel_id=1, source_target_pairs={{0,4},{1,5},{2,6},{3,7},{4,0},{5,1},{6,2},{7,3},{8,12},{9,13},{10,... | collective-permute-start | bytes 393224 | tf_op jit(solution)/shard_map/ppermute | solution.py:373
  27.7 3.1 %collective-permute-done.1 = bf16[2,128,256]{2,1,0:T(8,128)(2,1)S(1)} collective-permute-done((bf16[2,128,256]{2,1,0:T(8,128)(2,1)S(1)}, bf16[2,128,256]{2,1,0:T(8,128)(2,1)S(1)}, u32[]{:S(2)}, u32[]{:S(2)}) %collective-permute-start.1) | collective-permute-done | bytes 131104 | tf_op jit(solution)/shard_map/ppermute | solution.py:373
  30.9 0.7 collective-permute-start.2
  32.2 3.0 %collective-permute-done.2 = bf16[1,128,256]{2,1,0:T(8,128)(2,1)S(1)} collective-permute-done((bf16[1,128,256]{2,1,0:T(8,128)(2,1)S(1)}, bf16[1,128,256]{2,1,0:T(8,128)(2,1)S(1)}, u32[]{:S(2)}, u32[]{:S(2)}) %collective-permute-start.2) | collective-permute-done | bytes 65568 | tf_op jit(solution)/shard_map/ppermute | solution.py:373
  35.3 1.3 broadcast_in_dim.55.bias_ref
  36.6 3.2 %collective-permute-start.3 = (bf16[1,128,256]{2,1,0:T(8,128)(2,1)S(1)}, bf16[1,128,256]{2,1,0:T(8,128)(2,1)S(1)}, u32[]{:S(2)}, u32[]{:S(2)}) collective-permute-start(bf16[1,128,256]{2,1,0:T(8,128)(2,1)S(1)} %bitcast.19), channel_id=1, source_target_pairs={{0,4},{1,5},{2,6},{3,7},{4,0},{5,1},{6,2},{7,3},{8,12},{9,13},{10,... | collective-permute-start | bytes 196616 | tf_op jit(solution)/shard_map/ppermute | solution.py:373
  39.7 2.6 %collective-permute-done.3 = bf16[1,128,256]{2,1,0:T(8,128)(2,1)S(1)} collective-permute-done((bf16[1,128,256]{2,1,0:T(8,128)(2,1)S(1)}, bf16[1,128,256]{2,1,0:T(8,128)(2,1)S(1)}, u32[]{:S(2)}, u32[]{:S(2)}) %collective-permute-start.3) | collective-permute-done | bytes 65568 | tf_op jit(solution)/shard_map/ppermute | solution.py:373
  42.3 1.7 collective-permute-start.4
  44.0 3.4 %collective-permute-done.4 = bf16[2,128,256]{2,1,0:T(8,128)(2,1)S(1)} collective-permute-done((bf16[2,128,256]{2,1,0:T(8,128)(2,1)S(1)}, bf16[2,128,256]{2,1,0:T(8,128)(2,1)S(1)}, u32[]{:S(2)}, u32[]{:S(2)}) %collective-permute-start.4) | collective-permute-done | bytes 131104 | tf_op jit(solution)/shard_map/ppermute | solution.py:373
  47.4 0.7 collective-permute-start.5
  48.1 9.3 %collective-permute-done.5.far_ref = bf16[4,128,256]{2,1,0:T(8,128)(2,1)S(1)} collective-permute-done((bf16[4,128,256]{2,1,0:T(8,128)(2,1)S(1)}, bf16[4,128,256]{2,1,0:T(8,128)(2,1)S(1)}, u32[]{:S(2)}, u32[]{:S(2)}) %collective-permute-start.5) | collective-permute-done | bytes 262176 | tf_op jit(solution)/shard_map/ppermute | solution.py:373
  57.4 0.8 shard_map.113.up_ref
  58.2 7.9 %all-to-all-done.kv_ref = bf16[16,2,128,256]{3,2,1,0:T(8,128)(2,1)} async-done(((bf16[16,2,128,256]{3,2,1,0:T(8,128)(2,1)}), bf16[16,2,128,256]{3,2,1,0:T(8,128)(2,1)}, u32[]{:S(2)}, u32[]{:S(2)}) %all-to-all-start) | async-done | bytes 2097184 | tf_op jit(solution)/shard_map/all_to_all | solution.py:367
  66.1 14.8 %shard_map.114 = (bf16[2,2048,1024]{2,1,0:T(8,128)(2,1)}, bf16[8,256,128]{2,1,0:T(8,128)(2,1)}, f32[8,4,1024]{2,1,0:T(4,128)}, f32[2,1024]{1,0:T(2,128)}) custom-call(bf16[16,2,128,256]{3,2,1,0:T(8,128)(2,1)} %all-to-all-done.kv_ref, bf16[8,128,256]{2,1,0:T(8,128)(2,1)} %bitcast.23, bf16[8,128,256]{2,1,0:T(8,128)(2,1)} %shard_map.113.up_ref, ...), custom_call_target="tpu_custom_call" | custom-call | flops 2147483648 | bytes 12582912 | tf_op jit(solution)/shard_map/pallas_call | solution.py:116
  80.9 11.3 %all_to_all.15.stats_ref = f32[8,4,1024]{2,1,0:T(4,128)} all-to-all(f32[8,4,1024]{2,1,0:T(4,128)} %get-tuple-element.32.log_ref), channel_id=1, replica_groups=mesh['cfg'=2,'seq'=16,'fsdp'=8] {'fsdp'}, dimensions={0} | all-to-all | bytes 262144 | tf_op jit(solution)/shard_map/all_to_all | solution.py:370
  92.2 14.0 %shard_map.115 = (bf16[16,2,128,256]{3,2,1,0:T(8,128)(2,1)}, bf16[4,512,128]{2,1,0:T(8,128)(2,1)}, bf16[4,512,128]{2,1,0:T(8,128)(2,1)}) custom-call(s32[1]{0:T(128)} %bitcast.spot_ref, bf16[16,2,128,256]{3,2,1,0:T(8,128)(2,1)} %all-to-all-done.kv_ref, bf16[8,128,256]{2,1,0:T(8,128)(2,1)} %bitcast.24, bf16[8,128,256]{2,1,0:T(8,128)(2,1)} %shard_map.113.up_ref, ...), custom_call_target="tpu_custom_call" | custom-call | flops 4294967296 | bytes 14680064 | tf_op jit(solution)/shard_map/pallas_call | solution.py:245
  106.2 6.5 %all-to-all-start.2 = ((bf16[16,2,128,256]{3,2,1,0:T(8,128)(2,1)}), bf16[16,2,128,256]{3,2,1,0:T(8,128)(2,1)S(1)}, u32[]{:S(2)}, u32[]{:S(2)}) async-start(bf16[16,2,128,256]{3,2,1,0:T(8,128)(2,1)} %get-tuple-element.43), calls=%async_computation.2 | async-start | bytes 4194304 | tf_op jit(solution)/shard_map/all_to_all | solution.py:367
  112.7 0.4 collective-permute-start.6
  113.1 11.7 %collective-permute-done.6 = bf16[4,512,128]{2,1,0:T(8,128)(2,1)S(1)} collective-permute-done((bf16[4,512,128]{2,1,0:T(8,128)(2,1)}, bf16[4,512,128]{2,1,0:T(8,128)(2,1)S(1)}, u32[]{:S(2)}, u32[]{:S(2)}) %collective-permute-start.6) | collective-permute-done | bytes 524320 | tf_op jit(solution)/shard_map/ppermute | solution.py:373
  124.8 1.2 add_convert_fusion
  126.0 1.2 collective-permute-start.7
  127.2 6.7 %collective-permute-done.7 = bf16[2,512,128]{2,1,0:T(8,128)(2,1)S(1)} collective-permute-done((bf16[2,512,128]{2,1,0:T(8,128)(2,1)S(1)}, bf16[2,512,128]{2,1,0:T(8,128)(2,1)S(1)}, u32[]{:S(2)}, u32[]{:S(2)}) %collective-permute-start.7) | collective-permute-done | bytes 262176 | tf_op jit(solution)/shard_map/ppermute | solution.py:373
  134.2 5.8 %collective-permute-done.8.arrived_ref = bf16[1,512,128]{2,1,0:T(8,128)(2,1)S(1)} collective-permute-done((bf16[1,512,128]{2,1,0:T(8,128)(2,1)S(1)}, bf16[1,512,128]{2,1,0:T(8,128)(2,1)S(1)}, u32[]{:S(2)}, u32[]{:S(2)}) %collective-permute-start.8) | collective-permute-done | bytes 131104 | tf_op jit(solution)/shard_map/ppermute | solution.py:373
  140.0 0.6 fusion.1
  140.7 0.7 copy-done.3
  141.3 1.6 collective-permute-done.9
  142.9 0.9 fusion.2
  143.8 6.6 %collective-permute-start.10 = (bf16[1,256,128]{2,1,0:T(8,128)(2,1)S(1)}, bf16[1,256,128]{2,1,0:T(8,128)(2,1)S(1)}, u32[]{:S(2)}, u32[]{:S(2)}) collective-permute-start(bf16[1,256,128]{2,1,0:T(8,128)(2,1)S(1)} %fusion.2), channel_id=1, source_target_pairs={{0,4},{1,5},{2,6},{3,7},{4,0},{5,1},{6,2},{7,3},{8,12},{9,13},{10,... | collective-permute-start | bytes 196616 | tf_op jit(solution)/shard_map/ppermute | solution.py:373
  150.4 2.4 %collective-permute-done.10 = bf16[1,256,128]{2,1,0:T(8,128)(2,1)S(1)} collective-permute-done((bf16[1,256,128]{2,1,0:T(8,128)(2,1)S(1)}, bf16[1,256,128]{2,1,0:T(8,128)(2,1)S(1)}, u32[]{:S(2)}, u32[]{:S(2)}) %collective-permute-start.10) | collective-permute-done | bytes 65568 | tf_op jit(solution)/shard_map/ppermute | solution.py:373
  152.8 3.1 %collective-permute-start.11 = (bf16[2,256,128]{2,1,0:T(8,128)(2,1)S(1)}, bf16[2,256,128]{2,1,0:T(8,128)(2,1)S(1)}, u32[]{:S(2)}, u32[]{:S(2)}) collective-permute-start(bf16[2,256,128]{2,1,0:T(8,128)(2,1)S(1)} %pad_maximum_fusion.3), channel_id=1, source_target_pairs={{0,2},{1,3},{2,0},{3,1},{4,6},{5,7},{6,4},{7,5},{8,10},{9,11},{10,... | collective-permute-start | bytes 393224 | tf_op jit(solution)/shard_map/ppermute | solution.py:373
  155.9 3.0 %collective-permute-done.11 = bf16[2,256,128]{2,1,0:T(8,128)(2,1)S(1)} collective-permute-done((bf16[2,256,128]{2,1,0:T(8,128)(2,1)S(1)}, bf16[2,256,128]{2,1,0:T(8,128)(2,1)S(1)}, u32[]{:S(2)}, u32[]{:S(2)}) %collective-permute-start.11) | collective-permute-done | bytes 131104 | tf_op jit(solution)/shard_map/ppermute | solution.py:373
  159.0 0.9 copy-done.4
  159.9 0.8 copy-done.5
  160.6 0.8 copy-done.6
  161.4 0.7 shard_map.116
  162.1 3.7 %collective-permute-done.12.far_ref = bf16[4,256,128]{2,1,0:T(8,128)(2,1)S(1)} collective-permute-done((bf16[4,256,128]{2,1,0:T(8,128)(2,1)S(1)}, bf16[4,256,128]{2,1,0:T(8,128)(2,1)S(1)}, u32[]{:S(2)}, u32[]{:S(2)}) %collective-permute-start.12) | collective-permute-done | bytes 262176 | tf_op jit(solution)/shard_map/ppermute | solution.py:373
  165.9 0.8 shard_map.118.parts_ref
  166.7 1.0 copy-done.1
  167.8 1.4 shard_map.119
  169.2 1.9 %shard_map.117 = (bf16[1,128,4096]{2,1,0:T(8,128)(2,1)}, bf16[1,128,4096]{2,1,0:T(8,128)(2,1)}) custom-call(bf16[16,2,128,256]{3,2,1,0:T(8,128)(2,1)S(1)} %all-to-all-done.2.in_ref), custom_call_target="tpu_custom_call" | custom-call | tf_op jit(solution)/shard_map/pallas_call | solution.py:64
  (35 shorter events, 0.9 us)
Async XLA Ops:
  4.4 11.2 %copy-start = (bf16[1024,640]{1,0:T(8,128)(2,1)S(1)}, bf16[1024,640]{1,0:T(8,128)(2,1)}, u32[]{:S(2)}) copy-start(bf16[1024,640]{1,0:T(8,128)(2,1)} %cot_ref.2) | copy-start | bytes 3932164
  4.4 11.2 %copy-start.2 = (bf16[256,640]{1,0:T(8,128)(2,1)S(1)}, bf16[256,640]{1,0:T(8,128)(2,1)}, u32[]{:S(2)}) copy-start(bf16[256,640]{1,0:T(8,128)(2,1)} %weight_ref.1) | copy-start | bytes 983044
  4.4 61.7 %all-to-all-start = ((bf16[16,2,128,256]{3,2,1,0:T(8,128)(2,1)}), bf16[16,2,128,256]{3,2,1,0:T(8,128)(2,1)}, u32[]{:S(2)}, u32[]{:S(2)}) async-start(bf16[16,2,128,256]{3,2,1,0:T(8,128)(2,1)} %shard_map.111), calls=%async_computation | async-start | bytes 4194304 | tf_op jit(solution)/shard_map/all_to_all | solution.py:367
  15.6 12.0 %copy-start.7 = (s32[5]{0:T(128)S(1)}, s32[5]{0:T(128)}, u32[]{:S(2)}) copy-start(s32[5]{0:T(128)} %param.13) | copy-start | bytes 64
  16.6 7.6 %collective-permute-start = (bf16[4,128,256]{2,1,0:T(8,128)(2,1)S(1)}, bf16[4,128,256]{2,1,0:T(8,128)(2,1)S(1)}, u32[]{:S(2)}, u32[]{:S(2)}) collective-permute-start(bf16[4,128,256]{2,1,0:T(8,128)(2,1)S(1)} %get-tuple-element.28), channel_id=1, source_target_pairs={{0,2},{1,3},{2,0},{3,1},{4,6},{5,7},{6,4},{7,5},{8,10},{9,11},{10,... | collective-permute-start | bytes 786440 | tf_op jit(solution)/shard_map/ppermute | solution.py:373
  24.3 6.6 %collective-permute-start.1 = (bf16[2,128,256]{2,1,0:T(8,128)(2,1)S(1)}, bf16[2,128,256]{2,1,0:T(8,128)(2,1)S(1)}, u32[]{:S(2)}, u32[]{:S(2)}) collective-permute-start(bf16[2,128,256]{2,1,0:T(8,128)(2,1)S(1)} %slice.42), channel_id=1, source_target_pairs={{0,4},{1,5},{2,6},{3,7},{4,0},{5,1},{6,2},{7,3},{8,12},{9,13},{10,... | collective-permute-start | bytes 393224 | tf_op jit(solution)/shard_map/ppermute | solution.py:373
  30.9 4.4 %collective-permute-start.2 = (bf16[1,128,256]{2,1,0:T(8,128)(2,1)S(1)}, bf16[1,128,256]{2,1,0:T(8,128)(2,1)S(1)}, u32[]{:S(2)}, u32[]{:S(2)}) collective-permute-start(bf16[1,128,256]{2,1,0:T(8,128)(2,1)S(1)} %slice.44), channel_id=1, source_target_pairs={{0,1},{1,0},{2,3},{3,2},{4,5},{5,4},{6,7},{7,6},{8,9},{9,8},{10,11... | collective-permute-start | bytes 196616 | tf_op jit(solution)/shard_map/ppermute | solution.py:373
  36.6 5.8 %collective-permute-start.3 = (bf16[1,128,256]{2,1,0:T(8,128)(2,1)S(1)}, bf16[1,128,256]{2,1,0:T(8,128)(2,1)S(1)}, u32[]{:S(2)}, u32[]{:S(2)}) collective-permute-start(bf16[1,128,256]{2,1,0:T(8,128)(2,1)S(1)} %bitcast.19), channel_id=1, source_target_pairs={{0,4},{1,5},{2,6},{3,7},{4,0},{5,1},{6,2},{7,3},{8,12},{9,13},{10,... | collective-permute-start | bytes 196616 | tf_op jit(solution)/shard_map/ppermute | solution.py:373
  42.3 5.1 %collective-permute-start.4 = (bf16[2,128,256]{2,1,0:T(8,128)(2,1)S(1)}, bf16[2,128,256]{2,1,0:T(8,128)(2,1)S(1)}, u32[]{:S(2)}, u32[]{:S(2)}) collective-permute-start(bf16[2,128,256]{2,1,0:T(8,128)(2,1)S(1)} %pad_maximum_fusion.2), channel_id=1, source_target_pairs={{0,2},{1,3},{2,0},{3,1},{4,6},{5,7},{6,4},{7,5},{8,10},{9,11},{10,... | collective-permute-start | bytes 393224 | tf_op jit(solution)/shard_map/ppermute | solution.py:373
  47.4 10.0 %collective-permute-start.5 = (bf16[4,128,256]{2,1,0:T(8,128)(2,1)S(1)}, bf16[4,128,256]{2,1,0:T(8,128)(2,1)S(1)}, u32[]{:S(2)}, u32[]{:S(2)}) collective-permute-start(bf16[4,128,256]{2,1,0:T(8,128)(2,1)S(1)} %pad_maximum_fusion.near_ref), channel_id=1, source_target_pairs={{0,1},{1,0},{2,3},{3,2},{4,5},{5,4},{6,7},{7,6},{8,9},{9,8},{10,11... | collective-permute-start | bytes 786440 | tf_op jit(solution)/shard_map/ppermute | solution.py:373
  106.2 63.0 %all-to-all-start.2 = ((bf16[16,2,128,256]{3,2,1,0:T(8,128)(2,1)}), bf16[16,2,128,256]{3,2,1,0:T(8,128)(2,1)S(1)}, u32[]{:S(2)}, u32[]{:S(2)}) async-start(bf16[16,2,128,256]{3,2,1,0:T(8,128)(2,1)} %get-tuple-element.43), calls=%async_computation.2 | async-start | bytes 4194304 | tf_op jit(solution)/shard_map/all_to_all | solution.py:367
  112.7 12.1 %collective-permute-start.6 = (bf16[4,512,128]{2,1,0:T(8,128)(2,1)}, bf16[4,512,128]{2,1,0:T(8,128)(2,1)S(1)}, u32[]{:S(2)}, u32[]{:S(2)}) collective-permute-start(bf16[4,512,128]{2,1,0:T(8,128)(2,1)} %get-tuple-element.40), channel_id=1, source_target_pairs={{0,2},{1,3},{2,0},{3,1},{4,6},{5,7},{6,4},{7,5},{8,10},{9,11},{10,... | collective-permute-start | bytes 1572872 | tf_op jit(solution)/shard_map/ppermute | solution.py:373
  126.0 8.0 %collective-permute-start.7 = (bf16[2,512,128]{2,1,0:T(8,128)(2,1)S(1)}, bf16[2,512,128]{2,1,0:T(8,128)(2,1)S(1)}, u32[]{:S(2)}, u32[]{:S(2)}) collective-permute-start(bf16[2,512,128]{2,1,0:T(8,128)(2,1)S(1)} %slice.46), channel_id=1, source_target_pairs={{0,4},{1,5},{2,6},{3,7},{4,0},{5,1},{6,2},{7,3},{8,12},{9,13},{10,... | collective-permute-start | bytes 786440 | tf_op jit(solution)/shard_map/ppermute | solution.py:373
  134.1 6.0 %collective-permute-start.8 = (bf16[1,512,128]{2,1,0:T(8,128)(2,1)S(1)}, bf16[1,512,128]{2,1,0:T(8,128)(2,1)S(1)}, u32[]{:S(2)}, u32[]{:S(2)}) collective-permute-start(bf16[1,512,128]{2,1,0:T(8,128)(2,1)S(1)} %get-tuple-element.46), channel_id=1, source_target_pairs={{0,1},{1,0},{2,3},{3,2},{4,5},{5,4},{6,7},{7,6},{8,9},{9,8},{10,11... | collective-permute-start | bytes 393224 | tf_op jit(solution)/shard_map/ppermute | solution.py:373
  140.7 0.7 copy-start.3
  141.3 1.6 collective-permute-start.9
  143.8 9.0 %collective-permute-start.10 = (bf16[1,256,128]{2,1,0:T(8,128)(2,1)S(1)}, bf16[1,256,128]{2,1,0:T(8,128)(2,1)S(1)}, u32[]{:S(2)}, u32[]{:S(2)}) collective-permute-start(bf16[1,256,128]{2,1,0:T(8,128)(2,1)S(1)} %fusion.2), channel_id=1, source_target_pairs={{0,4},{1,5},{2,6},{3,7},{4,0},{5,1},{6,2},{7,3},{8,12},{9,13},{10,... | collective-permute-start | bytes 196616 | tf_op jit(solution)/shard_map/ppermute | solution.py:373
  152.8 6.0 %collective-permute-start.11 = (bf16[2,256,128]{2,1,0:T(8,128)(2,1)S(1)}, bf16[2,256,128]{2,1,0:T(8,128)(2,1)S(1)}, u32[]{:S(2)}, u32[]{:S(2)}) collective-permute-start(bf16[2,256,128]{2,1,0:T(8,128)(2,1)S(1)} %pad_maximum_fusion.3), channel_id=1, source_target_pairs={{0,2},{1,3},{2,0},{3,1},{4,6},{5,7},{6,4},{7,5},{8,10},{9,11},{10,... | collective-permute-start | bytes 393224 | tf_op jit(solution)/shard_map/ppermute | solution.py:373
  158.9 7.0 %collective-permute-start.12 = (bf16[4,256,128]{2,1,0:T(8,128)(2,1)S(1)}, bf16[4,256,128]{2,1,0:T(8,128)(2,1)S(1)}, u32[]{:S(2)}, u32[]{:S(2)}) collective-permute-start(bf16[4,256,128]{2,1,0:T(8,128)(2,1)S(1)} %pad_maximum_fusion.1.near_ref), channel_id=1, source_target_pairs={{0,1},{1,0},{2,3},{3,2},{4,5},{5,4},{6,7},{7,6},{8,9},{9,8},{10,11... | collective-permute-start | bytes 786440 | tf_op jit(solution)/shard_map/ppermute | solution.py:373
  159.0 0.9 copy-start.4
  159.9 0.8 copy-start.5
  160.6 0.8 copy-start.6
  166.7 1.0 copy-start.1

commit v8 on v7

--- a/solution.py
+++ b/solution.py
@@ -169,6 +169,8 @@
     grad_ref,
     keep_ref,
     send_ref,
+    out_keep_ref,
+    out_send_ref,
     acc_ref,
 ):
     step = pl.program_id(0)
@@ -227,10 +229,13 @@
                 log_total, _ = merged_stats(stats_ref[:, :, spread], head)
                 share = jnp.exp2(log_ref[0, 2 * head : 2 * head + 1, spread] - log_total)
                 weighted.append(part[head * HEAD_DIM : (head + 1) * HEAD_DIM, :] * share)
-            ref = keep_ref if slot < half else send_ref
-            width = query_part.shape[0]
-            ref[slot % half, :width] = jnp.concatenate(weighted, axis=0).astype(BF16)
-            ref[slot % half, width:] = query_part
+            out_part = jnp.concatenate(weighted, axis=0).astype(BF16)
+            if slot < half:
+                keep_ref[slot] = query_part
+                out_keep_ref[slot] = out_part
+            else:
+                send_ref[slot - half] = query_part
+                out_send_ref[slot - half] = out_part
 
 
 def backward(spot, kv, query, upstream, exponent, stats, own_stats, own_top, out_parts, tables):
@@ -241,7 +246,7 @@
     per = 4
     key_rows = blocks * block_rows
     whole = lambda shape: pl.BlockSpec(shape, lambda i, s: (0,) * len(shape))
-    half = pltpu.HBM((slices // 2, 2 * width, slice_rows), BF16)
+    half = pltpu.HBM((slices // 2, width, slice_rows), BF16)
     return pl.pallas_call(
         backward_kernel,
         grid_spec=pltpu.PrefetchScalarGridSpec(
@@ -264,10 +269,10 @@
             out_specs=(
                 pl.BlockSpec((per, 2, block_rows, width), lambda i, s: (i, 0, 0, 0)),
             )
-            + (whole((slices // 2, 2 * width, slice_rows)),) * 2,
+            + (whole((slices // 2, width, slice_rows)),) * 4,
             scratch_shapes=[pltpu.VMEM((width, queries), F32)],
         ),
-        out_shape=(pltpu.HBM((blocks, 2, block_rows, width), BF16), half, half),
+        out_shape=(pltpu.HBM((blocks, 2, block_rows, width), BF16), half, half, half, half),
         compiler_params=params(60),
         cost_estimate=pl.CostEstimate(
             flops=8 * heads * queries * key_rows * HEAD_DIM,
@@ -278,10 +283,8 @@
 
 
 def merge_query_grad(kept, arrived, cosine, sine):
-    width = kept.shape[1] // 2
-
     def kernel(kept_ref, arrived_ref, cos_ref, sin_ref, out_ref):
-        total = kept_ref[0, width:].astype(F32) + arrived_ref[0, width:].astype(F32)
+        total = kept_ref[0].astype(F32) + arrived_ref[0].astype(F32)
         half = HEAD_DIM // 2
         turned = []
         for head in range(total.shape[0] // HEAD_DIM):
@@ -293,23 +296,30 @@
 
     return pl.pallas_call(
         kernel,
-        out_shape=jax.ShapeDtypeStruct((kept.shape[2], width), BF16),
+        out_shape=jax.ShapeDtypeStruct((kept.shape[2], kept.shape[1]), BF16),
         compiler_params=params(8),
     )(kept, arrived, cosine, sine)
 
 
-def projection_grad(parts, cotangent):
-    count, width, _ = parts.shape
-
-    def kernel(parts_ref, cot_ref, out_ref):
-        joined = jnp.concatenate([parts_ref[part] for part in range(count)], axis=1)
-        out_ref[...] = matmul(joined, cot_ref[...]) * (1.0 / LOSS_SCALE)
-
+def projection_grad(spot, near, far, cotangent):
+    half, width, _ = near.shape
+
+    def kernel(spot_ref, near_ref, far_ref, cot_ref, out_ref, joined_ref):
+        for slot in range(2 * half):
+            first = pl.multiple_of(lax.bitwise_xor(spot_ref[0], DOUBLING[slot]) * 128, 128)
+            ref = near_ref if slot < half else far_ref
+            joined_ref[:, pl.ds(first, 128)] = ref[slot % half]
+        out_ref[...] = matmul(joined_ref[...], cot_ref[...]) * (1.0 / LOSS_SCALE)
+
+    vmem = pl.BlockSpec(memory_space=pltpu.VMEM)
     return pl.pallas_call(
         kernel,
         out_shape=jax.ShapeDtypeStruct((width, cotangent.shape[1]), F32),
+        in_specs=[pl.BlockSpec(memory_space=pltpu.SMEM), vmem, vmem, vmem],
+        out_specs=vmem,
+        scratch_shapes=[pltpu.VMEM((width, 2 * half * 128), BF16)],
         compiler_params=params(16),
-    )(parts, cotangent)
+    )(spot, near, far, cotangent)
 
 
 def assemble(spot, near, far):
@@ -383,7 +393,7 @@
         near = block[None]
         for bit in (4, 2):
             near = jnp.concatenate([near, partner(near, bit)])
-        return assemble(spot, near, partner(near, 1))
+        return near, partner(near, 1)
 
     spot = fsdp_index.astype(jnp.int32)[None]
     guide = 1.5 + guide_index[0].astype(F32) / 1024.0
@@ -418,25 +428,24 @@
     )
     query_angle = query_positions.astype(F32)[None, :] * frequency[:, None]
     query_tables = (jnp.cos(query_angle), jnp.sin(query_angle))
-    upstream, bias, tables, query_tables = tied(
-        (upstream.astype(BF16), bias, tables, query_tables)
-    )
-    upstream = doubled(upstream)
+    upstream, bias, tables = tied((upstream.astype(BF16), bias, tables))
+    upstream = assemble(spot, *doubled(upstream))
 
     exponent, out_parts, own_stats, own_top = forward(kv, query, upstream, bias)
     stats = over_fsdp(own_stats)
-    grads, keep, send = backward(
+    grads, query_keep, query_send, out_keep, out_send = backward(
         spot, kv, query, upstream, exponent, stats, own_stats, own_top, out_parts, tables
     )
     key_grad, value_grad = unpack_blocks(over_seq(grads))
 
-    keep, arrived = halved(keep, send)
-    query_grad = merge_query_grad(keep, arrived, *query_tables)[None]
-    attn_rows = keep[0, :width].astype(F32) + arrived[0, :width].astype(F32)
-    attn_rows = attn_rows.astype(BF16)
+    query_slice = merge_query_grad(*halved(query_keep, query_send), *query_tables)
+    query_grad = query_slice[None]
+
+    out_keep, arrived = halved(out_keep, out_send)
+    attn_rows = (out_keep[0].astype(F32) + arrived[0].astype(F32)).astype(BF16)
     other_rows = lax.ppermute(attn_rows, "cfg", [(0, 1), (1, 0)])
     mixed = own_weight * attn_rows.astype(F32) + (1.0 - own_weight) * other_rows.astype(F32)
-    weight_grad = projection_grad(doubled(mixed.astype(BF16)), cotangent)
+    weight_grad = projection_grad(spot, *doubled(mixed.astype(BF16)), cotangent)
     return (query_grad, key_grad, value_grad, weight_grad)
 
 

time: 173 us -> 165 us (0.954)
  local copies, waits for them, and re-layouts: 5.48 us -> 2 us
  starting transfers between devices: 40.3 us -> 38.1 us
    unnamed x16 -> x6, local copies, waits for them, and re-layouts: 4.12 us -> 0.01 us
    ppermute x12 -> x15, starting transfers between devices: 22.6 us -> 20.4 us  [partner(): return lax.ppermute(x, 'fsdp', [(s, s ^ bit) for s in range(fsdp_count)])]
    ppermute x12 -> x15, waiting for transfers between devices: 57.3 us -> 56.7 us  [partner(): return lax.ppermute(x, 'fsdp', [(s, s ^ bit) for s in range(fsdp_count)])]
  transfers between devices with their start and end apart: 15 -> 18, of which waited for: 14 -> 15; matrix products, arithmetic and copies ran while one was open for 4% -> 5% of each run, Pallas kernels for 3% -> 2%
where the time goes in v8:
time: 165 us; the launch traced here: 164 us
  waiting for transfers between devices  66 us (40%)
  Pallas kernels  38.5 us (23%)
  starting transfers between devices  38.1 us (23%)
  blocking collectives  11.3 us (7%)
  other arithmetic  5.65 us (3%)
  between operations  2.12 us (1%)
  local copies, waits for them, and re-layouts  2 us (1%)
    ppermute x15, waiting for transfers between devices, partner(): return lax.ppermute(x, 'fsdp', [(s, s ^ bit) for s in range(fsdp_count)])  56.7 us
    ppermute x15, starting transfers between devices, partner(): return lax.ppermute(x, 'fsdp', [(s, s ^ bit) for s in range(fsdp_count)])  20.4 us
    all_to_all x2, starting transfers between devices, over_seq(): return lax.all_to_all(x, 'seq', 0, 0, tiled=True)  17.6 us
    pallas_call x1, Pallas kernels, forward(): pl.pallas_call(forward_kernel, grid=(queries // step,), in_specs=[pl.Bloc...  14.8 us
    pallas_call x1, Pallas kernels, backward(): pl.pallas_call(backward_kernel, grid_spec=pltpu.PrefetchScalarGridSpec(nu...  14 us
    all_to_all x1, blocking collectives, over_fsdp(): return lax.all_to_all(x, 'fsdp', 0, 0, tiled=True)  11.3 us
    all_to_all x2, waiting for transfers between devices, over_seq(): return lax.all_to_all(x, 'seq', 0, 0, tiled=True)  9.31 us
    pallas_call x1, Pallas kernels, pack_blocks(): pl.pallas_call(kernel, grid=(parts // per,), out_shape=pltpu.HBM((parts,...  3.78 us
  transfers between devices with their start and end apart: 18, of which 15 were waited for; matrix products, arithmetic and copies ran while one was open for 5% of the time, Pallas kernels for 2%

profile of v8, /device:TPU:32, one launch (start us, length us, event | category | flops | bytes accessed | tf_op | source)
XLA Modules:
  0.0 163.6 jit_solution(1327097496490766598)
XLA Ops:
  0.6 3.8 %shard_map.111 = bf16[16,2,128,256]{3,2,1,0:T(8,128)(2,1)} custom-call(bf16[1,128,4096]{2,1,0:T(8,128)(2,1)} %k_ref.1, bf16[1,128,4096]{2,1,0:T(8,128)(2,1)} %v_ref.1), custom_call_target="tpu_custom_call" | custom-call | tf_op jit(solution)/shard_map/pallas_call | solution.py:44
  4.4 11.2 %all-to-all-start = ((bf16[16,2,128,256]{3,2,1,0:T(8,128)(2,1)}), bf16[16,2,128,256]{3,2,1,0:T(8,128)(2,1)}, u32[]{:S(2)}, u32[]{:S(2)}) async-start(bf16[16,2,128,256]{3,2,1,0:T(8,128)(2,1)} %shard_map.111), calls=%async_computation | async-start | bytes 4194304 | tf_op jit(solution)/shard_map/all_to_all | solution.py:377
  15.6 0.9 shard_map.112
  16.6 1.7 %collective-permute-start = (bf16[4,128,256]{2,1,0:T(8,128)(2,1)S(1)}, bf16[4,128,256]{2,1,0:T(8,128)(2,1)S(1)}, u32[]{:S(2)}, u32[]{:S(2)}) collective-permute-start(bf16[4,128,256]{2,1,0:T(8,128)(2,1)S(1)} %get-tuple-element.28), channel_id=1, source_target_pairs={{0,2},{1,3},{2,0},{3,1},{4,6},{5,7},{6,4},{7,5},{8,10},{9,11},{10,... | collective-permute-start | bytes 786440 | tf_op jit(solution)/shard_map/ppermute | solution.py:383
  18.3 0.9 multiply_sine_fusion.2
  19.3 1.0 multiply_sine_fusion
  20.2 3.9 %collective-permute-done = bf16[4,128,256]{2,1,0:T(8,128)(2,1)S(1)} collective-permute-done((bf16[4,128,256]{2,1,0:T(8,128)(2,1)S(1)}, bf16[4,128,256]{2,1,0:T(8,128)(2,1)S(1)}, u32[]{:S(2)}, u32[]{:S(2)}) %collective-permute-start) | collective-permute-done | bytes 262176 | tf_op jit(solution)/shard_map/ppermute | solution.py:383
  24.2 3.3 %collective-permute-start.1 = (bf16[2,128,256]{2,1,0:T(8,128)(2,1)S(1)}, bf16[2,128,256]{2,1,0:T(8,128)(2,1)S(1)}, u32[]{:S(2)}, u32[]{:S(2)}) collective-permute-start(bf16[2,128,256]{2,1,0:T(8,128)(2,1)S(1)} %slice.49), channel_id=1, source_target_pairs={{0,4},{1,5},{2,6},{3,7},{4,0},{5,1},{6,2},{7,3},{8,12},{9,13},{10,... | collective-permute-start | bytes 393224 | tf_op jit(solution)/shard_map/ppermute | solution.py:383
  27.7 3.1 %collective-permute-done.1 = bf16[2,128,256]{2,1,0:T(8,128)(2,1)S(1)} collective-permute-done((bf16[2,128,256]{2,1,0:T(8,128)(2,1)S(1)}, bf16[2,128,256]{2,1,0:T(8,128)(2,1)S(1)}, u32[]{:S(2)}, u32[]{:S(2)}) %collective-permute-start.1) | collective-permute-done | bytes 131104 | tf_op jit(solution)/shard_map/ppermute | solution.py:383
  30.8 0.7 collective-permute-start.2
  32.2 3.0 %collective-permute-done.2 = bf16[1,128,256]{2,1,0:T(8,128)(2,1)S(1)} collective-permute-done((bf16[1,128,256]{2,1,0:T(8,128)(2,1)S(1)}, bf16[1,128,256]{2,1,0:T(8,128)(2,1)S(1)}, u32[]{:S(2)}, u32[]{:S(2)}) %collective-permute-start.2) | collective-permute-done | bytes 65568 | tf_op jit(solution)/shard_map/ppermute | solution.py:383
  35.2 1.3 broadcast_in_dim.55.bias_ref
  36.5 3.2 %collective-permute-start.3 = (bf16[1,128,256]{2,1,0:T(8,128)(2,1)S(1)}, bf16[1,128,256]{2,1,0:T(8,128)(2,1)S(1)}, u32[]{:S(2)}, u32[]{:S(2)}) collective-permute-start(bf16[1,128,256]{2,1,0:T(8,128)(2,1)S(1)} %bitcast.19), channel_id=1, source_target_pairs={{0,4},{1,5},{2,6},{3,7},{4,0},{5,1},{6,2},{7,3},{8,12},{9,13},{10,... | collective-permute-start | bytes 196616 | tf_op jit(solution)/shard_map/ppermute | solution.py:383
  39.7 2.6 %collective-permute-done.3 = bf16[1,128,256]{2,1,0:T(8,128)(2,1)S(1)} collective-permute-done((bf16[1,128,256]{2,1,0:T(8,128)(2,1)S(1)}, bf16[1,128,256]{2,1,0:T(8,128)(2,1)S(1)}, u32[]{:S(2)}, u32[]{:S(2)}) %collective-permute-start.3) | collective-permute-done | bytes 65568 | tf_op jit(solution)/shard_map/ppermute | solution.py:383
  42.3 1.7 %collective-permute-start.4 = (bf16[2,128,256]{2,1,0:T(8,128)(2,1)S(1)}, bf16[2,128,256]{2,1,0:T(8,128)(2,1)S(1)}, u32[]{:S(2)}, u32[]{:S(2)}) collective-permute-start(bf16[2,128,256]{2,1,0:T(8,128)(2,1)S(1)} %pad_maximum_fusion.2), channel_id=1, source_target_pairs={{0,2},{1,3},{2,0},{3,1},{4,6},{5,7},{6,4},{7,5},{8,10},{9,11},{10,... | collective-permute-start | bytes 393224 | tf_op jit(solution)/shard_map/ppermute | solution.py:383
  44.0 3.4 %collective-permute-done.4 = bf16[2,128,256]{2,1,0:T(8,128)(2,1)S(1)} collective-permute-done((bf16[2,128,256]{2,1,0:T(8,128)(2,1)S(1)}, bf16[2,128,256]{2,1,0:T(8,128)(2,1)S(1)}, u32[]{:S(2)}, u32[]{:S(2)}) %collective-permute-start.4) | collective-permute-done | bytes 131104 | tf_op jit(solution)/shard_map/ppermute | solution.py:383
  47.4 0.7 collective-permute-start.5
  48.1 9.3 %collective-permute-done.5.far_ref = bf16[4,128,256]{2,1,0:T(8,128)(2,1)S(1)} collective-permute-done((bf16[4,128,256]{2,1,0:T(8,128)(2,1)S(1)}, bf16[4,128,256]{2,1,0:T(8,128)(2,1)S(1)}, u32[]{:S(2)}, u32[]{:S(2)}) %collective-permute-start.5) | collective-permute-done | bytes 262176 | tf_op jit(solution)/shard_map/ppermute | solution.py:383
  57.4 0.8 shard_map.113.up_ref
  58.2 7.9 %all-to-all-done.kv_ref = bf16[16,2,128,256]{3,2,1,0:T(8,128)(2,1)} async-done(((bf16[16,2,128,256]{3,2,1,0:T(8,128)(2,1)}), bf16[16,2,128,256]{3,2,1,0:T(8,128)(2,1)}, u32[]{:S(2)}, u32[]{:S(2)}) %all-to-all-start) | async-done | bytes 2097184 | tf_op jit(solution)/shard_map/all_to_all | solution.py:377
  66.1 14.8 %shard_map.114 = (bf16[2,2048,1024]{2,1,0:T(8,128)(2,1)}, bf16[8,256,128]{2,1,0:T(8,128)(2,1)}, f32[8,4,1024]{2,1,0:T(4,128)}, f32[2,1024]{1,0:T(2,128)}) custom-call(bf16[16,2,128,256]{3,2,1,0:T(8,128)(2,1)} %all-to-all-done.kv_ref, bf16[8,128,256]{2,1,0:T(8,128)(2,1)} %bitcast.23, bf16[8,128,256]{2,1,0:T(8,128)(2,1)} %shard_map.113.up_ref, ...), custom_call_target="tpu_custom_call" | custom-call | flops 2147483648 | bytes 12582912 | tf_op jit(solution)/shard_map/pallas_call | solution.py:116
  80.9 11.3 %all_to_all.15.stats_ref = f32[8,4,1024]{2,1,0:T(4,128)} all-to-all(f32[8,4,1024]{2,1,0:T(4,128)} %get-tuple-element.32.log_ref), channel_id=1, replica_groups=mesh['cfg'=2,'seq'=16,'fsdp'=8] {'fsdp'}, dimensions={0} | all-to-all | bytes 262144 | tf_op jit(solution)/shard_map/all_to_all | solution.py:380
  92.2 14.0 %shard_map.115 = (bf16[16,2,128,256]{3,2,1,0:T(8,128)(2,1)}, bf16[4,256,128]{2,1,0:T(8,128)(2,1)}, bf16[4,256,128]{2,1,0:T(8,128)(2,1)}, bf16[4,256,128]{2,1,0:T(8,128)(2,1)}, bf16[4,256,128]{2,1,0:T(8,128)(2,1)}) custom-call(s32[1]{0:T(128)} %bitcast.spot_ref, bf16[16,2,128,256]{3,2,1,0:T(8,128)(2,1)} %all-to-all-done.kv_ref, ...), custom_call_target="tpu_custom_call" | custom-call | flops 4294967296 | bytes 14680064 | tf_op jit(solution)/shard_map/pallas_call | solution.py:250
  106.2 6.5 %all-to-all-start.2 = ((bf16[16,2,128,256]{3,2,1,0:T(8,128)(2,1)}), bf16[16,2,128,256]{3,2,1,0:T(8,128)(2,1)S(1)}, u32[]{:S(2)}, u32[]{:S(2)}) async-start(bf16[16,2,128,256]{3,2,1,0:T(8,128)(2,1)} %get-tuple-element.41), calls=%async_computation.2 | async-start | bytes 4194304 | tf_op jit(solution)/shard_map/all_to_all | solution.py:377
  112.7 0.4 collective-permute-start.9
  113.0 6.2 %collective-permute-done.9 = bf16[4,256,128]{2,1,0:T(8,128)(2,1)S(1)} collective-permute-done((bf16[4,256,128]{2,1,0:T(8,128)(2,1)}, bf16[4,256,128]{2,1,0:T(8,128)(2,1)S(1)}, u32[]{:S(2)}, u32[]{:S(2)}) %collective-permute-start.9) | collective-permute-done | bytes 262176 | tf_op jit(solution)/shard_map/ppermute | solution.py:383
  119.2 1.0 add_convert_fusion
  120.3 1.4 collective-permute-start.10
  121.7 5.3 %collective-permute-done.10 = bf16[2,256,128]{2,1,0:T(8,128)(2,1)S(1)} collective-permute-done((bf16[2,256,128]{2,1,0:T(8,128)(2,1)S(1)}, bf16[2,256,128]{2,1,0:T(8,128)(2,1)S(1)}, u32[]{:S(2)}, u32[]{:S(2)}) %collective-permute-start.10) | collective-permute-done | bytes 131104 | tf_op jit(solution)/shard_map/ppermute | solution.py:383
  127.1 0.6 slice.59
  127.8 0.7 collective-permute-start.6
  129.2 3.1 %collective-permute-done.11 = bf16[1,256,128]{2,1,0:T(8,128)(2,1)} collective-permute-done((bf16[1,256,128]{2,1,0:T(8,128)(2,1)}, bf16[1,256,128]{2,1,0:T(8,128)(2,1)}, u32[]{:S(2)}, u32[]{:S(2)}) %collective-permute-start.11) | collective-permute-done | bytes 65568 | tf_op jit(solution)/shard_map/ppermute | solution.py:383
  132.3 0.9 fusion.1
  133.3 1.3 collective-permute-done.6
  134.5 1.1 add_convert_fusion.1
  135.6 1.1 collective-permute-start.7
  136.8 2.6 %collective-permute-start.13 = (bf16[1,256,128]{2,1,0:T(8,128)(2,1)S(1)}, bf16[1,256,128]{2,1,0:T(8,128)(2,1)S(1)}, u32[]{:S(2)}, u32[]{:S(2)}) collective-permute-start(bf16[1,256,128]{2,1,0:T(8,128)(2,1)S(1)} %fusion.2), channel_id=1, source_target_pairs={{0,4},{1,5},{2,6},{3,7},{4,0},{5,1},{6,2},{7,3},{8,12},{9,13},{10,... | collective-permute-start | bytes 196616 | tf_op jit(solution)/shard_map/ppermute | solution.py:383
  139.4 3.9 %collective-permute-done.13 = bf16[1,256,128]{2,1,0:T(8,128)(2,1)S(1)} collective-permute-done((bf16[1,256,128]{2,1,0:T(8,128)(2,1)S(1)}, bf16[1,256,128]{2,1,0:T(8,128)(2,1)S(1)}, u32[]{:S(2)}, u32[]{:S(2)}) %collective-permute-start.13) | collective-permute-done | bytes 65568 | tf_op jit(solution)/shard_map/ppermute | solution.py:383
  143.3 0.6 collective-permute-start.14
  143.9 4.4 %collective-permute-done.14 = bf16[2,256,128]{2,1,0:T(8,128)(2,1)S(1)} collective-permute-done((bf16[2,256,128]{2,1,0:T(8,128)(2,1)S(1)}, bf16[2,256,128]{2,1,0:T(8,128)(2,1)S(1)}, u32[]{:S(2)}, u32[]{:S(2)}) %collective-permute-start.14) | collective-permute-done | bytes 131104 | tf_op jit(solution)/shard_map/ppermute | solution.py:383
  148.4 1.6 collective-permute-start.15
  150.0 0.6 collective-permute-start.8
  150.6 0.2 multiply_sine_fusion.1
  150.8 7.2 %collective-permute-done.8.arrived_ref = bf16[1,256,128]{2,1,0:T(8,128)(2,1)S(1)} collective-permute-done((bf16[1,256,128]{2,1,0:T(8,128)(2,1)S(1)}, bf16[1,256,128]{2,1,0:T(8,128)(2,1)S(1)}, u32[]{:S(2)}, u32[]{:S(2)}) %collective-permute-start.8) | collective-permute-done | bytes 65568 | tf_op jit(solution)/shard_map/ppermute | solution.py:383
  158.0 0.7 shard_map.116
  158.8 1.5 shard_map.118
  160.3 1.4 all-to-all-done.2.in_ref
  161.8 1.9 %shard_map.117 = (bf16[1,128,4096]{2,1,0:T(8,128)(2,1)}, bf16[1,128,4096]{2,1,0:T(8,128)(2,1)}) custom-call(bf16[16,2,128,256]{3,2,1,0:T(8,128)(2,1)S(1)} %all-to-all-done.2.in_ref), custom_call_target="tpu_custom_call" | custom-call | tf_op jit(solution)/shard_map/pallas_call | solution.py:64
  (34 shorter events, 0.9 us)
Async XLA Ops:
  4.4 11.2 %copy-start = (bf16[1024,640]{1,0:T(8,128)(2,1)S(1)}, bf16[1024,640]{1,0:T(8,128)(2,1)}, u32[]{:S(2)}) copy-start(bf16[1024,640]{1,0:T(8,128)(2,1)} %cot_ref.2) | copy-start | bytes 3932164
  4.4 11.2 %copy-start.1 = (bf16[256,640]{1,0:T(8,128)(2,1)S(1)}, bf16[256,640]{1,0:T(8,128)(2,1)}, u32[]{:S(2)}) copy-start(bf16[256,640]{1,0:T(8,128)(2,1)} %weight_ref.1) | copy-start | bytes 983044
  4.4 61.7 %all-to-all-start = ((bf16[16,2,128,256]{3,2,1,0:T(8,128)(2,1)}), bf16[16,2,128,256]{3,2,1,0:T(8,128)(2,1)}, u32[]{:S(2)}, u32[]{:S(2)}) async-start(bf16[16,2,128,256]{3,2,1,0:T(8,128)(2,1)} %shard_map.111), calls=%async_computation | async-start | bytes 4194304 | tf_op jit(solution)/shard_map/all_to_all | solution.py:377
  15.6 12.0 %copy-start.2 = (s32[5]{0:T(128)S(1)}, s32[5]{0:T(128)}, u32[]{:S(2)}) copy-start(s32[5]{0:T(128)} %param.13) | copy-start | bytes 64
  16.6 7.6 %collective-permute-start = (bf16[4,128,256]{2,1,0:T(8,128)(2,1)S(1)}, bf16[4,128,256]{2,1,0:T(8,128)(2,1)S(1)}, u32[]{:S(2)}, u32[]{:S(2)}) collective-permute-start(bf16[4,128,256]{2,1,0:T(8,128)(2,1)S(1)} %get-tuple-element.28), channel_id=1, source_target_pairs={{0,2},{1,3},{2,0},{3,1},{4,6},{5,7},{6,4},{7,5},{8,10},{9,11},{10,... | collective-permute-start | bytes 786440 | tf_op jit(solution)/shard_map/ppermute | solution.py:383
  24.2 6.6 %collective-permute-start.1 = (bf16[2,128,256]{2,1,0:T(8,128)(2,1)S(1)}, bf16[2,128,256]{2,1,0:T(8,128)(2,1)S(1)}, u32[]{:S(2)}, u32[]{:S(2)}) collective-permute-start(bf16[2,128,256]{2,1,0:T(8,128)(2,1)S(1)} %slice.49), channel_id=1, source_target_pairs={{0,4},{1,5},{2,6},{3,7},{4,0},{5,1},{6,2},{7,3},{8,12},{9,13},{10,... | collective-permute-start | bytes 393224 | tf_op jit(solution)/shard_map/ppermute | solution.py:383
  30.8 4.4 %collective-permute-start.2 = (bf16[1,128,256]{2,1,0:T(8,128)(2,1)S(1)}, bf16[1,128,256]{2,1,0:T(8,128)(2,1)S(1)}, u32[]{:S(2)}, u32[]{:S(2)}) collective-permute-start(bf16[1,128,256]{2,1,0:T(8,128)(2,1)S(1)} %slice.51), channel_id=1, source_target_pairs={{0,1},{1,0},{2,3},{3,2},{4,5},{5,4},{6,7},{7,6},{8,9},{9,8},{10,11... | collective-permute-start | bytes 196616 | tf_op jit(solution)/shard_map/ppermute | solution.py:383
  36.5 5.8 %collective-permute-start.3 = (bf16[1,128,256]{2,1,0:T(8,128)(2,1)S(1)}, bf16[1,128,256]{2,1,0:T(8,128)(2,1)S(1)}, u32[]{:S(2)}, u32[]{:S(2)}) collective-permute-start(bf16[1,128,256]{2,1,0:T(8,128)(2,1)S(1)} %bitcast.19), channel_id=1, source_target_pairs={{0,4},{1,5},{2,6},{3,7},{4,0},{5,1},{6,2},{7,3},{8,12},{9,13},{10,... | collective-permute-start | bytes 196616 | tf_op jit(solution)/shard_map/ppermute | solution.py:383
  42.3 5.1 %collective-permute-start.4 = (bf16[2,128,256]{2,1,0:T(8,128)(2,1)S(1)}, bf16[2,128,256]{2,1,0:T(8,128)(2,1)S(1)}, u32[]{:S(2)}, u32[]{:S(2)}) collective-permute-start(bf16[2,128,256]{2,1,0:T(8,128)(2,1)S(1)} %pad_maximum_fusion.2), channel_id=1, source_target_pairs={{0,2},{1,3},{2,0},{3,1},{4,6},{5,7},{6,4},{7,5},{8,10},{9,11},{10,... | collective-permute-start | bytes 393224 | tf_op jit(solution)/shard_map/ppermute | solution.py:383
  47.4 10.0 %collective-permute-start.5 = (bf16[4,128,256]{2,1,0:T(8,128)(2,1)S(1)}, bf16[4,128,256]{2,1,0:T(8,128)(2,1)S(1)}, u32[]{:S(2)}, u32[]{:S(2)}) collective-permute-start(bf16[4,128,256]{2,1,0:T(8,128)(2,1)S(1)} %pad_maximum_fusion.near_ref), channel_id=1, source_target_pairs={{0,1},{1,0},{2,3},{3,2},{4,5},{5,4},{6,7},{7,6},{8,9},{9,8},{10,11... | collective-permute-start | bytes 786440 | tf_op jit(solution)/shard_map/ppermute | solution.py:383
  106.2 55.6 %all-to-all-start.2 = ((bf16[16,2,128,256]{3,2,1,0:T(8,128)(2,1)}), bf16[16,2,128,256]{3,2,1,0:T(8,128)(2,1)S(1)}, u32[]{:S(2)}, u32[]{:S(2)}) async-start(bf16[16,2,128,256]{3,2,1,0:T(8,128)(2,1)} %get-tuple-element.41), calls=%async_computation.2 | async-start | bytes 4194304 | tf_op jit(solution)/shard_map/all_to_all | solution.py:377
  112.7 6.6 %collective-permute-start.9 = (bf16[4,256,128]{2,1,0:T(8,128)(2,1)}, bf16[4,256,128]{2,1,0:T(8,128)(2,1)S(1)}, u32[]{:S(2)}, u32[]{:S(2)}) collective-permute-start(bf16[4,256,128]{2,1,0:T(8,128)(2,1)} %get-tuple-element.45), channel_id=1, source_target_pairs={{0,2},{1,3},{2,0},{3,1},{4,6},{5,7},{6,4},{7,5},{8,10},{9,11},{10,... | collective-permute-start | bytes 786440 | tf_op jit(solution)/shard_map/ppermute | solution.py:383
  120.3 6.7 %collective-permute-start.10 = (bf16[2,256,128]{2,1,0:T(8,128)(2,1)S(1)}, bf16[2,256,128]{2,1,0:T(8,128)(2,1)S(1)}, u32[]{:S(2)}, u32[]{:S(2)}) collective-permute-start(bf16[2,256,128]{2,1,0:T(8,128)(2,1)S(1)} %slice.57), channel_id=1, source_target_pairs={{0,4},{1,5},{2,6},{3,7},{4,0},{5,1},{6,2},{7,3},{8,12},{9,13},{10,... | collective-permute-start | bytes 393224 | tf_op jit(solution)/shard_map/ppermute | solution.py:383
  127.7 4.6 %collective-permute-start.11 = (bf16[1,256,128]{2,1,0:T(8,128)(2,1)}, bf16[1,256,128]{2,1,0:T(8,128)(2,1)}, u32[]{:S(2)}, u32[]{:S(2)}) collective-permute-start(bf16[1,256,128]{2,1,0:T(8,128)(2,1)} %slice.59), channel_id=1, source_target_pairs={{0,1},{1,0},{2,3},{3,2},{4,5},{5,4},{6,7},{7,6},{8,9},{9,8},{10,11... | collective-permute-start | bytes 196616 | tf_op jit(solution)/shard_map/ppermute | solution.py:383
  127.8 6.7 %collective-permute-start.6 = (bf16[4,256,128]{2,1,0:T(8,128)(2,1)}, bf16[4,256,128]{2,1,0:T(8,128)(2,1)}, u32[]{:S(2)}, u32[]{:S(2)}) collective-permute-start(bf16[4,256,128]{2,1,0:T(8,128)(2,1)} %get-tuple-element.40), channel_id=1, source_target_pairs={{0,2},{1,3},{2,0},{3,1},{4,6},{5,7},{6,4},{7,5},{8,10},{9,11},{10,... | collective-permute-start | bytes 786440 | tf_op jit(solution)/shard_map/ppermute | solution.py:383
  133.2 3.6 %collective-permute-start.12 = (bf16[256,128]{1,0:T(8,128)(2,1)S(1)}, bf16[256,128]{1,0:T(8,128)(2,1)S(1)}, u32[]{:S(2)}, u32[]{:S(2)}) collective-permute-start(bf16[256,128]{1,0:T(8,128)(2,1)S(1)} %fusion.1), channel_id=1, source_target_pairs={{0,128},{128,0},{1,129},{129,1},{2,130},{130,2},{3,131},{131,3},{4... | collective-permute-start | bytes 196616 | tf_op jit(solution)/shard_map/ppermute | solution.py:446
  135.6 8.3 %collective-permute-start.7 = (bf16[2,256,128]{2,1,0:T(8,128)(2,1)S(1)}, bf16[2,256,128]{2,1,0:T(8,128)(2,1)S(1)}, u32[]{:S(2)}, u32[]{:S(2)}) collective-permute-start(bf16[2,256,128]{2,1,0:T(8,128)(2,1)S(1)} %slice.53), channel_id=1, source_target_pairs={{0,4},{1,5},{2,6},{3,7},{4,0},{5,1},{6,2},{7,3},{8,12},{9,13},{10,... | collective-permute-start | bytes 393224 | tf_op jit(solution)/shard_map/ppermute | solution.py:383
  136.8 6.5 %collective-permute-start.13 = (bf16[1,256,128]{2,1,0:T(8,128)(2,1)S(1)}, bf16[1,256,128]{2,1,0:T(8,128)(2,1)S(1)}, u32[]{:S(2)}, u32[]{:S(2)}) collective-permute-start(bf16[1,256,128]{2,1,0:T(8,128)(2,1)S(1)} %fusion.2), channel_id=1, source_target_pairs={{0,4},{1,5},{2,6},{3,7},{4,0},{5,1},{6,2},{7,3},{8,12},{9,13},{10,... | collective-permute-start | bytes 196616 | tf_op jit(solution)/shard_map/ppermute | solution.py:383
  143.3 5.1 %collective-permute-start.14 = (bf16[2,256,128]{2,1,0:T(8,128)(2,1)S(1)}, bf16[2,256,128]{2,1,0:T(8,128)(2,1)S(1)}, u32[]{:S(2)}, u32[]{:S(2)}) collective-permute-start(bf16[2,256,128]{2,1,0:T(8,128)(2,1)S(1)} %pad_maximum_fusion.3), channel_id=1, source_target_pairs={{0,2},{1,3},{2,0},{3,1},{4,6},{5,7},{6,4},{7,5},{8,10},{9,11},{10,... | collective-permute-start | bytes 393224 | tf_op jit(solution)/shard_map/ppermute | solution.py:383
  148.4 10.4 %collective-permute-start.15 = (bf16[4,256,128]{2,1,0:T(8,128)(2,1)S(1)}, bf16[4,256,128]{2,1,0:T(8,128)(2,1)S(1)}, u32[]{:S(2)}, u32[]{:S(2)}) collective-permute-start(bf16[4,256,128]{2,1,0:T(8,128)(2,1)S(1)} %pad_maximum_fusion.1.near_ref), channel_id=1, source_target_pairs={{0,1},{1,0},{2,3},{3,2},{4,5},{5,4},{6,7},{7,6},{8,9},{9,8},{10,11... | collective-permute-start | bytes 786440 | tf_op jit(solution)/shard_map/ppermute | solution.py:383
  150.0 8.0 %collective-permute-start.8 = (bf16[1,256,128]{2,1,0:T(8,128)(2,1)S(1)}, bf16[1,256,128]{2,1,0:T(8,128)(2,1)S(1)}, u32[]{:S(2)}, u32[]{:S(2)}) collective-permute-start(bf16[1,256,128]{2,1,0:T(8,128)(2,1)S(1)} %get-tuple-element.46), channel_id=1, source_target_pairs={{0,1},{1,0},{2,3},{3,2},{4,5},{5,4},{6,7},{7,6},{8,9},{9,8},{10,11... | collective-permute-start | bytes 196616 | tf_op jit(solution)/shard_map/ppermute | solution.py:383

commit v9 on v8

--- a/solution.py
+++ b/solution.py
@@ -111,7 +111,7 @@
     slices, slice_rows, _ = query.shape
     queries = slices * slice_rows
     heads = width // HEAD_DIM
-    step = 256
+    step = 512
     per = step // slice_rows
     return pl.pallas_call(
         forward_kernel,

time: 165 us -> 162 us (0.982)
  Pallas kernels: 38.5 us -> 35.2 us
    pallas_call x1, Pallas kernels: 14.8 us -> 11.5 us  [forward(): pl.pallas_call(forward_kernel, grid=(queries // step,), in_specs=[pl.Bloc...]
  transfers between devices with their start and end apart: 18 -> 18, of which waited for: 15 -> 15; matrix products, arithmetic and copies ran while one was open for 5% -> 5% of each run, Pallas kernels for 2% -> 3%
where the time goes in v9:
time: 162 us; the launch traced here: 160 us
  waiting for transfers between devices  66.1 us (41%)
  starting transfers between devices  37.9 us (23%)
  Pallas kernels  35.2 us (22%)
  blocking collectives  11.3 us (7%)
  other arithmetic  5.65 us (3%)
  between operations  2.12 us (1%)
  local copies, waits for them, and re-layouts  2 us (1%)
    ppermute x15, waiting for transfers between devices, partner(): return lax.ppermute(x, 'fsdp', [(s, s ^ bit) for s in range(fsdp_count)])  56.7 us
    ppermute x15, starting transfers between devices, partner(): return lax.ppermute(x, 'fsdp', [(s, s ^ bit) for s in range(fsdp_count)])  20.2 us
    all_to_all x2, starting transfers between devices, over_seq(): return lax.all_to_all(x, 'seq', 0, 0, tiled=True)  17.6 us
    pallas_call x1, Pallas kernels, backward(): pl.pallas_call(backward_kernel, grid_spec=pltpu.PrefetchScalarGridSpec(nu...  14 us
    pallas_call x1, Pallas kernels, forward(): pl.pallas_call(forward_kernel, grid=(queries // step,), in_specs=[pl.Bloc...  11.5 us
    all_to_all x1, blocking collectives, over_fsdp(): return lax.all_to_all(x, 'fsdp', 0, 0, tiled=True)  11.3 us
    all_to_all x2, waiting for transfers between devices, over_seq(): return lax.all_to_all(x, 'seq', 0, 0, tiled=True)  9.44 us
    pallas_call x1, Pallas kernels, pack_blocks(): pl.pallas_call(kernel, grid=(parts // per,), out_shape=pltpu.HBM((parts,...  3.78 us
  transfers between devices with their start and end apart: 18, of which 15 were waited for; matrix products, arithmetic and copies ran while one was open for 5% of the time, Pallas kernels for 3%

profile of v9, /device:TPU:32, one launch (start us, length us, event | category | flops | bytes accessed | tf_op | source)
XLA Modules:
  0.0 160.4 jit_solution(4064605966776177130)
XLA Ops:
  0.6 3.8 %shard_map.111 = bf16[16,2,128,256]{3,2,1,0:T(8,128)(2,1)} custom-call(bf16[1,128,4096]{2,1,0:T(8,128)(2,1)} %k_ref.1, bf16[1,128,4096]{2,1,0:T(8,128)(2,1)} %v_ref.1), custom_call_target="tpu_custom_call" | custom-call | tf_op jit(solution)/shard_map/pallas_call | solution.py:44
  4.4 11.2 %all-to-all-start = ((bf16[16,2,128,256]{3,2,1,0:T(8,128)(2,1)}), bf16[16,2,128,256]{3,2,1,0:T(8,128)(2,1)}, u32[]{:S(2)}, u32[]{:S(2)}) async-start(bf16[16,2,128,256]{3,2,1,0:T(8,128)(2,1)} %shard_map.111), calls=%async_computation | async-start | bytes 4194304 | tf_op jit(solution)/shard_map/all_to_all | solution.py:377
  15.6 0.9 shard_map.112
  16.6 1.7 %collective-permute-start = (bf16[4,128,256]{2,1,0:T(8,128)(2,1)S(1)}, bf16[4,128,256]{2,1,0:T(8,128)(2,1)S(1)}, u32[]{:S(2)}, u32[]{:S(2)}) collective-permute-start(bf16[4,128,256]{2,1,0:T(8,128)(2,1)S(1)} %get-tuple-element.28), channel_id=1, source_target_pairs={{0,2},{1,3},{2,0},{3,1},{4,6},{5,7},{6,4},{7,5},{8,10},{9,11},{10,... | collective-permute-start | bytes 786440 | tf_op jit(solution)/shard_map/ppermute | solution.py:383
  18.3 0.9 multiply_sine_fusion.2
  19.3 1.0 multiply_sine_fusion
  20.2 3.9 %collective-permute-done = bf16[4,128,256]{2,1,0:T(8,128)(2,1)S(1)} collective-permute-done((bf16[4,128,256]{2,1,0:T(8,128)(2,1)S(1)}, bf16[4,128,256]{2,1,0:T(8,128)(2,1)S(1)}, u32[]{:S(2)}, u32[]{:S(2)}) %collective-permute-start) | collective-permute-done | bytes 262176 | tf_op jit(solution)/shard_map/ppermute | solution.py:383
  24.2 3.3 %collective-permute-start.1 = (bf16[2,128,256]{2,1,0:T(8,128)(2,1)S(1)}, bf16[2,128,256]{2,1,0:T(8,128)(2,1)S(1)}, u32[]{:S(2)}, u32[]{:S(2)}) collective-permute-start(bf16[2,128,256]{2,1,0:T(8,128)(2,1)S(1)} %slice.49), channel_id=1, source_target_pairs={{0,4},{1,5},{2,6},{3,7},{4,0},{5,1},{6,2},{7,3},{8,12},{9,13},{10,... | collective-permute-start | bytes 393224 | tf_op jit(solution)/shard_map/ppermute | solution.py:383
  27.7 3.1 %collective-permute-done.1 = bf16[2,128,256]{2,1,0:T(8,128)(2,1)S(1)} collective-permute-done((bf16[2,128,256]{2,1,0:T(8,128)(2,1)S(1)}, bf16[2,128,256]{2,1,0:T(8,128)(2,1)S(1)}, u32[]{:S(2)}, u32[]{:S(2)}) %collective-permute-start.1) | collective-permute-done | bytes 131104 | tf_op jit(solution)/shard_map/ppermute | solution.py:383
  30.8 0.7 collective-permute-start.2
  32.2 3.0 %collective-permute-done.2 = bf16[1,128,256]{2,1,0:T(8,128)(2,1)S(1)} collective-permute-done((bf16[1,128,256]{2,1,0:T(8,128)(2,1)S(1)}, bf16[1,128,256]{2,1,0:T(8,128)(2,1)S(1)}, u32[]{:S(2)}, u32[]{:S(2)}) %collective-permute-start.2) | collective-permute-done | bytes 65568 | tf_op jit(solution)/shard_map/ppermute | solution.py:383
  35.2 1.3 broadcast_in_dim.55.bias_ref
  36.5 3.2 %collective-permute-start.3 = (bf16[1,128,256]{2,1,0:T(8,128)(2,1)S(1)}, bf16[1,128,256]{2,1,0:T(8,128)(2,1)S(1)}, u32[]{:S(2)}, u32[]{:S(2)}) collective-permute-start(bf16[1,128,256]{2,1,0:T(8,128)(2,1)S(1)} %bitcast.19), channel_id=1, source_target_pairs={{0,4},{1,5},{2,6},{3,7},{4,0},{5,1},{6,2},{7,3},{8,12},{9,13},{10,... | collective-permute-start | bytes 196616 | tf_op jit(solution)/shard_map/ppermute | solution.py:383
  39.7 2.6 %collective-permute-done.3 = bf16[1,128,256]{2,1,0:T(8,128)(2,1)S(1)} collective-permute-done((bf16[1,128,256]{2,1,0:T(8,128)(2,1)S(1)}, bf16[1,128,256]{2,1,0:T(8,128)(2,1)S(1)}, u32[]{:S(2)}, u32[]{:S(2)}) %collective-permute-start.3) | collective-permute-done | bytes 65568 | tf_op jit(solution)/shard_map/ppermute | solution.py:383
  42.3 1.7 %collective-permute-start.4 = (bf16[2,128,256]{2,1,0:T(8,128)(2,1)S(1)}, bf16[2,128,256]{2,1,0:T(8,128)(2,1)S(1)}, u32[]{:S(2)}, u32[]{:S(2)}) collective-permute-start(bf16[2,128,256]{2,1,0:T(8,128)(2,1)S(1)} %pad_maximum_fusion.2), channel_id=1, source_target_pairs={{0,2},{1,3},{2,0},{3,1},{4,6},{5,7},{6,4},{7,5},{8,10},{9,11},{10,... | collective-permute-start | bytes 393224 | tf_op jit(solution)/shard_map/ppermute | solution.py:383
  44.0 3.4 %collective-permute-done.4 = bf16[2,128,256]{2,1,0:T(8,128)(2,1)S(1)} collective-permute-done((bf16[2,128,256]{2,1,0:T(8,128)(2,1)S(1)}, bf16[2,128,256]{2,1,0:T(8,128)(2,1)S(1)}, u32[]{:S(2)}, u32[]{:S(2)}) %collective-permute-start.4) | collective-permute-done | bytes 131104 | tf_op jit(solution)/shard_map/ppermute | solution.py:383
  47.4 0.7 collective-permute-start.5
  48.1 9.3 %collective-permute-done.5.far_ref = bf16[4,128,256]{2,1,0:T(8,128)(2,1)S(1)} collective-permute-done((bf16[4,128,256]{2,1,0:T(8,128)(2,1)S(1)}, bf16[4,128,256]{2,1,0:T(8,128)(2,1)S(1)}, u32[]{:S(2)}, u32[]{:S(2)}) %collective-permute-start.5) | collective-permute-done | bytes 262176 | tf_op jit(solution)/shard_map/ppermute | solution.py:383
  57.4 0.8 shard_map.113.up_ref
  58.2 7.9 %all-to-all-done.kv_ref = bf16[16,2,128,256]{3,2,1,0:T(8,128)(2,1)} async-done(((bf16[16,2,128,256]{3,2,1,0:T(8,128)(2,1)}), bf16[16,2,128,256]{3,2,1,0:T(8,128)(2,1)}, u32[]{:S(2)}, u32[]{:S(2)}) %all-to-all-start) | async-done | bytes 2097184 | tf_op jit(solution)/shard_map/all_to_all | solution.py:377
  66.1 11.5 %shard_map.114 = (bf16[2,2048,1024]{2,1,0:T(8,128)(2,1)}, bf16[8,256,128]{2,1,0:T(8,128)(2,1)}, f32[8,4,1024]{2,1,0:T(4,128)}, f32[2,1024]{1,0:T(2,128)}) custom-call(bf16[16,2,128,256]{3,2,1,0:T(8,128)(2,1)} %all-to-all-done.kv_ref, bf16[8,128,256]{2,1,0:T(8,128)(2,1)} %bitcast.23, bf16[8,128,256]{2,1,0:T(8,128)(2,1)} %shard_map.113.up_ref, ...), custom_call_target="tpu_custom_call" | custom-call | flops 2147483648 | bytes 12582912 | tf_op jit(solution)/shard_map/pallas_call | solution.py:116
  77.6 11.3 %all_to_all.15.stats_ref = f32[8,4,1024]{2,1,0:T(4,128)} all-to-all(f32[8,4,1024]{2,1,0:T(4,128)} %get-tuple-element.32.log_ref), channel_id=1, replica_groups=mesh['cfg'=2,'seq'=16,'fsdp'=8] {'fsdp'}, dimensions={0} | all-to-all | bytes 262144 | tf_op jit(solution)/shard_map/all_to_all | solution.py:380
  88.9 14.0 %shard_map.115 = (bf16[16,2,128,256]{3,2,1,0:T(8,128)(2,1)}, bf16[4,256,128]{2,1,0:T(8,128)(2,1)}, bf16[4,256,128]{2,1,0:T(8,128)(2,1)}, bf16[4,256,128]{2,1,0:T(8,128)(2,1)}, bf16[4,256,128]{2,1,0:T(8,128)(2,1)}) custom-call(s32[1]{0:T(128)} %bitcast.spot_ref, bf16[16,2,128,256]{3,2,1,0:T(8,128)(2,1)} %all-to-all-done.kv_ref, ...), custom_call_target="tpu_custom_call" | custom-call | flops 4294967296 | bytes 14680064 | tf_op jit(solution)/shard_map/pallas_call | solution.py:250
  102.9 6.4 %all-to-all-start.2 = ((bf16[16,2,128,256]{3,2,1,0:T(8,128)(2,1)}), bf16[16,2,128,256]{3,2,1,0:T(8,128)(2,1)S(1)}, u32[]{:S(2)}, u32[]{:S(2)}) async-start(bf16[16,2,128,256]{3,2,1,0:T(8,128)(2,1)} %get-tuple-element.41), calls=%async_computation.2 | async-start | bytes 4194304 | tf_op jit(solution)/shard_map/all_to_all | solution.py:377
  109.4 0.4 collective-permute-start.9
  109.8 6.2 %collective-permute-done.9 = bf16[4,256,128]{2,1,0:T(8,128)(2,1)S(1)} collective-permute-done((bf16[4,256,128]{2,1,0:T(8,128)(2,1)}, bf16[4,256,128]{2,1,0:T(8,128)(2,1)S(1)}, u32[]{:S(2)}, u32[]{:S(2)}) %collective-permute-start.9) | collective-permute-done | bytes 262176 | tf_op jit(solution)/shard_map/ppermute | solution.py:383
  116.0 1.0 add_convert_fusion
  117.0 1.3 collective-permute-start.10
  118.3 5.3 %collective-permute-done.10 = bf16[2,256,128]{2,1,0:T(8,128)(2,1)S(1)} collective-permute-done((bf16[2,256,128]{2,1,0:T(8,128)(2,1)S(1)}, bf16[2,256,128]{2,1,0:T(8,128)(2,1)S(1)}, u32[]{:S(2)}, u32[]{:S(2)}) %collective-permute-start.10) | collective-permute-done | bytes 131104 | tf_op jit(solution)/shard_map/ppermute | solution.py:383
  123.6 0.6 slice.59
  124.4 0.7 collective-permute-start.6
  125.8 3.1 %collective-permute-done.11 = bf16[1,256,128]{2,1,0:T(8,128)(2,1)} collective-permute-done((bf16[1,256,128]{2,1,0:T(8,128)(2,1)}, bf16[1,256,128]{2,1,0:T(8,128)(2,1)}, u32[]{:S(2)}, u32[]{:S(2)}) %collective-permute-start.11) | collective-permute-done | bytes 65568 | tf_op jit(solution)/shard_map/ppermute | solution.py:383
  128.8 0.9 fusion.1
  129.8 1.3 collective-permute-done.6
  131.1 1.1 add_convert_fusion.1
  132.2 1.1 collective-permute-start.7
  133.4 2.6 %collective-permute-start.13 = (bf16[1,256,128]{2,1,0:T(8,128)(2,1)S(1)}, bf16[1,256,128]{2,1,0:T(8,128)(2,1)S(1)}, u32[]{:S(2)}, u32[]{:S(2)}) collective-permute-start(bf16[1,256,128]{2,1,0:T(8,128)(2,1)S(1)} %fusion.2), channel_id=1, source_target_pairs={{0,4},{1,5},{2,6},{3,7},{4,0},{5,1},{6,2},{7,3},{8,12},{9,13},{10,... | collective-permute-start | bytes 196616 | tf_op jit(solution)/shard_map/ppermute | solution.py:383
  135.9 3.9 %collective-permute-done.13 = bf16[1,256,128]{2,1,0:T(8,128)(2,1)S(1)} collective-permute-done((bf16[1,256,128]{2,1,0:T(8,128)(2,1)S(1)}, bf16[1,256,128]{2,1,0:T(8,128)(2,1)S(1)}, u32[]{:S(2)}, u32[]{:S(2)}) %collective-permute-start.13) | collective-permute-done | bytes 65568 | tf_op jit(solution)/shard_map/ppermute | solution.py:383
  139.8 0.6 collective-permute-start.14
  140.5 4.4 %collective-permute-done.14 = bf16[2,256,128]{2,1,0:T(8,128)(2,1)S(1)} collective-permute-done((bf16[2,256,128]{2,1,0:T(8,128)(2,1)S(1)}, bf16[2,256,128]{2,1,0:T(8,128)(2,1)S(1)}, u32[]{:S(2)}, u32[]{:S(2)}) %collective-permute-start.14) | collective-permute-done | bytes 131104 | tf_op jit(solution)/shard_map/ppermute | solution.py:383
  144.9 1.6 %collective-permute-start.15 = (bf16[4,256,128]{2,1,0:T(8,128)(2,1)S(1)}, bf16[4,256,128]{2,1,0:T(8,128)(2,1)S(1)}, u32[]{:S(2)}, u32[]{:S(2)}) collective-permute-start(bf16[4,256,128]{2,1,0:T(8,128)(2,1)S(1)} %pad_maximum_fusion.1.near_ref), channel_id=1, source_target_pairs={{0,1},{1,0},{2,3},{3,2},{4,5},{5,4},{6,7},{7,6},{8,9},{9,8},{10,11... | collective-permute-start | bytes 786440 | tf_op jit(solution)/shard_map/ppermute | solution.py:383
  146.6 0.6 collective-permute-start.8
  147.1 0.2 multiply_sine_fusion.1
  147.3 7.3 %collective-permute-done.8.arrived_ref = bf16[1,256,128]{2,1,0:T(8,128)(2,1)S(1)} collective-permute-done((bf16[1,256,128]{2,1,0:T(8,128)(2,1)S(1)}, bf16[1,256,128]{2,1,0:T(8,128)(2,1)S(1)}, u32[]{:S(2)}, u32[]{:S(2)}) %collective-permute-start.8) | collective-permute-done | bytes 65568 | tf_op jit(solution)/shard_map/ppermute | solution.py:383
  154.6 0.7 shard_map.116
  155.4 1.5 shard_map.118
  156.9 1.6 all-to-all-done.2.in_ref
  158.5 1.9 %shard_map.117 = (bf16[1,128,4096]{2,1,0:T(8,128)(2,1)}, bf16[1,128,4096]{2,1,0:T(8,128)(2,1)}) custom-call(bf16[16,2,128,256]{3,2,1,0:T(8,128)(2,1)S(1)} %all-to-all-done.2.in_ref), custom_call_target="tpu_custom_call" | custom-call | tf_op jit(solution)/shard_map/pallas_call | solution.py:64
  (34 shorter events, 0.9 us)
Async XLA Ops:
  4.4 11.2 %copy-start = (bf16[1024,640]{1,0:T(8,128)(2,1)S(1)}, bf16[1024,640]{1,0:T(8,128)(2,1)}, u32[]{:S(2)}) copy-start(bf16[1024,640]{1,0:T(8,128)(2,1)} %cot_ref.2) | copy-start | bytes 3932164
  4.4 11.2 %copy-start.1 = (bf16[256,640]{1,0:T(8,128)(2,1)S(1)}, bf16[256,640]{1,0:T(8,128)(2,1)}, u32[]{:S(2)}) copy-start(bf16[256,640]{1,0:T(8,128)(2,1)} %weight_ref.1) | copy-start | bytes 983044
  4.4 61.7 %all-to-all-start = ((bf16[16,2,128,256]{3,2,1,0:T(8,128)(2,1)}), bf16[16,2,128,256]{3,2,1,0:T(8,128)(2,1)}, u32[]{:S(2)}, u32[]{:S(2)}) async-start(bf16[16,2,128,256]{3,2,1,0:T(8,128)(2,1)} %shard_map.111), calls=%async_computation | async-start | bytes 4194304 | tf_op jit(solution)/shard_map/all_to_all | solution.py:377
  15.6 12.0 %copy-start.2 = (s32[5]{0:T(128)S(1)}, s32[5]{0:T(128)}, u32[]{:S(2)}) copy-start(s32[5]{0:T(128)} %param.13) | copy-start | bytes 64
  16.6 7.6 %collective-permute-start = (bf16[4,128,256]{2,1,0:T(8,128)(2,1)S(1)}, bf16[4,128,256]{2,1,0:T(8,128)(2,1)S(1)}, u32[]{:S(2)}, u32[]{:S(2)}) collective-permute-start(bf16[4,128,256]{2,1,0:T(8,128)(2,1)S(1)} %get-tuple-element.28), channel_id=1, source_target_pairs={{0,2},{1,3},{2,0},{3,1},{4,6},{5,7},{6,4},{7,5},{8,10},{9,11},{10,... | collective-permute-start | bytes 786440 | tf_op jit(solution)/shard_map/ppermute | solution.py:383
  24.2 6.6 %collective-permute-start.1 = (bf16[2,128,256]{2,1,0:T(8,128)(2,1)S(1)}, bf16[2,128,256]{2,1,0:T(8,128)(2,1)S(1)}, u32[]{:S(2)}, u32[]{:S(2)}) collective-permute-start(bf16[2,128,256]{2,1,0:T(8,128)(2,1)S(1)} %slice.49), channel_id=1, source_target_pairs={{0,4},{1,5},{2,6},{3,7},{4,0},{5,1},{6,2},{7,3},{8,12},{9,13},{10,... | collective-permute-start | bytes 393224 | tf_op jit(solution)/shard_map/ppermute | solution.py:383
  30.8 4.4 %collective-permute-start.2 = (bf16[1,128,256]{2,1,0:T(8,128)(2,1)S(1)}, bf16[1,128,256]{2,1,0:T(8,128)(2,1)S(1)}, u32[]{:S(2)}, u32[]{:S(2)}) collective-permute-start(bf16[1,128,256]{2,1,0:T(8,128)(2,1)S(1)} %slice.51), channel_id=1, source_target_pairs={{0,1},{1,0},{2,3},{3,2},{4,5},{5,4},{6,7},{7,6},{8,9},{9,8},{10,11... | collective-permute-start | bytes 196616 | tf_op jit(solution)/shard_map/ppermute | solution.py:383
  36.5 5.8 %collective-permute-start.3 = (bf16[1,128,256]{2,1,0:T(8,128)(2,1)S(1)}, bf16[1,128,256]{2,1,0:T(8,128)(2,1)S(1)}, u32[]{:S(2)}, u32[]{:S(2)}) collective-permute-start(bf16[1,128,256]{2,1,0:T(8,128)(2,1)S(1)} %bitcast.19), channel_id=1, source_target_pairs={{0,4},{1,5},{2,6},{3,7},{4,0},{5,1},{6,2},{7,3},{8,12},{9,13},{10,... | collective-permute-start | bytes 196616 | tf_op jit(solution)/shard_map/ppermute | solution.py:383
  42.3 5.1 %collective-permute-start.4 = (bf16[2,128,256]{2,1,0:T(8,128)(2,1)S(1)}, bf16[2,128,256]{2,1,0:T(8,128)(2,1)S(1)}, u32[]{:S(2)}, u32[]{:S(2)}) collective-permute-start(bf16[2,128,256]{2,1,0:T(8,128)(2,1)S(1)} %pad_maximum_fusion.2), channel_id=1, source_target_pairs={{0,2},{1,3},{2,0},{3,1},{4,6},{5,7},{6,4},{7,5},{8,10},{9,11},{10,... | collective-permute-start | bytes 393224 | tf_op jit(solution)/shard_map/ppermute | solution.py:383
  47.4 10.0 %collective-permute-start.5 = (bf16[4,128,256]{2,1,0:T(8,128)(2,1)S(1)}, bf16[4,128,256]{2,1,0:T(8,128)(2,1)S(1)}, u32[]{:S(2)}, u32[]{:S(2)}) collective-permute-start(bf16[4,128,256]{2,1,0:T(8,128)(2,1)S(1)} %pad_maximum_fusion.near_ref), channel_id=1, source_target_pairs={{0,1},{1,0},{2,3},{3,2},{4,5},{5,4},{6,7},{7,6},{8,9},{9,8},{10,11... | collective-permute-start | bytes 786440 | tf_op jit(solution)/shard_map/ppermute | solution.py:383
  102.9 55.6 %all-to-all-start.2 = ((bf16[16,2,128,256]{3,2,1,0:T(8,128)(2,1)}), bf16[16,2,128,256]{3,2,1,0:T(8,128)(2,1)S(1)}, u32[]{:S(2)}, u32[]{:S(2)}) async-start(bf16[16,2,128,256]{3,2,1,0:T(8,128)(2,1)} %get-tuple-element.41), calls=%async_computation.2 | async-start | bytes 4194304 | tf_op jit(solution)/shard_map/all_to_all | solution.py:377
  109.4 6.6 %collective-permute-start.9 = (bf16[4,256,128]{2,1,0:T(8,128)(2,1)}, bf16[4,256,128]{2,1,0:T(8,128)(2,1)S(1)}, u32[]{:S(2)}, u32[]{:S(2)}) collective-permute-start(bf16[4,256,128]{2,1,0:T(8,128)(2,1)} %get-tuple-element.45), channel_id=1, source_target_pairs={{0,2},{1,3},{2,0},{3,1},{4,6},{5,7},{6,4},{7,5},{8,10},{9,11},{10,... | collective-permute-start | bytes 786440 | tf_op jit(solution)/shard_map/ppermute | solution.py:383
  117.0 6.6 %collective-permute-start.10 = (bf16[2,256,128]{2,1,0:T(8,128)(2,1)S(1)}, bf16[2,256,128]{2,1,0:T(8,128)(2,1)S(1)}, u32[]{:S(2)}, u32[]{:S(2)}) collective-permute-start(bf16[2,256,128]{2,1,0:T(8,128)(2,1)S(1)} %slice.57), channel_id=1, source_target_pairs={{0,4},{1,5},{2,6},{3,7},{4,0},{5,1},{6,2},{7,3},{8,12},{9,13},{10,... | collective-permute-start | bytes 393224 | tf_op jit(solution)/shard_map/ppermute | solution.py:383
  124.3 4.6 %collective-permute-start.11 = (bf16[1,256,128]{2,1,0:T(8,128)(2,1)}, bf16[1,256,128]{2,1,0:T(8,128)(2,1)}, u32[]{:S(2)}, u32[]{:S(2)}) collective-permute-start(bf16[1,256,128]{2,1,0:T(8,128)(2,1)} %slice.59), channel_id=1, source_target_pairs={{0,1},{1,0},{2,3},{3,2},{4,5},{5,4},{6,7},{7,6},{8,9},{9,8},{10,11... | collective-permute-start | bytes 196616 | tf_op jit(solution)/shard_map/ppermute | solution.py:383
  124.4 6.7 %collective-permute-start.6 = (bf16[4,256,128]{2,1,0:T(8,128)(2,1)}, bf16[4,256,128]{2,1,0:T(8,128)(2,1)}, u32[]{:S(2)}, u32[]{:S(2)}) collective-permute-start(bf16[4,256,128]{2,1,0:T(8,128)(2,1)} %get-tuple-element.40), channel_id=1, source_target_pairs={{0,2},{1,3},{2,0},{3,1},{4,6},{5,7},{6,4},{7,5},{8,10},{9,11},{10,... | collective-permute-start | bytes 786440 | tf_op jit(solution)/shard_map/ppermute | solution.py:383
  129.7 3.6 %collective-permute-start.12 = (bf16[256,128]{1,0:T(8,128)(2,1)S(1)}, bf16[256,128]{1,0:T(8,128)(2,1)S(1)}, u32[]{:S(2)}, u32[]{:S(2)}) collective-permute-start(bf16[256,128]{1,0:T(8,128)(2,1)S(1)} %fusion.1), channel_id=1, source_target_pairs={{0,128},{128,0},{1,129},{129,1},{2,130},{130,2},{3,131},{131,3},{4... | collective-permute-start | bytes 196616 | tf_op jit(solution)/shard_map/ppermute | solution.py:446
  132.2 8.3 %collective-permute-start.7 = (bf16[2,256,128]{2,1,0:T(8,128)(2,1)S(1)}, bf16[2,256,128]{2,1,0:T(8,128)(2,1)S(1)}, u32[]{:S(2)}, u32[]{:S(2)}) collective-permute-start(bf16[2,256,128]{2,1,0:T(8,128)(2,1)S(1)} %slice.53), channel_id=1, source_target_pairs={{0,4},{1,5},{2,6},{3,7},{4,0},{5,1},{6,2},{7,3},{8,12},{9,13},{10,... | collective-permute-start | bytes 393224 | tf_op jit(solution)/shard_map/ppermute | solution.py:383
  133.4 6.5 %collective-permute-start.13 = (bf16[1,256,128]{2,1,0:T(8,128)(2,1)S(1)}, bf16[1,256,128]{2,1,0:T(8,128)(2,1)S(1)}, u32[]{:S(2)}, u32[]{:S(2)}) collective-permute-start(bf16[1,256,128]{2,1,0:T(8,128)(2,1)S(1)} %fusion.2), channel_id=1, source_target_pairs={{0,4},{1,5},{2,6},{3,7},{4,0},{5,1},{6,2},{7,3},{8,12},{9,13},{10,... | collective-permute-start | bytes 196616 | tf_op jit(solution)/shard_map/ppermute | solution.py:383
  139.8 5.1 %collective-permute-start.14 = (bf16[2,256,128]{2,1,0:T(8,128)(2,1)S(1)}, bf16[2,256,128]{2,1,0:T(8,128)(2,1)S(1)}, u32[]{:S(2)}, u32[]{:S(2)}) collective-permute-start(bf16[2,256,128]{2,1,0:T(8,128)(2,1)S(1)} %pad_maximum_fusion.3), channel_id=1, source_target_pairs={{0,2},{1,3},{2,0},{3,1},{4,6},{5,7},{6,4},{7,5},{8,10},{9,11},{10,... | collective-permute-start | bytes 393224 | tf_op jit(solution)/shard_map/ppermute | solution.py:383
  144.9 10.4 %collective-permute-start.15 = (bf16[4,256,128]{2,1,0:T(8,128)(2,1)S(1)}, bf16[4,256,128]{2,1,0:T(8,128)(2,1)S(1)}, u32[]{:S(2)}, u32[]{:S(2)}) collective-permute-start(bf16[4,256,128]{2,1,0:T(8,128)(2,1)S(1)} %pad_maximum_fusion.1.near_ref), channel_id=1, source_target_pairs={{0,1},{1,0},{2,3},{3,2},{4,5},{5,4},{6,7},{7,6},{8,9},{9,8},{10,11... | collective-permute-start | bytes 786440 | tf_op jit(solution)/shard_map/ppermute | solution.py:383
  146.6 8.1 %collective-permute-start.8 = (bf16[1,256,128]{2,1,0:T(8,128)(2,1)S(1)}, bf16[1,256,128]{2,1,0:T(8,128)(2,1)S(1)}, u32[]{:S(2)}, u32[]{:S(2)}) collective-permute-start(bf16[1,256,128]{2,1,0:T(8,128)(2,1)S(1)} %get-tuple-element.46), channel_id=1, source_target_pairs={{0,1},{1,0},{2,3},{3,2},{4,5},{5,4},{6,7},{7,6},{8,9},{9,8},{10,11... | collective-permute-start | bytes 196616 | tf_op jit(solution)/shard_map/ppermute | solution.py:383

commit v10 on v9

--- a/solution.py
+++ b/solution.py
@@ -34,7 +34,7 @@
 
 def pack_blocks(keys, values, parts):
     rows, width = keys.shape[1], keys.shape[2] // parts
-    per = 4
+    per = 8
 
     def kernel(k_ref, v_ref, out_ref):
         for which, ref in enumerate((k_ref, v_ref)):

time: 162 us -> 161 us (level)
  no operation moved by 1% of the time
where the time goes in v10:
time: 161 us; the launch traced here: 159 us
  waiting for transfers between devices  66.1 us (41%)
  starting transfers between devices  37.9 us (24%)
  Pallas kernels  34.1 us (21%)
  blocking collectives  11.3 us (7%)
  other arithmetic  5.65 us (4%)
  between operations  2.12 us (1%)
  local copies, waits for them, and re-layouts  2 us (1%)
    ppermute x15, waiting for transfers between devices, partner(): return lax.ppermute(x, 'fsdp', [(s, s ^ bit) for s in range(fsdp_count)])  56.7 us
    ppermute x15, starting transfers between devices, partner(): return lax.ppermute(x, 'fsdp', [(s, s ^ bit) for s in range(fsdp_count)])  20.2 us
    all_to_all x2, starting transfers between devices, over_seq(): return lax.all_to_all(x, 'seq', 0, 0, tiled=True)  17.6 us
    pallas_call x1, Pallas kernels, backward(): pl.pallas_call(backward_kernel, grid_spec=pltpu.PrefetchScalarGridSpec(nu...  14 us
    pallas_call x1, Pallas kernels, forward(): pl.pallas_call(forward_kernel, grid=(queries // step,), in_specs=[pl.Bloc...  11.5 us
    all_to_all x1, blocking collectives, over_fsdp(): return lax.all_to_all(x, 'fsdp', 0, 0, tiled=True)  11.3 us
    all_to_all x2, waiting for transfers between devices, over_seq(): return lax.all_to_all(x, 'seq', 0, 0, tiled=True)  9.46 us
  transfers between devices with their start and end apart: 18, of which 15 were waited for; matrix products, arithmetic and copies ran while one was open for 5% of the time, Pallas kernels for 3%

profile of v10, /device:TPU:32, one launch (start us, length us, event | category | flops | bytes accessed | tf_op | source)
XLA Modules:
  0.0 159.2 jit_solution(15381573860040314393)
XLA Ops:
  0.6 2.6 %shard_map.111 = bf16[16,2,128,256]{3,2,1,0:T(8,128)(2,1)} custom-call(bf16[1,128,4096]{2,1,0:T(8,128)(2,1)} %k_ref.1, bf16[1,128,4096]{2,1,0:T(8,128)(2,1)} %v_ref.1), custom_call_target="tpu_custom_call" | custom-call | tf_op jit(solution)/shard_map/pallas_call | solution.py:44
  3.3 11.2 %all-to-all-start = ((bf16[16,2,128,256]{3,2,1,0:T(8,128)(2,1)}), bf16[16,2,128,256]{3,2,1,0:T(8,128)(2,1)}, u32[]{:S(2)}, u32[]{:S(2)}) async-start(bf16[16,2,128,256]{3,2,1,0:T(8,128)(2,1)} %shard_map.111), calls=%async_computation | async-start | bytes 4194304 | tf_op jit(solution)/shard_map/all_to_all | solution.py:377
  14.5 0.9 shard_map.112
  15.4 1.7 %collective-permute-start = (bf16[4,128,256]{2,1,0:T(8,128)(2,1)S(1)}, bf16[4,128,256]{2,1,0:T(8,128)(2,1)S(1)}, u32[]{:S(2)}, u32[]{:S(2)}) collective-permute-start(bf16[4,128,256]{2,1,0:T(8,128)(2,1)S(1)} %get-tuple-element.28), channel_id=1, source_target_pairs={{0,2},{1,3},{2,0},{3,1},{4,6},{5,7},{6,4},{7,5},{8,10},{9,11},{10,... | collective-permute-start | bytes 786440 | tf_op jit(solution)/shard_map/ppermute | solution.py:383
  17.2 0.9 multiply_sine_fusion.2
  18.1 1.0 multiply_sine_fusion
  19.1 3.9 %collective-permute-done = bf16[4,128,256]{2,1,0:T(8,128)(2,1)S(1)} collective-permute-done((bf16[4,128,256]{2,1,0:T(8,128)(2,1)S(1)}, bf16[4,128,256]{2,1,0:T(8,128)(2,1)S(1)}, u32[]{:S(2)}, u32[]{:S(2)}) %collective-permute-start) | collective-permute-done | bytes 262176 | tf_op jit(solution)/shard_map/ppermute | solution.py:383
  23.1 3.3 %collective-permute-start.1 = (bf16[2,128,256]{2,1,0:T(8,128)(2,1)S(1)}, bf16[2,128,256]{2,1,0:T(8,128)(2,1)S(1)}, u32[]{:S(2)}, u32[]{:S(2)}) collective-permute-start(bf16[2,128,256]{2,1,0:T(8,128)(2,1)S(1)} %slice.49), channel_id=1, source_target_pairs={{0,4},{1,5},{2,6},{3,7},{4,0},{5,1},{6,2},{7,3},{8,12},{9,13},{10,... | collective-permute-start | bytes 393224 | tf_op jit(solution)/shard_map/ppermute | solution.py:383
  26.6 3.1 %collective-permute-done.1 = bf16[2,128,256]{2,1,0:T(8,128)(2,1)S(1)} collective-permute-done((bf16[2,128,256]{2,1,0:T(8,128)(2,1)S(1)}, bf16[2,128,256]{2,1,0:T(8,128)(2,1)S(1)}, u32[]{:S(2)}, u32[]{:S(2)}) %collective-permute-start.1) | collective-permute-done | bytes 131104 | tf_op jit(solution)/shard_map/ppermute | solution.py:383
  29.7 0.7 collective-permute-start.2
  31.0 3.0 %collective-permute-done.2 = bf16[1,128,256]{2,1,0:T(8,128)(2,1)S(1)} collective-permute-done((bf16[1,128,256]{2,1,0:T(8,128)(2,1)S(1)}, bf16[1,128,256]{2,1,0:T(8,128)(2,1)S(1)}, u32[]{:S(2)}, u32[]{:S(2)}) %collective-permute-start.2) | collective-permute-done | bytes 65568 | tf_op jit(solution)/shard_map/ppermute | solution.py:383
  34.1 1.3 broadcast_in_dim.55.bias_ref
  35.4 3.2 %collective-permute-start.3 = (bf16[1,128,256]{2,1,0:T(8,128)(2,1)S(1)}, bf16[1,128,256]{2,1,0:T(8,128)(2,1)S(1)}, u32[]{:S(2)}, u32[]{:S(2)}) collective-permute-start(bf16[1,128,256]{2,1,0:T(8,128)(2,1)S(1)} %bitcast.19), channel_id=1, source_target_pairs={{0,4},{1,5},{2,6},{3,7},{4,0},{5,1},{6,2},{7,3},{8,12},{9,13},{10,... | collective-permute-start | bytes 196616 | tf_op jit(solution)/shard_map/ppermute | solution.py:383
  38.6 2.6 %collective-permute-done.3 = bf16[1,128,256]{2,1,0:T(8,128)(2,1)S(1)} collective-permute-done((bf16[1,128,256]{2,1,0:T(8,128)(2,1)S(1)}, bf16[1,128,256]{2,1,0:T(8,128)(2,1)S(1)}, u32[]{:S(2)}, u32[]{:S(2)}) %collective-permute-start.3) | collective-permute-done | bytes 65568 | tf_op jit(solution)/shard_map/ppermute | solution.py:383
  41.2 1.7 %collective-permute-start.4 = (bf16[2,128,256]{2,1,0:T(8,128)(2,1)S(1)}, bf16[2,128,256]{2,1,0:T(8,128)(2,1)S(1)}, u32[]{:S(2)}, u32[]{:S(2)}) collective-permute-start(bf16[2,128,256]{2,1,0:T(8,128)(2,1)S(1)} %pad_maximum_fusion.2), channel_id=1, source_target_pairs={{0,2},{1,3},{2,0},{3,1},{4,6},{5,7},{6,4},{7,5},{8,10},{9,11},{10,... | collective-permute-start | bytes 393224 | tf_op jit(solution)/shard_map/ppermute | solution.py:383
  42.8 3.4 %collective-permute-done.4 = bf16[2,128,256]{2,1,0:T(8,128)(2,1)S(1)} collective-permute-done((bf16[2,128,256]{2,1,0:T(8,128)(2,1)S(1)}, bf16[2,128,256]{2,1,0:T(8,128)(2,1)S(1)}, u32[]{:S(2)}, u32[]{:S(2)}) %collective-permute-start.4) | collective-permute-done | bytes 131104 | tf_op jit(solution)/shard_map/ppermute | solution.py:383
  46.3 0.7 collective-permute-start.5
  46.9 9.3 %collective-permute-done.5.far_ref = bf16[4,128,256]{2,1,0:T(8,128)(2,1)S(1)} collective-permute-done((bf16[4,128,256]{2,1,0:T(8,128)(2,1)S(1)}, bf16[4,128,256]{2,1,0:T(8,128)(2,1)S(1)}, u32[]{:S(2)}, u32[]{:S(2)}) %collective-permute-start.5) | collective-permute-done | bytes 262176 | tf_op jit(solution)/shard_map/ppermute | solution.py:383
  56.3 0.8 shard_map.113.up_ref
  57.1 7.9 %all-to-all-done.kv_ref = bf16[16,2,128,256]{3,2,1,0:T(8,128)(2,1)} async-done(((bf16[16,2,128,256]{3,2,1,0:T(8,128)(2,1)}), bf16[16,2,128,256]{3,2,1,0:T(8,128)(2,1)}, u32[]{:S(2)}, u32[]{:S(2)}) %all-to-all-start) | async-done | bytes 2097184 | tf_op jit(solution)/shard_map/all_to_all | solution.py:377
  64.9 11.5 %shard_map.114 = (bf16[2,2048,1024]{2,1,0:T(8,128)(2,1)}, bf16[8,256,128]{2,1,0:T(8,128)(2,1)}, f32[8,4,1024]{2,1,0:T(4,128)}, f32[2,1024]{1,0:T(2,128)}) custom-call(bf16[16,2,128,256]{3,2,1,0:T(8,128)(2,1)} %all-to-all-done.kv_ref, bf16[8,128,256]{2,1,0:T(8,128)(2,1)} %bitcast.23, bf16[8,128,256]{2,1,0:T(8,128)(2,1)} %shard_map.113.up_ref, ...), custom_call_target="tpu_custom_call" | custom-call | flops 2147483648 | bytes 12582912 | tf_op jit(solution)/shard_map/pallas_call | solution.py:116
  76.4 11.3 %all_to_all.15.stats_ref = f32[8,4,1024]{2,1,0:T(4,128)} all-to-all(f32[8,4,1024]{2,1,0:T(4,128)} %get-tuple-element.32.log_ref), channel_id=1, replica_groups=mesh['cfg'=2,'seq'=16,'fsdp'=8] {'fsdp'}, dimensions={0} | all-to-all | bytes 262144 | tf_op jit(solution)/shard_map/all_to_all | solution.py:380
  87.8 14.0 %shard_map.115 = (bf16[16,2,128,256]{3,2,1,0:T(8,128)(2,1)}, bf16[4,256,128]{2,1,0:T(8,128)(2,1)}, bf16[4,256,128]{2,1,0:T(8,128)(2,1)}, bf16[4,256,128]{2,1,0:T(8,128)(2,1)}, bf16[4,256,128]{2,1,0:T(8,128)(2,1)}) custom-call(s32[1]{0:T(128)} %bitcast.spot_ref, bf16[16,2,128,256]{3,2,1,0:T(8,128)(2,1)} %all-to-all-done.kv_ref, ...), custom_call_target="tpu_custom_call" | custom-call | flops 4294967296 | bytes 14680064 | tf_op jit(solution)/shard_map/pallas_call | solution.py:250
  101.8 6.4 %all-to-all-start.2 = ((bf16[16,2,128,256]{3,2,1,0:T(8,128)(2,1)}), bf16[16,2,128,256]{3,2,1,0:T(8,128)(2,1)S(1)}, u32[]{:S(2)}, u32[]{:S(2)}) async-start(bf16[16,2,128,256]{3,2,1,0:T(8,128)(2,1)} %get-tuple-element.41), calls=%async_computation.2 | async-start | bytes 4194304 | tf_op jit(solution)/shard_map/all_to_all | solution.py:377
  108.2 0.4 collective-permute-start.9
  108.6 6.2 %collective-permute-done.9 = bf16[4,256,128]{2,1,0:T(8,128)(2,1)S(1)} collective-permute-done((bf16[4,256,128]{2,1,0:T(8,128)(2,1)}, bf16[4,256,128]{2,1,0:T(8,128)(2,1)S(1)}, u32[]{:S(2)}, u32[]{:S(2)}) %collective-permute-start.9) | collective-permute-done | bytes 262176 | tf_op jit(solution)/shard_map/ppermute | solution.py:383
  114.8 1.0 add_convert_fusion
  115.8 1.4 collective-permute-start.10
  117.3 5.1 %collective-permute-done.10 = bf16[2,256,128]{2,1,0:T(8,128)(2,1)S(1)} collective-permute-done((bf16[2,256,128]{2,1,0:T(8,128)(2,1)S(1)}, bf16[2,256,128]{2,1,0:T(8,128)(2,1)S(1)}, u32[]{:S(2)}, u32[]{:S(2)}) %collective-permute-start.10) | collective-permute-done | bytes 131104 | tf_op jit(solution)/shard_map/ppermute | solution.py:383
  122.4 0.6 slice.59
  123.2 0.7 collective-permute-start.6
  124.6 3.1 %collective-permute-done.11 = bf16[1,256,128]{2,1,0:T(8,128)(2,1)} collective-permute-done((bf16[1,256,128]{2,1,0:T(8,128)(2,1)}, bf16[1,256,128]{2,1,0:T(8,128)(2,1)}, u32[]{:S(2)}, u32[]{:S(2)}) %collective-permute-start.11) | collective-permute-done | bytes 65568 | tf_op jit(solution)/shard_map/ppermute | solution.py:383
  127.7 0.9 fusion.1
  128.6 1.3 collective-permute-done.6
  129.9 1.1 add_convert_fusion.1
  131.0 1.3 collective-permute-start.7
  132.4 2.4 %collective-permute-start.13 = (bf16[1,256,128]{2,1,0:T(8,128)(2,1)S(1)}, bf16[1,256,128]{2,1,0:T(8,128)(2,1)S(1)}, u32[]{:S(2)}, u32[]{:S(2)}) collective-permute-start(bf16[1,256,128]{2,1,0:T(8,128)(2,1)S(1)} %fusion.2), channel_id=1, source_target_pairs={{0,4},{1,5},{2,6},{3,7},{4,0},{5,1},{6,2},{7,3},{8,12},{9,13},{10,... | collective-permute-start | bytes 196616 | tf_op jit(solution)/shard_map/ppermute | solution.py:383
  134.8 3.9 %collective-permute-done.13 = bf16[1,256,128]{2,1,0:T(8,128)(2,1)S(1)} collective-permute-done((bf16[1,256,128]{2,1,0:T(8,128)(2,1)S(1)}, bf16[1,256,128]{2,1,0:T(8,128)(2,1)S(1)}, u32[]{:S(2)}, u32[]{:S(2)}) %collective-permute-start.13) | collective-permute-done | bytes 65568 | tf_op jit(solution)/shard_map/ppermute | solution.py:383
  138.7 0.5 collective-permute-start.14
  139.2 4.5 %collective-permute-done.14 = bf16[2,256,128]{2,1,0:T(8,128)(2,1)S(1)} collective-permute-done((bf16[2,256,128]{2,1,0:T(8,128)(2,1)S(1)}, bf16[2,256,128]{2,1,0:T(8,128)(2,1)S(1)}, u32[]{:S(2)}, u32[]{:S(2)}) %collective-permute-start.14) | collective-permute-done | bytes 131104 | tf_op jit(solution)/shard_map/ppermute | solution.py:383
  143.8 1.7 %collective-permute-start.15 = (bf16[4,256,128]{2,1,0:T(8,128)(2,1)S(1)}, bf16[4,256,128]{2,1,0:T(8,128)(2,1)S(1)}, u32[]{:S(2)}, u32[]{:S(2)}) collective-permute-start(bf16[4,256,128]{2,1,0:T(8,128)(2,1)S(1)} %pad_maximum_fusion.1.near_ref), channel_id=1, source_target_pairs={{0,1},{1,0},{2,3},{3,2},{4,5},{5,4},{6,7},{7,6},{8,9},{9,8},{10,11... | collective-permute-start | bytes 786440 | tf_op jit(solution)/shard_map/ppermute | solution.py:383
  145.4 0.5 collective-permute-start.8
  146.0 0.2 multiply_sine_fusion.1
  146.2 7.3 %collective-permute-done.8.arrived_ref = bf16[1,256,128]{2,1,0:T(8,128)(2,1)S(1)} collective-permute-done((bf16[1,256,128]{2,1,0:T(8,128)(2,1)S(1)}, bf16[1,256,128]{2,1,0:T(8,128)(2,1)S(1)}, u32[]{:S(2)}, u32[]{:S(2)}) %collective-permute-start.8) | collective-permute-done | bytes 65568 | tf_op jit(solution)/shard_map/ppermute | solution.py:383
  153.4 0.7 shard_map.116
  154.2 1.5 shard_map.118
  155.7 1.6 %all-to-all-done.2.in_ref = bf16[16,2,128,256]{3,2,1,0:T(8,128)(2,1)S(1)} async-done(((bf16[16,2,128,256]{3,2,1,0:T(8,128)(2,1)}), bf16[16,2,128,256]{3,2,1,0:T(8,128)(2,1)S(1)}, u32[]{:S(2)}, u32[]{:S(2)}) %all-to-all-start.2) | async-done | bytes 2097184 | tf_op jit(solution)/shard_map/all_to_all | solution.py:377
  157.3 1.9 %shard_map.117 = (bf16[1,128,4096]{2,1,0:T(8,128)(2,1)}, bf16[1,128,4096]{2,1,0:T(8,128)(2,1)}) custom-call(bf16[16,2,128,256]{3,2,1,0:T(8,128)(2,1)S(1)} %all-to-all-done.2.in_ref), custom_call_target="tpu_custom_call" | custom-call | tf_op jit(solution)/shard_map/pallas_call | solution.py:64
  (34 shorter events, 0.9 us)
Async XLA Ops:
  3.3 11.2 %copy-start = (bf16[1024,640]{1,0:T(8,128)(2,1)S(1)}, bf16[1024,640]{1,0:T(8,128)(2,1)}, u32[]{:S(2)}) copy-start(bf16[1024,640]{1,0:T(8,128)(2,1)} %cot_ref.2) | copy-start | bytes 3932164
  3.3 11.2 %copy-start.1 = (bf16[256,640]{1,0:T(8,128)(2,1)S(1)}, bf16[256,640]{1,0:T(8,128)(2,1)}, u32[]{:S(2)}) copy-start(bf16[256,640]{1,0:T(8,128)(2,1)} %weight_ref.1) | copy-start | bytes 983044
  3.3 61.7 %all-to-all-start = ((bf16[16,2,128,256]{3,2,1,0:T(8,128)(2,1)}), bf16[16,2,128,256]{3,2,1,0:T(8,128)(2,1)}, u32[]{:S(2)}, u32[]{:S(2)}) async-start(bf16[16,2,128,256]{3,2,1,0:T(8,128)(2,1)} %shard_map.111), calls=%async_computation | async-start | bytes 4194304 | tf_op jit(solution)/shard_map/all_to_all | solution.py:377
  14.4 12.0 %copy-start.2 = (s32[5]{0:T(128)S(1)}, s32[5]{0:T(128)}, u32[]{:S(2)}) copy-start(s32[5]{0:T(128)} %param.13) | copy-start | bytes 64
  15.4 7.6 %collective-permute-start = (bf16[4,128,256]{2,1,0:T(8,128)(2,1)S(1)}, bf16[4,128,256]{2,1,0:T(8,128)(2,1)S(1)}, u32[]{:S(2)}, u32[]{:S(2)}) collective-permute-start(bf16[4,128,256]{2,1,0:T(8,128)(2,1)S(1)} %get-tuple-element.28), channel_id=1, source_target_pairs={{0,2},{1,3},{2,0},{3,1},{4,6},{5,7},{6,4},{7,5},{8,10},{9,11},{10,... | collective-permute-start | bytes 786440 | tf_op jit(solution)/shard_map/ppermute | solution.py:383
  23.1 6.6 %collective-permute-start.1 = (bf16[2,128,256]{2,1,0:T(8,128)(2,1)S(1)}, bf16[2,128,256]{2,1,0:T(8,128)(2,1)S(1)}, u32[]{:S(2)}, u32[]{:S(2)}) collective-permute-start(bf16[2,128,256]{2,1,0:T(8,128)(2,1)S(1)} %slice.49), channel_id=1, source_target_pairs={{0,4},{1,5},{2,6},{3,7},{4,0},{5,1},{6,2},{7,3},{8,12},{9,13},{10,... | collective-permute-start | bytes 393224 | tf_op jit(solution)/shard_map/ppermute | solution.py:383
  29.7 4.4 %collective-permute-start.2 = (bf16[1,128,256]{2,1,0:T(8,128)(2,1)S(1)}, bf16[1,128,256]{2,1,0:T(8,128)(2,1)S(1)}, u32[]{:S(2)}, u32[]{:S(2)}) collective-permute-start(bf16[1,128,256]{2,1,0:T(8,128)(2,1)S(1)} %slice.51), channel_id=1, source_target_pairs={{0,1},{1,0},{2,3},{3,2},{4,5},{5,4},{6,7},{7,6},{8,9},{9,8},{10,11... | collective-permute-start | bytes 196616 | tf_op jit(solution)/shard_map/ppermute | solution.py:383
  35.4 5.8 %collective-permute-start.3 = (bf16[1,128,256]{2,1,0:T(8,128)(2,1)S(1)}, bf16[1,128,256]{2,1,0:T(8,128)(2,1)S(1)}, u32[]{:S(2)}, u32[]{:S(2)}) collective-permute-start(bf16[1,128,256]{2,1,0:T(8,128)(2,1)S(1)} %bitcast.19), channel_id=1, source_target_pairs={{0,4},{1,5},{2,6},{3,7},{4,0},{5,1},{6,2},{7,3},{8,12},{9,13},{10,... | collective-permute-start | bytes 196616 | tf_op jit(solution)/shard_map/ppermute | solution.py:383
  41.2 5.1 %collective-permute-start.4 = (bf16[2,128,256]{2,1,0:T(8,128)(2,1)S(1)}, bf16[2,128,256]{2,1,0:T(8,128)(2,1)S(1)}, u32[]{:S(2)}, u32[]{:S(2)}) collective-permute-start(bf16[2,128,256]{2,1,0:T(8,128)(2,1)S(1)} %pad_maximum_fusion.2), channel_id=1, source_target_pairs={{0,2},{1,3},{2,0},{3,1},{4,6},{5,7},{6,4},{7,5},{8,10},{9,11},{10,... | collective-permute-start | bytes 393224 | tf_op jit(solution)/shard_map/ppermute | solution.py:383
  46.3 10.0 %collective-permute-start.5 = (bf16[4,128,256]{2,1,0:T(8,128)(2,1)S(1)}, bf16[4,128,256]{2,1,0:T(8,128)(2,1)S(1)}, u32[]{:S(2)}, u32[]{:S(2)}) collective-permute-start(bf16[4,128,256]{2,1,0:T(8,128)(2,1)S(1)} %pad_maximum_fusion.near_ref), channel_id=1, source_target_pairs={{0,1},{1,0},{2,3},{3,2},{4,5},{5,4},{6,7},{7,6},{8,9},{9,8},{10,11... | collective-permute-start | bytes 786440 | tf_op jit(solution)/shard_map/ppermute | solution.py:383
  101.8 55.6 %all-to-all-start.2 = ((bf16[16,2,128,256]{3,2,1,0:T(8,128)(2,1)}), bf16[16,2,128,256]{3,2,1,0:T(8,128)(2,1)S(1)}, u32[]{:S(2)}, u32[]{:S(2)}) async-start(bf16[16,2,128,256]{3,2,1,0:T(8,128)(2,1)} %get-tuple-element.41), calls=%async_computation.2 | async-start | bytes 4194304 | tf_op jit(solution)/shard_map/all_to_all | solution.py:377
  108.2 6.6 %collective-permute-start.9 = (bf16[4,256,128]{2,1,0:T(8,128)(2,1)}, bf16[4,256,128]{2,1,0:T(8,128)(2,1)S(1)}, u32[]{:S(2)}, u32[]{:S(2)}) collective-permute-start(bf16[4,256,128]{2,1,0:T(8,128)(2,1)} %get-tuple-element.45), channel_id=1, source_target_pairs={{0,2},{1,3},{2,0},{3,1},{4,6},{5,7},{6,4},{7,5},{8,10},{9,11},{10,... | collective-permute-start | bytes 786440 | tf_op jit(solution)/shard_map/ppermute | solution.py:383
  115.8 6.6 %collective-permute-start.10 = (bf16[2,256,128]{2,1,0:T(8,128)(2,1)S(1)}, bf16[2,256,128]{2,1,0:T(8,128)(2,1)S(1)}, u32[]{:S(2)}, u32[]{:S(2)}) collective-permute-start(bf16[2,256,128]{2,1,0:T(8,128)(2,1)S(1)} %slice.57), channel_id=1, source_target_pairs={{0,4},{1,5},{2,6},{3,7},{4,0},{5,1},{6,2},{7,3},{8,12},{9,13},{10,... | collective-permute-start | bytes 393224 | tf_op jit(solution)/shard_map/ppermute | solution.py:383
  123.1 4.6 %collective-permute-start.11 = (bf16[1,256,128]{2,1,0:T(8,128)(2,1)}, bf16[1,256,128]{2,1,0:T(8,128)(2,1)}, u32[]{:S(2)}, u32[]{:S(2)}) collective-permute-start(bf16[1,256,128]{2,1,0:T(8,128)(2,1)} %slice.59), channel_id=1, source_target_pairs={{0,1},{1,0},{2,3},{3,2},{4,5},{5,4},{6,7},{7,6},{8,9},{9,8},{10,11... | collective-permute-start | bytes 196616 | tf_op jit(solution)/shard_map/ppermute | solution.py:383
  123.2 6.7 %collective-permute-start.6 = (bf16[4,256,128]{2,1,0:T(8,128)(2,1)}, bf16[4,256,128]{2,1,0:T(8,128)(2,1)}, u32[]{:S(2)}, u32[]{:S(2)}) collective-permute-start(bf16[4,256,128]{2,1,0:T(8,128)(2,1)} %get-tuple-element.40), channel_id=1, source_target_pairs={{0,2},{1,3},{2,0},{3,1},{4,6},{5,7},{6,4},{7,5},{8,10},{9,11},{10,... | collective-permute-start | bytes 786440 | tf_op jit(solution)/shard_map/ppermute | solution.py:383
  128.5 3.8 %collective-permute-start.12 = (bf16[256,128]{1,0:T(8,128)(2,1)S(1)}, bf16[256,128]{1,0:T(8,128)(2,1)S(1)}, u32[]{:S(2)}, u32[]{:S(2)}) collective-permute-start(bf16[256,128]{1,0:T(8,128)(2,1)S(1)} %fusion.1), channel_id=1, source_target_pairs={{0,128},{128,0},{1,129},{129,1},{2,130},{130,2},{3,131},{131,3},{4... | collective-permute-start | bytes 196616 | tf_op jit(solution)/shard_map/ppermute | solution.py:446
  131.0 8.1 %collective-permute-start.7 = (bf16[2,256,128]{2,1,0:T(8,128)(2,1)S(1)}, bf16[2,256,128]{2,1,0:T(8,128)(2,1)S(1)}, u32[]{:S(2)}, u32[]{:S(2)}) collective-permute-start(bf16[2,256,128]{2,1,0:T(8,128)(2,1)S(1)} %slice.53), channel_id=1, source_target_pairs={{0,4},{1,5},{2,6},{3,7},{4,0},{5,1},{6,2},{7,3},{8,12},{9,13},{10,... | collective-permute-start | bytes 393224 | tf_op jit(solution)/shard_map/ppermute | solution.py:383
  132.4 6.3 %collective-permute-start.13 = (bf16[1,256,128]{2,1,0:T(8,128)(2,1)S(1)}, bf16[1,256,128]{2,1,0:T(8,128)(2,1)S(1)}, u32[]{:S(2)}, u32[]{:S(2)}) collective-permute-start(bf16[1,256,128]{2,1,0:T(8,128)(2,1)S(1)} %fusion.2), channel_id=1, source_target_pairs={{0,4},{1,5},{2,6},{3,7},{4,0},{5,1},{6,2},{7,3},{8,12},{9,13},{10,... | collective-permute-start | bytes 196616 | tf_op jit(solution)/shard_map/ppermute | solution.py:383
  138.7 5.1 %collective-permute-start.14 = (bf16[2,256,128]{2,1,0:T(8,128)(2,1)S(1)}, bf16[2,256,128]{2,1,0:T(8,128)(2,1)S(1)}, u32[]{:S(2)}, u32[]{:S(2)}) collective-permute-start(bf16[2,256,128]{2,1,0:T(8,128)(2,1)S(1)} %pad_maximum_fusion.3), channel_id=1, source_target_pairs={{0,2},{1,3},{2,0},{3,1},{4,6},{5,7},{6,4},{7,5},{8,10},{9,11},{10,... | collective-permute-start | bytes 393224 | tf_op jit(solution)/shard_map/ppermute | solution.py:383
  143.8 10.4 %collective-permute-start.15 = (bf16[4,256,128]{2,1,0:T(8,128)(2,1)S(1)}, bf16[4,256,128]{2,1,0:T(8,128)(2,1)S(1)}, u32[]{:S(2)}, u32[]{:S(2)}) collective-permute-start(bf16[4,256,128]{2,1,0:T(8,128)(2,1)S(1)} %pad_maximum_fusion.1.near_ref), channel_id=1, source_target_pairs={{0,1},{1,0},{2,3},{3,2},{4,5},{5,4},{6,7},{7,6},{8,9},{9,8},{10,11... | collective-permute-start | bytes 786440 | tf_op jit(solution)/shard_map/ppermute | solution.py:383
  145.4 8.0 %collective-permute-start.8 = (bf16[1,256,128]{2,1,0:T(8,128)(2,1)S(1)}, bf16[1,256,128]{2,1,0:T(8,128)(2,1)S(1)}, u32[]{:S(2)}, u32[]{:S(2)}) collective-permute-start(bf16[1,256,128]{2,1,0:T(8,128)(2,1)S(1)} %get-tuple-element.46), channel_id=1, source_target_pairs={{0,1},{1,0},{2,3},{3,2},{4,5},{5,4},{6,7},{7,6},{8,9},{9,8},{10,11... | collective-permute-start | bytes 196616 | tf_op jit(solution)/shard_map/ppermute | solution.py:383
